TPU v7x, 32 devices: a whole 2x2x4 slice. The times are simulated.
32 devices in a mesh: groups: 2 (over y), sub: 4 (over z), rhs: 2 (over x), face: 2 (over core).
Axes of the slice: x: 2, y: 2, z: 4, core: 2. Of those that a mesh axis runs over, the one named last changes fastest.
Arguments:
- mortar_in: bfloat16 [1024, 64, 256], P(('groups', 'sub'), 'rhs'), parts along dimension 0, may hold values from -6 to 6
- pump_rate: float32 [128], P(('groups', 'rhs')), parts along dimension 0, may hold values from 4 to 16
- well_cell: int32 [128], P(('groups', 'rhs')), parts along dimension 0, may hold values from 0 to 131071
- face_owner: int32 [2048, 1], P(('groups', 'sub', 'face')), parts along dimension 0, may hold values from 0 to 3; in each aligned block of 128 rows (0 to 127, 128 to 255, ...) at most 64 rows name the same one
- face_slot: int32 [2048], P(('groups', 'sub', 'face')), parts along dimension 0, may hold values from 0 to 127
- face_scale: bfloat16 [2048, 256], P(('groups', 'sub', 'face')), parts along dimension 0, may hold values from 0.5 to 2
- section: int32 [8], P(('groups', 'sub')), parts along dimension 0, may hold values 0 or 1
- basis: bfloat16 [8, 256, 256], P(('groups', 'sub')), parts along dimension 0, may hold values from -0.375 to 0.375
- projection: bfloat16 [256, 256], replicated, may hold values from -0.375 to 0.375
Outputs:
- result: float32 [1024, 64, 256], P(('groups', 'sub', 'face'), 'rhs'), parts along dimension 0
There are 2 independent parts, one for each index of `groups`. A program takes and returns all parts, laid end to end along the dimension named above; an argument that names none is the same for every part. Nothing has to cross between parts.
Inputs may be any that keep to these rules, and one draw needn't show every extreme that they name: `face_owner`: among the 128 faces of one device no subdomain is named by more than 64 faces, a bound that some block reaches.
All inputs are finite; a program needn't handle non-finite values. No bound on the sum of `section` on one device may be relied on, other than what follows from the above.
Results may differ from a plain program's by a relative error of at most 0.004.
Values may be sent and summed in bfloat16 or wider, within the bound.
No kernel may reach another device: no remote copies, remote signals or barrier semaphores. Data moves between devices by JAX's collectives and lax.ppermute only.
A program may use at most 64 MiB of HBM per device.

v0:
```python
import functools

import jax
import jax.numpy as jnp
from jax import lax
from jax.experimental import pallas as pl
from jax.experimental.pallas import tpu as pltpu
from jax.sharding import PartitionSpec as P

ROW_TILE = 16
VMEM = pl.BlockSpec(memory_space=pltpu.VMEM)
HBM = pl.BlockSpec(memory_space=pltpu.HBM)
SMEM = pl.BlockSpec(memory_space=pltpu.SMEM)
MIB = 1024 * 1024
PREPARE_VMEM = 52


def prepare_kernel(
    subdomains, mortar_ref, owner_any, slot_any, scale_any, rate_ref, cell_ref, section_ref, *refs
):
    packs, (pumped_ref, owner_ref, slot_ref, scale_ref, sems) = refs[:subdomains], refs[subdomains:]
    blocks_own, columns, dof_count = pumped_ref.shape
    here = lax.axis_index("sub")
    first_block = lax.axis_index("face") * blocks_own
    fetches = [
        pltpu.make_async_copy(source, target, sems.at[i])
        for i, (source, target) in enumerate(
            [
                (owner_any, owner_ref),
                (slot_any, slot_ref),
                (scale_any, scale_ref),
                (mortar_ref.at[pl.ds(first_block, blocks_own)], pumped_ref),
            ]
        )
    ]
    for fetch in fetches:
        fetch.start()

    faces = owner_ref.shape[1]
    rows = packs[0].shape[0] - ROW_TILE
    sign = (1 - 2 * section_ref[0]).astype(jnp.float32)
    shifts = lax.broadcasted_iota(jnp.int32, (subdomains, faces), 0)
    owner_ids = lax.rem(here + shifts, subdomains)
    earlier = lax.broadcasted_iota(jnp.int32, (faces, faces), 0) < lax.broadcasted_iota(
        jnp.int32, (faces, faces), 1
    )
    for fetch in fetches[:3]:
        fetch.wait()
    named = owner_ids == owner_ref[...]
    rank = jnp.dot(
        named.astype(jnp.bfloat16), earlier.astype(jnp.bfloat16), preferred_element_type=jnp.float32
    )
    place = jnp.where(named, rank.astype(jnp.int32), -1)
    slots = slot_ref[...].astype(jnp.bfloat16)
    for shift in range(subdomains):
        hit = place[shift : shift + 1, :] == lax.broadcasted_iota(jnp.int32, (rows, faces), 0)
        hit = hit.astype(jnp.bfloat16)
        packed = jnp.dot(hit, scale_ref[...], preferred_element_type=jnp.float32) * sign
        listed = lax.dot_general(
            slots, hit, (((1,), (1,)), ((), ())), preferred_element_type=jnp.float32
        )
        meta = jnp.concatenate([listed, jnp.zeros((1, dof_count - rows), jnp.float32)], axis=1)
        meta = jnp.broadcast_to(meta, (ROW_TILE, dof_count))
        packs[shift][:rows, :] = packed.astype(jnp.bfloat16)
        packs[shift][rows:, :] = meta.astype(jnp.bfloat16)

    fetches[3].wait()
    base = here * (mortar_ref.shape[0]) + first_block
    for column in range(columns):
        block = lax.div(cell_ref[column], dof_count) - base
        dof = lax.rem(cell_ref[column], dof_count)

        @pl.when((block >= 0) & (block < blocks_own))
        def _():
            slab = slice(column // ROW_TILE * ROW_TILE, (column // ROW_TILE + 1) * ROW_TILE)
            shape = (ROW_TILE, dof_count)
            at_well = (lax.broadcasted_iota(jnp.int32, shape, 0) == column % ROW_TILE) & (
                lax.broadcasted_iota(jnp.int32, shape, 1) == dof
            )
            well = jnp.where(at_well, rate_ref[column], 0.0)
            pumped_ref[block, slab, :] = (pumped_ref[block, slab, :].astype(jnp.float32) + well).astype(
                jnp.bfloat16
            )


def apply_kernel(order, groups, tiles, *refs):
    subdomains = len(order)
    pumped_ref, projection_ref, own_ref = refs[:3]
    bases, refs = refs[3 : 3 + 4 * len(groups)], refs[3 + 4 * len(groups) :]
    packs, refs = refs[: 2 * subdomains], refs[2 * subdomains :]
    result_ref, weight_ref, basis_ref, scaled_ref, out_ref, sems = refs
    blocks_own, columns, dof_count = pumped_ref.shape
    face_id = lax.axis_index("face")

    def put(shift, array):
        if not isinstance(shift, int):
            shift = pl.multiple_of(shift * dof_count, dof_count)
        else:
            shift = shift * dof_count
        basis_ref[pl.ds(shift, dof_count), :] = array[0]

    put(0, own_ref)
    for at, (a, b, c) in enumerate(groups):
        first, first_swapped, second, second_swapped = bases[4 * at : 4 * at + 4]
        put(jnp.where(face_id == 0, a, b), first)
        put(jnp.where(face_id == 0, b, a), first_swapped)
        if c < subdomains:
            put(jnp.where(face_id == 0, subdomains, c), second)
            put(jnp.where(face_id == 0, c, subdomains), second_swapped)

    rows = packs[0].shape[0] - ROW_TILE
    block_ids = face_id * blocks_own + lax.broadcasted_iota(jnp.int32, (blocks_own, rows), 0)
    for at, s in enumerate(order):
        total = None
        for pack in packs[2 * at : 2 * at + 2]:
            slots = pack[rows:, :].astype(jnp.int32)[:1, :rows]
            part = jnp.dot(
                (slots == block_ids).astype(jnp.bfloat16), pack[:rows, :], preferred_element_type=jnp.float32
            )
            total = part if total is None else total + part
        weight_ref[s] = total

    tile_blocks = blocks_own // tiles
    copies = []
    for tile in range(tiles):
        at = slice(tile * tile_blocks, (tile + 1) * tile_blocks)
        values = pumped_ref[at].astype(jnp.float32)
        for s in range(subdomains):
            scaled = (values * weight_ref[s, at][:, None, :]).astype(jnp.bfloat16)
            scaled_ref[tile % 2, :, s * dof_count : (s + 1) * dof_count] = scaled.reshape(
                tile_blocks * columns, dof_count
            )
        total = jnp.dot(
            scaled_ref[tile % 2],
            basis_ref[: subdomains * dof_count, :],
            preferred_element_type=jnp.float32,
        )
        result = jnp.dot(
            total.astype(jnp.bfloat16), projection_ref[...], preferred_element_type=jnp.float32
        )
        out_ref[at] = result.reshape(tile_blocks, columns, dof_count)
        copies.append(pltpu.make_async_copy(out_ref.at[at], result_ref.at[at], sems.at[tile]))
        copies[-1].start()
    for copy in copies:
        copy.wait()


def on_device(
    mortar_in, pump_rate, well_cell, face_owner, face_slot, face_scale, section, basis, projection
):
    blocks_dev, cols_dev, dof_count = mortar_in.shape
    faces_dev = face_slot.shape[0]
    subdomains, halves = lax.axis_size("sub"), lax.axis_size("face")
    blocks_own = blocks_dev // halves
    capacity = max(2, 2 * faces_dev // subdomains)
    pack_rows = -(-capacity // ROW_TILE) * ROW_TILE + ROW_TILE

    *packs, pumped = pl.pallas_call(
        functools.partial(prepare_kernel, subdomains),
        out_shape=[jax.ShapeDtypeStruct((pack_rows, dof_count), jnp.bfloat16)] * subdomains
        + [jax.ShapeDtypeStruct((blocks_own, cols_dev, dof_count), jnp.bfloat16)],
        in_specs=[HBM] * 4 + [SMEM] * 3,
        out_specs=[VMEM] * (subdomains + 1),
        scratch_shapes=[
            pltpu.VMEM((1, faces_dev), jnp.int32),
            pltpu.VMEM((1, faces_dev), jnp.int32),
            pltpu.VMEM((faces_dev, dof_count), jnp.bfloat16),
            pltpu.SemaphoreType.DMA((4,)),
        ],
        compiler_params=pltpu.CompilerParams(vmem_limit_bytes=PREPARE_VMEM * MIB),
        cost_estimate=pl.CostEstimate(flops=4_000_000_000, bytes_accessed=8 * MIB, transcendentals=0),
        name="prepare",
    )(
        mortar_in,
        face_owner.reshape(1, faces_dev),
        face_slot.reshape(1, faces_dev),
        face_scale,
        pump_rate,
        well_cell,
        section,
    )

    def flat(sub, face):
        return (sub % subdomains) * halves + face

    swap = [(i, i ^ 1) for i in range(halves)]
    shifts = list(range(1, subdomains))
    if len(shifts) > 1:
        shifts[0], shifts[1] = shifts[1], shifts[0]
    groups = [tuple(shifts[i : i + 3]) for i in range(0, len(shifts), 3)]
    groups = [g + (subdomains,) * (3 - len(g)) for g in groups]
    moved = []
    for a, b, c in groups:
        for send in [(0, a), (1, b)], [(1, c)]:
            pairs = [
                (flat(s, face), flat(s + shift, face))
                for s in range(subdomains)
                for face, shift in send
                if shift < subdomains
            ]
            moved.append(lax.ppermute(basis, ("sub", "face"), pairs) if pairs else basis)
    weights = [packs[0]]
    for shift in shifts:
        ring = [(i, (i + shift) % subdomains) for i in range(subdomains)]
        weights.append(lax.ppermute(packs[shift], "sub", ring))
    own_swapped = lax.ppermute(packs[0], "face", swap)
    moved, weights = lax.optimization_barrier((moved, weights))
    bases, pairs = [], [packs[0], own_swapped]
    for array in moved:
        bases += [array, lax.ppermute(array, "face", swap)]
    for array in weights[1:]:
        pairs += [array, lax.ppermute(array, "face", swap)]
    order = [0] + shifts

    tiles = 4
    operands = [pumped, projection, basis, *bases, *pairs]
    return pl.pallas_call(
        functools.partial(apply_kernel, order, groups, tiles),
        out_shape=jax.ShapeDtypeStruct((blocks_own, cols_dev, dof_count), jnp.float32),
        in_specs=[VMEM] * len(operands),
        out_specs=HBM,
        scratch_shapes=[
            pltpu.VMEM((subdomains, blocks_own, dof_count), jnp.float32),
            pltpu.VMEM(((subdomains + 1) * dof_count, dof_count), jnp.bfloat16),
            pltpu.VMEM((2, blocks_own // tiles * cols_dev, subdomains * dof_count), jnp.bfloat16),
            pltpu.VMEM((blocks_own, cols_dev, dof_count), jnp.float32),
            pltpu.SemaphoreType.DMA((tiles,)),
        ],
        compiler_params=pltpu.CompilerParams(vmem_limit_bytes=48 * MIB),
        name="apply_blocks",
    )(*operands)


def solution(mesh):
    in_specs = (
        P(("groups", "sub"), "rhs", None),
        P(("groups", "rhs")),
        P(("groups", "rhs")),
        P(("groups", "sub", "face"), None),
        P(("groups", "sub", "face")),
        P(("groups", "sub", "face"), None),
        P(("groups", "sub")),
        P(("groups", "sub"), None, None),
        P(),
    )
    out_specs = P(("groups", "sub", "face"), "rhs", None)
    return jax.shard_map(
        on_device, mesh=mesh, in_specs=in_specs, out_specs=out_specs, check_vma=False
    )
```

profile of v0, /device:TPU:0, one launch (start us, length us, event | category | flops | bytes accessed | tf_op | source)
XLA Modules:
  0.0 24.9 jit_solution(6360140004007675163)
XLA Ops:
  0.0 4.0 %collective-permute-start = (bf16[1,256,256]{2,1,0:T(8,128)(2,1)}, bf16[1,256,256]{2,1,0:T(8,128)(2,1)S(1)}, u32[]{:S(2)}, u32[]{:S(2)}) collective-permute-start(bf16[1,256,256]{2,1,0:T(8,128)(2,1)} %refs_2_.1), channel_id=1, source_target_pairs={{0,8},{1,5},{4,12},{5,9},{8,0},{9,13},{12,4},{13,1},{2,10},{3,7},{... | collective-permute-start | bytes 393224 | tf_op jit(solution)/shard_map/ppermute | solution.py:201
  4.0 0.7 %collective-permute-start.1 = (bf16[1,256,256]{2,1,0:T(8,128)(2,1)}, bf16[1,256,256]{2,1,0:T(8,128)(2,1)S(1)}, u32[]{:S(2)}, u32[]{:S(2)}) collective-permute-start(bf16[1,256,256]{2,1,0:T(8,128)(2,1)} %refs_2_.1), channel_id=1, source_target_pairs={{1,13},{5,1},{9,5},{13,9},{3,15},{7,3},{11,7},{15,11},{17,29},{21,... | collective-permute-start | bytes 393224 | tf_op jit(solution)/shard_map/ppermute | solution.py:201
  5.3 0.0 copy-start.2
  5.4 0.8 %copy-done.2 = bf16[128,256]{1,0:T(8,128)(2,1)S(1)} copy-done((bf16[128,256]{1,0:T(8,128)(2,1)S(1)}, bf16[128,256]{1,0:T(8,128)(2,1)}, u32[]{:S(2)}) %copy-start.2) | copy-done | bytes 65560
  6.2 0.0 copy-start.3
  6.2 0.7 %copy-done.3 = s32[128,1]{0,1:T(1,128)S(1)} copy-done((s32[128,1]{0,1:T(1,128)S(1)}, s32[128,1]{0,1:T(1,128)}, u32[]{:S(2)}) %copy-start.3) | copy-done | bytes 536
  6.8 0.0 copy-start.4
  6.8 0.7 %copy-done.4 = s32[128]{0:T(128)S(1)} copy-done((s32[128]{0:T(128)S(1)}, s32[128]{0:T(128)}, u32[]{:S(2)}) %copy-start.4) | copy-done | bytes 536
  7.5 0.0 copy-start.5
  7.5 0.7 %copy-done.5 = f32[32]{0:T(128)S(1)} copy-done((f32[32]{0:T(128)S(1)}, f32[32]{0:T(128)}, u32[]{:S(2)}) %copy-start.5) | copy-done | bytes 152
  8.2 0.0 copy-start.6
  8.2 0.7 %copy-done.6 = s32[32]{0:T(128)S(1)} copy-done((s32[32]{0:T(128)S(1)}, s32[32]{0:T(128)}, u32[]{:S(2)}) %copy-start.6) | copy-done | bytes 152
  8.8 0.0 copy-start
  8.8 0.0 copy-start.1
  8.8 2.2 %prepare.1 = (bf16[80,256]{1,0:T(8,128)(2,1)S(1)}, bf16[80,256]{1,0:T(8,128)(2,1)S(1)}, bf16[80,256]{1,0:T(8,128)(2,1)S(1)}, bf16[80,256]{1,0:T(8,128)(2,1)S(1)}, bf16[64,32,256]{2,1,0:T(8,128)(2,1)S(1)}) custom-call(bf16[128,32,256]{2,1,0:T(8,128)(2,1)} %mortar_ref.1, s32[1,128]{1,0:T(1,128)S(1)} %bitcast.2, s32[1,128]{1,0:T(1,128)S(1)} %bitcast.3, ...), custom_call_target="tpu_custom_call" | custom-call | flops 4000000000 | bytes 8388608 | tf_op jit(solution)/shard_map/prepare/pallas_call | solution.py:158
  11.1 0.1 collective-permute-start.2
  11.2 1.6 %collective-permute-start.3 = (bf16[80,256]{1,0:T(8,128)(2,1)S(1)}, bf16[80,256]{1,0:T(8,128)(2,1)S(1)}, u32[]{:S(2)}, u32[]{:S(2)}) collective-permute-start(bf16[80,256]{1,0:T(8,128)(2,1)S(1)} %get-tuple-element.18), channel_id=1, source_target_pairs={{0,4},{4,8},{8,12},{12,0},{1,5},{5,9},{9,13},{13,1},{2,6},{6,10},{... | collective-permute-start | bytes 122888 | tf_op jit(solution)/shard_map/ppermute | solution.py:205
  12.8 2.2 %collective-permute-start.4 = (bf16[80,256]{1,0:T(8,128)(2,1)S(1)}, bf16[80,256]{1,0:T(8,128)(2,1)S(1)}, u32[]{:S(2)}, u32[]{:S(2)}) collective-permute-start(bf16[80,256]{1,0:T(8,128)(2,1)S(1)} %get-tuple-element.19), channel_id=1, source_target_pairs={{0,12},{4,0},{8,4},{12,8},{1,13},{5,1},{9,5},{13,9},{2,14},{6,2},{... | collective-permute-start | bytes 122888 | tf_op jit(solution)/shard_map/ppermute | solution.py:205
  15.0 2.3 %collective-permute-done.2.refs_9_ = bf16[80,256]{1,0:T(8,128)(2,1)S(1)} collective-permute-done((bf16[80,256]{1,0:T(8,128)(2,1)S(1)}, bf16[80,256]{1,0:T(8,128)(2,1)S(1)}, u32[]{:S(2)}, u32[]{:S(2)}) %collective-permute-start.2) | collective-permute-done | bytes 40992 | tf_op jit(solution)/shard_map/ppermute | solution.py:205
  17.3 0.0 collective-permute-done.3.refs_11_
  17.3 0.0 collective-permute-done.4.refs_13_
  17.3 0.0 collective-permute-done.refs_3_
  17.3 0.0 collective-permute-done.1.refs_5_
  17.4 1.1 %collective-permute-start.5 = (bf16[1,256,256]{2,1,0:T(8,128)(2,1)S(1)}, bf16[1,256,256]{2,1,0:T(8,128)(2,1)S(1)}, u32[]{:S(2)}, u32[]{:S(2)}) collective-permute-start(bf16[1,256,256]{2,1,0:T(8,128)(2,1)S(1)} %collective-permute-done.refs_3_), channel_id=1, source_target_pairs={{0,1},{1,0},{2,3},{3,2},{4,5},{5,4},{6,7},{7,6},{8,9},{9,8},{10,11... | collective-permute-start | bytes 393224 | tf_op jit(solution)/shard_map/ppermute | solution.py:210
  18.4 0.1 collective-permute-start.6
  18.5 0.4 %collective-permute-start.7 = (bf16[80,256]{1,0:T(8,128)(2,1)S(1)}, bf16[80,256]{1,0:T(8,128)(2,1)S(1)}, u32[]{:S(2)}, u32[]{:S(2)}) collective-permute-start(bf16[80,256]{1,0:T(8,128)(2,1)S(1)} %get-tuple-element.16.refs_7_), channel_id=1, source_target_pairs={{0,1},{1,0},{2,3},{3,2},{4,5},{5,4},{6,7},{7,6},{8,9},{9,8},{10,11... | collective-permute-start | bytes 122888 | tf_op jit(solution)/shard_map/ppermute | solution.py:206
  18.9 0.1 collective-permute-start.8
  19.0 0.4 %collective-permute-start.9 = (bf16[80,256]{1,0:T(8,128)(2,1)S(1)}, bf16[80,256]{1,0:T(8,128)(2,1)S(1)}, u32[]{:S(2)}, u32[]{:S(2)}) collective-permute-start(bf16[80,256]{1,0:T(8,128)(2,1)S(1)} %collective-permute-done.3.refs_11_), channel_id=1, source_target_pairs={{0,1},{1,0},{2,3},{3,2},{4,5},{5,4},{6,7},{7,6},{8,9},{9,8},{10,11... | collective-permute-start | bytes 122888 | tf_op jit(solution)/shard_map/ppermute | solution.py:212
  19.4 0.4 %collective-permute-done.7.refs_8_ = bf16[80,256]{1,0:T(8,128)(2,1)S(1)} collective-permute-done((bf16[80,256]{1,0:T(8,128)(2,1)S(1)}, bf16[80,256]{1,0:T(8,128)(2,1)S(1)}, u32[]{:S(2)}, u32[]{:S(2)}) %collective-permute-start.7) | collective-permute-done | bytes 40992 | tf_op jit(solution)/shard_map/ppermute | solution.py:206
  19.8 0.3 %collective-permute-start.10 = (bf16[80,256]{1,0:T(8,128)(2,1)S(1)}, bf16[80,256]{1,0:T(8,128)(2,1)S(1)}, u32[]{:S(2)}, u32[]{:S(2)}) collective-permute-start(bf16[80,256]{1,0:T(8,128)(2,1)S(1)} %collective-permute-done.4.refs_13_), channel_id=1, source_target_pairs={{0,1},{1,0},{2,3},{3,2},{4,5},{5,4},{6,7},{7,6},{8,9},{9,8},{10,11... | collective-permute-start | bytes 122888 | tf_op jit(solution)/shard_map/ppermute | solution.py:212
  20.2 0.0 collective-permute-done.8.refs_10_
  20.2 0.2 collective-permute-done.9.refs_12_
  20.3 0.7 %collective-permute-done.10.refs_14_ = bf16[80,256]{1,0:T(8,128)(2,1)S(1)} collective-permute-done((bf16[80,256]{1,0:T(8,128)(2,1)S(1)}, bf16[80,256]{1,0:T(8,128)(2,1)S(1)}, u32[]{:S(2)}, u32[]{:S(2)}) %collective-permute-start.10) | collective-permute-done | bytes 40992 | tf_op jit(solution)/shard_map/ppermute | solution.py:212
  21.1 0.0 collective-permute-done.5.refs_4_
  21.1 0.0 collective-permute-done.6.refs_6_
  21.1 0.0 copy-done
  21.1 0.0 copy-done.1
  21.1 3.8 %apply_blocks.1 = f32[64,32,256]{2,1,0:T(8,128)} custom-call(bf16[64,32,256]{2,1,0:T(8,128)(2,1)S(1)} %get-tuple-element.15.refs_0_, bf16[256,256]{1,0:T(8,128)(2,1)S(1)} %copy-done, bf16[1,256,256]{2,1,0:T(8,128)(2,1)S(1)} %copy-done.1, bf16[1,256,256]{2,1,0:T(8,128)(2,1)S(1)} %collective-permute-done.refs_3_, ...), custom_call_target="tpu_custom_call" | custom-call | tf_op jit(solution)/shard_map/apply_blocks/pallas_call | solution.py:217
Async XLA Ops:
  0.0 17.3 %collective-permute-start = (bf16[1,256,256]{2,1,0:T(8,128)(2,1)}, bf16[1,256,256]{2,1,0:T(8,128)(2,1)S(1)}, u32[]{:S(2)}, u32[]{:S(2)}) collective-permute-start(bf16[1,256,256]{2,1,0:T(8,128)(2,1)} %refs_2_.1), channel_id=1, source_target_pairs={{0,8},{1,5},{4,12},{5,9},{8,0},{9,13},{12,4},{13,1},{2,10},{3,7},{... | collective-permute-start | bytes 393224 | tf_op jit(solution)/shard_map/ppermute | solution.py:201
  4.0 13.3 %collective-permute-start.1 = (bf16[1,256,256]{2,1,0:T(8,128)(2,1)}, bf16[1,256,256]{2,1,0:T(8,128)(2,1)S(1)}, u32[]{:S(2)}, u32[]{:S(2)}) collective-permute-start(bf16[1,256,256]{2,1,0:T(8,128)(2,1)} %refs_2_.1), channel_id=1, source_target_pairs={{1,13},{5,1},{9,5},{13,9},{3,15},{7,3},{11,7},{15,11},{17,29},{21,... | collective-permute-start | bytes 393224 | tf_op jit(solution)/shard_map/ppermute | solution.py:201
  5.3 0.8 %copy-start.2 = (bf16[128,256]{1,0:T(8,128)(2,1)S(1)}, bf16[128,256]{1,0:T(8,128)(2,1)}, u32[]{:S(2)}) copy-start(bf16[128,256]{1,0:T(8,128)(2,1)} %scale_any.1) | copy-start | bytes 196612
  6.2 0.7 %copy-start.3 = (s32[128,1]{0,1:T(1,128)S(1)}, s32[128,1]{0,1:T(1,128)}, u32[]{:S(2)}) copy-start(s32[128,1]{0,1:T(1,128)} %param.12) | copy-start | bytes 1540
  6.8 0.7 %copy-start.4 = (s32[128]{0:T(128)S(1)}, s32[128]{0:T(128)}, u32[]{:S(2)}) copy-start(s32[128]{0:T(128)} %param.13) | copy-start | bytes 1540
  7.5 0.7 %copy-start.5 = (f32[32]{0:T(128)S(1)}, f32[32]{0:T(128)}, u32[]{:S(2)}) copy-start(f32[32]{0:T(128)} %rate_ref.1) | copy-start | bytes 388
  8.2 0.7 %copy-start.6 = (s32[32]{0:T(128)S(1)}, s32[32]{0:T(128)}, u32[]{:S(2)}) copy-start(s32[32]{0:T(128)} %cell_ref.1) | copy-start | bytes 388
  8.8 12.2 %copy-start = (bf16[256,256]{1,0:T(8,128)(2,1)S(1)}, bf16[256,256]{1,0:T(8,128)(2,1)}, u32[]{:S(2)}) copy-start(bf16[256,256]{1,0:T(8,128)(2,1)} %refs_1_.1) | copy-start | bytes 393220
  8.8 12.3 %copy-start.1 = (bf16[1,256,256]{2,1,0:T(8,128)(2,1)S(1)}, bf16[1,256,256]{2,1,0:T(8,128)(2,1)}, u32[]{:S(2)}) copy-start(bf16[1,256,256]{2,1,0:T(8,128)(2,1)} %refs_2_.1) | copy-start | bytes 393220
  11.1 6.3 %collective-permute-start.2 = (bf16[80,256]{1,0:T(8,128)(2,1)S(1)}, bf16[80,256]{1,0:T(8,128)(2,1)S(1)}, u32[]{:S(2)}, u32[]{:S(2)}) collective-permute-start(bf16[80,256]{1,0:T(8,128)(2,1)S(1)} %get-tuple-element.17), channel_id=1, source_target_pairs={{0,8},{4,12},{8,0},{12,4},{1,9},{5,13},{9,1},{13,5},{2,10},{6,14},... | collective-permute-start | bytes 122888 | tf_op jit(solution)/shard_map/ppermute | solution.py:205
  11.2 6.2 %collective-permute-start.3 = (bf16[80,256]{1,0:T(8,128)(2,1)S(1)}, bf16[80,256]{1,0:T(8,128)(2,1)S(1)}, u32[]{:S(2)}, u32[]{:S(2)}) collective-permute-start(bf16[80,256]{1,0:T(8,128)(2,1)S(1)} %get-tuple-element.18), channel_id=1, source_target_pairs={{0,4},{4,8},{8,12},{12,0},{1,5},{5,9},{9,13},{13,1},{2,6},{6,10},{... | collective-permute-start | bytes 122888 | tf_op jit(solution)/shard_map/ppermute | solution.py:205
  12.8 4.6 %collective-permute-start.4 = (bf16[80,256]{1,0:T(8,128)(2,1)S(1)}, bf16[80,256]{1,0:T(8,128)(2,1)S(1)}, u32[]{:S(2)}, u32[]{:S(2)}) collective-permute-start(bf16[80,256]{1,0:T(8,128)(2,1)S(1)} %get-tuple-element.19), channel_id=1, source_target_pairs={{0,12},{4,0},{8,4},{12,8},{1,13},{5,1},{9,5},{13,9},{2,14},{6,2},{... | collective-permute-start | bytes 122888 | tf_op jit(solution)/shard_map/ppermute | solution.py:205
  17.4 3.7 %collective-permute-start.5 = (bf16[1,256,256]{2,1,0:T(8,128)(2,1)S(1)}, bf16[1,256,256]{2,1,0:T(8,128)(2,1)S(1)}, u32[]{:S(2)}, u32[]{:S(2)}) collective-permute-start(bf16[1,256,256]{2,1,0:T(8,128)(2,1)S(1)} %collective-permute-done.refs_3_), channel_id=1, source_target_pairs={{0,1},{1,0},{2,3},{3,2},{4,5},{5,4},{6,7},{7,6},{8,9},{9,8},{10,11... | collective-permute-start | bytes 393224 | tf_op jit(solution)/shard_map/ppermute | solution.py:210
  18.4 2.6 %collective-permute-start.6 = (bf16[1,256,256]{2,1,0:T(8,128)(2,1)S(1)}, bf16[1,256,256]{2,1,0:T(8,128)(2,1)S(1)}, u32[]{:S(2)}, u32[]{:S(2)}) collective-permute-start(bf16[1,256,256]{2,1,0:T(8,128)(2,1)S(1)} %collective-permute-done.1.refs_5_), channel_id=1, source_target_pairs={{0,1},{1,0},{2,3},{3,2},{4,5},{5,4},{6,7},{7,6},{8,9},{9,8},{10,11... | collective-permute-start | bytes 393224 | tf_op jit(solution)/shard_map/ppermute | solution.py:210
  18.5 1.3 %collective-permute-start.7 = (bf16[80,256]{1,0:T(8,128)(2,1)S(1)}, bf16[80,256]{1,0:T(8,128)(2,1)S(1)}, u32[]{:S(2)}, u32[]{:S(2)}) collective-permute-start(bf16[80,256]{1,0:T(8,128)(2,1)S(1)} %get-tuple-element.16.refs_7_), channel_id=1, source_target_pairs={{0,1},{1,0},{2,3},{3,2},{4,5},{5,4},{6,7},{7,6},{8,9},{9,8},{10,11... | collective-permute-start | bytes 122888 | tf_op jit(solution)/shard_map/ppermute | solution.py:206
  18.9 1.2 %collective-permute-start.8 = (bf16[80,256]{1,0:T(8,128)(2,1)S(1)}, bf16[80,256]{1,0:T(8,128)(2,1)S(1)}, u32[]{:S(2)}, u32[]{:S(2)}) collective-permute-start(bf16[80,256]{1,0:T(8,128)(2,1)S(1)} %collective-permute-done.2.refs_9_), channel_id=1, source_target_pairs={{0,1},{1,0},{2,3},{3,2},{4,5},{5,4},{6,7},{7,6},{8,9},{9,8},{10,11... | collective-permute-start | bytes 122888 | tf_op jit(solution)/shard_map/ppermute | solution.py:212
  19.0 1.3 %collective-permute-start.9 = (bf16[80,256]{1,0:T(8,128)(2,1)S(1)}, bf16[80,256]{1,0:T(8,128)(2,1)S(1)}, u32[]{:S(2)}, u32[]{:S(2)}) collective-permute-start(bf16[80,256]{1,0:T(8,128)(2,1)S(1)} %collective-permute-done.3.refs_11_), channel_id=1, source_target_pairs={{0,1},{1,0},{2,3},{3,2},{4,5},{5,4},{6,7},{7,6},{8,9},{9,8},{10,11... | collective-permute-start | bytes 122888 | tf_op jit(solution)/shard_map/ppermute | solution.py:212
  19.8 1.2 %collective-permute-start.10 = (bf16[80,256]{1,0:T(8,128)(2,1)S(1)}, bf16[80,256]{1,0:T(8,128)(2,1)S(1)}, u32[]{:S(2)}, u32[]{:S(2)}) collective-permute-start(bf16[80,256]{1,0:T(8,128)(2,1)S(1)} %collective-permute-done.4.refs_13_), channel_id=1, source_target_pairs={{0,1},{1,0},{2,3},{3,2},{4,5},{5,4},{6,7},{7,6},{8,9},{9,8},{10,11... | collective-permute-start | bytes 122888 | tf_op jit(solution)/shard_map/ppermute | solution.py:212
where the time goes:
time: 25.1 us; the launch traced here: 24.9 us
  starting transfers between devices  11.1 us (44%)
  Pallas kernels  6.03 us (24%)
  waiting for transfers between devices  3.59 us (14%)
  local copies, waits for them, and re-layouts  3.46 us (14%)
  between operations  0.72 us (3%)
    ppermute x2, starting transfers between devices, on_device(): lax.ppermute(basis, ('sub', 'face'), pairs)  4.69 us
    ppermute x3, starting transfers between devices, on_device(): weights.append(lax.ppermute(packs[shift], 'sub', ring))  3.95 us
    pallas_call x1, Pallas kernels, on_device(): pl.pallas_call(functools.partial(apply_kernel, order, groups, tiles), out...  3.78 us
    unnamed x14, local copies, waits for them, and re-layouts  3.46 us
    ppermute x3, waiting for transfers between devices, on_device(): weights.append(lax.ppermute(packs[shift], 'sub', ring))  2.3 us
    pallas_call x1, Pallas kernels, on_device(): pl.pallas_call(functools.partial(prepare_kernel, subdomains), out_shape=[...  2.25 us
    ppermute x2, starting transfers between devices, on_device(): bases += [array, lax.ppermute(array, 'face', swap)]  1.15 us
    ppermute x3, waiting for transfers between devices, on_device(): pairs += [array, lax.ppermute(array, 'face', swap)]  0.89 us
  transfers between devices with their start and end apart: 11, of which 4 were waited for; matrix products, arithmetic and copies ran while one was open for 0% of the time, Pallas kernels for 9%

commit v1 on v0

v1 whole, which is shorter than its diff:
```python
import functools

import jax
import jax.numpy as jnp
from jax import lax
from jax.experimental import pallas as pl
from jax.experimental.pallas import tpu as pltpu
from jax.sharding import PartitionSpec as P

ROW_TILE = 16
VMEM = pl.BlockSpec(memory_space=pltpu.VMEM)
HBM = pl.BlockSpec(memory_space=pltpu.HBM)
SMEM = pl.BlockSpec(memory_space=pltpu.SMEM)
MIB = 1024 * 1024


def pack_kernel(owner_ref, slot_ref, scale_ref, section_ref, packs_ref):
    subdomains, rows, dof_count = packs_ref.shape
    rows -= ROW_TILE
    faces = owner_ref.shape[1]
    sign = (1 - 2 * section_ref[0]).astype(jnp.float32)
    named = lax.broadcasted_iota(jnp.int32, (subdomains, faces), 0) == owner_ref[...]
    earlier = lax.broadcasted_iota(jnp.int32, (faces, faces), 0) < lax.broadcasted_iota(
        jnp.int32, (faces, faces), 1
    )
    rank = jnp.dot(
        named.astype(jnp.bfloat16), earlier.astype(jnp.bfloat16), preferred_element_type=jnp.float32
    )
    place = jnp.where(named, rank.astype(jnp.int32), -1)
    slots = slot_ref[...].astype(jnp.bfloat16)
    for owner in range(subdomains):
        hit = place[owner : owner + 1, :] == lax.broadcasted_iota(jnp.int32, (rows, faces), 0)
        hit = hit.astype(jnp.bfloat16)
        packed = jnp.dot(hit, scale_ref[...], preferred_element_type=jnp.float32) * sign
        listed = lax.dot_general(
            slots, hit, (((1,), (1,)), ((), ())), preferred_element_type=jnp.float32
        )
        meta = jnp.concatenate([listed, jnp.zeros((1, dof_count - rows), jnp.float32)], axis=1)
        meta = jnp.broadcast_to(meta, (ROW_TILE, dof_count))
        packs_ref[owner, :rows, :] = packed.astype(jnp.bfloat16)
        packs_ref[owner, rows:, :] = meta.astype(jnp.bfloat16)


def apply_kernel(groups, tiles, *refs):
    pumped_ref, projection_ref, own_ref = refs[:3]
    bases, refs = refs[3 : 3 + 4 * len(groups)], refs[3 + 4 * len(groups) :]
    packs, (result_ref, weight_ref, basis_ref, scaled_ref, out_ref, sems) = refs[:2], refs[2:]
    blocks_own, columns, dof_count = pumped_ref.shape
    subdomains = weight_ref.shape[0]
    face_id = lax.axis_index("face")
    sub_id = lax.axis_index("sub")

    def put(shift, array):
        source = jnp.where(shift < subdomains, lax.rem(sub_id + subdomains - shift, subdomains), subdomains)
        basis_ref[pl.ds(pl.multiple_of(source * dof_count, dof_count), dof_count), :] = array[0]

    put(jnp.int32(0), own_ref)
    for at, (a, b, c) in enumerate(groups):
        first, first_swapped, second, second_swapped = bases[4 * at : 4 * at + 4]
        put(jnp.where(face_id == 0, a, b), first)
        put(jnp.where(face_id == 0, b, a), first_swapped)
        if c < subdomains:
            put(jnp.where(face_id == 0, subdomains, c), second)
            put(jnp.where(face_id == 0, c, subdomains), second_swapped)

    rows = packs[0].shape[1] - ROW_TILE
    block_ids = face_id * blocks_own + lax.broadcasted_iota(jnp.int32, (blocks_own, rows), 0)
    for s in range(subdomains):
        total = None
        for pack in packs:
            slots = pack[s, rows:, :].astype(jnp.int32)[:1, :rows]
            part = jnp.dot(
                (slots == block_ids).astype(jnp.bfloat16), pack[s, :rows, :], preferred_element_type=jnp.float32
            )
            total = part if total is None else total + part
        weight_ref[s] = total

    tile_blocks = blocks_own // tiles
    copies = []
    for tile in range(tiles):
        at = slice(tile * tile_blocks, (tile + 1) * tile_blocks)
        values = pumped_ref[at].astype(jnp.float32)
        for s in range(subdomains):
            scaled = (values * weight_ref[s, at][:, None, :]).astype(jnp.bfloat16)
            scaled_ref[tile % 2, :, s * dof_count : (s + 1) * dof_count] = scaled.reshape(
                tile_blocks * columns, dof_count
            )
        total = jnp.dot(
            scaled_ref[tile % 2],
            basis_ref[: subdomains * dof_count, :],
            preferred_element_type=jnp.float32,
        )
        result = jnp.dot(
            total.astype(jnp.bfloat16), projection_ref[...], preferred_element_type=jnp.float32
        )
        out_ref[at] = result.reshape(tile_blocks, columns, dof_count)
        copies.append(pltpu.make_async_copy(out_ref.at[at], result_ref.at[at], sems.at[tile]))
        copies[-1].start()
    for copy in copies:
        copy.wait()


def on_device(
    mortar_in, pump_rate, well_cell, face_owner, face_slot, face_scale, section, basis, projection
):
    blocks_dev, cols_dev, dof_count = mortar_in.shape
    faces_dev = face_slot.shape[0]
    subdomains, halves = lax.axis_size("sub"), lax.axis_size("face")
    blocks_own = blocks_dev // halves
    capacity = max(2, 2 * faces_dev // subdomains)
    pack_rows = -(-capacity // ROW_TILE) * ROW_TILE + ROW_TILE

    packs = pl.pallas_call(
        pack_kernel,
        out_shape=jax.ShapeDtypeStruct((subdomains, pack_rows, dof_count), jnp.bfloat16),
        in_specs=[VMEM, VMEM, VMEM, SMEM],
        out_specs=VMEM,
        cost_estimate=pl.CostEstimate(flops=4_000_000_000, bytes_accessed=8 * MIB, transcendentals=0),
        name="pack_weights",
    )(face_owner.reshape(1, faces_dev), face_slot.reshape(1, faces_dev), face_scale, section)

    first_block = lax.axis_index("face") * blocks_own
    mine = lax.dynamic_slice_in_dim(mortar_in, first_block, blocks_own, 0)
    block_ids = lax.axis_index("sub") * blocks_dev + first_block + jnp.arange(blocks_own, dtype=jnp.int32)
    cell = block_ids[:, None, None] * dof_count + jnp.arange(dof_count, dtype=jnp.int32)[None, None, :]
    wells = jnp.where(cell == well_cell[None, :, None], pump_rate[None, :, None], 0.0)
    pumped = (mine.astype(jnp.float32) + wells).astype(jnp.bfloat16)

    def flat(sub, face):
        return (sub % subdomains) * halves + face

    swap = [(i, i ^ 1) for i in range(halves)]
    shifts = list(range(1, subdomains))
    if len(shifts) > 1:
        shifts[0], shifts[1] = shifts[1], shifts[0]
    groups = [tuple(shifts[i : i + 3]) for i in range(0, len(shifts), 3)]
    groups = [g + (subdomains,) * (3 - len(g)) for g in groups]
    moved = []
    for a, b, c in groups:
        for send in [(0, a), (1, b)], [(1, c)]:
            pairs = [
                (flat(s, face), flat(s + shift, face))
                for s in range(subdomains)
                for face, shift in send
                if shift < subdomains
            ]
            moved.append(lax.ppermute(basis, ("sub", "face"), pairs) if pairs else basis)
    weights = lax.all_to_all(packs, "sub", split_axis=0, concat_axis=0, tiled=True)
    moved, pumped = lax.optimization_barrier((moved, pumped))
    bases = []
    for array in moved:
        bases += [array, lax.ppermute(array, "face", swap)]

    tiles = 4
    operands = [pumped, projection, basis, *bases, weights, lax.ppermute(weights, "face", swap)]
    return pl.pallas_call(
        functools.partial(apply_kernel, groups, tiles),
        out_shape=jax.ShapeDtypeStruct((blocks_own, cols_dev, dof_count), jnp.float32),
        in_specs=[VMEM] * len(operands),
        out_specs=HBM,
        scratch_shapes=[
            pltpu.VMEM((subdomains, blocks_own, dof_count), jnp.float32),
            pltpu.VMEM(((subdomains + 1) * dof_count, dof_count), jnp.bfloat16),
            pltpu.VMEM((2, blocks_own // tiles * cols_dev, subdomains * dof_count), jnp.bfloat16),
            pltpu.VMEM((blocks_own, cols_dev, dof_count), jnp.float32),
            pltpu.SemaphoreType.DMA((tiles,)),
        ],
        compiler_params=pltpu.CompilerParams(vmem_limit_bytes=48 * MIB),
        name="apply_blocks",
    )(*operands)


def solution(mesh):
    in_specs = (
        P(("groups", "sub"), "rhs", None),
        P(("groups", "rhs")),
        P(("groups", "rhs")),
        P(("groups", "sub", "face"), None),
        P(("groups", "sub", "face")),
        P(("groups", "sub", "face"), None),
        P(("groups", "sub")),
        P(("groups", "sub"), None, None),
        P(),
    )
    out_specs = P(("groups", "sub", "face"), "rhs", None)
    return jax.shard_map(
        on_device, mesh=mesh, in_specs=in_specs, out_specs=out_specs, check_vma=False
    )
```

time: 25.1 us -> 24.6 us (0.980)
  local copies, waits for them, and re-layouts: 3.46 us -> 0.02 us
  waiting for transfers between devices: 3.59 us -> 7.02 us
  starting transfers between devices: 11.1 us -> 10.2 us
  other arithmetic: 0 us -> 0.58 us
  Pallas kernels: 6.03 us -> 5.76 us
    all_to_all x0 -> x1, waiting for transfers between devices: none -> 5.99 us  [on_device(): lax.all_to_all(packs, 'sub', split_axis=0, concat_axis=0, tiled=True)]
    ppermute x7 -> x1, starting transfers between devices: 5.22 us -> 1.44 us  [on_device(): lax.ppermute(weights, 'face', swap)]
    ppermute x7 -> x1, waiting for transfers between devices: 3.58 us -> 0.01 us  [on_device(): lax.ppermute(weights, 'face', swap)]
    all_to_all x0 -> x1, starting transfers between devices: none -> 3.48 us  [on_device(): lax.all_to_all(packs, 'sub', split_axis=0, concat_axis=0, tiled=True)]
    unnamed x14 -> x10, local copies, waits for them, and re-layouts: 3.46 us -> 0.02 us
    ppermute x2, waiting for transfers between devices: 0.01 us -> 1.02 us  [on_device(): bases += [array, lax.ppermute(array, 'face', swap)]]
    ppermute x2, starting transfers between devices: 1.15 us -> 0.58 us  [on_device(): bases += [array, lax.ppermute(array, 'face', swap)]]
    convert_element_type x0 -> x1, other arithmetic: none -> 0.5 us  [on_device(): pumped = (mine.astype(jnp.float32) + wells).astype(jnp.bfloat16)]
  transfers between devices with their start and end apart: 11 -> 6, of which waited for: 4 -> 3; matrix products, arithmetic and copies ran while one was open for 0% -> 2% of each run, Pallas kernels for 9% -> 8%
where the time goes in v1:
time: 24.6 us; the launch traced here: 24.3 us
  starting transfers between devices  10.2 us (41%)
  waiting for transfers between devices  7.02 us (29%)
  Pallas kernels  5.76 us (23%)
  between operations  0.73 us (3%)
  other arithmetic  0.58 us (2%)
    all_to_all x1, waiting for transfers between devices, on_device(): lax.all_to_all(packs, 'sub', split_axis=0, concat_axis=0, tiled=True)  5.99 us
    ppermute x2, starting transfers between devices, on_device(): lax.ppermute(basis, ('sub', 'face'), pairs)  4.69 us
    pallas_call x1, Pallas kernels, on_device(): pl.pallas_call(functools.partial(apply_kernel, groups, tiles), out_shape=...  3.75 us
    all_to_all x1, starting transfers between devices, on_device(): lax.all_to_all(packs, 'sub', split_axis=0, concat_axis=0, tiled=True)  3.48 us
    pallas_call x1, Pallas kernels, on_device(): pl.pallas_call(pack_kernel, out_shape=jax.ShapeDtypeStruct((subdomains, p...  2.01 us
    ppermute x1, starting transfers between devices, on_device(): lax.ppermute(weights, 'face', swap)  1.44 us
    ppermute x2, waiting for transfers between devices, on_device(): bases += [array, lax.ppermute(array, 'face', swap)]  1.02 us
    ppermute x2, starting transfers between devices, on_device(): bases += [array, lax.ppermute(array, 'face', swap)]  0.58 us
  transfers between devices with their start and end apart: 6, of which 3 were waited for; matrix products, arithmetic and copies ran while one was open for 2% of the time, Pallas kernels for 8%

profile of v1, /device:TPU:0, one launch (start us, length us, event | category | flops | bytes accessed | tf_op | source)
XLA Modules:
  0.0 24.3 jit_solution(18270596361222856632)
XLA Ops:
  0.0 4.0 %collective-permute-start = (bf16[1,256,256]{2,1,0:T(8,128)(2,1)}, bf16[1,256,256]{2,1,0:T(8,128)(2,1)S(1)}, u32[]{:S(2)}, u32[]{:S(2)}) collective-permute-start(bf16[1,256,256]{2,1,0:T(8,128)(2,1)} %refs_2_.1), channel_id=1, source_target_pairs={{0,8},{1,5},{4,12},{5,9},{8,0},{9,13},{12,4},{13,1},{2,10},{3,7},{... | collective-permute-start | bytes 393224 | tf_op jit(solution)/shard_map/ppermute | solution.py:147
  4.0 0.7 %collective-permute-start.1 = (bf16[1,256,256]{2,1,0:T(8,128)(2,1)}, bf16[1,256,256]{2,1,0:T(8,128)(2,1)S(1)}, u32[]{:S(2)}, u32[]{:S(2)}) collective-permute-start(bf16[1,256,256]{2,1,0:T(8,128)(2,1)} %refs_2_.1), channel_id=1, source_target_pairs={{1,13},{5,1},{9,5},{13,9},{3,15},{7,3},{11,7},{15,11},{17,29},{21,... | collective-permute-start | bytes 393224 | tf_op jit(solution)/shard_map/ppermute | solution.py:147
  5.3 0.0 copy-start.2
  5.4 0.0 copy-start.3
  5.4 0.0 copy-start.4
  5.4 2.0 %pack_weights.1 = bf16[4,80,256]{2,1,0:T(8,128)(2,1)} custom-call(s32[1,128]{1,0:T(1,128)} %bitcast.2, s32[1,128]{1,0:T(1,128)} %bitcast.3, bf16[128,256]{1,0:T(8,128)(2,1)} %scale_ref.1, s32[1]{0:T(128)S(6)} %copy.10.section_ref), custom_call_target="tpu_custom_call" | custom-call | flops 4000000000 | bytes 8388608 | tf_op jit(solution)/shard_map/pack_weights/pallas_call | solution.py:113
  7.4 0.0 copy-start
  7.4 0.0 copy-start.1
  7.4 3.5 %all-to-all-start = ((bf16[4,80,256]{2,1,0:T(8,128)(2,1)}), bf16[4,80,256]{2,1,0:T(8,128)(2,1)S(1)}, u32[]{:S(2)}, u32[]{:S(2)}) async-start(bf16[4,80,256]{2,1,0:T(8,128)(2,1)} %pack_weights.1), calls=%async_computation | async-start | bytes 327680 | tf_op jit(solution)/shard_map/all_to_all | solution.py:148
  10.9 0.1 iota_add_fusion
  11.0 6.0 %all-to-all-done.refs_7_ = bf16[4,80,256]{2,1,0:T(8,128)(2,1)S(1)} async-done(((bf16[4,80,256]{2,1,0:T(8,128)(2,1)}), bf16[4,80,256]{2,1,0:T(8,128)(2,1)S(1)}, u32[]{:S(2)}, u32[]{:S(2)}) %all-to-all-start) | async-done | bytes 163872 | tf_op jit(solution)/shard_map/all_to_all | solution.py:148
  17.0 1.4 %collective-permute-start.4 = (bf16[4,80,256]{2,1,0:T(8,128)(2,1)S(1)}, bf16[4,80,256]{2,1,0:T(8,128)(2,1)S(1)}, u32[]{:S(2)}, u32[]{:S(2)}) collective-permute-start(bf16[4,80,256]{2,1,0:T(8,128)(2,1)S(1)} %all-to-all-done.refs_7_), channel_id=1, source_target_pairs={{0,1},{1,0},{2,3},{3,2},{4,5},{5,4},{6,7},{7,6},{8,9},{9,8},{10,11... | collective-permute-start | bytes 491528 | tf_op jit(solution)/shard_map/ppermute | solution.py:155
  18.4 0.0 copy-done.2
  18.4 0.0 copy-done.3
  18.4 0.0 copy-done.4
  18.4 0.5 %add_convert_fusion.refs_0_ = bf16[64,32,256]{2,1,0:T(8,128)(2,1)S(1)} fusion(f32[32]{0:T(128)S(1)} %copy-done.3, s32[64,256]{1,0:T(8,128)S(1)} %iota_add_fusion, bf16[128,32,256]{2,1,0:T(8,128)(2,1)S(1)} %copy-done.2, s32[]{:T(128)S(6)} %select_n.7, s32[32]{0:T(128)S(1)} %copy-done.4), kind=kLoop, calls=%fused_computation | loop fusion | flops 2621440 | bytes 2162948 | tf_op jit(solution)/shard_map/convert_element_type | solution.py:127
  18.9 0.0 collective-permute-done.refs_3_
  18.9 0.0 collective-permute-done.1.refs_5_
  18.9 0.1 collective-permute-start.2
  19.0 0.5 %collective-permute-start.3 = (bf16[1,256,256]{2,1,0:T(8,128)(2,1)S(1)}, bf16[1,256,256]{2,1,0:T(8,128)(2,1)S(1)}, u32[]{:S(2)}, u32[]{:S(2)}) collective-permute-start(bf16[1,256,256]{2,1,0:T(8,128)(2,1)S(1)} %collective-permute-done.1.refs_5_), channel_id=1, source_target_pairs={{0,1},{1,0},{2,3},{3,2},{4,5},{5,4},{6,7},{7,6},{8,9},{9,8},{10,11... | collective-permute-start | bytes 393224 | tf_op jit(solution)/shard_map/ppermute | solution.py:152
  19.5 0.8 %collective-permute-done.2.refs_4_ = bf16[1,256,256]{2,1,0:T(8,128)(2,1)S(1)} collective-permute-done((bf16[1,256,256]{2,1,0:T(8,128)(2,1)S(1)}, bf16[1,256,256]{2,1,0:T(8,128)(2,1)S(1)}, u32[]{:S(2)}, u32[]{:S(2)}) %collective-permute-start.2) | collective-permute-done | bytes 131104 | tf_op jit(solution)/shard_map/ppermute | solution.py:152
  20.4 0.2 collective-permute-done.3.refs_6_
  20.5 0.0 collective-permute-done.4.refs_8_
  20.5 0.0 copy-done
  20.6 0.0 copy-done.1
  20.6 3.8 %apply_blocks.1 = f32[64,32,256]{2,1,0:T(8,128)} custom-call(bf16[64,32,256]{2,1,0:T(8,128)(2,1)S(1)} %add_convert_fusion.refs_0_, bf16[256,256]{1,0:T(8,128)(2,1)S(1)} %copy-done, bf16[1,256,256]{2,1,0:T(8,128)(2,1)S(1)} %copy-done.1, bf16[1,256,256]{2,1,0:T(8,128)(2,1)S(1)} %collective-permute-done.refs_3_, ...), custom_call_target="tpu_custom_call" | custom-call | tf_op jit(solution)/shard_map/apply_blocks/pallas_call | solution.py:156
  (1 shorter events, 0.0 us)
Async XLA Ops:
  0.0 18.9 %collective-permute-start = (bf16[1,256,256]{2,1,0:T(8,128)(2,1)}, bf16[1,256,256]{2,1,0:T(8,128)(2,1)S(1)}, u32[]{:S(2)}, u32[]{:S(2)}) collective-permute-start(bf16[1,256,256]{2,1,0:T(8,128)(2,1)} %refs_2_.1), channel_id=1, source_target_pairs={{0,8},{1,5},{4,12},{5,9},{8,0},{9,13},{12,4},{13,1},{2,10},{3,7},{... | collective-permute-start | bytes 393224 | tf_op jit(solution)/shard_map/ppermute | solution.py:147
  4.0 14.9 %collective-permute-start.1 = (bf16[1,256,256]{2,1,0:T(8,128)(2,1)}, bf16[1,256,256]{2,1,0:T(8,128)(2,1)S(1)}, u32[]{:S(2)}, u32[]{:S(2)}) collective-permute-start(bf16[1,256,256]{2,1,0:T(8,128)(2,1)} %refs_2_.1), channel_id=1, source_target_pairs={{1,13},{5,1},{9,5},{13,9},{3,15},{7,3},{11,7},{15,11},{17,29},{21,... | collective-permute-start | bytes 393224 | tf_op jit(solution)/shard_map/ppermute | solution.py:147
  5.3 13.1 %copy-start.2 = (bf16[128,32,256]{2,1,0:T(8,128)(2,1)S(1)}, bf16[128,32,256]{2,1,0:T(8,128)(2,1)}, u32[]{:S(2)}) copy-start(bf16[128,32,256]{2,1,0:T(8,128)(2,1)} %param.9) | copy-start | bytes 6291460
  5.4 13.1 %copy-start.3 = (f32[32]{0:T(128)S(1)}, f32[32]{0:T(128)}, u32[]{:S(2)}) copy-start(f32[32]{0:T(128)} %param.10) | copy-start | bytes 388
  5.4 13.0 %copy-start.4 = (s32[32]{0:T(128)S(1)}, s32[32]{0:T(128)}, u32[]{:S(2)}) copy-start(s32[32]{0:T(128)} %param.11) | copy-start | bytes 388
  7.4 13.2 %copy-start = (bf16[256,256]{1,0:T(8,128)(2,1)S(1)}, bf16[256,256]{1,0:T(8,128)(2,1)}, u32[]{:S(2)}) copy-start(bf16[256,256]{1,0:T(8,128)(2,1)} %refs_1_.1) | copy-start | bytes 393220
  7.4 13.2 %copy-start.1 = (bf16[1,256,256]{2,1,0:T(8,128)(2,1)S(1)}, bf16[1,256,256]{2,1,0:T(8,128)(2,1)}, u32[]{:S(2)}) copy-start(bf16[1,256,256]{2,1,0:T(8,128)(2,1)} %refs_2_.1) | copy-start | bytes 393220
  7.4 9.6 %all-to-all-start = ((bf16[4,80,256]{2,1,0:T(8,128)(2,1)}), bf16[4,80,256]{2,1,0:T(8,128)(2,1)S(1)}, u32[]{:S(2)}, u32[]{:S(2)}) async-start(bf16[4,80,256]{2,1,0:T(8,128)(2,1)} %pack_weights.1), calls=%async_computation | async-start | bytes 327680 | tf_op jit(solution)/shard_map/all_to_all | solution.py:148
  17.0 3.6 %collective-permute-start.4 = (bf16[4,80,256]{2,1,0:T(8,128)(2,1)S(1)}, bf16[4,80,256]{2,1,0:T(8,128)(2,1)S(1)}, u32[]{:S(2)}, u32[]{:S(2)}) collective-permute-start(bf16[4,80,256]{2,1,0:T(8,128)(2,1)S(1)} %all-to-all-done.refs_7_), channel_id=1, source_target_pairs={{0,1},{1,0},{2,3},{3,2},{4,5},{5,4},{6,7},{7,6},{8,9},{9,8},{10,11... | collective-permute-start | bytes 491528 | tf_op jit(solution)/shard_map/ppermute | solution.py:155
  18.9 1.4 %collective-permute-start.2 = (bf16[1,256,256]{2,1,0:T(8,128)(2,1)S(1)}, bf16[1,256,256]{2,1,0:T(8,128)(2,1)S(1)}, u32[]{:S(2)}, u32[]{:S(2)}) collective-permute-start(bf16[1,256,256]{2,1,0:T(8,128)(2,1)S(1)} %collective-permute-done.refs_3_), channel_id=1, source_target_pairs={{0,1},{1,0},{2,3},{3,2},{4,5},{5,4},{6,7},{7,6},{8,9},{9,8},{10,11... | collective-permute-start | bytes 393224 | tf_op jit(solution)/shard_map/ppermute | solution.py:152
  19.0 1.5 %collective-permute-start.3 = (bf16[1,256,256]{2,1,0:T(8,128)(2,1)S(1)}, bf16[1,256,256]{2,1,0:T(8,128)(2,1)S(1)}, u32[]{:S(2)}, u32[]{:S(2)}) collective-permute-start(bf16[1,256,256]{2,1,0:T(8,128)(2,1)S(1)} %collective-permute-done.1.refs_5_), channel_id=1, source_target_pairs={{0,1},{1,0},{2,3},{3,2},{4,5},{5,4},{6,7},{7,6},{8,9},{9,8},{10,11... | collective-permute-start | bytes 393224 | tf_op jit(solution)/shard_map/ppermute | solution.py:152

commit v2 on v1

v2 whole, which is shorter than its diff:
```python
import functools

import jax
import jax.numpy as jnp
from jax import lax
from jax.experimental import pallas as pl
from jax.experimental.pallas import tpu as pltpu
from jax.sharding import PartitionSpec as P

ROW_TILE = 16
VMEM = pl.BlockSpec(memory_space=pltpu.VMEM)
HBM = pl.BlockSpec(memory_space=pltpu.HBM)
SMEM = pl.BlockSpec(memory_space=pltpu.SMEM)
MIB = 1024 * 1024
TILES = 4


def pack_kernel(owner_ref, slot_ref, scale_ref, section_ref, *packs):
    subdomains = len(packs)
    rows, dof_count = packs[0].shape
    rows -= ROW_TILE
    faces = owner_ref.shape[1]
    sign = (1 - 2 * section_ref[0]).astype(jnp.float32)
    partners = lax.broadcasted_iota(jnp.int32, (subdomains, faces), 0)
    named = (lax.axis_index("sub") ^ partners) == owner_ref[...]
    earlier = lax.broadcasted_iota(jnp.int32, (faces, faces), 0) < lax.broadcasted_iota(
        jnp.int32, (faces, faces), 1
    )
    rank = jnp.dot(
        named.astype(jnp.bfloat16), earlier.astype(jnp.bfloat16), preferred_element_type=jnp.float32
    )
    place = jnp.where(named, rank.astype(jnp.int32), -1)
    slots = slot_ref[...].astype(jnp.bfloat16)
    for partner, pack_ref in enumerate(packs):
        hit = place[partner : partner + 1, :] == lax.broadcasted_iota(jnp.int32, (rows, faces), 0)
        hit = hit.astype(jnp.bfloat16)
        packed = jnp.dot(hit, scale_ref[...], preferred_element_type=jnp.float32) * sign
        listed = lax.dot_general(
            slots, hit, (((1,), (1,)), ((), ())), preferred_element_type=jnp.float32
        )
        meta = jnp.concatenate([listed, jnp.zeros((1, dof_count - rows), jnp.float32)], axis=1)
        meta = jnp.broadcast_to(meta, (ROW_TILE, dof_count))
        pack_ref[:rows, :] = packed.astype(jnp.bfloat16)
        pack_ref[rows:, :] = meta.astype(jnp.bfloat16)


def block_weights(packs, blocks_own):
    rows = packs[0].shape[0] - ROW_TILE
    first = lax.axis_index("face") * blocks_own
    block_ids = first + lax.broadcasted_iota(jnp.int32, (blocks_own, rows), 0)
    total = None
    for pack in packs:
        slots = pack[rows:, :].astype(jnp.int32)[:1, :rows]
        hit = (slots == block_ids).astype(jnp.bfloat16)
        part = jnp.dot(hit, pack[:rows, :], preferred_element_type=jnp.float32)
        total = part if total is None else total + part
    return total


def apply_kernel(groups, *refs):
    pumped_ref, projection_ref, own_ref = refs[:3]
    bases, refs = refs[3 : 3 + 4 * len(groups)], refs[3 + 4 * len(groups) :]
    packs, (result_ref, weight_ref, basis_ref, scaled_ref, out_ref, sems) = refs[:-6], refs[-6:]
    blocks_own, columns, dof_count = pumped_ref.shape
    subdomains = weight_ref.shape[0]
    lane = 2 * lax.rem(lax.axis_index("rhs"), 2) + lax.axis_index("face")

    def put(array, *by_lane):
        partner = jnp.int32(by_lane[3])
        for which in range(3):
            partner = jnp.where(lane == which, by_lane[which], partner)
        basis_ref[pl.ds(pl.multiple_of(partner * dof_count, dof_count), dof_count), :] = array[0]

    basis_ref[:dof_count, :] = own_ref[0]
    for at, (a, b, c) in enumerate(groups):
        first, first_swapped, second, second_swapped = bases[4 * at : 4 * at + 4]
        put(first, a, c, b, c)
        put(second, c, b, c, a)
        put(first_swapped, c, a, c, b)
        put(second_swapped, b, c, a, c)
    for partner in range(subdomains):
        weight_ref[partner] = block_weights(packs[2 * partner : 2 * partner + 2], blocks_own)

    tile_blocks = blocks_own // TILES
    copies = []
    for tile in range(TILES):
        at = slice(tile * tile_blocks, (tile + 1) * tile_blocks)
        values = pumped_ref[at].astype(jnp.float32)
        for partner in range(subdomains):
            scaled = (values * weight_ref[partner, at][:, None, :]).astype(jnp.bfloat16)
            scaled_ref[tile % 2, :, partner * dof_count : (partner + 1) * dof_count] = scaled.reshape(
                tile_blocks * columns, dof_count
            )
        total = jnp.dot(scaled_ref[tile % 2], basis_ref[...], preferred_element_type=jnp.float32)
        result = jnp.dot(
            total.astype(jnp.bfloat16), projection_ref[...], preferred_element_type=jnp.float32
        )
        out_ref[at] = result.reshape(tile_blocks, columns, dof_count)
        copies.append(pltpu.make_async_copy(out_ref.at[at], result_ref.at[at], sems.at[tile]))
        copies[-1].start()
    for copy in copies:
        copy.wait()


def on_device(
    mortar_in, pump_rate, well_cell, face_owner, face_slot, face_scale, section, basis, projection
):
    blocks_dev, cols_dev, dof_count = mortar_in.shape
    faces_dev = face_slot.shape[0]
    subdomains, rights, halves = lax.axis_size("sub"), lax.axis_size("rhs"), lax.axis_size("face")
    blocks_own = blocks_dev // halves
    capacity = max(2, 2 * faces_dev // subdomains)
    pack_rows = -(-capacity // ROW_TILE) * ROW_TILE + ROW_TILE
    block_shape = (blocks_own, cols_dev, dof_count)

    def flat(sub, right, face):
        return (sub * rights + right) * halves + face

    partners = list(range(1, subdomains))
    groups = [partners[i : i + 3] for i in range(0, len(partners), 3)]
    groups = [(g[1], g[2], g[0]) if len(g) == 3 else (g[0], g[-1], g[0]) for g in groups]
    firsts = []
    for a, b, c in groups:
        pairs = [
            (flat(s, r, face), flat(s ^ (c if face else b if r % 2 else a), r, face))
            for s in range(subdomains)
            for r in range(rights)
            for face in range(halves)
        ]
        firsts.append(lax.ppermute(basis, ("sub", "rhs", "face"), pairs))

    packs = pl.pallas_call(
        pack_kernel,
        out_shape=[jax.ShapeDtypeStruct((pack_rows, dof_count), jnp.bfloat16)] * subdomains,
        in_specs=[VMEM, VMEM, VMEM, SMEM],
        out_specs=[VMEM] * subdomains,
        cost_estimate=pl.CostEstimate(flops=4_000_000_000, bytes_accessed=8 * MIB, transcendentals=0),
        name="pack_weights",
    )(face_owner.reshape(1, faces_dev), face_slot.reshape(1, faces_dev), face_scale, section)
    swap = [(i, i ^ 1) for i in range(halves)]
    weights = []
    for partner, pack in enumerate(packs):
        if partner:
            here = lax.ppermute(pack, "sub", [(i, i ^ partner) for i in range(subdomains)])
            weights += [here, lax.ppermute(here, "face", swap)]
        else:
            here = lax.ppermute(pack, "rhs", [(i, i ^ 1) for i in range(rights)])
            weights += [here, lax.ppermute(pack, "face", swap)]

    first_block = lax.axis_index("face") * blocks_own
    mine = lax.dynamic_slice_in_dim(mortar_in, first_block, blocks_own, 0)
    block_ids = lax.axis_index("sub") * blocks_dev + first_block + jnp.arange(blocks_own, dtype=jnp.int32)
    cell = block_ids[:, None, None] * dof_count + jnp.arange(dof_count, dtype=jnp.int32)[None, None, :]
    wells = jnp.where(cell == well_cell[None, :, None], pump_rate[None, :, None], 0.0)
    pumped = (mine.astype(jnp.float32) + wells).astype(jnp.bfloat16)

    pairs = [
        (r * halves + face, r * halves if face else (r ^ 1) * halves + 1)
        for r in range(rights)
        for face in range(halves)
    ]
    bases = []
    for first in firsts:
        second = lax.ppermute(first, ("rhs", "face"), pairs)
        bases += [first, lax.ppermute(first, "face", swap), second, lax.ppermute(second, "face", swap)]

    operands = [pumped, projection, basis, *bases, *weights]
    return pl.pallas_call(
        functools.partial(apply_kernel, groups),
        out_shape=jax.ShapeDtypeStruct(block_shape, jnp.float32),
        in_specs=[VMEM] * len(operands),
        out_specs=HBM,
        scratch_shapes=[
            pltpu.VMEM((subdomains, blocks_own, dof_count), jnp.float32),
            pltpu.VMEM((subdomains * dof_count, dof_count), jnp.bfloat16),
            pltpu.VMEM((2, blocks_own // TILES * cols_dev, subdomains * dof_count), jnp.bfloat16),
            pltpu.VMEM(block_shape, jnp.float32),
            pltpu.SemaphoreType.DMA((TILES,)),
        ],
        compiler_params=pltpu.CompilerParams(vmem_limit_bytes=48 * MIB),
        name="apply_blocks",
    )(*operands)


def solution(mesh):
    in_specs = (
        P(("groups", "sub"), "rhs", None),
        P(("groups", "rhs")),
        P(("groups", "rhs")),
        P(("groups", "sub", "face"), None),
        P(("groups", "sub", "face")),
        P(("groups", "sub", "face"), None),
        P(("groups", "sub")),
        P(("groups", "sub"), None, None),
        P(),
    )
    out_specs = P(("groups", "sub", "face"), "rhs", None)
    return jax.shard_map(
        on_device, mesh=mesh, in_specs=in_specs, out_specs=out_specs, check_vma=False
    )
```

time: 24.6 us -> 25.9 us (1.053)
  waiting for transfers between devices: 7.02 us -> 10.1 us
  starting transfers between devices: 10.2 us -> 8.65 us
    ppermute x5 -> x12, waiting for transfers between devices: 1.03 us -> 10.1 us  [the longest x3 9.59 us: on_device(): lax.ppermute(pack, 'sub', [(i, i ^ partner) for i in range(subdomains)])]
    all_to_all x1 -> x0, waiting for transfers between devices: 5.99 us -> none  [on_device(): lax.all_to_all(packs, 'sub', split_axis=0, concat_axis=0, tiled=True)]
    all_to_all x1 -> x0, starting transfers between devices: 3.48 us -> none  [on_device(): lax.all_to_all(packs, 'sub', split_axis=0, concat_axis=0, tiled=True)]
    ppermute x5 -> x12, starting transfers between devices: 6.71 us -> 8.65 us  [the longest x1 4.04 us: on_device(): firsts.append(lax.ppermute(basis, ('sub', 'rhs', 'face'), pairs))]
  transfers between devices with their start and end apart: 6 -> 12, of which waited for: 3 -> 5; matrix products, arithmetic and copies ran while one was open for 2% -> 2% of each run, Pallas kernels for 8% -> 8%
where the time goes in v2:
time: 25.9 us; the launch traced here: 25.8 us
  waiting for transfers between devices  10.1 us (39%)
  starting transfers between devices  8.65 us (33%)
  Pallas kernels  5.72 us (22%)
  between operations  0.73 us (3%)
  other arithmetic  0.61 us (2%)
    ppermute x3, waiting for transfers between devices, on_device(): lax.ppermute(pack, 'sub', [(i, i ^ partner) for i in range(subdomains)])  9.59 us
    ppermute x1, starting transfers between devices, on_device(): firsts.append(lax.ppermute(basis, ('sub', 'rhs', 'face'), pairs))  4.04 us
    pallas_call x1, Pallas kernels, on_device(): pl.pallas_call(functools.partial(apply_kernel, groups), out_shape=jax.Sha...  3.76 us
    ppermute x1, starting transfers between devices, on_device(): here = lax.ppermute(pack, 'rhs', [(i, i ^ 1) for i in range(rights)])  2.57 us
    pallas_call x1, Pallas kernels, on_device(): pl.pallas_call(pack_kernel, out_shape=[jax.ShapeDtypeStruct((pack_rows, d...  1.96 us
    ppermute x3, starting transfers between devices, on_device(): lax.ppermute(pack, 'sub', [(i, i ^ partner) for i in range(subdomains)])  0.79 us
    ppermute x3, starting transfers between devices, on_device(): weights += [here, lax.ppermute(here, 'face', swap)]  0.7 us
    convert_element_type x1, other arithmetic, on_device(): pumped = (mine.astype(jnp.float32) + wells).astype(jnp.bfloat16)  0.53 us
  transfers between devices with their start and end apart: 12, of which 5 were waited for; matrix products, arithmetic and copies ran while one was open for 2% of the time, Pallas kernels for 8%

profile of v2, /device:TPU:0, one launch (start us, length us, event | category | flops | bytes accessed | tf_op | source)
XLA Modules:
  0.0 25.8 jit_solution(14943479309613999832)
XLA Ops:
  0.0 4.0 %collective-permute-start = (bf16[1,256,256]{2,1,0:T(8,128)(2,1)}, bf16[1,256,256]{2,1,0:T(8,128)(2,1)S(1)}, u32[]{:S(2)}, u32[]{:S(2)}) collective-permute-start(bf16[1,256,256]{2,1,0:T(8,128)(2,1)} %refs_2_.1), channel_id=1, source_target_pairs={{0,8},{1,5},{2,14},{3,7},{4,12},{5,1},{6,10},{7,3},{8,0},{9,13},{1... | collective-permute-start | bytes 393224 | tf_op jit(solution)/shard_map/ppermute | solution.py:130
  4.7 0.0 copy-start.2
  4.7 0.0 copy-start.3
  4.7 0.0 copy-start.4
  4.7 2.0 %pack_weights.1 = (bf16[80,256]{1,0:T(8,128)(2,1)}, bf16[80,256]{1,0:T(8,128)(2,1)}, bf16[80,256]{1,0:T(8,128)(2,1)}, bf16[80,256]{1,0:T(8,128)(2,1)}) custom-call(s32[1,128]{1,0:T(1,128)} %bitcast.2, s32[1,128]{1,0:T(1,128)} %bitcast.3, bf16[128,256]{1,0:T(8,128)(2,1)} %scale_ref.1, s32[1]{0:T(128)S(6)} %copy.10.section_ref), custom_call_target="tpu_custom_call" | custom-call | flops 4000000000 | bytes 8388608 | tf_op jit(solution)/shard_map/pack_weights/pallas_call | solution.py:132
  6.7 0.0 copy-start
  6.7 0.0 copy-start.1
  6.7 0.0 collective-permute-start.5
  6.7 2.6 %collective-permute-start.4 = (bf16[80,256]{1,0:T(8,128)(2,1)}, bf16[80,256]{1,0:T(8,128)(2,1)S(1)}, u32[]{:S(2)}, u32[]{:S(2)}) collective-permute-start(bf16[80,256]{1,0:T(8,128)(2,1)} %get-tuple-element.9), channel_id=1, source_target_pairs={{0,2},{2,0},{1,3},{3,1},{4,6},{6,4},{5,7},{7,5},{8,10},{10,8},{9,1... | collective-permute-start | bytes 122888 | tf_op jit(solution)/shard_map/ppermute | solution.py:147
  9.3 0.0 collective-permute-start.6
  9.3 0.8 %collective-permute-start.8 = (bf16[80,256]{1,0:T(8,128)(2,1)}, bf16[80,256]{1,0:T(8,128)(2,1)S(1)}, u32[]{:S(2)}, u32[]{:S(2)}) collective-permute-start(bf16[80,256]{1,0:T(8,128)(2,1)} %get-tuple-element.11), channel_id=1, source_target_pairs={{0,8},{4,12},{8,0},{12,4},{1,9},{5,13},{9,1},{13,5},{2,10},{6,14},... | collective-permute-start | bytes 122888 | tf_op jit(solution)/shard_map/ppermute | solution.py:144
  10.1 3.9 %collective-permute-done.6.refs_9_ = bf16[80,256]{1,0:T(8,128)(2,1)S(1)} collective-permute-done((bf16[80,256]{1,0:T(8,128)(2,1)}, bf16[80,256]{1,0:T(8,128)(2,1)S(1)}, u32[]{:S(2)}, u32[]{:S(2)}) %collective-permute-start.6) | collective-permute-done | bytes 40992 | tf_op jit(solution)/shard_map/ppermute | solution.py:144
  14.0 0.0 collective-permute-start.10
  14.0 0.0 collective-permute-done.refs_3_
  14.0 0.0 collective-permute-start.2
  14.0 0.1 iota_add_fusion
  14.0 0.4 %collective-permute-done.8.refs_11_ = bf16[80,256]{1,0:T(8,128)(2,1)S(1)} collective-permute-done((bf16[80,256]{1,0:T(8,128)(2,1)}, bf16[80,256]{1,0:T(8,128)(2,1)S(1)}, u32[]{:S(2)}, u32[]{:S(2)}) %collective-permute-start.8) | collective-permute-done | bytes 40992 | tf_op jit(solution)/shard_map/ppermute | solution.py:144
  14.4 0.2 collective-permute-start.7
  14.6 5.3 %collective-permute-done.10.refs_13_ = bf16[80,256]{1,0:T(8,128)(2,1)S(1)} collective-permute-done((bf16[80,256]{1,0:T(8,128)(2,1)}, bf16[80,256]{1,0:T(8,128)(2,1)S(1)}, u32[]{:S(2)}, u32[]{:S(2)}) %collective-permute-start.10) | collective-permute-done | bytes 40992 | tf_op jit(solution)/shard_map/ppermute | solution.py:144
  20.0 0.0 collective-permute-start.9
  20.0 0.0 collective-permute-done.5.refs_8_
  20.0 0.5 %collective-permute-start.11 = (bf16[80,256]{1,0:T(8,128)(2,1)S(1)}, bf16[80,256]{1,0:T(8,128)(2,1)S(1)}, u32[]{:S(2)}, u32[]{:S(2)}) collective-permute-start(bf16[80,256]{1,0:T(8,128)(2,1)S(1)} %collective-permute-done.10.refs_13_), channel_id=1, source_target_pairs={{0,1},{1,0},{2,3},{3,2},{4,5},{5,4},{6,7},{7,6},{8,9},{9,8},{10,11... | collective-permute-start | bytes 122888 | tf_op jit(solution)/shard_map/ppermute | solution.py:145
  20.5 0.0 collective-permute-done.4.refs_7_
  20.5 0.1 collective-permute-start.1
  20.6 0.0 collective-permute-done.2.refs_5_
  20.6 0.4 %collective-permute-start.3 = (bf16[1,256,256]{2,1,0:T(8,128)(2,1)S(1)}, bf16[1,256,256]{2,1,0:T(8,128)(2,1)S(1)}, u32[]{:S(2)}, u32[]{:S(2)}) collective-permute-start(bf16[1,256,256]{2,1,0:T(8,128)(2,1)S(1)} %collective-permute-done.2.refs_5_), channel_id=1, source_target_pairs={{0,1},{1,0},{2,3},{3,2},{4,5},{5,4},{6,7},{7,6},{8,9},{9,8},{10,11... | collective-permute-start | bytes 393224 | tf_op jit(solution)/shard_map/ppermute | solution.py:165
  21.0 0.0 copy-done.2
  21.0 0.0 copy-done.3
  21.0 0.0 copy-done.4
  21.0 0.5 %add_convert_fusion.refs_0_ = bf16[64,32,256]{2,1,0:T(8,128)(2,1)S(1)} fusion(f32[32]{0:T(128)S(1)} %copy-done.3, s32[64,256]{1,0:T(8,128)S(1)} %iota_add_fusion, bf16[128,32,256]{2,1,0:T(8,128)(2,1)S(1)} %copy-done.2, s32[]{:T(128)S(6)} %select_n.7, s32[32]{0:T(128)S(1)} %copy-done.4), kind=kLoop, calls=%fused_computation | loop fusion | flops 2621440 | bytes 2162948 | tf_op jit(solution)/shard_map/convert_element_type | solution.py:155
  21.5 0.0 collective-permute-done.7.refs_10_
  21.6 0.0 collective-permute-done.9.refs_12_
  21.6 0.0 collective-permute-done.11.refs_14_
  21.6 0.3 %collective-permute-done.1.refs_4_ = bf16[1,256,256]{2,1,0:T(8,128)(2,1)S(1)} collective-permute-done((bf16[1,256,256]{2,1,0:T(8,128)(2,1)S(1)}, bf16[1,256,256]{2,1,0:T(8,128)(2,1)S(1)}, u32[]{:S(2)}, u32[]{:S(2)}) %collective-permute-start.1) | collective-permute-done | bytes 131104 | tf_op jit(solution)/shard_map/ppermute | solution.py:165
  21.8 0.2 collective-permute-done.3.refs_6_
  22.0 0.0 copy-done
  22.0 0.0 copy-done.1
  22.0 3.8 %apply_blocks.1 = f32[64,32,256]{2,1,0:T(8,128)} custom-call(bf16[64,32,256]{2,1,0:T(8,128)(2,1)S(1)} %add_convert_fusion.refs_0_, bf16[256,256]{1,0:T(8,128)(2,1)S(1)} %copy-done, bf16[1,256,256]{2,1,0:T(8,128)(2,1)S(1)} %copy-done.1, bf16[1,256,256]{2,1,0:T(8,128)(2,1)S(1)} %collective-permute-done.refs_3_, ...), custom_call_target="tpu_custom_call" | custom-call | tf_op jit(solution)/shard_map/apply_blocks/pallas_call | solution.py:168
  (1 shorter events, 0.0 us)
Async XLA Ops:
  0.0 14.0 %collective-permute-start = (bf16[1,256,256]{2,1,0:T(8,128)(2,1)}, bf16[1,256,256]{2,1,0:T(8,128)(2,1)S(1)}, u32[]{:S(2)}, u32[]{:S(2)}) collective-permute-start(bf16[1,256,256]{2,1,0:T(8,128)(2,1)} %refs_2_.1), channel_id=1, source_target_pairs={{0,8},{1,5},{2,14},{3,7},{4,12},{5,1},{6,10},{7,3},{8,0},{9,13},{1... | collective-permute-start | bytes 393224 | tf_op jit(solution)/shard_map/ppermute | solution.py:130
  4.7 16.3 %copy-start.2 = (bf16[128,32,256]{2,1,0:T(8,128)(2,1)S(1)}, bf16[128,32,256]{2,1,0:T(8,128)(2,1)}, u32[]{:S(2)}) copy-start(bf16[128,32,256]{2,1,0:T(8,128)(2,1)} %param.9) | copy-start | bytes 6291460
  4.7 16.3 %copy-start.3 = (f32[32]{0:T(128)S(1)}, f32[32]{0:T(128)}, u32[]{:S(2)}) copy-start(f32[32]{0:T(128)} %param.10) | copy-start | bytes 388
  4.7 16.3 %copy-start.4 = (s32[32]{0:T(128)S(1)}, s32[32]{0:T(128)}, u32[]{:S(2)}) copy-start(s32[32]{0:T(128)} %param.11) | copy-start | bytes 388
  6.7 15.3 %copy-start = (bf16[256,256]{1,0:T(8,128)(2,1)S(1)}, bf16[256,256]{1,0:T(8,128)(2,1)}, u32[]{:S(2)}) copy-start(bf16[256,256]{1,0:T(8,128)(2,1)} %refs_1_.1) | copy-start | bytes 393220
  6.7 15.3 %copy-start.1 = (bf16[1,256,256]{2,1,0:T(8,128)(2,1)S(1)}, bf16[1,256,256]{2,1,0:T(8,128)(2,1)}, u32[]{:S(2)}) copy-start(bf16[1,256,256]{2,1,0:T(8,128)(2,1)} %refs_2_.1) | copy-start | bytes 393220
  6.7 13.3 %collective-permute-start.5 = (bf16[80,256]{1,0:T(8,128)(2,1)}, bf16[80,256]{1,0:T(8,128)(2,1)S(1)}, u32[]{:S(2)}, u32[]{:S(2)}) collective-permute-start(bf16[80,256]{1,0:T(8,128)(2,1)} %get-tuple-element.9), channel_id=1, source_target_pairs={{0,1},{1,0},{2,3},{3,2},{4,5},{5,4},{6,7},{7,6},{8,9},{9,8},{10,11... | collective-permute-start | bytes 122888 | tf_op jit(solution)/shard_map/ppermute | solution.py:148
  6.7 13.8 %collective-permute-start.4 = (bf16[80,256]{1,0:T(8,128)(2,1)}, bf16[80,256]{1,0:T(8,128)(2,1)S(1)}, u32[]{:S(2)}, u32[]{:S(2)}) collective-permute-start(bf16[80,256]{1,0:T(8,128)(2,1)} %get-tuple-element.9), channel_id=1, source_target_pairs={{0,2},{2,0},{1,3},{3,1},{4,6},{6,4},{5,7},{7,5},{8,10},{10,8},{9,1... | collective-permute-start | bytes 122888 | tf_op jit(solution)/shard_map/ppermute | solution.py:147
  9.3 4.7 %collective-permute-start.6 = (bf16[80,256]{1,0:T(8,128)(2,1)}, bf16[80,256]{1,0:T(8,128)(2,1)S(1)}, u32[]{:S(2)}, u32[]{:S(2)}) collective-permute-start(bf16[80,256]{1,0:T(8,128)(2,1)} %get-tuple-element.10), channel_id=1, source_target_pairs={{0,4},{4,0},{8,12},{12,8},{1,5},{5,1},{9,13},{13,9},{2,6},{6,2},{1... | collective-permute-start | bytes 122888 | tf_op jit(solution)/shard_map/ppermute | solution.py:144
  9.3 5.1 %collective-permute-start.8 = (bf16[80,256]{1,0:T(8,128)(2,1)}, bf16[80,256]{1,0:T(8,128)(2,1)S(1)}, u32[]{:S(2)}, u32[]{:S(2)}) collective-permute-start(bf16[80,256]{1,0:T(8,128)(2,1)} %get-tuple-element.11), channel_id=1, source_target_pairs={{0,8},{4,12},{8,0},{12,4},{1,9},{5,13},{9,1},{13,5},{2,10},{6,14},... | collective-permute-start | bytes 122888 | tf_op jit(solution)/shard_map/ppermute | solution.py:144
  14.0 6.0 %collective-permute-start.10 = (bf16[80,256]{1,0:T(8,128)(2,1)}, bf16[80,256]{1,0:T(8,128)(2,1)S(1)}, u32[]{:S(2)}, u32[]{:S(2)}) collective-permute-start(bf16[80,256]{1,0:T(8,128)(2,1)} %get-tuple-element.12), channel_id=1, source_target_pairs={{0,12},{4,8},{8,4},{12,0},{1,13},{5,9},{9,5},{13,1},{2,14},{6,10},... | collective-permute-start | bytes 122888 | tf_op jit(solution)/shard_map/ppermute | solution.py:144
  14.0 6.6 %collective-permute-start.2 = (bf16[1,256,256]{2,1,0:T(8,128)(2,1)S(1)}, bf16[1,256,256]{2,1,0:T(8,128)(2,1)S(1)}, u32[]{:S(2)}, u32[]{:S(2)}) collective-permute-start(bf16[1,256,256]{2,1,0:T(8,128)(2,1)S(1)} %collective-permute-done.refs_3_), channel_id=1, source_target_pairs={{0,3},{1,0},{2,1},{3,2},{4,7},{5,4},{6,5},{7,6},{8,11},{9,8},{10,9... | collective-permute-start | bytes 393224 | tf_op jit(solution)/shard_map/ppermute | solution.py:164
  14.4 7.1 %collective-permute-start.7 = (bf16[80,256]{1,0:T(8,128)(2,1)S(1)}, bf16[80,256]{1,0:T(8,128)(2,1)S(1)}, u32[]{:S(2)}, u32[]{:S(2)}) collective-permute-start(bf16[80,256]{1,0:T(8,128)(2,1)S(1)} %collective-permute-done.6.refs_9_), channel_id=1, source_target_pairs={{0,1},{1,0},{2,3},{3,2},{4,5},{5,4},{6,7},{7,6},{8,9},{9,8},{10,11... | collective-permute-start | bytes 122888 | tf_op jit(solution)/shard_map/ppermute | solution.py:145
  20.0 1.6 %collective-permute-start.9 = (bf16[80,256]{1,0:T(8,128)(2,1)S(1)}, bf16[80,256]{1,0:T(8,128)(2,1)S(1)}, u32[]{:S(2)}, u32[]{:S(2)}) collective-permute-start(bf16[80,256]{1,0:T(8,128)(2,1)S(1)} %collective-permute-done.8.refs_11_), channel_id=1, source_target_pairs={{0,1},{1,0},{2,3},{3,2},{4,5},{5,4},{6,7},{7,6},{8,9},{9,8},{10,11... | collective-permute-start | bytes 122888 | tf_op jit(solution)/shard_map/ppermute | solution.py:145
  20.0 1.6 %collective-permute-start.11 = (bf16[80,256]{1,0:T(8,128)(2,1)S(1)}, bf16[80,256]{1,0:T(8,128)(2,1)S(1)}, u32[]{:S(2)}, u32[]{:S(2)}) collective-permute-start(bf16[80,256]{1,0:T(8,128)(2,1)S(1)} %collective-permute-done.10.refs_13_), channel_id=1, source_target_pairs={{0,1},{1,0},{2,3},{3,2},{4,5},{5,4},{6,7},{7,6},{8,9},{9,8},{10,11... | collective-permute-start | bytes 122888 | tf_op jit(solution)/shard_map/ppermute | solution.py:145
  20.5 1.3 %collective-permute-start.1 = (bf16[1,256,256]{2,1,0:T(8,128)(2,1)S(1)}, bf16[1,256,256]{2,1,0:T(8,128)(2,1)S(1)}, u32[]{:S(2)}, u32[]{:S(2)}) collective-permute-start(bf16[1,256,256]{2,1,0:T(8,128)(2,1)S(1)} %collective-permute-done.refs_3_), channel_id=1, source_target_pairs={{0,1},{1,0},{2,3},{3,2},{4,5},{5,4},{6,7},{7,6},{8,9},{9,8},{10,11... | collective-permute-start | bytes 393224 | tf_op jit(solution)/shard_map/ppermute | solution.py:165
  20.6 1.5 %collective-permute-start.3 = (bf16[1,256,256]{2,1,0:T(8,128)(2,1)S(1)}, bf16[1,256,256]{2,1,0:T(8,128)(2,1)S(1)}, u32[]{:S(2)}, u32[]{:S(2)}) collective-permute-start(bf16[1,256,256]{2,1,0:T(8,128)(2,1)S(1)} %collective-permute-done.2.refs_5_), channel_id=1, source_target_pairs={{0,1},{1,0},{2,3},{3,2},{4,5},{5,4},{6,7},{7,6},{8,9},{9,8},{10,11... | collective-permute-start | bytes 393224 | tf_op jit(solution)/shard_map/ppermute | solution.py:165

commit v3 on v2

v3 whole, which is shorter than its diff:
```python
import functools

import jax
import jax.numpy as jnp
from jax import lax
from jax.experimental import pallas as pl
from jax.experimental.pallas import tpu as pltpu
from jax.sharding import PartitionSpec as P

ROW_TILE = 16
VMEM = pl.BlockSpec(memory_space=pltpu.VMEM)
HBM = pl.BlockSpec(memory_space=pltpu.HBM)
SMEM = pl.BlockSpec(memory_space=pltpu.SMEM)
MIB = 1024 * 1024
TILES = 4
WORK = pl.CostEstimate(flops=4_000_000_000, bytes_accessed=8 * MIB, transcendentals=0)


def pack_kernel(owner_ref, slot_ref, scale_ref, section_ref, *packs):
    subdomains = len(packs)
    rows, dof_count = packs[0].shape
    rows -= ROW_TILE
    faces = owner_ref.shape[1]
    sign = (1 - 2 * section_ref[0]).astype(jnp.float32)
    partners = lax.broadcasted_iota(jnp.int32, (subdomains, faces), 0)
    named = (lax.axis_index("sub") ^ partners) == owner_ref[...]
    earlier = lax.broadcasted_iota(jnp.int32, (faces, faces), 0) < lax.broadcasted_iota(
        jnp.int32, (faces, faces), 1
    )
    rank = jnp.dot(
        named.astype(jnp.bfloat16), earlier.astype(jnp.bfloat16), preferred_element_type=jnp.float32
    )
    place = jnp.where(named, rank, -1.0)
    at = lax.broadcasted_iota(jnp.int32, (rows, faces), 0).astype(jnp.float32)
    hit = jnp.concatenate([place[p : p + 1, :] == at for p in range(subdomains)], axis=0)
    hit = hit.astype(jnp.bfloat16)
    packed = jnp.dot(hit, scale_ref[...], preferred_element_type=jnp.float32) * sign
    listed = lax.dot_general(
        slot_ref[...].astype(jnp.bfloat16), hit, (((1,), (1,)), ((), ())), preferred_element_type=jnp.float32
    )
    packed = packed.astype(jnp.bfloat16)
    for p, pack_ref in enumerate(packs):
        pack_ref[:rows, :] = packed[p * rows : (p + 1) * rows, :]
        meta = jnp.concatenate(
            [listed[:, p * rows : (p + 1) * rows], jnp.zeros((1, dof_count - rows), jnp.float32)], axis=1
        )
        pack_ref[rows:, :] = jnp.broadcast_to(meta, (ROW_TILE, dof_count)).astype(jnp.bfloat16)


def block_weights(packs, rows, blocks_own):
    first = lax.axis_index("face") * blocks_own
    block_ids = first + lax.broadcasted_iota(jnp.int32, (blocks_own, rows), 0)
    total = None
    for pack in packs:
        slots = pack[rows : rows + ROW_TILE, :].astype(jnp.int32)[:1, :rows]
        hit = (slots == block_ids).astype(jnp.bfloat16)
        part = jnp.dot(hit, pack[:rows, :], preferred_element_type=jnp.float32)
        total = part if total is None else total + part
    return total


def pump_kernel(mortar_ref, rate_ref, cell_ref, pumped_ref, sem):
    blocks_own, columns, dof_count = pumped_ref.shape
    first_block = lax.axis_index("face") * blocks_own
    fetch = pltpu.make_async_copy(mortar_ref.at[pl.ds(first_block, blocks_own)], pumped_ref, sem)
    fetch.start()
    fetch.wait()
    base = lax.axis_index("sub") * mortar_ref.shape[0] + first_block
    for column in range(columns):
        block = lax.div(cell_ref[column], dof_count) - base
        dof = lax.rem(cell_ref[column], dof_count)

        @pl.when((block >= 0) & (block < blocks_own))
        def _():
            slab = slice(column // ROW_TILE * ROW_TILE, (column // ROW_TILE + 1) * ROW_TILE)
            shape = (ROW_TILE, dof_count)
            at_well = (lax.broadcasted_iota(jnp.int32, shape, 0) == column % ROW_TILE) & (
                lax.broadcasted_iota(jnp.int32, shape, 1) == dof
            )
            well = jnp.where(at_well, rate_ref[column], 0.0)
            pumped_ref[block, slab, :] = (pumped_ref[block, slab, :].astype(jnp.float32) + well).astype(
                jnp.bfloat16
            )


def own_kernel(pumped_ref, basis_ref, pack_ref, swapped_ref, sum_ref, weight_ref):
    blocks_own, columns, dof_count = pumped_ref.shape
    weight_ref[...] = block_weights((pack_ref, swapped_ref), pack_ref.shape[0] - ROW_TILE, blocks_own)
    tile_blocks = blocks_own // TILES
    for tile in range(TILES):
        at = slice(tile * tile_blocks, (tile + 1) * tile_blocks)
        scaled = (pumped_ref[at].astype(jnp.float32) * weight_ref[at][:, None, :]).astype(jnp.bfloat16)
        flux = jnp.dot(
            scaled.reshape(tile_blocks * columns, dof_count), basis_ref[0], preferred_element_type=jnp.float32
        )
        sum_ref[at] = flux.reshape(tile_blocks, columns, dof_count)


def last_kernel(groups, order, pumped_ref, sum_ref, projection_ref, *refs):
    bases, refs = refs[: 4 * len(groups)], refs[4 * len(groups) :]
    packs, (result_ref, weight_ref, basis_ref, scaled_ref, out_ref, sems) = refs[:-6], refs[-6:]
    blocks_own, columns, dof_count = pumped_ref.shape
    others = len(order)
    lane = 2 * lax.rem(lax.axis_index("rhs"), 2) + lax.axis_index("face")

    def put(array, *by_lane):
        partner = jnp.int32(by_lane[3])
        for which in range(3):
            partner = jnp.where(lane == which, by_lane[which], partner)
        start = pl.multiple_of((partner - 1) * dof_count, dof_count)
        basis_ref[pl.ds(start, dof_count), :] = array[0]

    for at, (a, b, c) in enumerate(groups):
        first, first_swapped, second, second_swapped = bases[4 * at : 4 * at + 4]
        put(first, a, c, b, c)
        put(second, c, b, c, a)
        put(first_swapped, c, a, c, b)
        put(second_swapped, b, c, a, c)
    for at, partner in enumerate(order):
        pair = packs[2 * at : 2 * at + 2]
        weight_ref[partner - 1] = block_weights(pair, pair[0].shape[0] - ROW_TILE, blocks_own)

    tile_blocks = blocks_own // TILES
    copies = []
    for tile in range(TILES):
        at = slice(tile * tile_blocks, (tile + 1) * tile_blocks)
        values = pumped_ref[at].astype(jnp.float32)
        for other in range(others):
            scaled = (values * weight_ref[other, at][:, None, :]).astype(jnp.bfloat16)
            scaled_ref[tile % 2, :, other * dof_count : (other + 1) * dof_count] = scaled.reshape(
                tile_blocks * columns, dof_count
            )
        total = jnp.dot(scaled_ref[tile % 2], basis_ref[...], preferred_element_type=jnp.float32)
        total = total + sum_ref[at].reshape(tile_blocks * columns, dof_count)
        result = jnp.dot(
            total.astype(jnp.bfloat16), projection_ref[...], preferred_element_type=jnp.float32
        )
        out_ref[at] = result.reshape(tile_blocks, columns, dof_count)
        copies.append(pltpu.make_async_copy(out_ref.at[at], result_ref.at[at], sems.at[tile]))
        copies[-1].start()
    for copy in copies:
        copy.wait()


def on_device(
    mortar_in, pump_rate, well_cell, face_owner, face_slot, face_scale, section, basis, projection
):
    blocks_dev, cols_dev, dof_count = mortar_in.shape
    faces_dev = face_slot.shape[0]
    subdomains, rights, halves = lax.axis_size("sub"), lax.axis_size("rhs"), lax.axis_size("face")
    others = subdomains - 1
    blocks_own = blocks_dev // halves
    capacity = max(2, 2 * faces_dev // subdomains)
    pack_rows = -(-capacity // ROW_TILE) * ROW_TILE + ROW_TILE
    block_shape = (blocks_own, cols_dev, dof_count)
    swap = [(i, i ^ 1) for i in range(halves)]

    def flat(sub, right, face):
        return (sub * rights + right) * halves + face

    partners = sorted(range(1, subdomains), key=lambda p: (p < subdomains // 2, p))
    groups = [partners[i : i + 3] for i in range(0, others, 3)]
    groups = [tuple(g) if len(g) == 3 else (g[0], g[-1], g[0]) for g in groups]
    firsts = []
    for a, b, c in groups:
        pairs = [
            (flat(s, r, face), flat(s ^ (c if face else b if r % 2 else a), r, face))
            for s in range(subdomains)
            for r in range(rights)
            for face in range(halves)
        ]
        firsts.append(lax.ppermute(basis, ("sub", "rhs", "face"), pairs))

    packs = pl.pallas_call(
        pack_kernel,
        out_shape=[jax.ShapeDtypeStruct((pack_rows, dof_count), jnp.bfloat16)] * subdomains,
        in_specs=[VMEM, VMEM, VMEM, SMEM],
        out_specs=[VMEM] * subdomains,
        cost_estimate=WORK,
        name="pack_weights",
    )(face_owner.reshape(1, faces_dev), face_slot.reshape(1, faces_dev), face_scale, section)
    arrived = [lax.ppermute(packs[p], "sub", [(i, i ^ p) for i in range(subdomains)]) for p in partners]
    own_swapped = lax.ppermute(packs[0], "face", swap)

    pairs = [
        (r * halves + face, r * halves if face else (r ^ 1) * halves + 1)
        for r in range(rights)
        for face in range(halves)
    ]
    bases = []
    for first in firsts:
        second = lax.ppermute(first, ("rhs", "face"), pairs)
        bases += [first, lax.ppermute(first, "face", swap), second, lax.ppermute(second, "face", swap)]

    pumped = pl.pallas_call(
        pump_kernel,
        out_shape=jax.ShapeDtypeStruct(block_shape, jnp.bfloat16),
        in_specs=[HBM, SMEM, SMEM],
        out_specs=VMEM,
        scratch_shapes=[pltpu.SemaphoreType.DMA(())],
        compiler_params=pltpu.CompilerParams(vmem_limit_bytes=32 * MIB),
        cost_estimate=WORK,
        name="pump",
    )(mortar_in, pump_rate, well_cell)
    own_sum = pl.pallas_call(
        own_kernel,
        out_shape=jax.ShapeDtypeStruct(block_shape, jnp.float32),
        in_specs=[VMEM] * 4,
        out_specs=VMEM,
        scratch_shapes=[pltpu.VMEM((blocks_own, dof_count), jnp.float32)],
        compiler_params=pltpu.CompilerParams(vmem_limit_bytes=32 * MIB),
        cost_estimate=WORK,
        name="own_blocks",
    )(pumped, basis, packs[0], own_swapped)

    arrived, own_sum = lax.optimization_barrier((arrived, own_sum))
    weights = []
    for array in arrived:
        weights += [array, lax.ppermute(array, "face", swap)]

    operands = [pumped, own_sum, projection, *bases, *weights]
    return pl.pallas_call(
        functools.partial(last_kernel, groups, partners),
        out_shape=jax.ShapeDtypeStruct(block_shape, jnp.float32),
        in_specs=[VMEM] * len(operands),
        out_specs=HBM,
        scratch_shapes=[
            pltpu.VMEM((others, blocks_own, dof_count), jnp.float32),
            pltpu.VMEM((others * dof_count, dof_count), jnp.bfloat16),
            pltpu.VMEM((2, blocks_own // TILES * cols_dev, others * dof_count), jnp.bfloat16),
            pltpu.VMEM(block_shape, jnp.float32),
            pltpu.SemaphoreType.DMA((TILES,)),
        ],
        compiler_params=pltpu.CompilerParams(vmem_limit_bytes=40 * MIB),
        name="last_stage",
    )(*operands)


def solution(mesh):
    in_specs = (
        P(("groups", "sub"), "rhs", None),
        P(("groups", "rhs")),
        P(("groups", "rhs")),
        P(("groups", "sub", "face"), None),
        P(("groups", "sub", "face")),
        P(("groups", "sub", "face"), None),
        P(("groups", "sub")),
        P(("groups", "sub"), None, None),
        P(),
    )
    out_specs = P(("groups", "sub", "face"), "rhs", None)
    return jax.shard_map(
        on_device, mesh=mesh, in_specs=in_specs, out_specs=out_specs, check_vma=False
    )
```

time: 25.9 us -> 21.4 us (0.83)
  waiting for transfers between devices: 10.1 us -> 2.32 us
  starting transfers between devices: 8.65 us -> 11.3 us
  Pallas kernels: 5.72 us -> 6.84 us
  other arithmetic: 0.61 us -> 0 us
    ppermute x8 -> x7, waiting for transfers between devices: 9.6 us -> 0.94 us  [the longest x3 0.92 us: on_device(): weights += [array, lax.ppermute(array, 'face', swap)]]
    ppermute x1, starting transfers between devices: 0.01 us -> 2.15 us  [on_device(): second = lax.ppermute(first, ('rhs', 'face'), pairs)]
    ppermute x1, waiting for transfers between devices: 0.01 us -> 1.38 us  [on_device(): second = lax.ppermute(first, ('rhs', 'face'), pairs)]
    pallas_call x1 -> x3, Pallas kernels: 3.76 us -> 4.82 us  [the longest x1 3.25 us: on_device(): pl.pallas_call(functools.partial(last_kernel, groups, partners), out_shap...]
    ppermute x8 -> x7, starting transfers between devices: 4.1 us -> 4.81 us  [the longest x3 3.94 us: on_device(): lax.ppermute(packs[p], 'sub', [(i, i ^ p) for i in range(subdomains)])]
    convert_element_type x1 -> x0, other arithmetic: 0.53 us -> none  [on_device(): pumped = (mine.astype(jnp.float32) + wells).astype(jnp.bfloat16)]
  transfers between devices with their start and end apart: 12 -> 11, of which waited for: 5 -> 4; matrix products, arithmetic and copies ran while one was open for 2% -> 0% of each run, Pallas kernels for 8% -> 17%
where the time goes in v3:
time: 21.4 us; the launch traced here: 21.2 us
  starting transfers between devices  11.3 us (53%)
  Pallas kernels  6.84 us (32%)
  waiting for transfers between devices  2.32 us (11%)
  between operations  0.77 us (4%)
    ppermute x1, starting transfers between devices, on_device(): firsts.append(lax.ppermute(basis, ('sub', 'rhs', 'face'), pairs))  4.04 us
    ppermute x3, starting transfers between devices, on_device(): lax.ppermute(packs[p], 'sub', [(i, i ^ p) for i in range(subdomains)])  3.94 us
    pallas_call x1, Pallas kernels, on_device(): pl.pallas_call(functools.partial(last_kernel, groups, partners), out_shap...  3.25 us
    ppermute x1, starting transfers between devices, on_device(): second = lax.ppermute(first, ('rhs', 'face'), pairs)  2.15 us
    pallas_call x1, Pallas kernels, on_device(): pl.pallas_call(pack_kernel, out_shape=[jax.ShapeDtypeStruct((pack_rows, d...  2.02 us
    ppermute x1, waiting for transfers between devices, on_device(): second = lax.ppermute(first, ('rhs', 'face'), pairs)  1.38 us
    pallas_call x1, Pallas kernels, on_device(): pl.pallas_call(pump_kernel, out_shape=jax.ShapeDtypeStruct(block_shape, j...  1.03 us
    ppermute x3, waiting for transfers between devices, on_device(): weights += [array, lax.ppermute(array, 'face', swap)]  0.92 us
  transfers between devices with their start and end apart: 11, of which 4 were waited for; matrix products, arithmetic and copies ran while one was open for 0% of the time, Pallas kernels for 17%

profile of v3, /device:TPU:0, one launch (start us, length us, event | category | flops | bytes accessed | tf_op | source)
XLA Modules:
  0.0 21.2 jit_solution(13229779880478689292)
XLA Ops:
  0.0 4.0 %collective-permute-start.4 = (bf16[1,256,256]{2,1,0:T(8,128)(2,1)}, bf16[1,256,256]{2,1,0:T(8,128)(2,1)S(1)}, u32[]{:S(2)}, u32[]{:S(2)}) collective-permute-start(bf16[1,256,256]{2,1,0:T(8,128)(2,1)} %basis_ref.1), channel_id=1, source_target_pairs={{0,8},{1,5},{2,14},{3,7},{4,12},{5,1},{6,10},{7,3},{8,0},{9,13},{1... | collective-permute-start | bytes 393224 | tf_op jit(solution)/shard_map/ppermute | solution.py:172
  4.7 0.0 copy-start.1
  4.7 0.0 copy-start.4
  4.7 0.0 copy-start.5
  4.7 2.0 %pack_weights.1 = (bf16[80,256]{1,0:T(8,128)(2,1)}, bf16[80,256]{1,0:T(8,128)(2,1)}, bf16[80,256]{1,0:T(8,128)(2,1)}, bf16[80,256]{1,0:T(8,128)(2,1)}) custom-call(s32[1,128]{1,0:T(1,128)} %bitcast.2, s32[1,128]{1,0:T(1,128)} %bitcast.3, bf16[128,256]{1,0:T(8,128)(2,1)} %scale_ref.1, s32[1]{0:T(128)S(6)} %copy.10.section_ref), custom_call_target="tpu_custom_call" | custom-call | flops 4000000000 | bytes 8388608 | tf_op jit(solution)/shard_map/pack_weights/pallas_call | solution.py:174
  6.7 0.0 collective-permute-start
  6.7 3.9 %collective-permute-start.1 = (bf16[80,256]{1,0:T(8,128)(2,1)}, bf16[80,256]{1,0:T(8,128)(2,1)S(1)}, u32[]{:S(2)}, u32[]{:S(2)}) collective-permute-start(bf16[80,256]{1,0:T(8,128)(2,1)} %get-tuple-element.14), channel_id=1, source_target_pairs={{0,12},{4,8},{8,4},{12,0},{1,13},{5,9},{9,5},{13,1},{2,14},{6,10},... | collective-permute-start | bytes 122888 | tf_op jit(solution)/shard_map/ppermute | solution.py:182
  10.7 0.0 collective-permute-start.2
  10.7 0.0 copy-start.2
  10.7 0.0 copy-start.3
  10.7 0.0 collective-permute-start.3
  10.7 0.0 collective-permute-done.4.refs_0_
  10.7 2.2 %collective-permute-start.6 = (bf16[1,256,256]{2,1,0:T(8,128)(2,1)S(1)}, bf16[1,256,256]{2,1,0:T(8,128)(2,1)S(1)}, u32[]{:S(2)}, u32[]{:S(2)}) collective-permute-start(bf16[1,256,256]{2,1,0:T(8,128)(2,1)S(1)} %collective-permute-done.4.refs_0_), channel_id=1, source_target_pairs={{0,3},{1,0},{2,1},{3,2},{4,7},{5,4},{6,5},{7,6},{8,11},{9,8},{10,9... | collective-permute-start | bytes 393224 | tf_op jit(solution)/shard_map/ppermute | solution.py:192
  12.9 0.0 copy-done.1
  12.9 0.0 copy-done.4
  12.9 0.0 copy-done.5
  12.9 1.0 %pump.1.pumped_ref = bf16[64,32,256]{2,1,0:T(8,128)(2,1)S(1)} custom-call(bf16[128,32,256]{2,1,0:T(8,128)(2,1)S(1)} %copy-done.1, f32[32]{0:T(128)S(1)} %copy-done.4, s32[32]{0:T(128)S(1)} %copy-done.5), custom_call_target="tpu_custom_call" | custom-call | flops 4000000000 | bytes 8388608 | tf_op jit(solution)/shard_map/pump/pallas_call | solution.py:195
  13.9 0.0 copy-start
  13.9 0.0 collective-permute-done.3.swapped_ref
  13.9 0.1 collective-permute-start.5
  14.0 1.4 %collective-permute-done.6.refs_2_ = bf16[1,256,256]{2,1,0:T(8,128)(2,1)S(1)} collective-permute-done((bf16[1,256,256]{2,1,0:T(8,128)(2,1)S(1)}, bf16[1,256,256]{2,1,0:T(8,128)(2,1)S(1)}, u32[]{:S(2)}, u32[]{:S(2)}) %collective-permute-start.6) | collective-permute-done | bytes 131104 | tf_op jit(solution)/shard_map/ppermute | solution.py:192
  15.4 0.2 %collective-permute-start.7 = (bf16[1,256,256]{2,1,0:T(8,128)(2,1)S(1)}, bf16[1,256,256]{2,1,0:T(8,128)(2,1)S(1)}, u32[]{:S(2)}, u32[]{:S(2)}) collective-permute-start(bf16[1,256,256]{2,1,0:T(8,128)(2,1)S(1)} %collective-permute-done.6.refs_2_), channel_id=1, source_target_pairs={{0,1},{1,0},{2,3},{3,2},{4,5},{5,4},{6,7},{7,6},{8,9},{9,8},{10,11... | collective-permute-start | bytes 393224 | tf_op jit(solution)/shard_map/ppermute | solution.py:193
  15.6 0.0 copy-done.2
  15.6 0.0 copy-done.3
  15.6 0.5 %own_blocks.1.sum_ref = f32[64,32,256]{2,1,0:T(8,128)S(1)} custom-call(bf16[64,32,256]{2,1,0:T(8,128)(2,1)S(1)} %pump.1.pumped_ref, bf16[1,256,256]{2,1,0:T(8,128)(2,1)S(1)} %copy-done.2, bf16[80,256]{1,0:T(8,128)(2,1)S(1)} %copy-done.3, bf16[80,256]{1,0:T(8,128)(2,1)S(1)} %collective-permute-done.3.swapped_ref), custom_call_target="tpu_custom_call" | custom-call | flops 4000000000 | bytes 8388608 | tf_op jit(solution)/shard_map/own_blocks/pallas_call | solution.py:205
  16.1 0.0 collective-permute-done.refs_4_
  16.2 0.0 collective-permute-done.1.refs_6_
  16.2 0.0 collective-permute-done.2.refs_8_
  16.2 0.4 %collective-permute-start.8 = (bf16[80,256]{1,0:T(8,128)(2,1)S(1)}, bf16[80,256]{1,0:T(8,128)(2,1)S(1)}, u32[]{:S(2)}, u32[]{:S(2)}) collective-permute-start(bf16[80,256]{1,0:T(8,128)(2,1)S(1)} %collective-permute-done.refs_4_), channel_id=1, source_target_pairs={{0,1},{1,0},{2,3},{3,2},{4,5},{5,4},{6,7},{7,6},{8,9},{9,8},{10,11... | collective-permute-start | bytes 122888 | tf_op jit(solution)/shard_map/ppermute | solution.py:219
  16.5 0.2 %collective-permute-start.9 = (bf16[80,256]{1,0:T(8,128)(2,1)S(1)}, bf16[80,256]{1,0:T(8,128)(2,1)S(1)}, u32[]{:S(2)}, u32[]{:S(2)}) collective-permute-start(bf16[80,256]{1,0:T(8,128)(2,1)S(1)} %collective-permute-done.1.refs_6_), channel_id=1, source_target_pairs={{0,1},{1,0},{2,3},{3,2},{4,5},{5,4},{6,7},{7,6},{8,9},{9,8},{10,11... | collective-permute-start | bytes 122888 | tf_op jit(solution)/shard_map/ppermute | solution.py:219
  16.8 0.3 %collective-permute-start.10 = (bf16[80,256]{1,0:T(8,128)(2,1)S(1)}, bf16[80,256]{1,0:T(8,128)(2,1)S(1)}, u32[]{:S(2)}, u32[]{:S(2)}) collective-permute-start(bf16[80,256]{1,0:T(8,128)(2,1)S(1)} %collective-permute-done.2.refs_8_), channel_id=1, source_target_pairs={{0,1},{1,0},{2,3},{3,2},{4,5},{5,4},{6,7},{7,6},{8,9},{9,8},{10,11... | collective-permute-start | bytes 122888 | tf_op jit(solution)/shard_map/ppermute | solution.py:219
  17.0 0.4 %collective-permute-done.8.refs_5_ = bf16[80,256]{1,0:T(8,128)(2,1)S(1)} collective-permute-done((bf16[80,256]{1,0:T(8,128)(2,1)S(1)}, bf16[80,256]{1,0:T(8,128)(2,1)S(1)}, u32[]{:S(2)}, u32[]{:S(2)}) %collective-permute-start.8) | collective-permute-done | bytes 40992 | tf_op jit(solution)/shard_map/ppermute | solution.py:219
  17.5 0.3 %collective-permute-done.9.refs_7_ = bf16[80,256]{1,0:T(8,128)(2,1)S(1)} collective-permute-done((bf16[80,256]{1,0:T(8,128)(2,1)S(1)}, bf16[80,256]{1,0:T(8,128)(2,1)S(1)}, u32[]{:S(2)}, u32[]{:S(2)}) %collective-permute-start.9) | collective-permute-done | bytes 40992 | tf_op jit(solution)/shard_map/ppermute | solution.py:219
  17.8 0.2 %collective-permute-done.10.refs_9_ = bf16[80,256]{1,0:T(8,128)(2,1)S(1)} collective-permute-done((bf16[80,256]{1,0:T(8,128)(2,1)S(1)}, bf16[80,256]{1,0:T(8,128)(2,1)S(1)}, u32[]{:S(2)}, u32[]{:S(2)}) %collective-permute-start.10) | collective-permute-done | bytes 40992 | tf_op jit(solution)/shard_map/ppermute | solution.py:219
  18.0 0.0 collective-permute-done.5.refs_1_
  18.0 0.0 collective-permute-done.7.refs_3_
  18.0 0.0 copy-done
  18.0 3.2 %last_stage.1 = f32[64,32,256]{2,1,0:T(8,128)} custom-call(bf16[64,32,256]{2,1,0:T(8,128)(2,1)S(1)} %pump.1.pumped_ref, f32[64,32,256]{2,1,0:T(8,128)S(1)} %own_blocks.1.sum_ref, bf16[256,256]{1,0:T(8,128)(2,1)S(1)} %copy-done, bf16[1,256,256]{2,1,0:T(8,128)(2,1)S(1)} %collective-permute-done.4.refs_0_, ...), custom_call_target="tpu_custom_call" | custom-call | tf_op jit(solution)/shard_map/last_stage/pallas_call | solution.py:222
Async XLA Ops:
  0.0 10.7 %collective-permute-start.4 = (bf16[1,256,256]{2,1,0:T(8,128)(2,1)}, bf16[1,256,256]{2,1,0:T(8,128)(2,1)S(1)}, u32[]{:S(2)}, u32[]{:S(2)}) collective-permute-start(bf16[1,256,256]{2,1,0:T(8,128)(2,1)} %basis_ref.1), channel_id=1, source_target_pairs={{0,8},{1,5},{2,14},{3,7},{4,12},{5,1},{6,10},{7,3},{8,0},{9,13},{1... | collective-permute-start | bytes 393224 | tf_op jit(solution)/shard_map/ppermute | solution.py:172
  4.7 8.2 %copy-start.1 = (bf16[128,32,256]{2,1,0:T(8,128)(2,1)S(1)}, bf16[128,32,256]{2,1,0:T(8,128)(2,1)}, u32[]{:S(2)}) copy-start(bf16[128,32,256]{2,1,0:T(8,128)(2,1)} %mortar_ref.1) | copy-start | bytes 6291460
  4.7 8.2 %copy-start.4 = (f32[32]{0:T(128)S(1)}, f32[32]{0:T(128)}, u32[]{:S(2)}) copy-start(f32[32]{0:T(128)} %rate_ref.1) | copy-start | bytes 388
  4.7 8.2 %copy-start.5 = (s32[32]{0:T(128)S(1)}, s32[32]{0:T(128)}, u32[]{:S(2)}) copy-start(s32[32]{0:T(128)} %cell_ref.1) | copy-start | bytes 388
  6.7 9.4 %collective-permute-start = (bf16[80,256]{1,0:T(8,128)(2,1)}, bf16[80,256]{1,0:T(8,128)(2,1)S(1)}, u32[]{:S(2)}, u32[]{:S(2)}) collective-permute-start(bf16[80,256]{1,0:T(8,128)(2,1)} %get-tuple-element.13), channel_id=1, source_target_pairs={{0,8},{4,12},{8,0},{12,4},{1,9},{5,13},{9,1},{13,5},{2,10},{6,14},... | collective-permute-start | bytes 122888 | tf_op jit(solution)/shard_map/ppermute | solution.py:182
  6.7 9.4 %collective-permute-start.1 = (bf16[80,256]{1,0:T(8,128)(2,1)}, bf16[80,256]{1,0:T(8,128)(2,1)S(1)}, u32[]{:S(2)}, u32[]{:S(2)}) collective-permute-start(bf16[80,256]{1,0:T(8,128)(2,1)} %get-tuple-element.14), channel_id=1, source_target_pairs={{0,12},{4,8},{8,4},{12,0},{1,13},{5,9},{9,5},{13,1},{2,14},{6,10},... | collective-permute-start | bytes 122888 | tf_op jit(solution)/shard_map/ppermute | solution.py:182
  10.7 5.5 %collective-permute-start.2 = (bf16[80,256]{1,0:T(8,128)(2,1)}, bf16[80,256]{1,0:T(8,128)(2,1)S(1)}, u32[]{:S(2)}, u32[]{:S(2)}) collective-permute-start(bf16[80,256]{1,0:T(8,128)(2,1)} %get-tuple-element.15), channel_id=1, source_target_pairs={{0,4},{4,0},{8,12},{12,8},{1,5},{5,1},{9,13},{13,9},{2,6},{6,2},{1... | collective-permute-start | bytes 122888 | tf_op jit(solution)/shard_map/ppermute | solution.py:182
  10.7 4.9 %copy-start.2 = (bf16[1,256,256]{2,1,0:T(8,128)(2,1)S(1)}, bf16[1,256,256]{2,1,0:T(8,128)(2,1)}, u32[]{:S(2)}) copy-start(bf16[1,256,256]{2,1,0:T(8,128)(2,1)} %basis_ref.1) | copy-start | bytes 393220
  10.7 4.9 %copy-start.3 = (bf16[80,256]{1,0:T(8,128)(2,1)S(1)}, bf16[80,256]{1,0:T(8,128)(2,1)}, u32[]{:S(2)}) copy-start(bf16[80,256]{1,0:T(8,128)(2,1)} %get-tuple-element.16.pack_ref) | copy-start | bytes 122884
  10.7 3.2 %collective-permute-start.3 = (bf16[80,256]{1,0:T(8,128)(2,1)}, bf16[80,256]{1,0:T(8,128)(2,1)S(1)}, u32[]{:S(2)}, u32[]{:S(2)}) collective-permute-start(bf16[80,256]{1,0:T(8,128)(2,1)} %get-tuple-element.16.pack_ref), channel_id=1, source_target_pairs={{0,1},{1,0},{2,3},{3,2},{4,5},{5,4},{6,7},{7,6},{8,9},{9,8},{10,11... | collective-permute-start | bytes 122888 | tf_op jit(solution)/shard_map/ppermute | solution.py:183
  10.7 4.7 %collective-permute-start.6 = (bf16[1,256,256]{2,1,0:T(8,128)(2,1)S(1)}, bf16[1,256,256]{2,1,0:T(8,128)(2,1)S(1)}, u32[]{:S(2)}, u32[]{:S(2)}) collective-permute-start(bf16[1,256,256]{2,1,0:T(8,128)(2,1)S(1)} %collective-permute-done.4.refs_0_), channel_id=1, source_target_pairs={{0,3},{1,0},{2,1},{3,2},{4,7},{5,4},{6,5},{7,6},{8,11},{9,8},{10,9... | collective-permute-start | bytes 393224 | tf_op jit(solution)/shard_map/ppermute | solution.py:192
  13.9 4.1 %copy-start = (bf16[256,256]{1,0:T(8,128)(2,1)S(1)}, bf16[256,256]{1,0:T(8,128)(2,1)}, u32[]{:S(2)}) copy-start(bf16[256,256]{1,0:T(8,128)(2,1)} %projection_ref.1) | copy-start | bytes 393220
  13.9 4.1 %collective-permute-start.5 = (bf16[1,256,256]{2,1,0:T(8,128)(2,1)S(1)}, bf16[1,256,256]{2,1,0:T(8,128)(2,1)S(1)}, u32[]{:S(2)}, u32[]{:S(2)}) collective-permute-start(bf16[1,256,256]{2,1,0:T(8,128)(2,1)S(1)} %collective-permute-done.4.refs_0_), channel_id=1, source_target_pairs={{0,1},{1,0},{2,3},{3,2},{4,5},{5,4},{6,7},{7,6},{8,9},{9,8},{10,11... | collective-permute-start | bytes 393224 | tf_op jit(solution)/shard_map/ppermute | solution.py:193
  15.4 2.6 %collective-permute-start.7 = (bf16[1,256,256]{2,1,0:T(8,128)(2,1)S(1)}, bf16[1,256,256]{2,1,0:T(8,128)(2,1)S(1)}, u32[]{:S(2)}, u32[]{:S(2)}) collective-permute-start(bf16[1,256,256]{2,1,0:T(8,128)(2,1)S(1)} %collective-permute-done.6.refs_2_), channel_id=1, source_target_pairs={{0,1},{1,0},{2,3},{3,2},{4,5},{5,4},{6,7},{7,6},{8,9},{9,8},{10,11... | collective-permute-start | bytes 393224 | tf_op jit(solution)/shard_map/ppermute | solution.py:193
  16.2 1.3 %collective-permute-start.8 = (bf16[80,256]{1,0:T(8,128)(2,1)S(1)}, bf16[80,256]{1,0:T(8,128)(2,1)S(1)}, u32[]{:S(2)}, u32[]{:S(2)}) collective-permute-start(bf16[80,256]{1,0:T(8,128)(2,1)S(1)} %collective-permute-done.refs_4_), channel_id=1, source_target_pairs={{0,1},{1,0},{2,3},{3,2},{4,5},{5,4},{6,7},{7,6},{8,9},{9,8},{10,11... | collective-permute-start | bytes 122888 | tf_op jit(solution)/shard_map/ppermute | solution.py:219
  16.5 1.2 %collective-permute-start.9 = (bf16[80,256]{1,0:T(8,128)(2,1)S(1)}, bf16[80,256]{1,0:T(8,128)(2,1)S(1)}, u32[]{:S(2)}, u32[]{:S(2)}) collective-permute-start(bf16[80,256]{1,0:T(8,128)(2,1)S(1)} %collective-permute-done.1.refs_6_), channel_id=1, source_target_pairs={{0,1},{1,0},{2,3},{3,2},{4,5},{5,4},{6,7},{7,6},{8,9},{9,8},{10,11... | collective-permute-start | bytes 122888 | tf_op jit(solution)/shard_map/ppermute | solution.py:219
  16.8 1.2 %collective-permute-start.10 = (bf16[80,256]{1,0:T(8,128)(2,1)S(1)}, bf16[80,256]{1,0:T(8,128)(2,1)S(1)}, u32[]{:S(2)}, u32[]{:S(2)}) collective-permute-start(bf16[80,256]{1,0:T(8,128)(2,1)S(1)} %collective-permute-done.2.refs_8_), channel_id=1, source_target_pairs={{0,1},{1,0},{2,3},{3,2},{4,5},{5,4},{6,7},{7,6},{8,9},{9,8},{10,11... | collective-permute-start | bytes 122888 | tf_op jit(solution)/shard_map/ppermute | solution.py:219

commit v4 on v3

--- a/solution.py
+++ b/solution.py
@@ -13,6 +13,8 @@
 SMEM = pl.BlockSpec(memory_space=pltpu.SMEM)
 MIB = 1024 * 1024
 TILES = 4
+LAST_TILES = 8
+LIGHT = pl.CostEstimate(flops=1_000_000, bytes_accessed=1024, transcendentals=0)
 WORK = pl.CostEstimate(flops=4_000_000_000, bytes_accessed=8 * MIB, transcendentals=0)
 
 
@@ -96,38 +98,81 @@
         sum_ref[at] = flux.reshape(tile_blocks, columns, dof_count)
 
 
-def last_kernel(groups, order, pumped_ref, sum_ref, projection_ref, *refs):
-    bases, refs = refs[: 4 * len(groups)], refs[4 * len(groups) :]
-    packs, (result_ref, weight_ref, basis_ref, scaled_ref, out_ref, sems) = refs[:-6], refs[-6:]
+def on_even(even, odd):
+    return jnp.where(lax.rem(lax.axis_index("rhs"), 2) == 0, even, odd)
+
+
+def stage_kernel(groups, pumped_ref, sum_ref, *refs):
+    bases, refs = refs[: 2 * len(groups)], refs[2 * len(groups) :]
+    packs, (out_ref, late_ref, weight_ref, basis_ref, scaled_ref) = refs[:-5], refs[-5:]
     blocks_own, columns, dof_count = pumped_ref.shape
-    others = len(order)
-    lane = 2 * lax.rem(lax.axis_index("rhs"), 2) + lax.axis_index("face")
-
-    def put(array, *by_lane):
-        partner = jnp.int32(by_lane[3])
-        for which in range(3):
-            partner = jnp.where(lane == which, by_lane[which], partner)
-        start = pl.multiple_of((partner - 1) * dof_count, dof_count)
-        basis_ref[pl.ds(start, dof_count), :] = array[0]
-
+    face_id = lax.axis_index("face")
+    rows = packs[0].shape[0] - ROW_TILE
+    weights = {}
+
+    def weight(partner):
+        if partner not in weights:
+            weights[partner] = block_weights(packs[2 * partner - 2 : 2 * partner], rows, blocks_own)
+        return weights[partner]
+
+    count = late = 0
     for at, (a, b, c) in enumerate(groups):
-        first, first_swapped, second, second_swapped = bases[4 * at : 4 * at + 4]
-        put(first, a, c, b, c)
-        put(second, c, b, c, a)
-        put(first_swapped, c, a, c, b)
-        put(second_swapped, b, c, a, c)
-    for at, partner in enumerate(order):
-        pair = packs[2 * at : 2 * at + 2]
-        weight_ref[partner - 1] = block_weights(pair, pair[0].shape[0] - ROW_TILE, blocks_own)
+        first, first_swapped = bases[2 * at : 2 * at + 2]
+        spots = [None, None]
+        if a != b:
+            spots[0] = count
+            weight_ref[count] = on_even(weight(a), weight(b))
+            late_ref[late] = on_even(weight(b), weight(a))
+            count, late = count + 1, late + 1
+        if c != a:
+            spots[1] = count
+            weight_ref[count] = weight(c)
+            count += 1
+        elif a == b:
+            spots = [count, count]
+            weight_ref[count] = weight(c)
+            count += 1
+        spare = weight_ref.shape[0]
+        spots = [spare if spot is None else spot for spot in spots]
+        for array, core_0, core_1 in ((first, *spots), (first_swapped, *spots[::-1])):
+            start = pl.multiple_of(jnp.where(face_id == 0, core_0, core_1) * dof_count, dof_count)
+            basis_ref[pl.ds(start, dof_count), :] = array[0]
 
     tile_blocks = blocks_own // TILES
-    copies = []
     for tile in range(TILES):
         at = slice(tile * tile_blocks, (tile + 1) * tile_blocks)
         values = pumped_ref[at].astype(jnp.float32)
-        for other in range(others):
-            scaled = (values * weight_ref[other, at][:, None, :]).astype(jnp.bfloat16)
-            scaled_ref[tile % 2, :, other * dof_count : (other + 1) * dof_count] = scaled.reshape(
+        for spot in range(count):
+            scaled = (values * weight_ref[spot, at][:, None, :]).astype(jnp.bfloat16)
+            scaled_ref[tile % 2, :, spot * dof_count : (spot + 1) * dof_count] = scaled.reshape(
+                tile_blocks * columns, dof_count
+            )
+        total = jnp.dot(
+            scaled_ref[tile % 2], basis_ref[: count * dof_count, :], preferred_element_type=jnp.float32
+        )
+        out_ref[at] = total.reshape(tile_blocks, columns, dof_count) + sum_ref[at]
+
+
+def last_kernel(pumped_ref, sum_ref, weight_ref, projection_ref, *refs):
+    bases, (result_ref, basis_ref, scaled_ref, out_ref, sems) = refs[:-5], refs[-5:]
+    blocks_own, columns, dof_count = pumped_ref.shape
+    count = weight_ref.shape[0]
+    for at in range(count):
+        for core, array in ((1, bases[2 * at]), (0, bases[2 * at + 1])):
+
+            @pl.when(lax.axis_index("face") == core)
+            def _():
+                basis_ref[at * dof_count : (at + 1) * dof_count, :] = array[0]
+
+    tiles = sems.shape[0]
+    tile_blocks = blocks_own // tiles
+    copies = []
+    for tile in range(tiles):
+        at = slice(tile * tile_blocks, (tile + 1) * tile_blocks)
+        values = pumped_ref[at].astype(jnp.float32)
+        for spot in range(count):
+            scaled = (values * weight_ref[spot, at][:, None, :]).astype(jnp.bfloat16)
+            scaled_ref[tile % 2, :, spot * dof_count : (spot + 1) * dof_count] = scaled.reshape(
                 tile_blocks * columns, dof_count
             )
         total = jnp.dot(scaled_ref[tile % 2], basis_ref[...], preferred_element_type=jnp.float32)
@@ -182,16 +227,6 @@
     arrived = [lax.ppermute(packs[p], "sub", [(i, i ^ p) for i in range(subdomains)]) for p in partners]
     own_swapped = lax.ppermute(packs[0], "face", swap)
 
-    pairs = [
-        (r * halves + face, r * halves if face else (r ^ 1) * halves + 1)
-        for r in range(rights)
-        for face in range(halves)
-    ]
-    bases = []
-    for first in firsts:
-        second = lax.ppermute(first, ("rhs", "face"), pairs)
-        bases += [first, lax.ppermute(first, "face", swap), second, lax.ppermute(second, "face", swap)]
-
     pumped = pl.pallas_call(
         pump_kernel,
         out_shape=jax.ShapeDtypeStruct(block_shape, jnp.bfloat16),
@@ -199,7 +234,7 @@
         out_specs=VMEM,
         scratch_shapes=[pltpu.SemaphoreType.DMA(())],
         compiler_params=pltpu.CompilerParams(vmem_limit_bytes=32 * MIB),
-        cost_estimate=WORK,
+        cost_estimate=LIGHT,
         name="pump",
     )(mortar_in, pump_rate, well_cell)
     own_sum = pl.pallas_call(
@@ -209,27 +244,60 @@
         out_specs=VMEM,
         scratch_shapes=[pltpu.VMEM((blocks_own, dof_count), jnp.float32)],
         compiler_params=pltpu.CompilerParams(vmem_limit_bytes=32 * MIB),
-        cost_estimate=WORK,
+        cost_estimate=LIGHT,
         name="own_blocks",
     )(pumped, basis, packs[0], own_swapped)
 
-    arrived, own_sum = lax.optimization_barrier((arrived, own_sum))
+    firsts, arrived, own_sum = lax.optimization_barrier((firsts, arrived, own_sum))
+    pairs = [
+        (r * halves + face, r * halves if face else (r ^ 1) * halves + 1)
+        for r in range(rights)
+        for face in range(halves)
+    ]
+    early, late = [], []
+    for (a, b, _), first in zip(groups, firsts):
+        early += [first, lax.ppermute(first, "face", swap)]
+        if a != b:
+            second = lax.ppermute(first, ("rhs", "face"), pairs)
+            late += [second, lax.ppermute(second, "face", swap)]
     weights = []
-    for array in arrived:
+    for partner in range(1, subdomains):
+        array = arrived[partners.index(partner)]
         weights += [array, lax.ppermute(array, "face", swap)]
 
-    operands = [pumped, own_sum, projection, *bases, *weights]
+    late_count = len(late) // 2
+    count = others - late_count
+    operands = [pumped, own_sum, *early, *weights]
+    total, late_weight = pl.pallas_call(
+        functools.partial(stage_kernel, groups),
+        out_shape=[
+            jax.ShapeDtypeStruct(block_shape, jnp.float32),
+            jax.ShapeDtypeStruct((late_count, blocks_own, dof_count), jnp.float32),
+        ],
+        in_specs=[VMEM] * len(operands),
+        out_specs=[VMEM, VMEM],
+        scratch_shapes=[
+            pltpu.VMEM((count, blocks_own, dof_count), jnp.float32),
+            pltpu.VMEM(((count + 1) * dof_count, dof_count), jnp.bfloat16),
+            pltpu.VMEM((2, blocks_own // TILES * cols_dev, count * dof_count), jnp.bfloat16),
+        ],
+        input_output_aliases={1: 0},
+        compiler_params=pltpu.CompilerParams(vmem_limit_bytes=40 * MIB),
+        cost_estimate=WORK,
+        name="stage",
+    )(*operands)
+
+    operands = [pumped, total, late_weight, projection, *late]
     return pl.pallas_call(
-        functools.partial(last_kernel, groups, partners),
+        last_kernel,
         out_shape=jax.ShapeDtypeStruct(block_shape, jnp.float32),
         in_specs=[VMEM] * len(operands),
         out_specs=HBM,
         scratch_shapes=[
-            pltpu.VMEM((others, blocks_own, dof_count), jnp.float32),
-            pltpu.VMEM((others * dof_count, dof_count), jnp.bfloat16),
-            pltpu.VMEM((2, blocks_own // TILES * cols_dev, others * dof_count), jnp.bfloat16),
+            pltpu.VMEM((late_count * dof_count, dof_count), jnp.bfloat16),
+            pltpu.VMEM((2, blocks_own // LAST_TILES * cols_dev, late_count * dof_count), jnp.bfloat16),
             pltpu.VMEM(block_shape, jnp.float32),
-            pltpu.SemaphoreType.DMA((TILES,)),
+            pltpu.SemaphoreType.DMA((LAST_TILES,)),
         ],
         compiler_params=pltpu.CompilerParams(vmem_limit_bytes=40 * MIB),
         name="last_stage",

time: 21.4 us -> 22 us (1.028)
  waiting for transfers between devices: 2.32 us -> 4.07 us
  starting transfers between devices: 11.3 us -> 10.5 us
  Pallas kernels: 6.84 us -> 6.52 us
    ppermute x3, waiting for transfers between devices: 0.01 us -> 2.56 us  [on_device(): lax.ppermute(packs[p], 'sub', [(i, i ^ p) for i in range(subdomains)])]
    ppermute x1, starting transfers between devices: 2.15 us -> 0.55 us  [on_device(): second = lax.ppermute(first, ('rhs', 'face'), pairs)]
    ppermute x3, waiting for transfers between devices: 0.92 us -> 0.01 us  [on_device(): weights += [array, lax.ppermute(array, 'face', swap)]]
    ppermute x2, starting transfers between devices: 0.29 us -> 0.84 us  [the longest x1 0.84 us: on_device(): late += [second, lax.ppermute(second, 'face', swap)]]
    pallas_call x1 -> x2, Pallas kernels: 3.25 us -> 2.91 us  [the longest x1 1.73 us: on_device(): pl.pallas_call(last_kernel, out_shape=jax.ShapeDtypeStruct(block_shape, j...]
  transfers between devices with their start and end apart: 11 -> 11, of which waited for: 4 -> 4; matrix products, arithmetic and copies ran while one was open for 0% -> 0% of each run, Pallas kernels for 17% -> 22%
where the time goes in v4:
time: 22 us; the launch traced here: 21.9 us
  starting transfers between devices  10.5 us (48%)
  Pallas kernels  6.52 us (30%)
  waiting for transfers between devices  4.07 us (18%)
  between operations  0.79 us (4%)
    ppermute x1, starting transfers between devices, on_device(): firsts.append(lax.ppermute(basis, ('sub', 'rhs', 'face'), pairs))  4.04 us
    ppermute x3, starting transfers between devices, on_device(): lax.ppermute(packs[p], 'sub', [(i, i ^ p) for i in range(subdomains)])  4.01 us
    ppermute x3, waiting for transfers between devices, on_device(): lax.ppermute(packs[p], 'sub', [(i, i ^ p) for i in range(subdomains)])  2.56 us
    pallas_call x1, Pallas kernels, on_device(): pl.pallas_call(pack_kernel, out_shape=[jax.ShapeDtypeStruct((pack_rows, d...  2.02 us
    pallas_call x1, Pallas kernels, on_device(): pl.pallas_call(last_kernel, out_shape=jax.ShapeDtypeStruct(block_shape, j...  1.73 us
    ppermute x1, waiting for transfers between devices, on_device(): second = lax.ppermute(first, ('rhs', 'face'), pairs)  1.5 us
    pallas_call x1, Pallas kernels, on_device(): pl.pallas_call(functools.partial(stage_kernel, groups), out_shape=[jax.Sh...  1.18 us
    pallas_call x1, Pallas kernels, on_device(): pl.pallas_call(pump_kernel, out_shape=jax.ShapeDtypeStruct(block_shape, j...  1.03 us
  transfers between devices with their start and end apart: 11, of which 4 were waited for; matrix products, arithmetic and copies ran while one was open for 0% of the time, Pallas kernels for 22%

profile of v4, /device:TPU:0, one launch (start us, length us, event | category | flops | bytes accessed | tf_op | source)
XLA Modules:
  0.0 21.9 jit_solution(5076084894498618611)
XLA Ops:
  0.0 4.0 %collective-permute-start = (bf16[1,256,256]{2,1,0:T(8,128)(2,1)}, bf16[1,256,256]{2,1,0:T(8,128)(2,1)S(1)}, u32[]{:S(2)}, u32[]{:S(2)}) collective-permute-start(bf16[1,256,256]{2,1,0:T(8,128)(2,1)} %basis_ref.1), channel_id=1, source_target_pairs={{0,8},{1,5},{2,14},{3,7},{4,12},{5,1},{6,10},{7,3},{8,0},{9,13},{1... | collective-permute-start | bytes 393224 | tf_op jit(solution)/shard_map/ppermute | solution.py:217
  4.7 0.0 copy-start
  4.7 0.0 copy-start.4
  4.7 0.0 copy-start.5
  4.7 2.0 %pack_weights.1 = (bf16[80,256]{1,0:T(8,128)(2,1)}, bf16[80,256]{1,0:T(8,128)(2,1)}, bf16[80,256]{1,0:T(8,128)(2,1)}, bf16[80,256]{1,0:T(8,128)(2,1)}) custom-call(s32[1,128]{1,0:T(1,128)} %bitcast.2, s32[1,128]{1,0:T(1,128)} %bitcast.3, bf16[128,256]{1,0:T(8,128)(2,1)} %scale_ref.1, s32[1]{0:T(128)S(6)} %copy.12.section_ref), custom_call_target="tpu_custom_call" | custom-call | flops 4000000000 | bytes 8388608 | tf_op jit(solution)/shard_map/pack_weights/pallas_call | solution.py:219
  6.7 0.0 copy-start.1
  6.7 0.0 copy-start.3
  6.7 0.0 collective-permute-start.4
  6.8 1.1 %collective-permute-start.1 = (bf16[80,256]{1,0:T(8,128)(2,1)}, bf16[80,256]{1,0:T(8,128)(2,1)S(1)}, u32[]{:S(2)}, u32[]{:S(2)}) collective-permute-start(bf16[80,256]{1,0:T(8,128)(2,1)} %get-tuple-element.16), channel_id=1, source_target_pairs={{0,8},{4,12},{8,0},{12,4},{1,9},{5,13},{9,1},{13,5},{2,10},{6,14},... | collective-permute-start | bytes 122888 | tf_op jit(solution)/shard_map/ppermute | solution.py:227
  7.9 2.9 %collective-permute-start.2 = (bf16[80,256]{1,0:T(8,128)(2,1)}, bf16[80,256]{1,0:T(8,128)(2,1)S(1)}, u32[]{:S(2)}, u32[]{:S(2)}) collective-permute-start(bf16[80,256]{1,0:T(8,128)(2,1)} %get-tuple-element.17), channel_id=1, source_target_pairs={{0,12},{4,8},{8,4},{12,0},{1,13},{5,9},{9,5},{13,1},{2,14},{6,10},... | collective-permute-start | bytes 122888 | tf_op jit(solution)/shard_map/ppermute | solution.py:227
  10.8 0.0 collective-permute-start.3
  10.8 0.0 copy-done
  10.8 0.0 copy-done.4
  10.8 0.0 copy-done.5
  10.8 1.0 %pump.1.pumped_ref = bf16[64,32,256]{2,1,0:T(8,128)(2,1)S(1)} custom-call(bf16[128,32,256]{2,1,0:T(8,128)(2,1)S(1)} %copy-done, f32[32]{0:T(128)S(1)} %copy-done.4, s32[32]{0:T(128)S(1)} %copy-done.5), custom_call_target="tpu_custom_call" | custom-call | flops 1000000 | bytes 1024 | tf_op jit(solution)/shard_map/pump/pallas_call | solution.py:230
  11.9 0.0 collective-permute-done.4.swapped_ref
  11.9 0.0 copy-done.1
  11.9 0.0 copy-done.3
  11.9 0.5 %own_blocks.1.sum_ref = f32[64,32,256]{2,1,0:T(8,128)S(1)} custom-call(bf16[64,32,256]{2,1,0:T(8,128)(2,1)S(1)} %pump.1.pumped_ref, bf16[1,256,256]{2,1,0:T(8,128)(2,1)S(1)} %copy-done.1, bf16[80,256]{1,0:T(8,128)(2,1)S(1)} %copy-done.3, bf16[80,256]{1,0:T(8,128)(2,1)S(1)} %collective-permute-done.4.swapped_ref), custom_call_target="tpu_custom_call" | custom-call | flops 1000000 | bytes 1024 | tf_op jit(solution)/shard_map/own_blocks/pallas_call | solution.py:240
  12.4 0.0 copy-start.2
  12.4 1.3 %collective-permute-done.1.refs_4_ = bf16[80,256]{1,0:T(8,128)(2,1)S(1)} collective-permute-done((bf16[80,256]{1,0:T(8,128)(2,1)}, bf16[80,256]{1,0:T(8,128)(2,1)S(1)}, u32[]{:S(2)}, u32[]{:S(2)}) %collective-permute-start.1) | collective-permute-done | bytes 40992 | tf_op jit(solution)/shard_map/ppermute | solution.py:227
  13.8 0.5 %collective-permute-done.2.refs_6_ = bf16[80,256]{1,0:T(8,128)(2,1)S(1)} collective-permute-done((bf16[80,256]{1,0:T(8,128)(2,1)}, bf16[80,256]{1,0:T(8,128)(2,1)S(1)}, u32[]{:S(2)}, u32[]{:S(2)}) %collective-permute-start.2) | collective-permute-done | bytes 40992 | tf_op jit(solution)/shard_map/ppermute | solution.py:227
  14.3 0.7 %collective-permute-done.3.refs_2_ = bf16[80,256]{1,0:T(8,128)(2,1)S(1)} collective-permute-done((bf16[80,256]{1,0:T(8,128)(2,1)}, bf16[80,256]{1,0:T(8,128)(2,1)S(1)}, u32[]{:S(2)}, u32[]{:S(2)}) %collective-permute-start.3) | collective-permute-done | bytes 40992 | tf_op jit(solution)/shard_map/ppermute | solution.py:227
  15.0 0.0 collective-permute-done.refs_0_
  15.0 0.6 %collective-permute-start.9 = (bf16[1,256,256]{2,1,0:T(8,128)(2,1)S(1)}, bf16[1,256,256]{2,1,0:T(8,128)(2,1)S(1)}, u32[]{:S(2)}, u32[]{:S(2)}) collective-permute-start(bf16[1,256,256]{2,1,0:T(8,128)(2,1)S(1)} %collective-permute-done.refs_0_), channel_id=1, source_target_pairs={{0,3},{1,0},{2,1},{3,2},{4,7},{5,4},{6,5},{7,6},{8,11},{9,8},{10,9... | collective-permute-start | bytes 393224 | tf_op jit(solution)/shard_map/ppermute | solution.py:261
  15.6 0.0 collective-permute-start.5
  15.6 0.5 %collective-permute-start.6 = (bf16[80,256]{1,0:T(8,128)(2,1)S(1)}, bf16[80,256]{1,0:T(8,128)(2,1)S(1)}, u32[]{:S(2)}, u32[]{:S(2)}) collective-permute-start(bf16[80,256]{1,0:T(8,128)(2,1)S(1)} %collective-permute-done.3.refs_2_), channel_id=1, source_target_pairs={{0,1},{1,0},{2,3},{3,2},{4,5},{5,4},{6,7},{7,6},{8,9},{9,8},{10,11... | collective-permute-start | bytes 122888 | tf_op jit(solution)/shard_map/ppermute | solution.py:266
  16.1 0.0 collective-permute-start.7
  16.1 0.5 %collective-permute-start.8 = (bf16[80,256]{1,0:T(8,128)(2,1)S(1)}, bf16[80,256]{1,0:T(8,128)(2,1)S(1)}, u32[]{:S(2)}, u32[]{:S(2)}) collective-permute-start(bf16[80,256]{1,0:T(8,128)(2,1)S(1)} %collective-permute-done.2.refs_6_), channel_id=1, source_target_pairs={{0,1},{1,0},{2,3},{3,2},{4,5},{5,4},{6,7},{7,6},{8,9},{9,8},{10,11... | collective-permute-start | bytes 122888 | tf_op jit(solution)/shard_map/ppermute | solution.py:266
  16.6 1.5 %collective-permute-done.9.refs_0_ = bf16[1,256,256]{2,1,0:T(8,128)(2,1)S(1)} collective-permute-done((bf16[1,256,256]{2,1,0:T(8,128)(2,1)S(1)}, bf16[1,256,256]{2,1,0:T(8,128)(2,1)S(1)}, u32[]{:S(2)}, u32[]{:S(2)}) %collective-permute-start.9) | collective-permute-done | bytes 131104 | tf_op jit(solution)/shard_map/ppermute | solution.py:261
  18.1 0.8 %collective-permute-start.10 = (bf16[1,256,256]{2,1,0:T(8,128)(2,1)S(1)}, bf16[1,256,256]{2,1,0:T(8,128)(2,1)S(1)}, u32[]{:S(2)}, u32[]{:S(2)}) collective-permute-start(bf16[1,256,256]{2,1,0:T(8,128)(2,1)S(1)} %collective-permute-done.9.refs_0_), channel_id=1, source_target_pairs={{0,1},{1,0},{2,3},{3,2},{4,5},{5,4},{6,7},{7,6},{8,9},{9,8},{10,11... | collective-permute-start | bytes 393224 | tf_op jit(solution)/shard_map/ppermute | solution.py:262
  18.9 0.0 collective-permute-done.6.refs_3_
  18.9 0.0 collective-permute-done.7.refs_5_
  18.9 0.0 collective-permute-done.8.refs_7_
  18.9 0.0 collective-permute-done.5.refs_1_
  18.9 1.2 %stage.1 = (f32[64,32,256]{2,1,0:T(8,128)S(1)}, f32[1,64,256]{2,1,0:T(8,128)S(1)}) custom-call(bf16[64,32,256]{2,1,0:T(8,128)(2,1)S(1)} %pump.1.pumped_ref, f32[64,32,256]{2,1,0:T(8,128)S(1)} %own_blocks.1.sum_ref, bf16[1,256,256]{2,1,0:T(8,128)(2,1)S(1)} %collective-permute-done.refs_0_, ...), custom_call_target="tpu_custom_call", output_to_operand_aliasing={{0}: (1, {})} | custom-call | flops 4000000000 | bytes 8388608 | tf_op jit(solution)/shard_map/stage/pallas_call | solution.py:271
  20.1 0.0 collective-permute-done.10.refs_1_
  20.1 0.0 copy-done.2
  20.2 1.7 %last_stage.1 = f32[64,32,256]{2,1,0:T(8,128)} custom-call(bf16[64,32,256]{2,1,0:T(8,128)(2,1)S(1)} %pump.1.pumped_ref, f32[64,32,256]{2,1,0:T(8,128)S(1)} %get-tuple-element.25.sum_ref, f32[1,64,256]{2,1,0:T(8,128)S(1)} %get-tuple-element.26.weight_ref, bf16[256,256]{1,0:T(8,128)(2,1)S(1)} %copy-done.2, ...), custom_call_target="tpu_custom_call" | custom-call | tf_op jit(solution)/shard_map/last_stage/pallas_call | solution.py:291
Async XLA Ops:
  0.0 15.0 %collective-permute-start = (bf16[1,256,256]{2,1,0:T(8,128)(2,1)}, bf16[1,256,256]{2,1,0:T(8,128)(2,1)S(1)}, u32[]{:S(2)}, u32[]{:S(2)}) collective-permute-start(bf16[1,256,256]{2,1,0:T(8,128)(2,1)} %basis_ref.1), channel_id=1, source_target_pairs={{0,8},{1,5},{2,14},{3,7},{4,12},{5,1},{6,10},{7,3},{8,0},{9,13},{1... | collective-permute-start | bytes 393224 | tf_op jit(solution)/shard_map/ppermute | solution.py:217
  4.7 6.1 %copy-start = (bf16[128,32,256]{2,1,0:T(8,128)(2,1)S(1)}, bf16[128,32,256]{2,1,0:T(8,128)(2,1)}, u32[]{:S(2)}) copy-start(bf16[128,32,256]{2,1,0:T(8,128)(2,1)} %mortar_ref.1) | copy-start | bytes 6291460
  4.7 6.1 %copy-start.4 = (f32[32]{0:T(128)S(1)}, f32[32]{0:T(128)}, u32[]{:S(2)}) copy-start(f32[32]{0:T(128)} %rate_ref.1) | copy-start | bytes 388
  4.7 6.1 %copy-start.5 = (s32[32]{0:T(128)S(1)}, s32[32]{0:T(128)}, u32[]{:S(2)}) copy-start(s32[32]{0:T(128)} %cell_ref.1) | copy-start | bytes 388
  6.7 5.1 %copy-start.1 = (bf16[1,256,256]{2,1,0:T(8,128)(2,1)S(1)}, bf16[1,256,256]{2,1,0:T(8,128)(2,1)}, u32[]{:S(2)}) copy-start(bf16[1,256,256]{2,1,0:T(8,128)(2,1)} %basis_ref.1) | copy-start | bytes 393220
  6.7 5.1 %copy-start.3 = (bf16[80,256]{1,0:T(8,128)(2,1)S(1)}, bf16[80,256]{1,0:T(8,128)(2,1)}, u32[]{:S(2)}) copy-start(bf16[80,256]{1,0:T(8,128)(2,1)} %get-tuple-element.19.pack_ref) | copy-start | bytes 122884
  6.7 5.1 %collective-permute-start.4 = (bf16[80,256]{1,0:T(8,128)(2,1)}, bf16[80,256]{1,0:T(8,128)(2,1)S(1)}, u32[]{:S(2)}, u32[]{:S(2)}) collective-permute-start(bf16[80,256]{1,0:T(8,128)(2,1)} %get-tuple-element.19.pack_ref), channel_id=1, source_target_pairs={{0,1},{1,0},{2,3},{3,2},{4,5},{5,4},{6,7},{7,6},{8,9},{9,8},{10,11... | collective-permute-start | bytes 122888 | tf_op jit(solution)/shard_map/ppermute | solution.py:228
  6.8 7.0 %collective-permute-start.1 = (bf16[80,256]{1,0:T(8,128)(2,1)}, bf16[80,256]{1,0:T(8,128)(2,1)S(1)}, u32[]{:S(2)}, u32[]{:S(2)}) collective-permute-start(bf16[80,256]{1,0:T(8,128)(2,1)} %get-tuple-element.16), channel_id=1, source_target_pairs={{0,8},{4,12},{8,0},{12,4},{1,9},{5,13},{9,1},{13,5},{2,10},{6,14},... | collective-permute-start | bytes 122888 | tf_op jit(solution)/shard_map/ppermute | solution.py:227
  7.9 6.4 %collective-permute-start.2 = (bf16[80,256]{1,0:T(8,128)(2,1)}, bf16[80,256]{1,0:T(8,128)(2,1)S(1)}, u32[]{:S(2)}, u32[]{:S(2)}) collective-permute-start(bf16[80,256]{1,0:T(8,128)(2,1)} %get-tuple-element.17), channel_id=1, source_target_pairs={{0,12},{4,8},{8,4},{12,0},{1,13},{5,9},{9,5},{13,1},{2,14},{6,10},... | collective-permute-start | bytes 122888 | tf_op jit(solution)/shard_map/ppermute | solution.py:227
  10.8 4.2 %collective-permute-start.3 = (bf16[80,256]{1,0:T(8,128)(2,1)}, bf16[80,256]{1,0:T(8,128)(2,1)S(1)}, u32[]{:S(2)}, u32[]{:S(2)}) collective-permute-start(bf16[80,256]{1,0:T(8,128)(2,1)} %get-tuple-element.18), channel_id=1, source_target_pairs={{0,4},{4,0},{8,12},{12,8},{1,5},{5,1},{9,13},{13,9},{2,6},{6,2},{1... | collective-permute-start | bytes 122888 | tf_op jit(solution)/shard_map/ppermute | solution.py:227
  12.4 7.7 %copy-start.2 = (bf16[256,256]{1,0:T(8,128)(2,1)S(1)}, bf16[256,256]{1,0:T(8,128)(2,1)}, u32[]{:S(2)}) copy-start(bf16[256,256]{1,0:T(8,128)(2,1)} %projection_ref.1) | copy-start | bytes 393220
  15.0 3.1 %collective-permute-start.9 = (bf16[1,256,256]{2,1,0:T(8,128)(2,1)S(1)}, bf16[1,256,256]{2,1,0:T(8,128)(2,1)S(1)}, u32[]{:S(2)}, u32[]{:S(2)}) collective-permute-start(bf16[1,256,256]{2,1,0:T(8,128)(2,1)S(1)} %collective-permute-done.refs_0_), channel_id=1, source_target_pairs={{0,3},{1,0},{2,1},{3,2},{4,7},{5,4},{6,5},{7,6},{8,11},{9,8},{10,9... | collective-permute-start | bytes 393224 | tf_op jit(solution)/shard_map/ppermute | solution.py:261
  15.6 3.4 %collective-permute-start.5 = (bf16[1,256,256]{2,1,0:T(8,128)(2,1)S(1)}, bf16[1,256,256]{2,1,0:T(8,128)(2,1)S(1)}, u32[]{:S(2)}, u32[]{:S(2)}) collective-permute-start(bf16[1,256,256]{2,1,0:T(8,128)(2,1)S(1)} %collective-permute-done.refs_0_), channel_id=1, source_target_pairs={{0,1},{1,0},{2,3},{3,2},{4,5},{5,4},{6,7},{7,6},{8,9},{9,8},{10,11... | collective-permute-start | bytes 393224 | tf_op jit(solution)/shard_map/ppermute | solution.py:259
  15.6 3.4 %collective-permute-start.6 = (bf16[80,256]{1,0:T(8,128)(2,1)S(1)}, bf16[80,256]{1,0:T(8,128)(2,1)S(1)}, u32[]{:S(2)}, u32[]{:S(2)}) collective-permute-start(bf16[80,256]{1,0:T(8,128)(2,1)S(1)} %collective-permute-done.3.refs_2_), channel_id=1, source_target_pairs={{0,1},{1,0},{2,3},{3,2},{4,5},{5,4},{6,7},{7,6},{8,9},{9,8},{10,11... | collective-permute-start | bytes 122888 | tf_op jit(solution)/shard_map/ppermute | solution.py:266
  16.1 2.9 %collective-permute-start.7 = (bf16[80,256]{1,0:T(8,128)(2,1)S(1)}, bf16[80,256]{1,0:T(8,128)(2,1)S(1)}, u32[]{:S(2)}, u32[]{:S(2)}) collective-permute-start(bf16[80,256]{1,0:T(8,128)(2,1)S(1)} %collective-permute-done.1.refs_4_), channel_id=1, source_target_pairs={{0,1},{1,0},{2,3},{3,2},{4,5},{5,4},{6,7},{7,6},{8,9},{9,8},{10,11... | collective-permute-start | bytes 122888 | tf_op jit(solution)/shard_map/ppermute | solution.py:266
  16.1 2.9 %collective-permute-start.8 = (bf16[80,256]{1,0:T(8,128)(2,1)S(1)}, bf16[80,256]{1,0:T(8,128)(2,1)S(1)}, u32[]{:S(2)}, u32[]{:S(2)}) collective-permute-start(bf16[80,256]{1,0:T(8,128)(2,1)S(1)} %collective-permute-done.2.refs_6_), channel_id=1, source_target_pairs={{0,1},{1,0},{2,3},{3,2},{4,5},{5,4},{6,7},{7,6},{8,9},{9,8},{10,11... | collective-permute-start | bytes 122888 | tf_op jit(solution)/shard_map/ppermute | solution.py:266
  18.1 2.1 %collective-permute-start.10 = (bf16[1,256,256]{2,1,0:T(8,128)(2,1)S(1)}, bf16[1,256,256]{2,1,0:T(8,128)(2,1)S(1)}, u32[]{:S(2)}, u32[]{:S(2)}) collective-permute-start(bf16[1,256,256]{2,1,0:T(8,128)(2,1)S(1)} %collective-permute-done.9.refs_0_), channel_id=1, source_target_pairs={{0,1},{1,0},{2,3},{3,2},{4,5},{5,4},{6,7},{7,6},{8,9},{9,8},{10,11... | collective-permute-start | bytes 393224 | tf_op jit(solution)/shard_map/ppermute | solution.py:262

commit v5 on v4

--- a/solution.py
+++ b/solution.py
@@ -18,14 +18,20 @@
 WORK = pl.CostEstimate(flops=4_000_000_000, bytes_accessed=8 * MIB, transcendentals=0)
 
 
-def pack_kernel(owner_ref, slot_ref, scale_ref, section_ref, *packs):
-    subdomains = len(packs)
+def on_even(even, odd):
+    return jnp.where(lax.rem(lax.axis_index("rhs"), 2) == 0, even, odd)
+
+
+def pack_kernel(partners, owner_ref, slot_ref, scale_ref, section_ref, *packs):
     rows, dof_count = packs[0].shape
     rows -= ROW_TILE
     faces = owner_ref.shape[1]
     sign = (1 - 2 * section_ref[0]).astype(jnp.float32)
-    partners = lax.broadcasted_iota(jnp.int32, (subdomains, faces), 0)
-    named = (lax.axis_index("sub") ^ partners) == owner_ref[...]
+    here = lax.axis_index("sub")
+    owners = jnp.concatenate(
+        [jnp.full((1, faces), here ^ on_even(even, odd), jnp.int32) for even, odd in partners], axis=0
+    )
+    named = owners == owner_ref[...]
     earlier = lax.broadcasted_iota(jnp.int32, (faces, faces), 0) < lax.broadcasted_iota(
         jnp.int32, (faces, faces), 1
     )
@@ -34,7 +40,7 @@
     )
     place = jnp.where(named, rank, -1.0)
     at = lax.broadcasted_iota(jnp.int32, (rows, faces), 0).astype(jnp.float32)
-    hit = jnp.concatenate([place[p : p + 1, :] == at for p in range(subdomains)], axis=0)
+    hit = jnp.concatenate([place[p : p + 1, :] == at for p in range(len(packs))], axis=0)
     hit = hit.astype(jnp.bfloat16)
     packed = jnp.dot(hit, scale_ref[...], preferred_element_type=jnp.float32) * sign
     listed = lax.dot_general(
@@ -98,43 +104,22 @@
         sum_ref[at] = flux.reshape(tile_blocks, columns, dof_count)
 
 
-def on_even(even, odd):
-    return jnp.where(lax.rem(lax.axis_index("rhs"), 2) == 0, even, odd)
-
-
-def stage_kernel(groups, pumped_ref, sum_ref, *refs):
-    bases, refs = refs[: 2 * len(groups)], refs[2 * len(groups) :]
-    packs, (out_ref, late_ref, weight_ref, basis_ref, scaled_ref) = refs[:-5], refs[-5:]
+def stage_kernel(kinds, pumped_ref, sum_ref, *refs):
+    bases, refs = refs[: 2 * len(kinds)], refs[2 * len(kinds) :]
+    packs, (out_ref, weight_ref, basis_ref, scaled_ref) = refs[:-4], refs[-4:]
     blocks_own, columns, dof_count = pumped_ref.shape
     face_id = lax.axis_index("face")
     rows = packs[0].shape[0] - ROW_TILE
-    weights = {}
-
-    def weight(partner):
-        if partner not in weights:
-            weights[partner] = block_weights(packs[2 * partner - 2 : 2 * partner], rows, blocks_own)
-        return weights[partner]
-
-    count = late = 0
-    for at, (a, b, c) in enumerate(groups):
-        first, first_swapped = bases[2 * at : 2 * at + 2]
-        spots = [None, None]
-        if a != b:
-            spots[0] = count
-            weight_ref[count] = on_even(weight(a), weight(b))
-            late_ref[late] = on_even(weight(b), weight(a))
-            count, late = count + 1, late + 1
-        if c != a:
-            spots[1] = count
-            weight_ref[count] = weight(c)
-            count += 1
-        elif a == b:
-            spots = [count, count]
-            weight_ref[count] = weight(c)
-            count += 1
-        spare = weight_ref.shape[0]
-        spots = [spare if spot is None else spot for spot in spots]
-        for array, core_0, core_1 in ((first, *spots), (first_swapped, *spots[::-1])):
+    count = weight_ref.shape[0]
+    for spot in range(count):
+        weight_ref[spot] = block_weights(packs[2 * spot : 2 * spot + 2], rows, blocks_own)
+    spot = 0
+    for at, (far, near) in enumerate(kinds):
+        spots = []
+        for wanted in (far, near):
+            spots.append(spot if wanted else count)
+            spot += wanted
+        for array, core_0, core_1 in ((bases[2 * at], *spots), (bases[2 * at + 1], *spots[::-1])):
             start = pl.multiple_of(jnp.where(face_id == 0, core_0, core_1) * dof_count, dof_count)
             basis_ref[pl.ds(start, dof_count), :] = array[0]
 
@@ -153,12 +138,14 @@
         out_ref[at] = total.reshape(tile_blocks, columns, dof_count) + sum_ref[at]
 
 
-def last_kernel(pumped_ref, sum_ref, weight_ref, projection_ref, *refs):
-    bases, (result_ref, basis_ref, scaled_ref, out_ref, sems) = refs[:-5], refs[-5:]
+def last_kernel(pumped_ref, sum_ref, projection_ref, *refs):
+    arrays, (result_ref, weight_ref, basis_ref, scaled_ref, out_ref, sems) = refs[:-6], refs[-6:]
     blocks_own, columns, dof_count = pumped_ref.shape
     count = weight_ref.shape[0]
     for at in range(count):
-        for core, array in ((1, bases[2 * at]), (0, bases[2 * at + 1])):
+        basis, basis_swapped, pack, pack_swapped = arrays[4 * at : 4 * at + 4]
+        weight_ref[at] = block_weights((pack, pack_swapped), pack.shape[0] - ROW_TILE, blocks_own)
+        for core, array in ((1, basis), (0, basis_swapped)):
 
             @pl.when(lax.axis_index("face") == core)
             def _():
@@ -216,15 +203,26 @@
         ]
         firsts.append(lax.ppermute(basis, ("sub", "rhs", "face"), pairs))
 
+    kinds = [(a != b, c != a or a == b) for a, b, c in groups]
+    ways = [(0, 0)]
+    for (a, b, c), (far, near) in zip(groups, kinds):
+        ways += [(a, b)] * far + [(c, c)] * near
     packs = pl.pallas_call(
-        pack_kernel,
-        out_shape=[jax.ShapeDtypeStruct((pack_rows, dof_count), jnp.bfloat16)] * subdomains,
+        functools.partial(pack_kernel, ways),
+        out_shape=[jax.ShapeDtypeStruct((pack_rows, dof_count), jnp.bfloat16)] * len(ways),
         in_specs=[VMEM, VMEM, VMEM, SMEM],
-        out_specs=[VMEM] * subdomains,
+        out_specs=[VMEM] * len(ways),
         cost_estimate=WORK,
         name="pack_weights",
     )(face_owner.reshape(1, faces_dev), face_slot.reshape(1, faces_dev), face_scale, section)
-    arrived = [lax.ppermute(packs[p], "sub", [(i, i ^ p) for i in range(subdomains)]) for p in partners]
+    arrived = []
+    for (even, odd), pack in zip(ways[1:], packs[1:]):
+        pairs = [
+            (s * rights + r, (s ^ (odd if r % 2 else even)) * rights + r)
+            for s in range(subdomains)
+            for r in range(rights)
+        ]
+        arrived.append(lax.ppermute(pack, ("sub", "rhs"), pairs))
     own_swapped = lax.ppermute(packs[0], "face", swap)
 
     pumped = pl.pallas_call(
@@ -254,28 +252,28 @@
         for r in range(rights)
         for face in range(halves)
     ]
+    cross = [(i, i ^ 1) for i in range(rights)]
     early, late = [], []
-    for (a, b, _), first in zip(groups, firsts):
+    for (far, _), first in zip(kinds, firsts):
         early += [first, lax.ppermute(first, "face", swap)]
-        if a != b:
+        if far:
             second = lax.ppermute(first, ("rhs", "face"), pairs)
-            late += [second, lax.ppermute(second, "face", swap)]
-    weights = []
-    for partner in range(1, subdomains):
-        array = arrived[partners.index(partner)]
+            late.append([second, lax.ppermute(second, "face", swap)])
+    weights, others_late = [], iter(late)
+    for (even, odd), array in zip(ways[1:], arrived):
         weights += [array, lax.ppermute(array, "face", swap)]
-
-    late_count = len(late) // 2
+        if even != odd:
+            second = lax.ppermute(array, "rhs", cross)
+            next(others_late).extend([second, lax.ppermute(second, "face", swap)])
+
+    late_count = len(late)
     count = others - late_count
     operands = [pumped, own_sum, *early, *weights]
-    total, late_weight = pl.pallas_call(
-        functools.partial(stage_kernel, groups),
-        out_shape=[
-            jax.ShapeDtypeStruct(block_shape, jnp.float32),
-            jax.ShapeDtypeStruct((late_count, blocks_own, dof_count), jnp.float32),
-        ],
+    total = pl.pallas_call(
+        functools.partial(stage_kernel, kinds),
+        out_shape=jax.ShapeDtypeStruct(block_shape, jnp.float32),
         in_specs=[VMEM] * len(operands),
-        out_specs=[VMEM, VMEM],
+        out_specs=VMEM,
         scratch_shapes=[
             pltpu.VMEM((count, blocks_own, dof_count), jnp.float32),
             pltpu.VMEM(((count + 1) * dof_count, dof_count), jnp.bfloat16),
@@ -287,13 +285,14 @@
         name="stage",
     )(*operands)
 
-    operands = [pumped, total, late_weight, projection, *late]
+    operands = [pumped, total, projection, *sum(late, [])]
     return pl.pallas_call(
         last_kernel,
         out_shape=jax.ShapeDtypeStruct(block_shape, jnp.float32),
         in_specs=[VMEM] * len(operands),
         out_specs=HBM,
         scratch_shapes=[
+            pltpu.VMEM((late_count, blocks_own, dof_count), jnp.float32),
             pltpu.VMEM((late_count * dof_count, dof_count), jnp.bfloat16),
             pltpu.VMEM((2, blocks_own // LAST_TILES * cols_dev, late_count * dof_count), jnp.bfloat16),
             pltpu.VMEM(block_shape, jnp.float32),

time: 22 us -> 23.2 us (1.055)
  waiting for transfers between devices: 4.07 us -> 4.82 us
  starting transfers between devices: 10.5 us -> 10.9 us
    ppermute x4 -> x5, waiting for transfers between devices: 2.56 us -> 4.8 us  [the longest x1 2.8 us: on_device(): second = lax.ppermute(array, 'rhs', cross)]
    ppermute x1, waiting for transfers between devices: 1.5 us -> 0.01 us  [on_device(): second = lax.ppermute(first, ('rhs', 'face'), pairs)]
    ppermute x1, starting transfers between devices: 0.55 us -> 1.86 us  [on_device(): second = lax.ppermute(first, ('rhs', 'face'), pairs)]
    ppermute x3 -> x2, starting transfers between devices: 1.02 us -> 0.51 us  [on_device(): weights += [array, lax.ppermute(array, 'face', swap)]]
    ppermute x4 -> x5, starting transfers between devices: 4.85 us -> 4.45 us  [the longest x2 1.98 us: on_device(): arrived.append(lax.ppermute(pack, ('sub', 'rhs'), pairs))]
  transfers between devices with their start and end apart: 11 -> 11, of which waited for: 4 -> 3; matrix products, arithmetic and copies ran while one was open for 0% -> 0% of each run, Pallas kernels for 22% -> 21%
where the time goes in v5:
time: 23.2 us; the launch traced here: 23.1 us
  starting transfers between devices  10.9 us (47%)
  Pallas kernels  6.61 us (28%)
  waiting for transfers between devices  4.82 us (21%)
  between operations  0.77 us (3%)
    ppermute x1, starting transfers between devices, on_device(): firsts.append(lax.ppermute(basis, ('sub', 'rhs', 'face'), pairs))  4.04 us
    ppermute x1, waiting for transfers between devices, on_device(): second = lax.ppermute(array, 'rhs', cross)  2.8 us
    pallas_call x1, Pallas kernels, on_device(): pl.pallas_call(functools.partial(pack_kernel, ways), out_shape=[jax.Shape...  2.01 us
    ppermute x2, waiting for transfers between devices, on_device(): arrived.append(lax.ppermute(pack, ('sub', 'rhs'), pairs))  2 us
    ppermute x2, starting transfers between devices, on_device(): arrived.append(lax.ppermute(pack, ('sub', 'rhs'), pairs))  1.98 us
    ppermute x1, starting transfers between devices, on_device(): second = lax.ppermute(array, 'rhs', cross)  1.96 us
    pallas_call x1, Pallas kernels, on_device(): pl.pallas_call(last_kernel, out_shape=jax.ShapeDtypeStruct(block_shape, j...  1.86 us
    ppermute x1, starting transfers between devices, on_device(): second = lax.ppermute(first, ('rhs', 'face'), pairs)  1.86 us
  transfers between devices with their start and end apart: 11, of which 3 were waited for; matrix products, arithmetic and copies ran while one was open for 0% of the time, Pallas kernels for 21%

profile of v5, /device:TPU:0, one launch (start us, length us, event | category | flops | bytes accessed | tf_op | source)
XLA Modules:
  0.0 23.1 jit_solution(1373989314158281620)
XLA Ops:
  0.0 4.0 %collective-permute-start = (bf16[1,256,256]{2,1,0:T(8,128)(2,1)}, bf16[1,256,256]{2,1,0:T(8,128)(2,1)S(1)}, u32[]{:S(2)}, u32[]{:S(2)}) collective-permute-start(bf16[1,256,256]{2,1,0:T(8,128)(2,1)} %basis_ref.1), channel_id=1, source_target_pairs={{0,8},{1,5},{2,14},{3,7},{4,12},{5,1},{6,10},{7,3},{8,0},{9,13},{1... | collective-permute-start | bytes 393224 | tf_op jit(solution)/shard_map/ppermute | solution.py:204
  4.7 0.0 copy-start
  4.7 0.0 copy-start.4
  4.7 0.0 copy-start.5
  4.7 2.0 %pack_weights.1 = (bf16[80,256]{1,0:T(8,128)(2,1)}, bf16[80,256]{1,0:T(8,128)(2,1)}, bf16[80,256]{1,0:T(8,128)(2,1)}) custom-call(s32[1,128]{1,0:T(1,128)} %bitcast.2, s32[1,128]{1,0:T(1,128)} %bitcast.3, bf16[128,256]{1,0:T(8,128)(2,1)} %scale_ref.1, s32[1]{0:T(128)S(6)} %copy.12.section_ref), custom_call_target="tpu_custom_call" | custom-call | flops 4000000000 | bytes 8388608 | tf_op jit(solution)/shard_map/pack_weights/pallas_call | solution.py:210
  6.7 0.0 copy-start.1
  6.7 0.0 copy-start.3
  6.7 0.0 collective-permute-start.3
  6.7 1.1 %collective-permute-start.1 = (bf16[80,256]{1,0:T(8,128)(2,1)}, bf16[80,256]{1,0:T(8,128)(2,1)S(1)}, u32[]{:S(2)}, u32[]{:S(2)}) collective-permute-start(bf16[80,256]{1,0:T(8,128)(2,1)} %get-tuple-element.12), channel_id=1, source_target_pairs={{0,8},{2,14},{4,12},{6,10},{8,0},{10,6},{12,4},{14,2},{1,9},{3,15}... | collective-permute-start | bytes 122888 | tf_op jit(solution)/shard_map/ppermute | solution.py:225
  7.9 0.9 %collective-permute-start.2 = (bf16[80,256]{1,0:T(8,128)(2,1)}, bf16[80,256]{1,0:T(8,128)(2,1)S(1)}, u32[]{:S(2)}, u32[]{:S(2)}) collective-permute-start(bf16[80,256]{1,0:T(8,128)(2,1)} %get-tuple-element.13), channel_id=1, source_target_pairs={{0,4},{2,6},{4,0},{6,2},{8,12},{10,14},{12,8},{14,10},{1,5},{3,7},... | collective-permute-start | bytes 122888 | tf_op jit(solution)/shard_map/ppermute | solution.py:225
  8.7 0.0 copy-done
  8.7 0.0 copy-done.4
  8.7 0.0 copy-done.5
  8.7 1.0 %pump.1.pumped_ref = bf16[64,32,256]{2,1,0:T(8,128)(2,1)S(1)} custom-call(bf16[128,32,256]{2,1,0:T(8,128)(2,1)S(1)} %copy-done, f32[32]{0:T(128)S(1)} %copy-done.4, s32[32]{0:T(128)S(1)} %copy-done.5), custom_call_target="tpu_custom_call" | custom-call | flops 1000000 | bytes 1024 | tf_op jit(solution)/shard_map/pump/pallas_call | solution.py:228
  9.8 0.0 collective-permute-done.3.swapped_ref
  9.8 0.0 copy-done.1
  9.8 0.0 copy-done.3
  9.8 0.5 %own_blocks.1.sum_ref = f32[64,32,256]{2,1,0:T(8,128)S(1)} custom-call(bf16[64,32,256]{2,1,0:T(8,128)(2,1)S(1)} %pump.1.pumped_ref, bf16[1,256,256]{2,1,0:T(8,128)(2,1)S(1)} %copy-done.1, bf16[80,256]{1,0:T(8,128)(2,1)S(1)} %copy-done.3, bf16[80,256]{1,0:T(8,128)(2,1)S(1)} %collective-permute-done.3.swapped_ref), custom_call_target="tpu_custom_call" | custom-call | flops 1000000 | bytes 1024 | tf_op jit(solution)/shard_map/own_blocks/pallas_call | solution.py:238
  10.3 0.0 copy-start.2
  10.4 1.6 %collective-permute-done.1.refs_2_ = bf16[80,256]{1,0:T(8,128)(2,1)S(1)} collective-permute-done((bf16[80,256]{1,0:T(8,128)(2,1)}, bf16[80,256]{1,0:T(8,128)(2,1)S(1)}, u32[]{:S(2)}, u32[]{:S(2)}) %collective-permute-start.1) | collective-permute-done | bytes 40992 | tf_op jit(solution)/shard_map/ppermute | solution.py:225
  11.9 0.4 %collective-permute-done.2.refs_4_ = bf16[80,256]{1,0:T(8,128)(2,1)S(1)} collective-permute-done((bf16[80,256]{1,0:T(8,128)(2,1)}, bf16[80,256]{1,0:T(8,128)(2,1)S(1)}, u32[]{:S(2)}, u32[]{:S(2)}) %collective-permute-start.2) | collective-permute-done | bytes 40992 | tf_op jit(solution)/shard_map/ppermute | solution.py:225
  12.4 0.0 collective-permute-done.refs_0_
  12.4 1.9 %collective-permute-start.7 = (bf16[1,256,256]{2,1,0:T(8,128)(2,1)S(1)}, bf16[1,256,256]{2,1,0:T(8,128)(2,1)S(1)}, u32[]{:S(2)}, u32[]{:S(2)}) collective-permute-start(bf16[1,256,256]{2,1,0:T(8,128)(2,1)S(1)} %collective-permute-done.refs_0_), channel_id=1, source_target_pairs={{0,3},{1,0},{2,1},{3,2},{4,7},{5,4},{6,5},{7,6},{8,11},{9,8},{10,9... | collective-permute-start | bytes 393224 | tf_op jit(solution)/shard_map/ppermute | solution.py:260
  14.2 0.0 collective-permute-start.4
  14.2 2.0 %collective-permute-start.9 = (bf16[80,256]{1,0:T(8,128)(2,1)S(1)}, bf16[80,256]{1,0:T(8,128)(2,1)S(1)}, u32[]{:S(2)}, u32[]{:S(2)}) collective-permute-start(bf16[80,256]{1,0:T(8,128)(2,1)S(1)} %collective-permute-done.1.refs_2_), channel_id=1, source_target_pairs={{0,2},{2,0},{1,3},{3,1},{4,6},{6,4},{5,7},{7,5},{8,10},{10,8},{9,1... | collective-permute-start | bytes 122888 | tf_op jit(solution)/shard_map/ppermute | solution.py:266
  16.2 0.0 collective-permute-start.5
  16.2 0.5 %collective-permute-start.6 = (bf16[80,256]{1,0:T(8,128)(2,1)S(1)}, bf16[80,256]{1,0:T(8,128)(2,1)S(1)}, u32[]{:S(2)}, u32[]{:S(2)}) collective-permute-start(bf16[80,256]{1,0:T(8,128)(2,1)S(1)} %collective-permute-done.2.refs_4_), channel_id=1, source_target_pairs={{0,1},{1,0},{2,3},{3,2},{4,5},{5,4},{6,7},{7,6},{8,9},{9,8},{10,11... | collective-permute-start | bytes 122888 | tf_op jit(solution)/shard_map/ppermute | solution.py:264
  16.7 2.8 %collective-permute-done.9.refs_2_ = bf16[80,256]{1,0:T(8,128)(2,1)S(1)} collective-permute-done((bf16[80,256]{1,0:T(8,128)(2,1)S(1)}, bf16[80,256]{1,0:T(8,128)(2,1)S(1)}, u32[]{:S(2)}, u32[]{:S(2)}) %collective-permute-start.9) | collective-permute-done | bytes 40992 | tf_op jit(solution)/shard_map/ppermute | solution.py:266
  19.5 0.0 collective-permute-start.10
  19.5 0.0 collective-permute-done.7.refs_0_
  19.5 0.5 %collective-permute-start.8 = (bf16[1,256,256]{2,1,0:T(8,128)(2,1)S(1)}, bf16[1,256,256]{2,1,0:T(8,128)(2,1)S(1)}, u32[]{:S(2)}, u32[]{:S(2)}) collective-permute-start(bf16[1,256,256]{2,1,0:T(8,128)(2,1)S(1)} %collective-permute-done.7.refs_0_), channel_id=1, source_target_pairs={{0,1},{1,0},{2,3},{3,2},{4,5},{5,4},{6,7},{7,6},{8,9},{9,8},{10,11... | collective-permute-start | bytes 393224 | tf_op jit(solution)/shard_map/ppermute | solution.py:261
  20.0 0.0 collective-permute-done.5.refs_3_
  20.0 0.0 collective-permute-done.6.refs_5_
  20.0 0.0 collective-permute-done.4.refs_1_
  20.0 1.2 %stage.1.sum_ref = f32[64,32,256]{2,1,0:T(8,128)S(1)} custom-call(bf16[64,32,256]{2,1,0:T(8,128)(2,1)S(1)} %pump.1.pumped_ref, f32[64,32,256]{2,1,0:T(8,128)S(1)} %own_blocks.1.sum_ref, bf16[1,256,256]{2,1,0:T(8,128)(2,1)S(1)} %collective-permute-done.refs_0_, ...), custom_call_target="tpu_custom_call", output_to_operand_aliasing={{}: (1, {})} | custom-call | flops 4000000000 | bytes 8388608 | tf_op jit(solution)/shard_map/stage/pallas_call | solution.py:272
  21.2 0.0 collective-permute-done.10.refs_3_
  21.2 0.0 collective-permute-done.8.refs_1_
  21.2 0.0 copy-done.2
  21.2 1.9 %last_stage.1 = f32[64,32,256]{2,1,0:T(8,128)} custom-call(bf16[64,32,256]{2,1,0:T(8,128)(2,1)S(1)} %pump.1.pumped_ref, f32[64,32,256]{2,1,0:T(8,128)S(1)} %stage.1.sum_ref, bf16[256,256]{1,0:T(8,128)(2,1)S(1)} %copy-done.2, bf16[1,256,256]{2,1,0:T(8,128)(2,1)S(1)} %collective-permute-done.7.refs_0_, ...), custom_call_target="tpu_custom_call" | custom-call | tf_op jit(solution)/shard_map/last_stage/pallas_call | solution.py:289
Async XLA Ops:
  0.0 12.4 %collective-permute-start = (bf16[1,256,256]{2,1,0:T(8,128)(2,1)}, bf16[1,256,256]{2,1,0:T(8,128)(2,1)S(1)}, u32[]{:S(2)}, u32[]{:S(2)}) collective-permute-start(bf16[1,256,256]{2,1,0:T(8,128)(2,1)} %basis_ref.1), channel_id=1, source_target_pairs={{0,8},{1,5},{2,14},{3,7},{4,12},{5,1},{6,10},{7,3},{8,0},{9,13},{1... | collective-permute-start | bytes 393224 | tf_op jit(solution)/shard_map/ppermute | solution.py:204
  4.7 4.0 %copy-start = (bf16[128,32,256]{2,1,0:T(8,128)(2,1)S(1)}, bf16[128,32,256]{2,1,0:T(8,128)(2,1)}, u32[]{:S(2)}) copy-start(bf16[128,32,256]{2,1,0:T(8,128)(2,1)} %mortar_ref.1) | copy-start | bytes 6291460
  4.7 4.0 %copy-start.4 = (f32[32]{0:T(128)S(1)}, f32[32]{0:T(128)}, u32[]{:S(2)}) copy-start(f32[32]{0:T(128)} %rate_ref.1) | copy-start | bytes 388
  4.7 4.0 %copy-start.5 = (s32[32]{0:T(128)S(1)}, s32[32]{0:T(128)}, u32[]{:S(2)}) copy-start(s32[32]{0:T(128)} %cell_ref.1) | copy-start | bytes 388
  6.7 3.0 %copy-start.1 = (bf16[1,256,256]{2,1,0:T(8,128)(2,1)S(1)}, bf16[1,256,256]{2,1,0:T(8,128)(2,1)}, u32[]{:S(2)}) copy-start(bf16[1,256,256]{2,1,0:T(8,128)(2,1)} %basis_ref.1) | copy-start | bytes 393220
  6.7 3.1 %copy-start.3 = (bf16[80,256]{1,0:T(8,128)(2,1)S(1)}, bf16[80,256]{1,0:T(8,128)(2,1)}, u32[]{:S(2)}) copy-start(bf16[80,256]{1,0:T(8,128)(2,1)} %get-tuple-element.14.pack_ref) | copy-start | bytes 122884
  6.7 3.0 %collective-permute-start.3 = (bf16[80,256]{1,0:T(8,128)(2,1)}, bf16[80,256]{1,0:T(8,128)(2,1)S(1)}, u32[]{:S(2)}, u32[]{:S(2)}) collective-permute-start(bf16[80,256]{1,0:T(8,128)(2,1)} %get-tuple-element.14.pack_ref), channel_id=1, source_target_pairs={{0,1},{1,0},{2,3},{3,2},{4,5},{5,4},{6,7},{7,6},{8,9},{9,8},{10,11... | collective-permute-start | bytes 122888 | tf_op jit(solution)/shard_map/ppermute | solution.py:226
  6.7 5.2 %collective-permute-start.1 = (bf16[80,256]{1,0:T(8,128)(2,1)}, bf16[80,256]{1,0:T(8,128)(2,1)S(1)}, u32[]{:S(2)}, u32[]{:S(2)}) collective-permute-start(bf16[80,256]{1,0:T(8,128)(2,1)} %get-tuple-element.12), channel_id=1, source_target_pairs={{0,8},{2,14},{4,12},{6,10},{8,0},{10,6},{12,4},{14,2},{1,9},{3,15}... | collective-permute-start | bytes 122888 | tf_op jit(solution)/shard_map/ppermute | solution.py:225
  7.9 4.5 %collective-permute-start.2 = (bf16[80,256]{1,0:T(8,128)(2,1)}, bf16[80,256]{1,0:T(8,128)(2,1)S(1)}, u32[]{:S(2)}, u32[]{:S(2)}) collective-permute-start(bf16[80,256]{1,0:T(8,128)(2,1)} %get-tuple-element.13), channel_id=1, source_target_pairs={{0,4},{2,6},{4,0},{6,2},{8,12},{10,14},{12,8},{14,10},{1,5},{3,7},... | collective-permute-start | bytes 122888 | tf_op jit(solution)/shard_map/ppermute | solution.py:225
  10.3 10.9 %copy-start.2 = (bf16[256,256]{1,0:T(8,128)(2,1)S(1)}, bf16[256,256]{1,0:T(8,128)(2,1)}, u32[]{:S(2)}) copy-start(bf16[256,256]{1,0:T(8,128)(2,1)} %projection_ref.1) | copy-start | bytes 393220
  12.4 7.1 %collective-permute-start.7 = (bf16[1,256,256]{2,1,0:T(8,128)(2,1)S(1)}, bf16[1,256,256]{2,1,0:T(8,128)(2,1)S(1)}, u32[]{:S(2)}, u32[]{:S(2)}) collective-permute-start(bf16[1,256,256]{2,1,0:T(8,128)(2,1)S(1)} %collective-permute-done.refs_0_), channel_id=1, source_target_pairs={{0,3},{1,0},{2,1},{3,2},{4,7},{5,4},{6,5},{7,6},{8,11},{9,8},{10,9... | collective-permute-start | bytes 393224 | tf_op jit(solution)/shard_map/ppermute | solution.py:260
  14.2 5.8 %collective-permute-start.4 = (bf16[1,256,256]{2,1,0:T(8,128)(2,1)S(1)}, bf16[1,256,256]{2,1,0:T(8,128)(2,1)S(1)}, u32[]{:S(2)}, u32[]{:S(2)}) collective-permute-start(bf16[1,256,256]{2,1,0:T(8,128)(2,1)S(1)} %collective-permute-done.refs_0_), channel_id=1, source_target_pairs={{0,1},{1,0},{2,3},{3,2},{4,5},{5,4},{6,7},{7,6},{8,9},{9,8},{10,11... | collective-permute-start | bytes 393224 | tf_op jit(solution)/shard_map/ppermute | solution.py:258
  14.2 5.3 %collective-permute-start.9 = (bf16[80,256]{1,0:T(8,128)(2,1)S(1)}, bf16[80,256]{1,0:T(8,128)(2,1)S(1)}, u32[]{:S(2)}, u32[]{:S(2)}) collective-permute-start(bf16[80,256]{1,0:T(8,128)(2,1)S(1)} %collective-permute-done.1.refs_2_), channel_id=1, source_target_pairs={{0,2},{2,0},{1,3},{3,1},{4,6},{6,4},{5,7},{7,5},{8,10},{10,8},{9,1... | collective-permute-start | bytes 122888 | tf_op jit(solution)/shard_map/ppermute | solution.py:266
  16.2 3.8 %collective-permute-start.5 = (bf16[80,256]{1,0:T(8,128)(2,1)S(1)}, bf16[80,256]{1,0:T(8,128)(2,1)S(1)}, u32[]{:S(2)}, u32[]{:S(2)}) collective-permute-start(bf16[80,256]{1,0:T(8,128)(2,1)S(1)} %collective-permute-done.1.refs_2_), channel_id=1, source_target_pairs={{0,1},{1,0},{2,3},{3,2},{4,5},{5,4},{6,7},{7,6},{8,9},{9,8},{10,11... | collective-permute-start | bytes 122888 | tf_op jit(solution)/shard_map/ppermute | solution.py:264
  16.2 3.8 %collective-permute-start.6 = (bf16[80,256]{1,0:T(8,128)(2,1)S(1)}, bf16[80,256]{1,0:T(8,128)(2,1)S(1)}, u32[]{:S(2)}, u32[]{:S(2)}) collective-permute-start(bf16[80,256]{1,0:T(8,128)(2,1)S(1)} %collective-permute-done.2.refs_4_), channel_id=1, source_target_pairs={{0,1},{1,0},{2,3},{3,2},{4,5},{5,4},{6,7},{7,6},{8,9},{9,8},{10,11... | collective-permute-start | bytes 122888 | tf_op jit(solution)/shard_map/ppermute | solution.py:264
  19.5 1.7 %collective-permute-start.10 = (bf16[80,256]{1,0:T(8,128)(2,1)S(1)}, bf16[80,256]{1,0:T(8,128)(2,1)S(1)}, u32[]{:S(2)}, u32[]{:S(2)}) collective-permute-start(bf16[80,256]{1,0:T(8,128)(2,1)S(1)} %collective-permute-done.9.refs_2_), channel_id=1, source_target_pairs={{0,1},{1,0},{2,3},{3,2},{4,5},{5,4},{6,7},{7,6},{8,9},{9,8},{10,11... | collective-permute-start | bytes 122888 | tf_op jit(solution)/shard_map/ppermute | solution.py:267
  19.5 1.7 %collective-permute-start.8 = (bf16[1,256,256]{2,1,0:T(8,128)(2,1)S(1)}, bf16[1,256,256]{2,1,0:T(8,128)(2,1)S(1)}, u32[]{:S(2)}, u32[]{:S(2)}) collective-permute-start(bf16[1,256,256]{2,1,0:T(8,128)(2,1)S(1)} %collective-permute-done.7.refs_0_), channel_id=1, source_target_pairs={{0,1},{1,0},{2,3},{3,2},{4,5},{5,4},{6,7},{7,6},{8,9},{9,8},{10,11... | collective-permute-start | bytes 393224 | tf_op jit(solution)/shard_map/ppermute | solution.py:261

commit v6 on v5

--- a/solution.py
+++ b/solution.py
@@ -242,11 +242,10 @@
         out_specs=VMEM,
         scratch_shapes=[pltpu.VMEM((blocks_own, dof_count), jnp.float32)],
         compiler_params=pltpu.CompilerParams(vmem_limit_bytes=32 * MIB),
-        cost_estimate=LIGHT,
+        cost_estimate=WORK,
         name="own_blocks",
     )(pumped, basis, packs[0], own_swapped)
 
-    firsts, arrived, own_sum = lax.optimization_barrier((firsts, arrived, own_sum))
     pairs = [
         (r * halves + face, r * halves if face else (r ^ 1) * halves + 1)
         for r in range(rights)
@@ -259,6 +258,7 @@
         if far:
             second = lax.ppermute(first, ("rhs", "face"), pairs)
             late.append([second, lax.ppermute(second, "face", swap)])
+    arrived, own_sum, early = lax.optimization_barrier((arrived, own_sum, early))
     weights, others_late = [], iter(late)
     for (even, odd), array in zip(ways[1:], arrived):
         weights += [array, lax.ppermute(array, "face", swap)]

time: 23.2 us -> 20.9 us (0.901)
  waiting for transfers between devices: 4.82 us -> 2.13 us
  starting transfers between devices: 10.9 us -> 11.2 us
    ppermute x2, waiting for transfers between devices: 2 us -> 0.62 us  [on_device(): arrived.append(lax.ppermute(pack, ('sub', 'rhs'), pairs))]
    ppermute x1, starting transfers between devices: 1.96 us -> 3.31 us  [on_device(): second = lax.ppermute(array, 'rhs', cross)]
    ppermute x1, waiting for transfers between devices: 2.8 us -> 1.46 us  [on_device(): second = lax.ppermute(array, 'rhs', cross)]
    ppermute x1, starting transfers between devices: 1.86 us -> 1.31 us  [on_device(): second = lax.ppermute(first, ('rhs', 'face'), pairs)]
    ppermute x1, starting transfers between devices: 0.51 us -> 0.01 us  [on_device(): late.append([second, lax.ppermute(second, 'face', swap)])]
  transfers between devices with their start and end apart: 11 -> 11, of which waited for: 3 -> 3; matrix products, arithmetic and copies ran while one was open for 0% -> 0% of each run, Pallas kernels for 21% -> 23%
where the time goes in v6:
time: 20.9 us; the launch traced here: 20.7 us
  starting transfers between devices  11.2 us (54%)
  Pallas kernels  6.62 us (32%)
  waiting for transfers between devices  2.13 us (10%)
  between operations  0.75 us (4%)
    ppermute x1, starting transfers between devices, on_device(): firsts.append(lax.ppermute(basis, ('sub', 'rhs', 'face'), pairs))  4.04 us
    ppermute x1, starting transfers between devices, on_device(): second = lax.ppermute(array, 'rhs', cross)  3.31 us
    pallas_call x1, Pallas kernels, on_device(): pl.pallas_call(functools.partial(pack_kernel, ways), out_shape=[jax.Shape...  2.01 us
    ppermute x2, starting transfers between devices, on_device(): arrived.append(lax.ppermute(pack, ('sub', 'rhs'), pairs))  1.98 us
    pallas_call x1, Pallas kernels, on_device(): pl.pallas_call(last_kernel, out_shape=jax.ShapeDtypeStruct(block_shape, j...  1.86 us
    ppermute x1, waiting for transfers between devices, on_device(): second = lax.ppermute(array, 'rhs', cross)  1.46 us
    ppermute x1, starting transfers between devices, on_device(): second = lax.ppermute(first, ('rhs', 'face'), pairs)  1.31 us
    pallas_call x1, Pallas kernels, on_device(): pl.pallas_call(functools.partial(stage_kernel, kinds), out_shape=jax.Shap...  1.17 us
  transfers between devices with their start and end apart: 11, of which 3 were waited for; matrix products, arithmetic and copies ran while one was open for 0% of the time, Pallas kernels for 23%

profile of v6, /device:TPU:0, one launch (start us, length us, event | category | flops | bytes accessed | tf_op | source)
XLA Modules:
  0.0 20.7 jit_solution(15303929944660611507)
XLA Ops:
  0.0 4.0 %collective-permute-start.3 = (bf16[1,256,256]{2,1,0:T(8,128)(2,1)}, bf16[1,256,256]{2,1,0:T(8,128)(2,1)S(1)}, u32[]{:S(2)}, u32[]{:S(2)}) collective-permute-start(bf16[1,256,256]{2,1,0:T(8,128)(2,1)} %basis_ref.1), channel_id=1, source_target_pairs={{0,8},{1,5},{2,14},{3,7},{4,12},{5,1},{6,10},{7,3},{8,0},{9,13},{1... | collective-permute-start | bytes 393224 | tf_op jit(solution)/shard_map/ppermute | solution.py:204
  4.7 0.0 copy-start
  4.7 0.0 copy-start.2
  4.7 0.0 copy-start.3
  4.7 2.0 %pack_weights.1 = (bf16[80,256]{1,0:T(8,128)(2,1)}, bf16[80,256]{1,0:T(8,128)(2,1)}, bf16[80,256]{1,0:T(8,128)(2,1)}) custom-call(s32[1,128]{1,0:T(1,128)} %bitcast.2, s32[1,128]{1,0:T(1,128)} %bitcast.3, bf16[128,256]{1,0:T(8,128)(2,1)} %scale_ref.1, s32[1]{0:T(128)S(6)} %copy.12.section_ref), custom_call_target="tpu_custom_call" | custom-call | flops 4000000000 | bytes 8388608 | tf_op jit(solution)/shard_map/pack_weights/pallas_call | solution.py:210
  6.7 0.0 copy-start.4
  6.7 0.0 copy-start.5
  6.7 0.0 collective-permute-start.2
  6.7 1.1 %collective-permute-start = (bf16[80,256]{1,0:T(8,128)(2,1)}, bf16[80,256]{1,0:T(8,128)(2,1)S(1)}, u32[]{:S(2)}, u32[]{:S(2)}) collective-permute-start(bf16[80,256]{1,0:T(8,128)(2,1)} %get-tuple-element.13), channel_id=1, source_target_pairs={{0,8},{2,14},{4,12},{6,10},{8,0},{10,6},{12,4},{14,2},{1,9},{3,15}... | collective-permute-start | bytes 122888 | tf_op jit(solution)/shard_map/ppermute | solution.py:225
  7.9 0.9 %collective-permute-start.1 = (bf16[80,256]{1,0:T(8,128)(2,1)}, bf16[80,256]{1,0:T(8,128)(2,1)S(1)}, u32[]{:S(2)}, u32[]{:S(2)}) collective-permute-start(bf16[80,256]{1,0:T(8,128)(2,1)} %get-tuple-element.14), channel_id=1, source_target_pairs={{0,4},{2,6},{4,0},{6,2},{8,12},{10,14},{12,8},{14,10},{1,5},{3,7},... | collective-permute-start | bytes 122888 | tf_op jit(solution)/shard_map/ppermute | solution.py:225
  8.7 0.0 copy-done
  8.7 0.0 copy-done.2
  8.7 0.0 copy-done.3
  8.7 1.0 %pump.1.pumped_ref = bf16[64,32,256]{2,1,0:T(8,128)(2,1)S(1)} custom-call(bf16[128,32,256]{2,1,0:T(8,128)(2,1)S(1)} %copy-done, f32[32]{0:T(128)S(1)} %copy-done.2, s32[32]{0:T(128)S(1)} %copy-done.3), custom_call_target="tpu_custom_call" | custom-call | flops 1000000 | bytes 1024 | tf_op jit(solution)/shard_map/pump/pallas_call | solution.py:228
  9.8 0.0 collective-permute-done.3.refs_0_
  9.8 0.1 collective-permute-start.4
  9.8 1.3 %collective-permute-start.7 = (bf16[1,256,256]{2,1,0:T(8,128)(2,1)S(1)}, bf16[1,256,256]{2,1,0:T(8,128)(2,1)S(1)}, u32[]{:S(2)}, u32[]{:S(2)}) collective-permute-start(bf16[1,256,256]{2,1,0:T(8,128)(2,1)S(1)} %collective-permute-done.3.refs_0_), channel_id=1, source_target_pairs={{0,3},{1,0},{2,1},{3,2},{4,7},{5,4},{6,5},{7,6},{8,11},{9,8},{10,9... | collective-permute-start | bytes 393224 | tf_op jit(solution)/shard_map/ppermute | solution.py:259
  11.2 0.0 collective-permute-done.2.swapped_ref
  11.2 0.0 copy-done.4
  11.2 0.0 copy-done.5
  11.2 0.5 %own_blocks.1.sum_ref = f32[64,32,256]{2,1,0:T(8,128)S(1)} custom-call(bf16[64,32,256]{2,1,0:T(8,128)(2,1)S(1)} %pump.1.pumped_ref, bf16[1,256,256]{2,1,0:T(8,128)(2,1)S(1)} %copy-done.4, bf16[80,256]{1,0:T(8,128)(2,1)S(1)} %copy-done.5, bf16[80,256]{1,0:T(8,128)(2,1)S(1)} %collective-permute-done.2.swapped_ref), custom_call_target="tpu_custom_call" | custom-call | flops 4000000000 | bytes 8388608 | tf_op jit(solution)/shard_map/own_blocks/pallas_call | solution.py:238
  11.7 0.0 copy-start.1
  11.7 0.2 %collective-permute-done.refs_2_ = bf16[80,256]{1,0:T(8,128)(2,1)S(1)} collective-permute-done((bf16[80,256]{1,0:T(8,128)(2,1)}, bf16[80,256]{1,0:T(8,128)(2,1)S(1)}, u32[]{:S(2)}, u32[]{:S(2)}) %collective-permute-start) | collective-permute-done | bytes 40992 | tf_op jit(solution)/shard_map/ppermute | solution.py:225
  11.9 0.4 %collective-permute-done.1.refs_4_ = bf16[80,256]{1,0:T(8,128)(2,1)S(1)} collective-permute-done((bf16[80,256]{1,0:T(8,128)(2,1)}, bf16[80,256]{1,0:T(8,128)(2,1)S(1)}, u32[]{:S(2)}, u32[]{:S(2)}) %collective-permute-start.1) | collective-permute-done | bytes 40992 | tf_op jit(solution)/shard_map/ppermute | solution.py:225
  12.4 0.0 collective-permute-done.4.refs_1_
  12.4 3.3 %collective-permute-start.9 = (bf16[80,256]{1,0:T(8,128)(2,1)S(1)}, bf16[80,256]{1,0:T(8,128)(2,1)S(1)}, u32[]{:S(2)}, u32[]{:S(2)}) collective-permute-start(bf16[80,256]{1,0:T(8,128)(2,1)S(1)} %collective-permute-done.refs_2_), channel_id=1, source_target_pairs={{0,2},{2,0},{1,3},{3,1},{4,6},{6,4},{5,7},{7,5},{8,10},{10,8},{9,1... | collective-permute-start | bytes 122888 | tf_op jit(solution)/shard_map/ppermute | solution.py:266
  15.7 0.0 collective-permute-start.5
  15.7 0.5 %collective-permute-start.6 = (bf16[80,256]{1,0:T(8,128)(2,1)S(1)}, bf16[80,256]{1,0:T(8,128)(2,1)S(1)}, u32[]{:S(2)}, u32[]{:S(2)}) collective-permute-start(bf16[80,256]{1,0:T(8,128)(2,1)S(1)} %collective-permute-done.1.refs_4_), channel_id=1, source_target_pairs={{0,1},{1,0},{2,3},{3,2},{4,5},{5,4},{6,7},{7,6},{8,9},{9,8},{10,11... | collective-permute-start | bytes 122888 | tf_op jit(solution)/shard_map/ppermute | solution.py:264
  16.2 0.0 collective-permute-done.7.refs_0_
  16.2 0.0 collective-permute-start.8
  16.2 1.5 %collective-permute-done.9.refs_2_ = bf16[80,256]{1,0:T(8,128)(2,1)S(1)} collective-permute-done((bf16[80,256]{1,0:T(8,128)(2,1)S(1)}, bf16[80,256]{1,0:T(8,128)(2,1)S(1)}, u32[]{:S(2)}, u32[]{:S(2)}) %collective-permute-start.9) | collective-permute-done | bytes 40992 | tf_op jit(solution)/shard_map/ppermute | solution.py:266
  17.7 0.0 collective-permute-start.10
  17.7 0.0 collective-permute-done.5.refs_3_
  17.7 0.0 collective-permute-done.6.refs_5_
  17.7 1.2 %stage.1.sum_ref = f32[64,32,256]{2,1,0:T(8,128)S(1)} custom-call(bf16[64,32,256]{2,1,0:T(8,128)(2,1)S(1)} %pump.1.pumped_ref, f32[64,32,256]{2,1,0:T(8,128)S(1)} %own_blocks.1.sum_ref, bf16[1,256,256]{2,1,0:T(8,128)(2,1)S(1)} %collective-permute-done.3.refs_0_, ...), custom_call_target="tpu_custom_call", output_to_operand_aliasing={{}: (1, {})} | custom-call | flops 4000000000 | bytes 8388608 | tf_op jit(solution)/shard_map/stage/pallas_call | solution.py:272
  18.8 0.0 collective-permute-done.10.refs_3_
  18.9 0.0 collective-permute-done.8.refs_1_
  18.9 0.0 copy-done.1
  18.9 1.9 %last_stage.1 = f32[64,32,256]{2,1,0:T(8,128)} custom-call(bf16[64,32,256]{2,1,0:T(8,128)(2,1)S(1)} %pump.1.pumped_ref, f32[64,32,256]{2,1,0:T(8,128)S(1)} %stage.1.sum_ref, bf16[256,256]{1,0:T(8,128)(2,1)S(1)} %copy-done.1, bf16[1,256,256]{2,1,0:T(8,128)(2,1)S(1)} %collective-permute-done.7.refs_0_, ...), custom_call_target="tpu_custom_call" | custom-call | tf_op jit(solution)/shard_map/last_stage/pallas_call | solution.py:289
Async XLA Ops:
  0.0 9.8 %collective-permute-start.3 = (bf16[1,256,256]{2,1,0:T(8,128)(2,1)}, bf16[1,256,256]{2,1,0:T(8,128)(2,1)S(1)}, u32[]{:S(2)}, u32[]{:S(2)}) collective-permute-start(bf16[1,256,256]{2,1,0:T(8,128)(2,1)} %basis_ref.1), channel_id=1, source_target_pairs={{0,8},{1,5},{2,14},{3,7},{4,12},{5,1},{6,10},{7,3},{8,0},{9,13},{1... | collective-permute-start | bytes 393224 | tf_op jit(solution)/shard_map/ppermute | solution.py:204
  4.7 4.0 %copy-start = (bf16[128,32,256]{2,1,0:T(8,128)(2,1)S(1)}, bf16[128,32,256]{2,1,0:T(8,128)(2,1)}, u32[]{:S(2)}) copy-start(bf16[128,32,256]{2,1,0:T(8,128)(2,1)} %mortar_ref.1) | copy-start | bytes 6291460
  4.7 4.0 %copy-start.2 = (f32[32]{0:T(128)S(1)}, f32[32]{0:T(128)}, u32[]{:S(2)}) copy-start(f32[32]{0:T(128)} %rate_ref.1) | copy-start | bytes 388
  4.7 4.0 %copy-start.3 = (s32[32]{0:T(128)S(1)}, s32[32]{0:T(128)}, u32[]{:S(2)}) copy-start(s32[32]{0:T(128)} %cell_ref.1) | copy-start | bytes 388
  6.7 4.4 %copy-start.4 = (bf16[1,256,256]{2,1,0:T(8,128)(2,1)S(1)}, bf16[1,256,256]{2,1,0:T(8,128)(2,1)}, u32[]{:S(2)}) copy-start(bf16[1,256,256]{2,1,0:T(8,128)(2,1)} %basis_ref.1) | copy-start | bytes 393220
  6.7 4.4 %copy-start.5 = (bf16[80,256]{1,0:T(8,128)(2,1)S(1)}, bf16[80,256]{1,0:T(8,128)(2,1)}, u32[]{:S(2)}) copy-start(bf16[80,256]{1,0:T(8,128)(2,1)} %get-tuple-element.15.pack_ref) | copy-start | bytes 122884
  6.7 4.4 %collective-permute-start.2 = (bf16[80,256]{1,0:T(8,128)(2,1)}, bf16[80,256]{1,0:T(8,128)(2,1)S(1)}, u32[]{:S(2)}, u32[]{:S(2)}) collective-permute-start(bf16[80,256]{1,0:T(8,128)(2,1)} %get-tuple-element.15.pack_ref), channel_id=1, source_target_pairs={{0,1},{1,0},{2,3},{3,2},{4,5},{5,4},{6,7},{7,6},{8,9},{9,8},{10,11... | collective-permute-start | bytes 122888 | tf_op jit(solution)/shard_map/ppermute | solution.py:226
  6.7 5.2 %collective-permute-start = (bf16[80,256]{1,0:T(8,128)(2,1)}, bf16[80,256]{1,0:T(8,128)(2,1)S(1)}, u32[]{:S(2)}, u32[]{:S(2)}) collective-permute-start(bf16[80,256]{1,0:T(8,128)(2,1)} %get-tuple-element.13), channel_id=1, source_target_pairs={{0,8},{2,14},{4,12},{6,10},{8,0},{10,6},{12,4},{14,2},{1,9},{3,15}... | collective-permute-start | bytes 122888 | tf_op jit(solution)/shard_map/ppermute | solution.py:225
  7.9 4.5 %collective-permute-start.1 = (bf16[80,256]{1,0:T(8,128)(2,1)}, bf16[80,256]{1,0:T(8,128)(2,1)S(1)}, u32[]{:S(2)}, u32[]{:S(2)}) collective-permute-start(bf16[80,256]{1,0:T(8,128)(2,1)} %get-tuple-element.14), channel_id=1, source_target_pairs={{0,4},{2,6},{4,0},{6,2},{8,12},{10,14},{12,8},{14,10},{1,5},{3,7},... | collective-permute-start | bytes 122888 | tf_op jit(solution)/shard_map/ppermute | solution.py:225
  9.8 2.6 %collective-permute-start.4 = (bf16[1,256,256]{2,1,0:T(8,128)(2,1)S(1)}, bf16[1,256,256]{2,1,0:T(8,128)(2,1)S(1)}, u32[]{:S(2)}, u32[]{:S(2)}) collective-permute-start(bf16[1,256,256]{2,1,0:T(8,128)(2,1)S(1)} %collective-permute-done.3.refs_0_), channel_id=1, source_target_pairs={{0,1},{1,0},{2,3},{3,2},{4,5},{5,4},{6,7},{7,6},{8,9},{9,8},{10,11... | collective-permute-start | bytes 393224 | tf_op jit(solution)/shard_map/ppermute | solution.py:257
  9.8 6.3 %collective-permute-start.7 = (bf16[1,256,256]{2,1,0:T(8,128)(2,1)S(1)}, bf16[1,256,256]{2,1,0:T(8,128)(2,1)S(1)}, u32[]{:S(2)}, u32[]{:S(2)}) collective-permute-start(bf16[1,256,256]{2,1,0:T(8,128)(2,1)S(1)} %collective-permute-done.3.refs_0_), channel_id=1, source_target_pairs={{0,3},{1,0},{2,1},{3,2},{4,7},{5,4},{6,5},{7,6},{8,11},{9,8},{10,9... | collective-permute-start | bytes 393224 | tf_op jit(solution)/shard_map/ppermute | solution.py:259
  11.7 7.2 %copy-start.1 = (bf16[256,256]{1,0:T(8,128)(2,1)S(1)}, bf16[256,256]{1,0:T(8,128)(2,1)}, u32[]{:S(2)}) copy-start(bf16[256,256]{1,0:T(8,128)(2,1)} %projection_ref.1) | copy-start | bytes 393220
  12.4 5.3 %collective-permute-start.9 = (bf16[80,256]{1,0:T(8,128)(2,1)S(1)}, bf16[80,256]{1,0:T(8,128)(2,1)S(1)}, u32[]{:S(2)}, u32[]{:S(2)}) collective-permute-start(bf16[80,256]{1,0:T(8,128)(2,1)S(1)} %collective-permute-done.refs_2_), channel_id=1, source_target_pairs={{0,2},{2,0},{1,3},{3,1},{4,6},{6,4},{5,7},{7,5},{8,10},{10,8},{9,1... | collective-permute-start | bytes 122888 | tf_op jit(solution)/shard_map/ppermute | solution.py:266
  15.7 2.0 %collective-permute-start.5 = (bf16[80,256]{1,0:T(8,128)(2,1)S(1)}, bf16[80,256]{1,0:T(8,128)(2,1)S(1)}, u32[]{:S(2)}, u32[]{:S(2)}) collective-permute-start(bf16[80,256]{1,0:T(8,128)(2,1)S(1)} %collective-permute-done.refs_2_), channel_id=1, source_target_pairs={{0,1},{1,0},{2,3},{3,2},{4,5},{5,4},{6,7},{7,6},{8,9},{9,8},{10,11... | collective-permute-start | bytes 122888 | tf_op jit(solution)/shard_map/ppermute | solution.py:264
  15.7 2.0 %collective-permute-start.6 = (bf16[80,256]{1,0:T(8,128)(2,1)S(1)}, bf16[80,256]{1,0:T(8,128)(2,1)S(1)}, u32[]{:S(2)}, u32[]{:S(2)}) collective-permute-start(bf16[80,256]{1,0:T(8,128)(2,1)S(1)} %collective-permute-done.1.refs_4_), channel_id=1, source_target_pairs={{0,1},{1,0},{2,3},{3,2},{4,5},{5,4},{6,7},{7,6},{8,9},{9,8},{10,11... | collective-permute-start | bytes 122888 | tf_op jit(solution)/shard_map/ppermute | solution.py:264
  16.2 2.7 %collective-permute-start.8 = (bf16[1,256,256]{2,1,0:T(8,128)(2,1)S(1)}, bf16[1,256,256]{2,1,0:T(8,128)(2,1)S(1)}, u32[]{:S(2)}, u32[]{:S(2)}) collective-permute-start(bf16[1,256,256]{2,1,0:T(8,128)(2,1)S(1)} %collective-permute-done.7.refs_0_), channel_id=1, source_target_pairs={{0,1},{1,0},{2,3},{3,2},{4,5},{5,4},{6,7},{7,6},{8,9},{9,8},{10,11... | collective-permute-start | bytes 393224 | tf_op jit(solution)/shard_map/ppermute | solution.py:260
  17.7 1.2 %collective-permute-start.10 = (bf16[80,256]{1,0:T(8,128)(2,1)S(1)}, bf16[80,256]{1,0:T(8,128)(2,1)S(1)}, u32[]{:S(2)}, u32[]{:S(2)}) collective-permute-start(bf16[80,256]{1,0:T(8,128)(2,1)S(1)} %collective-permute-done.9.refs_2_), channel_id=1, source_target_pairs={{0,1},{1,0},{2,3},{3,2},{4,5},{5,4},{6,7},{7,6},{8,9},{9,8},{10,11... | collective-permute-start | bytes 122888 | tf_op jit(solution)/shard_map/ppermute | solution.py:267

commit v7 on v6

--- a/solution.py
+++ b/solution.py
@@ -67,12 +67,14 @@
     return total
 
 
-def pump_kernel(mortar_ref, rate_ref, cell_ref, pumped_ref, sem):
+def own_kernel(mortar_ref, rate_ref, cell_ref, basis_ref, pack_ref, swapped_ref, pumped_ref, sum_ref, weight_ref, sem):
     blocks_own, columns, dof_count = pumped_ref.shape
     first_block = lax.axis_index("face") * blocks_own
     fetch = pltpu.make_async_copy(mortar_ref.at[pl.ds(first_block, blocks_own)], pumped_ref, sem)
     fetch.start()
+    weight_ref[...] = block_weights((pack_ref, swapped_ref), pack_ref.shape[0] - ROW_TILE, blocks_own)
     fetch.wait()
+
     base = lax.axis_index("sub") * mortar_ref.shape[0] + first_block
     for column in range(columns):
         block = lax.div(cell_ref[column], dof_count) - base
@@ -90,10 +92,6 @@
                 jnp.bfloat16
             )
 
-
-def own_kernel(pumped_ref, basis_ref, pack_ref, swapped_ref, sum_ref, weight_ref):
-    blocks_own, columns, dof_count = pumped_ref.shape
-    weight_ref[...] = block_weights((pack_ref, swapped_ref), pack_ref.shape[0] - ROW_TILE, blocks_own)
     tile_blocks = blocks_own // TILES
     for tile in range(TILES):
         at = slice(tile * tile_blocks, (tile + 1) * tile_blocks)
@@ -204,9 +202,9 @@
         firsts.append(lax.ppermute(basis, ("sub", "rhs", "face"), pairs))
 
     kinds = [(a != b, c != a or a == b) for a, b, c in groups]
-    ways = [(0, 0)]
-    for (a, b, c), (far, near) in zip(groups, kinds):
-        ways += [(a, b)] * far + [(c, c)] * near
+    near = [(c, c) for (_, _, c), (_, has) in zip(groups, kinds) if has]
+    far = [(a, b) for (a, b, _), (has, _) in zip(groups, kinds) if has]
+    ways = [(0, 0), *near, *far, *[(b, a) for a, b in far]]
     packs = pl.pallas_call(
         functools.partial(pack_kernel, ways),
         out_shape=[jax.ShapeDtypeStruct((pack_rows, dof_count), jnp.bfloat16)] * len(ways),
@@ -215,56 +213,53 @@
         cost_estimate=WORK,
         name="pack_weights",
     )(face_owner.reshape(1, faces_dev), face_slot.reshape(1, faces_dev), face_scale, section)
-    arrived = []
-    for (even, odd), pack in zip(ways[1:], packs[1:]):
+
+    def along_sub(way, pack):
         pairs = [
-            (s * rights + r, (s ^ (odd if r % 2 else even)) * rights + r)
-            for s in range(subdomains)
-            for r in range(rights)
+            (s * rights + r, (s ^ way[r % 2]) * rights + r) for s in range(subdomains) for r in range(rights)
         ]
-        arrived.append(lax.ppermute(pack, ("sub", "rhs"), pairs))
+        return lax.ppermute(pack, ("sub", "rhs"), pairs)
+
+    early_count = 1 + len(near) + len(far)
+    arrived = [along_sub(way, pack) for way, pack in zip(ways[1:early_count], packs[1:])]
     own_swapped = lax.ppermute(packs[0], "face", swap)
 
-    pumped = pl.pallas_call(
-        pump_kernel,
-        out_shape=jax.ShapeDtypeStruct(block_shape, jnp.bfloat16),
-        in_specs=[HBM, SMEM, SMEM],
-        out_specs=VMEM,
-        scratch_shapes=[pltpu.SemaphoreType.DMA(())],
-        compiler_params=pltpu.CompilerParams(vmem_limit_bytes=32 * MIB),
-        cost_estimate=LIGHT,
-        name="pump",
-    )(mortar_in, pump_rate, well_cell)
-    own_sum = pl.pallas_call(
+    firsts, own_swapped = lax.optimization_barrier((firsts, own_swapped))
+    pumped, own_sum = pl.pallas_call(
         own_kernel,
-        out_shape=jax.ShapeDtypeStruct(block_shape, jnp.float32),
-        in_specs=[VMEM] * 4,
-        out_specs=VMEM,
-        scratch_shapes=[pltpu.VMEM((blocks_own, dof_count), jnp.float32)],
+        out_shape=[
+            jax.ShapeDtypeStruct(block_shape, jnp.bfloat16),
+            jax.ShapeDtypeStruct(block_shape, jnp.float32),
+        ],
+        in_specs=[HBM, SMEM, SMEM, VMEM, VMEM, VMEM],
+        out_specs=[VMEM, VMEM],
+        scratch_shapes=[pltpu.VMEM((blocks_own, dof_count), jnp.float32), pltpu.SemaphoreType.DMA(())],
         compiler_params=pltpu.CompilerParams(vmem_limit_bytes=32 * MIB),
         cost_estimate=WORK,
         name="own_blocks",
-    )(pumped, basis, packs[0], own_swapped)
+    )(mortar_in, pump_rate, well_cell, basis, packs[0], own_swapped)
 
     pairs = [
         (r * halves + face, r * halves if face else (r ^ 1) * halves + 1)
         for r in range(rights)
         for face in range(halves)
     ]
-    cross = [(i, i ^ 1) for i in range(rights)]
     early, late = [], []
-    for (far, _), first in zip(kinds, firsts):
+    for (has_far, _), first in zip(kinds, firsts):
         early += [first, lax.ppermute(first, "face", swap)]
-        if far:
+        if has_far:
             second = lax.ppermute(first, ("rhs", "face"), pairs)
             late.append([second, lax.ppermute(second, "face", swap)])
+    *late_packs, firsts = lax.optimization_barrier((*packs[early_count:], firsts))
+    late_arrived = [along_sub(way, pack) for way, pack in zip(ways[early_count:], late_packs)]
     arrived, own_sum, early = lax.optimization_barrier((arrived, own_sum, early))
-    weights, others_late = [], iter(late)
-    for (even, odd), array in zip(ways[1:], arrived):
-        weights += [array, lax.ppermute(array, "face", swap)]
-        if even != odd:
-            second = lax.ppermute(array, "rhs", cross)
-            next(others_late).extend([second, lax.ppermute(second, "face", swap)])
+    swapped = [lax.ppermute(array, "face", swap) for array in arrived]
+    places = dict(zip(ways[1:early_count], zip(arrived, swapped)))
+    weights = []
+    for (a, b, c), (has_far, has_near) in zip(groups, kinds):
+        weights += list(places[a, b]) * has_far + list(places[c, c]) * has_near
+    for arrays, array in zip(late, late_arrived):
+        arrays += [array, lax.ppermute(array, "face", swap)]
 
     late_count = len(late)
     count = others - late_count

time: 20.9 us -> 20.9 us (level)
  waiting for transfers between devices: 2.13 us -> 0.38 us
  starting transfers between devices: 11.2 us -> 12.1 us
  local copies, waits for them, and re-layouts: 0.03 us -> 0.79 us
    ppermute x6, waiting for transfers between devices: 2.12 us -> 0.36 us  [the longest x3 0.25 us: along_sub(): return lax.ppermute(pack, ('sub', 'rhs'), pairs)]
    ppermute x1, starting transfers between devices: 1.31 us -> 2.28 us  [on_device(): second = lax.ppermute(first, ('rhs', 'face'), pairs)]
    unnamed x12, local copies, waits for them, and re-layouts: 0.03 us -> 0.79 us
    ppermute x6, starting transfers between devices: 5.8 us -> 5.22 us  [the longest x3 4.65 us: along_sub(): return lax.ppermute(pack, ('sub', 'rhs'), pairs)]
    ppermute x1, starting transfers between devices: 0.01 us -> 0.51 us  [on_device(): late.append([second, lax.ppermute(second, 'face', swap)])]
    pallas_call x2 -> x1, Pallas kernels: 1.57 us -> 1.61 us  [on_device(): pl.pallas_call(own_kernel, out_shape=[jax.ShapeDtypeStruct(block_shape, j...]
  transfers between devices with their start and end apart: 11 -> 11, of which waited for: 3 -> 2; matrix products, arithmetic and copies ran while one was open for 0% -> 0% of each run, Pallas kernels for 23% -> 23%
where the time goes in v7:
time: 20.9 us; the launch traced here: 20.7 us
  starting transfers between devices  12.1 us (58%)
  Pallas kernels  6.68 us (32%)
  local copies, waits for them, and re-layouts  0.79 us (4%)
  between operations  0.78 us (4%)
  waiting for transfers between devices  0.38 us (2%)
    ppermute x3, starting transfers between devices, along_sub(): return lax.ppermute(pack, ('sub', 'rhs'), pairs)  4.65 us
    ppermute x1, starting transfers between devices, on_device(): firsts.append(lax.ppermute(basis, ('sub', 'rhs', 'face'), pairs))  4.04 us
    ppermute x1, starting transfers between devices, on_device(): second = lax.ppermute(first, ('rhs', 'face'), pairs)  2.28 us
    pallas_call x1, Pallas kernels, on_device(): pl.pallas_call(functools.partial(pack_kernel, ways), out_shape=[jax.Shape...  2.03 us
    pallas_call x1, Pallas kernels, on_device(): pl.pallas_call(last_kernel, out_shape=jax.ShapeDtypeStruct(block_shape, j...  1.87 us
    pallas_call x1, Pallas kernels, on_device(): pl.pallas_call(own_kernel, out_shape=[jax.ShapeDtypeStruct(block_shape, j...  1.61 us
    pallas_call x1, Pallas kernels, on_device(): pl.pallas_call(functools.partial(stage_kernel, kinds), out_shape=jax.Shap...  1.18 us
    unnamed x12, local copies, waits for them, and re-layouts  0.79 us
  transfers between devices with their start and end apart: 11, of which 2 were waited for; matrix products, arithmetic and copies ran while one was open for 0% of the time, Pallas kernels for 23%

profile of v7, /device:TPU:0, one launch (start us, length us, event | category | flops | bytes accessed | tf_op | source)
XLA Modules:
  0.0 20.7 jit_solution(16307171867548046869)
XLA Ops:
  0.0 4.0 %collective-permute-start = (bf16[1,256,256]{2,1,0:T(8,128)(2,1)}, bf16[1,256,256]{2,1,0:T(8,128)(2,1)S(1)}, u32[]{:S(2)}, u32[]{:S(2)}) collective-permute-start(bf16[1,256,256]{2,1,0:T(8,128)(2,1)} %basis_ref.1), channel_id=1, source_target_pairs={{0,8},{1,5},{2,14},{3,7},{4,12},{5,1},{6,10},{7,3},{8,0},{9,13},{1... | collective-permute-start | bytes 393224 | tf_op jit(solution)/shard_map/ppermute | solution.py:202
  4.7 0.0 copy-start.1
  4.7 0.0 copy-start.2
  4.7 0.0 copy-start.4
  4.7 0.0 copy-start.5
  4.7 2.0 %pack_weights.1 = (bf16[80,256]{1,0:T(8,128)(2,1)}, bf16[80,256]{1,0:T(8,128)(2,1)}, bf16[80,256]{1,0:T(8,128)(2,1)}, bf16[80,256]{1,0:T(8,128)(2,1)}) custom-call(s32[1,128]{1,0:T(1,128)} %bitcast.2, s32[1,128]{1,0:T(1,128)} %bitcast.3, bf16[128,256]{1,0:T(8,128)(2,1)} %scale_ref.1, s32[1]{0:T(128)S(6)} %copy.12.section_ref), custom_call_target="tpu_custom_call" | custom-call | flops 4000000000 | bytes 8388608 | tf_op jit(solution)/shard_map/pack_weights/pallas_call | solution.py:208
  6.8 0.0 collective-permute-start.1
  6.8 1.6 %collective-permute-start.2 = (bf16[80,256]{1,0:T(8,128)(2,1)}, bf16[80,256]{1,0:T(8,128)(2,1)S(1)}, u32[]{:S(2)}, u32[]{:S(2)}) collective-permute-start(bf16[80,256]{1,0:T(8,128)(2,1)} %get-tuple-element.22), channel_id=1, source_target_pairs={{0,4},{2,6},{4,0},{6,2},{8,12},{10,14},{12,8},{14,10},{1,5},{3,7},... | collective-permute-start | bytes 122888 | tf_op jit(solution)/shard_map/ppermute | solution.py:221
  8.3 0.3 %collective-permute-start.3 = (bf16[80,256]{1,0:T(8,128)(2,1)}, bf16[80,256]{1,0:T(8,128)(2,1)S(1)}, u32[]{:S(2)}, u32[]{:S(2)}) collective-permute-start(bf16[80,256]{1,0:T(8,128)(2,1)} %get-tuple-element.23), channel_id=1, source_target_pairs={{0,8},{2,14},{4,12},{6,10},{8,0},{10,6},{12,4},{14,2},{1,9},{3,15}... | collective-permute-start | bytes 122888 | tf_op jit(solution)/shard_map/ppermute | solution.py:221
  8.7 0.0 collective-permute-done.1.swapped_ref
  8.7 0.0 collective-permute-done.refs_0_
  8.7 0.0 collective-permute-start.4
  8.7 2.3 %collective-permute-start.7 = (bf16[1,256,256]{2,1,0:T(8,128)(2,1)S(1)}, bf16[1,256,256]{2,1,0:T(8,128)(2,1)S(1)}, u32[]{:S(2)}, u32[]{:S(2)}) collective-permute-start(bf16[1,256,256]{2,1,0:T(8,128)(2,1)S(1)} %collective-permute-done.refs_0_), channel_id=1, source_target_pairs={{0,3},{1,0},{2,1},{3,2},{4,7},{5,4},{6,5},{7,6},{8,11},{9,8},{10,9... | collective-permute-start | bytes 393224 | tf_op jit(solution)/shard_map/ppermute | solution.py:251
  11.0 2.7 %collective-permute-start.9 = (bf16[80,256]{1,0:T(8,128)(2,1)}, bf16[80,256]{1,0:T(8,128)(2,1)S(1)}, u32[]{:S(2)}, u32[]{:S(2)}) collective-permute-start(bf16[80,256]{1,0:T(8,128)(2,1)} %get-tuple-element.32), channel_id=1, source_target_pairs={{0,12},{2,10},{4,8},{6,14},{8,4},{10,2},{12,0},{14,6},{1,13},{3,11... | collective-permute-start | bytes 122888 | tf_op jit(solution)/shard_map/ppermute | solution.py:221
  13.7 0.0 copy-done.1
  13.7 0.0 copy-done.2
  13.7 0.0 copy-done.4
  13.7 0.0 copy-done.5
  13.7 0.0 copy-start.3
  13.7 0.8 %copy-done.3 = bf16[80,256]{1,0:T(8,128)(2,1)S(1)} copy-done((bf16[80,256]{1,0:T(8,128)(2,1)S(1)}, bf16[80,256]{1,0:T(8,128)(2,1)}, u32[]{:S(2)}) %copy-start.3) | copy-done | bytes 40984
  14.5 1.6 %own_blocks.1 = (bf16[64,32,256]{2,1,0:T(8,128)(2,1)S(1)}, f32[64,32,256]{2,1,0:T(8,128)S(1)}) custom-call(bf16[128,32,256]{2,1,0:T(8,128)(2,1)S(1)} %copy-done.1, f32[32]{0:T(128)S(1)} %copy-done.4, s32[32]{0:T(128)S(1)} %copy-done.5, bf16[1,256,256]{2,1,0:T(8,128)(2,1)S(1)} %copy-done.2, bf16[80,256]{1,0:T(8,128)(2,1)S(1)} %copy-done.3, ...), custom_call_target="tpu_custom_call" | custom-call | flops 4000000000 | bytes 8388608 | tf_op jit(solution)/shard_map/own_blocks/pallas_call | solution.py:228
  16.1 0.0 collective-permute-done.2.refs_4_
  16.1 0.0 collective-permute-done.3.refs_2_
  16.1 0.0 collective-permute-done.4.refs_1_
  16.2 0.1 collective-permute-start.5
  16.2 0.5 %collective-permute-start.6 = (bf16[80,256]{1,0:T(8,128)(2,1)S(1)}, bf16[80,256]{1,0:T(8,128)(2,1)S(1)}, u32[]{:S(2)}, u32[]{:S(2)}) collective-permute-start(bf16[80,256]{1,0:T(8,128)(2,1)S(1)} %collective-permute-done.2.refs_4_), channel_id=1, source_target_pairs={{0,1},{1,0},{2,3},{3,2},{4,5},{5,4},{6,7},{7,6},{8,9},{9,8},{10,11... | collective-permute-start | bytes 122888 | tf_op jit(solution)/shard_map/ppermute | solution.py:256
  16.7 0.2 %collective-permute-done.9.refs_2_ = bf16[80,256]{1,0:T(8,128)(2,1)S(1)} collective-permute-done((bf16[80,256]{1,0:T(8,128)(2,1)}, bf16[80,256]{1,0:T(8,128)(2,1)S(1)}, u32[]{:S(2)}, u32[]{:S(2)}) %collective-permute-start.9) | collective-permute-done | bytes 40992 | tf_op jit(solution)/shard_map/ppermute | solution.py:221
  17.0 0.0 collective-permute-start.10
  17.0 0.0 collective-permute-done.7.refs_0_
  17.0 0.5 %collective-permute-start.8 = (bf16[1,256,256]{2,1,0:T(8,128)(2,1)S(1)}, bf16[1,256,256]{2,1,0:T(8,128)(2,1)S(1)}, u32[]{:S(2)}, u32[]{:S(2)}) collective-permute-start(bf16[1,256,256]{2,1,0:T(8,128)(2,1)S(1)} %collective-permute-done.7.refs_0_), channel_id=1, source_target_pairs={{0,1},{1,0},{2,3},{3,2},{4,5},{5,4},{6,7},{7,6},{8,9},{9,8},{10,11... | collective-permute-start | bytes 393224 | tf_op jit(solution)/shard_map/ppermute | solution.py:252
  17.5 0.0 collective-permute-done.5.refs_3_
  17.5 0.1 collective-permute-done.6.refs_5_
  17.6 0.0 copy-start
  17.6 1.2 %stage.1.sum_ref = f32[64,32,256]{2,1,0:T(8,128)S(1)} custom-call(bf16[64,32,256]{2,1,0:T(8,128)(2,1)S(1)} %get-tuple-element.21.pumped_ref, f32[64,32,256]{2,1,0:T(8,128)S(1)} %get-tuple-element.26.sum_ref, bf16[1,256,256]{2,1,0:T(8,128)(2,1)S(1)} %collective-permute-done.refs_0_, ...), custom_call_target="tpu_custom_call", output_to_operand_aliasing={{}: (1, {})} | custom-call | flops 4000000000 | bytes 8388608 | tf_op jit(solution)/shard_map/stage/pallas_call | solution.py:267
  18.8 0.0 collective-permute-done.10.refs_3_
  18.8 0.0 collective-permute-done.8.refs_1_
  18.8 0.0 copy-done
  18.8 1.9 %last_stage.1 = f32[64,32,256]{2,1,0:T(8,128)} custom-call(bf16[64,32,256]{2,1,0:T(8,128)(2,1)S(1)} %get-tuple-element.21.pumped_ref, f32[64,32,256]{2,1,0:T(8,128)S(1)} %stage.1.sum_ref, bf16[256,256]{1,0:T(8,128)(2,1)S(1)} %copy-done, bf16[1,256,256]{2,1,0:T(8,128)(2,1)S(1)} %collective-permute-done.7.refs_0_, ...), custom_call_target="tpu_custom_call" | custom-call | tf_op jit(solution)/shard_map/last_stage/pallas_call | solution.py:284
Async XLA Ops:
  0.0 8.7 %collective-permute-start = (bf16[1,256,256]{2,1,0:T(8,128)(2,1)}, bf16[1,256,256]{2,1,0:T(8,128)(2,1)S(1)}, u32[]{:S(2)}, u32[]{:S(2)}) collective-permute-start(bf16[1,256,256]{2,1,0:T(8,128)(2,1)} %basis_ref.1), channel_id=1, source_target_pairs={{0,8},{1,5},{2,14},{3,7},{4,12},{5,1},{6,10},{7,3},{8,0},{9,13},{1... | collective-permute-start | bytes 393224 | tf_op jit(solution)/shard_map/ppermute | solution.py:202
  4.7 9.0 %copy-start.1 = (bf16[128,32,256]{2,1,0:T(8,128)(2,1)S(1)}, bf16[128,32,256]{2,1,0:T(8,128)(2,1)}, u32[]{:S(2)}) copy-start(bf16[128,32,256]{2,1,0:T(8,128)(2,1)} %mortar_ref.1) | copy-start | bytes 6291460
  4.7 9.0 %copy-start.2 = (bf16[1,256,256]{2,1,0:T(8,128)(2,1)S(1)}, bf16[1,256,256]{2,1,0:T(8,128)(2,1)}, u32[]{:S(2)}) copy-start(bf16[1,256,256]{2,1,0:T(8,128)(2,1)} %basis_ref.1) | copy-start | bytes 393220
  4.7 9.0 %copy-start.4 = (f32[32]{0:T(128)S(1)}, f32[32]{0:T(128)}, u32[]{:S(2)}) copy-start(f32[32]{0:T(128)} %rate_ref.1) | copy-start | bytes 388
  4.7 9.0 %copy-start.5 = (s32[32]{0:T(128)S(1)}, s32[32]{0:T(128)}, u32[]{:S(2)}) copy-start(s32[32]{0:T(128)} %cell_ref.1) | copy-start | bytes 388
  6.8 1.9 %collective-permute-start.1 = (bf16[80,256]{1,0:T(8,128)(2,1)}, bf16[80,256]{1,0:T(8,128)(2,1)S(1)}, u32[]{:S(2)}, u32[]{:S(2)}) collective-permute-start(bf16[80,256]{1,0:T(8,128)(2,1)} %get-tuple-element.19.pack_ref), channel_id=1, source_target_pairs={{0,1},{1,0},{2,3},{3,2},{4,5},{5,4},{6,7},{7,6},{8,9},{9,8},{10,11... | collective-permute-start | bytes 122888 | tf_op jit(solution)/shard_map/ppermute | solution.py:225
  6.8 9.4 %collective-permute-start.2 = (bf16[80,256]{1,0:T(8,128)(2,1)}, bf16[80,256]{1,0:T(8,128)(2,1)S(1)}, u32[]{:S(2)}, u32[]{:S(2)}) collective-permute-start(bf16[80,256]{1,0:T(8,128)(2,1)} %get-tuple-element.22), channel_id=1, source_target_pairs={{0,4},{2,6},{4,0},{6,2},{8,12},{10,14},{12,8},{14,10},{1,5},{3,7},... | collective-permute-start | bytes 122888 | tf_op jit(solution)/shard_map/ppermute | solution.py:221
  8.3 7.8 %collective-permute-start.3 = (bf16[80,256]{1,0:T(8,128)(2,1)}, bf16[80,256]{1,0:T(8,128)(2,1)S(1)}, u32[]{:S(2)}, u32[]{:S(2)}) collective-permute-start(bf16[80,256]{1,0:T(8,128)(2,1)} %get-tuple-element.23), channel_id=1, source_target_pairs={{0,8},{2,14},{4,12},{6,10},{8,0},{10,6},{12,4},{14,2},{1,9},{3,15}... | collective-permute-start | bytes 122888 | tf_op jit(solution)/shard_map/ppermute | solution.py:221
  8.7 7.5 %collective-permute-start.4 = (bf16[1,256,256]{2,1,0:T(8,128)(2,1)S(1)}, bf16[1,256,256]{2,1,0:T(8,128)(2,1)S(1)}, u32[]{:S(2)}, u32[]{:S(2)}) collective-permute-start(bf16[1,256,256]{2,1,0:T(8,128)(2,1)S(1)} %collective-permute-done.refs_0_), channel_id=1, source_target_pairs={{0,1},{1,0},{2,3},{3,2},{4,5},{5,4},{6,7},{7,6},{8,9},{9,8},{10,11... | collective-permute-start | bytes 393224 | tf_op jit(solution)/shard_map/ppermute | solution.py:249
  8.7 8.3 %collective-permute-start.7 = (bf16[1,256,256]{2,1,0:T(8,128)(2,1)S(1)}, bf16[1,256,256]{2,1,0:T(8,128)(2,1)S(1)}, u32[]{:S(2)}, u32[]{:S(2)}) collective-permute-start(bf16[1,256,256]{2,1,0:T(8,128)(2,1)S(1)} %collective-permute-done.refs_0_), channel_id=1, source_target_pairs={{0,3},{1,0},{2,1},{3,2},{4,7},{5,4},{6,5},{7,6},{8,11},{9,8},{10,9... | collective-permute-start | bytes 393224 | tf_op jit(solution)/shard_map/ppermute | solution.py:251
  11.0 6.0 %collective-permute-start.9 = (bf16[80,256]{1,0:T(8,128)(2,1)}, bf16[80,256]{1,0:T(8,128)(2,1)S(1)}, u32[]{:S(2)}, u32[]{:S(2)}) collective-permute-start(bf16[80,256]{1,0:T(8,128)(2,1)} %get-tuple-element.32), channel_id=1, source_target_pairs={{0,12},{2,10},{4,8},{6,14},{8,4},{10,2},{12,0},{14,6},{1,13},{3,11... | collective-permute-start | bytes 122888 | tf_op jit(solution)/shard_map/ppermute | solution.py:221
  13.7 0.8 %copy-start.3 = (bf16[80,256]{1,0:T(8,128)(2,1)S(1)}, bf16[80,256]{1,0:T(8,128)(2,1)}, u32[]{:S(2)}) copy-start(bf16[80,256]{1,0:T(8,128)(2,1)} %get-tuple-element.19.pack_ref) | copy-start | bytes 122884
  16.2 1.3 %collective-permute-start.5 = (bf16[80,256]{1,0:T(8,128)(2,1)S(1)}, bf16[80,256]{1,0:T(8,128)(2,1)S(1)}, u32[]{:S(2)}, u32[]{:S(2)}) collective-permute-start(bf16[80,256]{1,0:T(8,128)(2,1)S(1)} %collective-permute-done.3.refs_2_), channel_id=1, source_target_pairs={{0,1},{1,0},{2,3},{3,2},{4,5},{5,4},{6,7},{7,6},{8,9},{9,8},{10,11... | collective-permute-start | bytes 122888 | tf_op jit(solution)/shard_map/ppermute | solution.py:256
  16.2 1.4 %collective-permute-start.6 = (bf16[80,256]{1,0:T(8,128)(2,1)S(1)}, bf16[80,256]{1,0:T(8,128)(2,1)S(1)}, u32[]{:S(2)}, u32[]{:S(2)}) collective-permute-start(bf16[80,256]{1,0:T(8,128)(2,1)S(1)} %collective-permute-done.2.refs_4_), channel_id=1, source_target_pairs={{0,1},{1,0},{2,3},{3,2},{4,5},{5,4},{6,7},{7,6},{8,9},{9,8},{10,11... | collective-permute-start | bytes 122888 | tf_op jit(solution)/shard_map/ppermute | solution.py:256
  17.0 1.8 %collective-permute-start.10 = (bf16[80,256]{1,0:T(8,128)(2,1)S(1)}, bf16[80,256]{1,0:T(8,128)(2,1)S(1)}, u32[]{:S(2)}, u32[]{:S(2)}) collective-permute-start(bf16[80,256]{1,0:T(8,128)(2,1)S(1)} %collective-permute-done.9.refs_2_), channel_id=1, source_target_pairs={{0,1},{1,0},{2,3},{3,2},{4,5},{5,4},{6,7},{7,6},{8,9},{9,8},{10,11... | collective-permute-start | bytes 122888 | tf_op jit(solution)/shard_map/ppermute | solution.py:262
  17.0 1.8 %collective-permute-start.8 = (bf16[1,256,256]{2,1,0:T(8,128)(2,1)S(1)}, bf16[1,256,256]{2,1,0:T(8,128)(2,1)S(1)}, u32[]{:S(2)}, u32[]{:S(2)}) collective-permute-start(bf16[1,256,256]{2,1,0:T(8,128)(2,1)S(1)} %collective-permute-done.7.refs_0_), channel_id=1, source_target_pairs={{0,1},{1,0},{2,3},{3,2},{4,5},{5,4},{6,7},{7,6},{8,9},{9,8},{10,11... | collective-permute-start | bytes 393224 | tf_op jit(solution)/shard_map/ppermute | solution.py:252
  17.6 1.2 %copy-start = (bf16[256,256]{1,0:T(8,128)(2,1)S(1)}, bf16[256,256]{1,0:T(8,128)(2,1)}, u32[]{:S(2)}) copy-start(bf16[256,256]{1,0:T(8,128)(2,1)} %projection_ref.1) | copy-start | bytes 393220

commit v8 on v7

--- a/solution.py
+++ b/solution.py
@@ -67,11 +67,16 @@
     return total
 
 
-def own_kernel(mortar_ref, rate_ref, cell_ref, basis_ref, pack_ref, swapped_ref, pumped_ref, sum_ref, weight_ref, sem):
+def own_kernel(
+    mortar_ref, rate_ref, cell_ref, basis_ref, pack_any, swapped_ref, pumped_ref, sum_ref, weight_ref, pack_ref, sem, pack_sem
+):
     blocks_own, columns, dof_count = pumped_ref.shape
     first_block = lax.axis_index("face") * blocks_own
+    pack_fetch = pltpu.make_async_copy(pack_any, pack_ref, pack_sem)
     fetch = pltpu.make_async_copy(mortar_ref.at[pl.ds(first_block, blocks_own)], pumped_ref, sem)
+    pack_fetch.start()
     fetch.start()
+    pack_fetch.wait()
     weight_ref[...] = block_weights((pack_ref, swapped_ref), pack_ref.shape[0] - ROW_TILE, blocks_own)
     fetch.wait()
 
@@ -220,8 +225,7 @@
         ]
         return lax.ppermute(pack, ("sub", "rhs"), pairs)
 
-    early_count = 1 + len(near) + len(far)
-    arrived = [along_sub(way, pack) for way, pack in zip(ways[1:early_count], packs[1:])]
+    arrived = [along_sub(way, pack) for way, pack in zip(ways[1:], packs[1:])]
     own_swapped = lax.ppermute(packs[0], "face", swap)
 
     firsts, own_swapped = lax.optimization_barrier((firsts, own_swapped))
@@ -231,9 +235,14 @@
             jax.ShapeDtypeStruct(block_shape, jnp.bfloat16),
             jax.ShapeDtypeStruct(block_shape, jnp.float32),
         ],
-        in_specs=[HBM, SMEM, SMEM, VMEM, VMEM, VMEM],
+        in_specs=[HBM, SMEM, SMEM, VMEM, HBM, VMEM],
         out_specs=[VMEM, VMEM],
-        scratch_shapes=[pltpu.VMEM((blocks_own, dof_count), jnp.float32), pltpu.SemaphoreType.DMA(())],
+        scratch_shapes=[
+            pltpu.VMEM((blocks_own, dof_count), jnp.float32),
+            pltpu.VMEM((pack_rows, dof_count), jnp.bfloat16),
+            pltpu.SemaphoreType.DMA(()),
+            pltpu.SemaphoreType.DMA(()),
+        ],
         compiler_params=pltpu.CompilerParams(vmem_limit_bytes=32 * MIB),
         cost_estimate=WORK,
         name="own_blocks",
@@ -250,16 +259,14 @@
         if has_far:
             second = lax.ppermute(first, ("rhs", "face"), pairs)
             late.append([second, lax.ppermute(second, "face", swap)])
-    *late_packs, firsts = lax.optimization_barrier((*packs[early_count:], firsts))
-    late_arrived = [along_sub(way, pack) for way, pack in zip(ways[early_count:], late_packs)]
     arrived, own_sum, early = lax.optimization_barrier((arrived, own_sum, early))
     swapped = [lax.ppermute(array, "face", swap) for array in arrived]
-    places = dict(zip(ways[1:early_count], zip(arrived, swapped)))
+    places = dict(zip(ways[1:], zip(arrived, swapped)))
     weights = []
     for (a, b, c), (has_far, has_near) in zip(groups, kinds):
         weights += list(places[a, b]) * has_far + list(places[c, c]) * has_near
-    for arrays, array in zip(late, late_arrived):
-        arrays += [array, lax.ppermute(array, "face", swap)]
+    for arrays, (a, b) in zip(late, far):
+        arrays += places[b, a]
 
     late_count = len(late)
     count = others - late_count

time: 20.9 us -> 20.1 us (0.962)
  starting transfers between devices: 12.1 us -> 11.2 us
    ppermute x1, starting transfers between devices: 2.28 us -> 1.71 us  [on_device(): second = lax.ppermute(first, ('rhs', 'face'), pairs)]
    ppermute x3, starting transfers between devices: 4.65 us -> 4.39 us  [along_sub(): return lax.ppermute(pack, ('sub', 'rhs'), pairs)]
    ppermute x2 -> x3, waiting for transfers between devices: 0.11 us -> 0.36 us  [on_device(): swapped = [lax.ppermute(array, 'face', swap) for array in arrived]]
    ppermute x3, waiting for transfers between devices: 0.25 us -> 0.01 us  [along_sub(): return lax.ppermute(pack, ('sub', 'rhs'), pairs)]
    ppermute x2 -> x3, starting transfers between devices: 0.57 us -> 0.65 us  [on_device(): swapped = [lax.ppermute(array, 'face', swap) for array in arrived]]
  transfers between devices with their start and end apart: 11 -> 11, of which waited for: 2 -> 2; matrix products, arithmetic and copies ran while one was open for 0% -> 0% of each run, Pallas kernels for 23% -> 24%
where the time goes in v8:
time: 20.1 us; the launch traced here: 19.9 us
  starting transfers between devices  11.2 us (56%)
  Pallas kernels  6.74 us (34%)
  local copies, waits for them, and re-layouts  0.79 us (4%)
  between operations  0.79 us (4%)
  waiting for transfers between devices  0.38 us (2%)
    ppermute x3, starting transfers between devices, along_sub(): return lax.ppermute(pack, ('sub', 'rhs'), pairs)  4.39 us
    ppermute x1, starting transfers between devices, on_device(): firsts.append(lax.ppermute(basis, ('sub', 'rhs', 'face'), pairs))  4.04 us
    pallas_call x1, Pallas kernels, on_device(): pl.pallas_call(functools.partial(pack_kernel, ways), out_shape=[jax.Shape...  2.03 us
    pallas_call x1, Pallas kernels, on_device(): pl.pallas_call(last_kernel, out_shape=jax.ShapeDtypeStruct(block_shape, j...  1.86 us
    ppermute x1, starting transfers between devices, on_device(): second = lax.ppermute(first, ('rhs', 'face'), pairs)  1.71 us
    pallas_call x1, Pallas kernels, on_device(): pl.pallas_call(own_kernel, out_shape=[jax.ShapeDtypeStruct(block_shape, j...  1.67 us
    pallas_call x1, Pallas kernels, on_device(): pl.pallas_call(functools.partial(stage_kernel, kinds), out_shape=jax.Shap...  1.18 us
    unnamed x12, local copies, waits for them, and re-layouts  0.79 us
  transfers between devices with their start and end apart: 11, of which 2 were waited for; matrix products, arithmetic and copies ran while one was open for 0% of the time, Pallas kernels for 24%

profile of v8, /device:TPU:0, one launch (start us, length us, event | category | flops | bytes accessed | tf_op | source)
XLA Modules:
  0.0 19.9 jit_solution(234077079344339406)
XLA Ops:
  0.0 4.0 %collective-permute-start = (bf16[1,256,256]{2,1,0:T(8,128)(2,1)}, bf16[1,256,256]{2,1,0:T(8,128)(2,1)S(1)}, u32[]{:S(2)}, u32[]{:S(2)}) collective-permute-start(bf16[1,256,256]{2,1,0:T(8,128)(2,1)} %basis_ref.1), channel_id=1, source_target_pairs={{0,8},{1,5},{2,14},{3,7},{4,12},{5,1},{6,10},{7,3},{8,0},{9,13},{1... | collective-permute-start | bytes 393224 | tf_op jit(solution)/shard_map/ppermute | solution.py:207
  4.7 0.0 copy-start.1
  4.7 0.0 copy-start.2
  4.7 0.0 copy-start.4
  4.7 0.0 copy-start.5
  4.7 2.0 %pack_weights.1 = (bf16[80,256]{1,0:T(8,128)(2,1)}, bf16[80,256]{1,0:T(8,128)(2,1)}, bf16[80,256]{1,0:T(8,128)(2,1)}, bf16[80,256]{1,0:T(8,128)(2,1)}) custom-call(s32[1,128]{1,0:T(1,128)} %bitcast.2, s32[1,128]{1,0:T(1,128)} %bitcast.3, bf16[128,256]{1,0:T(8,128)(2,1)} %scale_ref.1, s32[1]{0:T(128)S(6)} %copy.12.section_ref), custom_call_target="tpu_custom_call" | custom-call | flops 4000000000 | bytes 8388608 | tf_op jit(solution)/shard_map/pack_weights/pallas_call | solution.py:213
  6.8 0.0 collective-permute-start.1
  6.8 1.6 %collective-permute-start.2 = (bf16[80,256]{1,0:T(8,128)(2,1)}, bf16[80,256]{1,0:T(8,128)(2,1)S(1)}, u32[]{:S(2)}, u32[]{:S(2)}) collective-permute-start(bf16[80,256]{1,0:T(8,128)(2,1)} %get-tuple-element.22), channel_id=1, source_target_pairs={{0,4},{2,6},{4,0},{6,2},{8,12},{10,14},{12,8},{14,10},{1,5},{3,7},... | collective-permute-start | bytes 122888 | tf_op jit(solution)/shard_map/ppermute | solution.py:226
  8.3 0.3 %collective-permute-start.3 = (bf16[80,256]{1,0:T(8,128)(2,1)}, bf16[80,256]{1,0:T(8,128)(2,1)S(1)}, u32[]{:S(2)}, u32[]{:S(2)}) collective-permute-start(bf16[80,256]{1,0:T(8,128)(2,1)} %get-tuple-element.23), channel_id=1, source_target_pairs={{0,8},{2,14},{4,12},{6,10},{8,0},{10,6},{12,4},{14,2},{1,9},{3,15}... | collective-permute-start | bytes 122888 | tf_op jit(solution)/shard_map/ppermute | solution.py:226
  8.7 2.5 %collective-permute-start.4 = (bf16[80,256]{1,0:T(8,128)(2,1)}, bf16[80,256]{1,0:T(8,128)(2,1)S(1)}, u32[]{:S(2)}, u32[]{:S(2)}) collective-permute-start(bf16[80,256]{1,0:T(8,128)(2,1)} %get-tuple-element.24), channel_id=1, source_target_pairs={{0,12},{2,10},{4,8},{6,14},{8,4},{10,2},{12,0},{14,6},{1,13},{3,11... | collective-permute-start | bytes 122888 | tf_op jit(solution)/shard_map/ppermute | solution.py:226
  11.2 0.0 collective-permute-done.1.swapped_ref
  11.2 0.0 collective-permute-done.refs_0_
  11.2 0.0 collective-permute-start.5
  11.2 1.7 %collective-permute-start.8 = (bf16[1,256,256]{2,1,0:T(8,128)(2,1)S(1)}, bf16[1,256,256]{2,1,0:T(8,128)(2,1)S(1)}, u32[]{:S(2)}, u32[]{:S(2)}) collective-permute-start(bf16[1,256,256]{2,1,0:T(8,128)(2,1)S(1)} %collective-permute-done.refs_0_), channel_id=1, source_target_pairs={{0,3},{1,0},{2,1},{3,2},{4,7},{5,4},{6,5},{7,6},{8,11},{9,8},{10,9... | collective-permute-start | bytes 393224 | tf_op jit(solution)/shard_map/ppermute | solution.py:260
  12.9 0.0 copy-done.1
  12.9 0.0 copy-done.2
  12.9 0.0 copy-done.4
  12.9 0.0 copy-done.5
  12.9 0.0 copy-start.3
  12.9 0.8 %copy-done.3 = bf16[80,256]{1,0:T(8,128)(2,1)S(1)} copy-done((bf16[80,256]{1,0:T(8,128)(2,1)S(1)}, bf16[80,256]{1,0:T(8,128)(2,1)}, u32[]{:S(2)}) %copy-start.3) | copy-done | bytes 40984
  13.7 1.7 %own_blocks.1 = (bf16[64,32,256]{2,1,0:T(8,128)(2,1)S(1)}, f32[64,32,256]{2,1,0:T(8,128)S(1)}) custom-call(bf16[128,32,256]{2,1,0:T(8,128)(2,1)S(1)} %copy-done.1, f32[32]{0:T(128)S(1)} %copy-done.4, s32[32]{0:T(128)S(1)} %copy-done.5, bf16[1,256,256]{2,1,0:T(8,128)(2,1)S(1)} %copy-done.2, bf16[80,256]{1,0:T(8,128)(2,1)S(1)} %copy-done.3, ...), custom_call_target="tpu_custom_call" | custom-call | flops 4000000000 | bytes 8388608 | tf_op jit(solution)/shard_map/own_blocks/pallas_call | solution.py:232
  15.3 0.0 collective-permute-done.2.refs_4_
  15.4 0.0 collective-permute-done.3.refs_2_
  15.4 0.0 collective-permute-done.4.refs_2_
  15.4 0.0 collective-permute-done.5.refs_1_
  15.4 0.1 collective-permute-start.6
  15.5 0.5 %collective-permute-start.7 = (bf16[80,256]{1,0:T(8,128)(2,1)S(1)}, bf16[80,256]{1,0:T(8,128)(2,1)S(1)}, u32[]{:S(2)}, u32[]{:S(2)}) collective-permute-start(bf16[80,256]{1,0:T(8,128)(2,1)S(1)} %collective-permute-done.2.refs_4_), channel_id=1, source_target_pairs={{0,1},{1,0},{2,3},{3,2},{4,5},{5,4},{6,7},{7,6},{8,9},{9,8},{10,11... | collective-permute-start | bytes 122888 | tf_op jit(solution)/shard_map/ppermute | solution.py:263
  16.0 0.1 collective-permute-start.10
  16.0 0.0 collective-permute-done.8.refs_0_
  16.0 0.4 %collective-permute-start.9 = (bf16[1,256,256]{2,1,0:T(8,128)(2,1)S(1)}, bf16[1,256,256]{2,1,0:T(8,128)(2,1)S(1)}, u32[]{:S(2)}, u32[]{:S(2)}) collective-permute-start(bf16[1,256,256]{2,1,0:T(8,128)(2,1)S(1)} %collective-permute-done.8.refs_0_), channel_id=1, source_target_pairs={{0,1},{1,0},{2,3},{3,2},{4,5},{5,4},{6,7},{7,6},{8,9},{9,8},{10,11... | collective-permute-start | bytes 393224 | tf_op jit(solution)/shard_map/ppermute | solution.py:261
  16.5 0.2 collective-permute-done.6.refs_3_
  16.7 0.2 collective-permute-done.7.refs_5_
  16.8 0.0 copy-start
  16.8 1.2 %stage.1.sum_ref = f32[64,32,256]{2,1,0:T(8,128)S(1)} custom-call(bf16[64,32,256]{2,1,0:T(8,128)(2,1)S(1)} %get-tuple-element.21.pumped_ref, f32[64,32,256]{2,1,0:T(8,128)S(1)} %get-tuple-element.27.sum_ref, bf16[1,256,256]{2,1,0:T(8,128)(2,1)S(1)} %collective-permute-done.refs_0_, ...), custom_call_target="tpu_custom_call", output_to_operand_aliasing={{}: (1, {})} | custom-call | flops 4000000000 | bytes 8388608 | tf_op jit(solution)/shard_map/stage/pallas_call | solution.py:274
  18.0 0.0 collective-permute-done.10.refs_3_
  18.0 0.0 collective-permute-done.9.refs_1_
  18.0 0.0 copy-done
  18.1 1.9 %last_stage.1 = f32[64,32,256]{2,1,0:T(8,128)} custom-call(bf16[64,32,256]{2,1,0:T(8,128)(2,1)S(1)} %get-tuple-element.21.pumped_ref, f32[64,32,256]{2,1,0:T(8,128)S(1)} %stage.1.sum_ref, bf16[256,256]{1,0:T(8,128)(2,1)S(1)} %copy-done, bf16[1,256,256]{2,1,0:T(8,128)(2,1)S(1)} %collective-permute-done.8.refs_0_, ...), custom_call_target="tpu_custom_call" | custom-call | tf_op jit(solution)/shard_map/last_stage/pallas_call | solution.py:291
Async XLA Ops:
  0.0 11.2 %collective-permute-start = (bf16[1,256,256]{2,1,0:T(8,128)(2,1)}, bf16[1,256,256]{2,1,0:T(8,128)(2,1)S(1)}, u32[]{:S(2)}, u32[]{:S(2)}) collective-permute-start(bf16[1,256,256]{2,1,0:T(8,128)(2,1)} %basis_ref.1), channel_id=1, source_target_pairs={{0,8},{1,5},{2,14},{3,7},{4,12},{5,1},{6,10},{7,3},{8,0},{9,13},{1... | collective-permute-start | bytes 393224 | tf_op jit(solution)/shard_map/ppermute | solution.py:207
  4.7 8.2 %copy-start.1 = (bf16[128,32,256]{2,1,0:T(8,128)(2,1)S(1)}, bf16[128,32,256]{2,1,0:T(8,128)(2,1)}, u32[]{:S(2)}) copy-start(bf16[128,32,256]{2,1,0:T(8,128)(2,1)} %mortar_ref.1) | copy-start | bytes 6291460
  4.7 8.2 %copy-start.2 = (bf16[1,256,256]{2,1,0:T(8,128)(2,1)S(1)}, bf16[1,256,256]{2,1,0:T(8,128)(2,1)}, u32[]{:S(2)}) copy-start(bf16[1,256,256]{2,1,0:T(8,128)(2,1)} %basis_ref.1) | copy-start | bytes 393220
  4.7 8.2 %copy-start.4 = (f32[32]{0:T(128)S(1)}, f32[32]{0:T(128)}, u32[]{:S(2)}) copy-start(f32[32]{0:T(128)} %rate_ref.1) | copy-start | bytes 388
  4.7 8.2 %copy-start.5 = (s32[32]{0:T(128)S(1)}, s32[32]{0:T(128)}, u32[]{:S(2)}) copy-start(s32[32]{0:T(128)} %cell_ref.1) | copy-start | bytes 388
  6.8 4.4 %collective-permute-start.1 = (bf16[80,256]{1,0:T(8,128)(2,1)}, bf16[80,256]{1,0:T(8,128)(2,1)S(1)}, u32[]{:S(2)}, u32[]{:S(2)}) collective-permute-start(bf16[80,256]{1,0:T(8,128)(2,1)} %get-tuple-element.19.pack_any), channel_id=1, source_target_pairs={{0,1},{1,0},{2,3},{3,2},{4,5},{5,4},{6,7},{7,6},{8,9},{9,8},{10,11... | collective-permute-start | bytes 122888 | tf_op jit(solution)/shard_map/ppermute | solution.py:229
  6.8 8.6 %collective-permute-start.2 = (bf16[80,256]{1,0:T(8,128)(2,1)}, bf16[80,256]{1,0:T(8,128)(2,1)S(1)}, u32[]{:S(2)}, u32[]{:S(2)}) collective-permute-start(bf16[80,256]{1,0:T(8,128)(2,1)} %get-tuple-element.22), channel_id=1, source_target_pairs={{0,4},{2,6},{4,0},{6,2},{8,12},{10,14},{12,8},{14,10},{1,5},{3,7},... | collective-permute-start | bytes 122888 | tf_op jit(solution)/shard_map/ppermute | solution.py:226
  8.3 7.0 %collective-permute-start.3 = (bf16[80,256]{1,0:T(8,128)(2,1)}, bf16[80,256]{1,0:T(8,128)(2,1)S(1)}, u32[]{:S(2)}, u32[]{:S(2)}) collective-permute-start(bf16[80,256]{1,0:T(8,128)(2,1)} %get-tuple-element.23), channel_id=1, source_target_pairs={{0,8},{2,14},{4,12},{6,10},{8,0},{10,6},{12,4},{14,2},{1,9},{3,15}... | collective-permute-start | bytes 122888 | tf_op jit(solution)/shard_map/ppermute | solution.py:226
  8.7 6.7 %collective-permute-start.4 = (bf16[80,256]{1,0:T(8,128)(2,1)}, bf16[80,256]{1,0:T(8,128)(2,1)S(1)}, u32[]{:S(2)}, u32[]{:S(2)}) collective-permute-start(bf16[80,256]{1,0:T(8,128)(2,1)} %get-tuple-element.24), channel_id=1, source_target_pairs={{0,12},{2,10},{4,8},{6,14},{8,4},{10,2},{12,0},{14,6},{1,13},{3,11... | collective-permute-start | bytes 122888 | tf_op jit(solution)/shard_map/ppermute | solution.py:226
  11.2 4.2 %collective-permute-start.5 = (bf16[1,256,256]{2,1,0:T(8,128)(2,1)S(1)}, bf16[1,256,256]{2,1,0:T(8,128)(2,1)S(1)}, u32[]{:S(2)}, u32[]{:S(2)}) collective-permute-start(bf16[1,256,256]{2,1,0:T(8,128)(2,1)S(1)} %collective-permute-done.refs_0_), channel_id=1, source_target_pairs={{0,1},{1,0},{2,3},{3,2},{4,5},{5,4},{6,7},{7,6},{8,9},{9,8},{10,11... | collective-permute-start | bytes 393224 | tf_op jit(solution)/shard_map/ppermute | solution.py:258
  11.2 4.9 %collective-permute-start.8 = (bf16[1,256,256]{2,1,0:T(8,128)(2,1)S(1)}, bf16[1,256,256]{2,1,0:T(8,128)(2,1)S(1)}, u32[]{:S(2)}, u32[]{:S(2)}) collective-permute-start(bf16[1,256,256]{2,1,0:T(8,128)(2,1)S(1)} %collective-permute-done.refs_0_), channel_id=1, source_target_pairs={{0,3},{1,0},{2,1},{3,2},{4,7},{5,4},{6,5},{7,6},{8,11},{9,8},{10,9... | collective-permute-start | bytes 393224 | tf_op jit(solution)/shard_map/ppermute | solution.py:260
  12.9 0.8 %copy-start.3 = (bf16[80,256]{1,0:T(8,128)(2,1)S(1)}, bf16[80,256]{1,0:T(8,128)(2,1)}, u32[]{:S(2)}) copy-start(bf16[80,256]{1,0:T(8,128)(2,1)} %get-tuple-element.19.pack_any) | copy-start | bytes 122884
  15.4 1.3 %collective-permute-start.6 = (bf16[80,256]{1,0:T(8,128)(2,1)S(1)}, bf16[80,256]{1,0:T(8,128)(2,1)S(1)}, u32[]{:S(2)}, u32[]{:S(2)}) collective-permute-start(bf16[80,256]{1,0:T(8,128)(2,1)S(1)} %collective-permute-done.3.refs_2_), channel_id=1, source_target_pairs={{0,1},{1,0},{2,3},{3,2},{4,5},{5,4},{6,7},{7,6},{8,9},{9,8},{10,11... | collective-permute-start | bytes 122888 | tf_op jit(solution)/shard_map/ppermute | solution.py:263
  15.5 1.4 %collective-permute-start.7 = (bf16[80,256]{1,0:T(8,128)(2,1)S(1)}, bf16[80,256]{1,0:T(8,128)(2,1)S(1)}, u32[]{:S(2)}, u32[]{:S(2)}) collective-permute-start(bf16[80,256]{1,0:T(8,128)(2,1)S(1)} %collective-permute-done.2.refs_4_), channel_id=1, source_target_pairs={{0,1},{1,0},{2,3},{3,2},{4,5},{5,4},{6,7},{7,6},{8,9},{9,8},{10,11... | collective-permute-start | bytes 122888 | tf_op jit(solution)/shard_map/ppermute | solution.py:263
  16.0 2.1 %collective-permute-start.10 = (bf16[80,256]{1,0:T(8,128)(2,1)S(1)}, bf16[80,256]{1,0:T(8,128)(2,1)S(1)}, u32[]{:S(2)}, u32[]{:S(2)}) collective-permute-start(bf16[80,256]{1,0:T(8,128)(2,1)S(1)} %collective-permute-done.4.refs_2_), channel_id=1, source_target_pairs={{0,1},{1,0},{2,3},{3,2},{4,5},{5,4},{6,7},{7,6},{8,9},{9,8},{10,11... | collective-permute-start | bytes 122888 | tf_op jit(solution)/shard_map/ppermute | solution.py:263
  16.0 2.0 %collective-permute-start.9 = (bf16[1,256,256]{2,1,0:T(8,128)(2,1)S(1)}, bf16[1,256,256]{2,1,0:T(8,128)(2,1)S(1)}, u32[]{:S(2)}, u32[]{:S(2)}) collective-permute-start(bf16[1,256,256]{2,1,0:T(8,128)(2,1)S(1)} %collective-permute-done.8.refs_0_), channel_id=1, source_target_pairs={{0,1},{1,0},{2,3},{3,2},{4,5},{5,4},{6,7},{7,6},{8,9},{9,8},{10,11... | collective-permute-start | bytes 393224 | tf_op jit(solution)/shard_map/ppermute | solution.py:261
  16.8 1.2 %copy-start = (bf16[256,256]{1,0:T(8,128)(2,1)S(1)}, bf16[256,256]{1,0:T(8,128)(2,1)}, u32[]{:S(2)}) copy-start(bf16[256,256]{1,0:T(8,128)(2,1)} %projection_ref.1) | copy-start | bytes 393220

commit v9 on v8

--- a/solution.py
+++ b/solution.py
@@ -68,19 +68,31 @@
 
 
 def own_kernel(
-    mortar_ref, rate_ref, cell_ref, basis_ref, pack_any, swapped_ref, pumped_ref, sum_ref, weight_ref, pack_ref, sem, pack_sem
+    mortar_ref,
+    rate_ref,
+    cell_ref,
+    owner_ref,
+    slot_ref,
+    scale_ref,
+    section_ref,
+    basis_ref,
+    swapped_ref,
+    pumped_ref,
+    sum_ref,
+    weight_ref,
 ):
     blocks_own, columns, dof_count = pumped_ref.shape
+    faces = owner_ref.shape[1]
+    here = lax.axis_index("sub")
     first_block = lax.axis_index("face") * blocks_own
-    pack_fetch = pltpu.make_async_copy(pack_any, pack_ref, pack_sem)
-    fetch = pltpu.make_async_copy(mortar_ref.at[pl.ds(first_block, blocks_own)], pumped_ref, sem)
-    pack_fetch.start()
-    fetch.start()
-    pack_fetch.wait()
-    weight_ref[...] = block_weights((pack_ref, swapped_ref), pack_ref.shape[0] - ROW_TILE, blocks_own)
-    fetch.wait()
-
-    base = lax.axis_index("sub") * mortar_ref.shape[0] + first_block
+    sign = (1 - 2 * section_ref[0]).astype(jnp.float32)
+    block_ids = first_block + lax.broadcasted_iota(jnp.int32, (blocks_own, faces), 0)
+    hit = (slot_ref[...] == block_ids) & (owner_ref[...] == here)
+    weight = jnp.dot(hit.astype(jnp.bfloat16), scale_ref[...], preferred_element_type=jnp.float32) * sign
+    weight_ref[...] = weight + block_weights((swapped_ref,), swapped_ref.shape[0] - ROW_TILE, blocks_own)
+    pumped_ref[...] = mortar_ref[pl.ds(first_block, blocks_own)]
+
+    base = here * mortar_ref.shape[0] + first_block
     for column in range(columns):
         block = lax.div(cell_ref[column], dof_count) - base
         dof = lax.rem(cell_ref[column], dof_count)
@@ -210,6 +222,7 @@
     near = [(c, c) for (_, _, c), (_, has) in zip(groups, kinds) if has]
     far = [(a, b) for (a, b, _), (has, _) in zip(groups, kinds) if has]
     ways = [(0, 0), *near, *far, *[(b, a) for a, b in far]]
+    faces = [face_owner.reshape(1, faces_dev), face_slot.reshape(1, faces_dev), face_scale]
     packs = pl.pallas_call(
         functools.partial(pack_kernel, ways),
         out_shape=[jax.ShapeDtypeStruct((pack_rows, dof_count), jnp.bfloat16)] * len(ways),
@@ -217,7 +230,7 @@
         out_specs=[VMEM] * len(ways),
         cost_estimate=WORK,
         name="pack_weights",
-    )(face_owner.reshape(1, faces_dev), face_slot.reshape(1, faces_dev), face_scale, section)
+    )(*faces, section)
 
     def along_sub(way, pack):
         pairs = [
@@ -235,18 +248,13 @@
             jax.ShapeDtypeStruct(block_shape, jnp.bfloat16),
             jax.ShapeDtypeStruct(block_shape, jnp.float32),
         ],
-        in_specs=[HBM, SMEM, SMEM, VMEM, HBM, VMEM],
+        in_specs=[VMEM, SMEM, SMEM, VMEM, VMEM, VMEM, SMEM, VMEM, VMEM],
         out_specs=[VMEM, VMEM],
-        scratch_shapes=[
-            pltpu.VMEM((blocks_own, dof_count), jnp.float32),
-            pltpu.VMEM((pack_rows, dof_count), jnp.bfloat16),
-            pltpu.SemaphoreType.DMA(()),
-            pltpu.SemaphoreType.DMA(()),
-        ],
+        scratch_shapes=[pltpu.VMEM((blocks_own, dof_count), jnp.float32)],
         compiler_params=pltpu.CompilerParams(vmem_limit_bytes=32 * MIB),
         cost_estimate=WORK,
         name="own_blocks",
-    )(mortar_in, pump_rate, well_cell, basis, packs[0], own_swapped)
+    )(mortar_in, pump_rate, well_cell, *faces, section, basis, own_swapped)
 
     pairs = [
         (r * halves + face, r * halves if face else (r ^ 1) * halves + 1)
@@ -259,7 +267,8 @@
         if has_far:
             second = lax.ppermute(first, ("rhs", "face"), pairs)
             late.append([second, lax.ppermute(second, "face", swap)])
-    arrived, own_sum, early = lax.optimization_barrier((arrived, own_sum, early))
+    soon = len(near) + len(far)
+    arrived[:soon], own_sum, early = lax.optimization_barrier((arrived[:soon], own_sum, early))
     swapped = [lax.ppermute(array, "face", swap) for array in arrived]
     places = dict(zip(ways[1:], zip(arrived, swapped)))
     weights = []

time: 20.1 us -> 19.7 us (0.980)
  local copies, waits for them, and re-layouts: 0.79 us -> 0.03 us
  waiting for transfers between devices: 0.38 us -> 0.94 us
    unnamed x12 -> x16, local copies, waits for them, and re-layouts: 0.79 us -> 0.03 us
    ppermute x3, waiting for transfers between devices: 0.01 us -> 0.57 us  [along_sub(): return lax.ppermute(pack, ('sub', 'rhs'), pairs)]
  transfers between devices with their start and end apart: 11 -> 11, of which waited for: 2 -> 3; matrix products, arithmetic and copies ran while one was open for 0% -> 0% of each run, Pallas kernels for 24% -> 24%
where the time goes in v9:
time: 19.7 us; the launch traced here: 19.6 us
  starting transfers between devices  11.2 us (57%)
  Pallas kernels  6.64 us (34%)
  waiting for transfers between devices  0.94 us (5%)
  between operations  0.8 us (4%)
    ppermute x3, starting transfers between devices, along_sub(): return lax.ppermute(pack, ('sub', 'rhs'), pairs)  4.39 us
    ppermute x1, starting transfers between devices, on_device(): firsts.append(lax.ppermute(basis, ('sub', 'rhs', 'face'), pairs))  4.04 us
    pallas_call x1, Pallas kernels, on_device(): pl.pallas_call(functools.partial(pack_kernel, ways), out_shape=[jax.Shape...  2 us
    pallas_call x1, Pallas kernels, on_device(): pl.pallas_call(last_kernel, out_shape=jax.ShapeDtypeStruct(block_shape, j...  1.87 us
    ppermute x1, starting transfers between devices, on_device(): second = lax.ppermute(first, ('rhs', 'face'), pairs)  1.71 us
    pallas_call x1, Pallas kernels, on_device(): pl.pallas_call(own_kernel, out_shape=[jax.ShapeDtypeStruct(block_shape, j...  1.59 us
    pallas_call x1, Pallas kernels, on_device(): pl.pallas_call(functools.partial(stage_kernel, kinds), out_shape=jax.Shap...  1.18 us
    ppermute x3, waiting for transfers between devices, along_sub(): return lax.ppermute(pack, ('sub', 'rhs'), pairs)  0.57 us
  transfers between devices with their start and end apart: 11, of which 3 were waited for; matrix products, arithmetic and copies ran while one was open for 0% of the time, Pallas kernels for 24%

profile of v9, /device:TPU:0, one launch (start us, length us, event | category | flops | bytes accessed | tf_op | source)
XLA Modules:
  0.0 19.6 jit_solution(5957265139102282016)
XLA Ops:
  0.0 4.0 %collective-permute-start = (bf16[1,256,256]{2,1,0:T(8,128)(2,1)}, bf16[1,256,256]{2,1,0:T(8,128)(2,1)S(1)}, u32[]{:S(2)}, u32[]{:S(2)}) collective-permute-start(bf16[1,256,256]{2,1,0:T(8,128)(2,1)} %basis_ref.1), channel_id=1, source_target_pairs={{0,8},{1,5},{2,14},{3,7},{4,12},{5,1},{6,10},{7,3},{8,0},{9,13},{1... | collective-permute-start | bytes 393224 | tf_op jit(solution)/shard_map/ppermute | solution.py:219
  4.7 0.0 copy-start.1
  4.7 0.0 copy-start.2
  4.7 0.0 copy-start.3
  4.7 0.0 copy-start.4
  4.7 0.0 copy-start.5
  4.7 0.0 copy-start.6
  4.7 0.0 copy-start.7
  4.8 2.0 %pack_weights.1 = (bf16[80,256]{1,0:T(8,128)(2,1)}, bf16[80,256]{1,0:T(8,128)(2,1)}, bf16[80,256]{1,0:T(8,128)(2,1)}, bf16[80,256]{1,0:T(8,128)(2,1)}) custom-call(s32[1,128]{1,0:T(1,128)} %bitcast.2, s32[1,128]{1,0:T(1,128)} %bitcast.4, bf16[128,256]{1,0:T(8,128)(2,1)} %scale_ref.3, s32[1]{0:T(128)S(6)} %copy.12.section_ref), custom_call_target="tpu_custom_call" | custom-call | flops 4000000000 | bytes 8388608 | tf_op jit(solution)/shard_map/pack_weights/pallas_call | solution.py:226
  6.8 0.0 collective-permute-start.1
  6.8 1.6 %collective-permute-start.2 = (bf16[80,256]{1,0:T(8,128)(2,1)}, bf16[80,256]{1,0:T(8,128)(2,1)S(1)}, u32[]{:S(2)}, u32[]{:S(2)}) collective-permute-start(bf16[80,256]{1,0:T(8,128)(2,1)} %get-tuple-element.21), channel_id=1, source_target_pairs={{0,4},{2,6},{4,0},{6,2},{8,12},{10,14},{12,8},{14,10},{1,5},{3,7},... | collective-permute-start | bytes 122888 | tf_op jit(solution)/shard_map/ppermute | solution.py:239
  8.3 0.3 %collective-permute-start.3 = (bf16[80,256]{1,0:T(8,128)(2,1)}, bf16[80,256]{1,0:T(8,128)(2,1)S(1)}, u32[]{:S(2)}, u32[]{:S(2)}) collective-permute-start(bf16[80,256]{1,0:T(8,128)(2,1)} %get-tuple-element.22), channel_id=1, source_target_pairs={{0,8},{2,14},{4,12},{6,10},{8,0},{10,6},{12,4},{14,2},{1,9},{3,15}... | collective-permute-start | bytes 122888 | tf_op jit(solution)/shard_map/ppermute | solution.py:239
  8.7 2.5 %collective-permute-start.9 = (bf16[80,256]{1,0:T(8,128)(2,1)}, bf16[80,256]{1,0:T(8,128)(2,1)S(1)}, u32[]{:S(2)}, u32[]{:S(2)}) collective-permute-start(bf16[80,256]{1,0:T(8,128)(2,1)} %get-tuple-element.30), channel_id=1, source_target_pairs={{0,12},{2,10},{4,8},{6,14},{8,4},{10,2},{12,0},{14,6},{1,13},{3,11... | collective-permute-start | bytes 122888 | tf_op jit(solution)/shard_map/ppermute | solution.py:239
  11.2 0.0 collective-permute-done.1.swapped_ref
  11.2 0.0 collective-permute-done.refs_0_
  11.2 0.0 collective-permute-start.4
  11.2 1.7 %collective-permute-start.7 = (bf16[1,256,256]{2,1,0:T(8,128)(2,1)S(1)}, bf16[1,256,256]{2,1,0:T(8,128)(2,1)S(1)}, u32[]{:S(2)}, u32[]{:S(2)}) collective-permute-start(bf16[1,256,256]{2,1,0:T(8,128)(2,1)S(1)} %collective-permute-done.refs_0_), channel_id=1, source_target_pairs={{0,3},{1,0},{2,1},{3,2},{4,7},{5,4},{6,5},{7,6},{8,11},{9,8},{10,9... | collective-permute-start | bytes 393224 | tf_op jit(solution)/shard_map/ppermute | solution.py:268
  12.9 0.0 copy-done.1
  12.9 0.0 copy-done.2
  12.9 0.0 copy-done.3
  12.9 0.0 copy-done.4
  12.9 0.0 copy-done.5
  12.9 0.0 copy-done.6
  12.9 0.0 copy-done.7
  12.9 1.6 %own_blocks.1 = (bf16[64,32,256]{2,1,0:T(8,128)(2,1)S(1)}, f32[64,32,256]{2,1,0:T(8,128)S(1)}) custom-call(bf16[128,32,256]{2,1,0:T(8,128)(2,1)S(1)} %copy-done.1, f32[32]{0:T(128)S(1)} %copy-done.4, s32[32]{0:T(128)S(1)} %copy-done.5, s32[1,128]{1,0:T(1,128)S(1)} %bitcast.3, s32[1,128]{1,0:T(1,128)S(1)} %bitcast.5, bf16[128,256]{1,0:T(8,128)(2,1)S(1)} %copy-done.3, ...), custom_call_target="tpu_custom_call" | custom-call | flops 4000000000 | bytes 8388608 | tf_op jit(solution)/shard_map/own_blocks/pallas_call | solution.py:245
  14.5 0.0 collective-permute-done.2.refs_4_
  14.5 0.6 %collective-permute-done.3.refs_2_ = bf16[80,256]{1,0:T(8,128)(2,1)S(1)} collective-permute-done((bf16[80,256]{1,0:T(8,128)(2,1)}, bf16[80,256]{1,0:T(8,128)(2,1)S(1)}, u32[]{:S(2)}, u32[]{:S(2)}) %collective-permute-start.3) | collective-permute-done | bytes 40992 | tf_op jit(solution)/shard_map/ppermute | solution.py:239
  15.1 0.0 collective-permute-done.4.refs_1_
  15.1 0.0 collective-permute-start.5
  15.1 0.5 %collective-permute-start.6 = (bf16[80,256]{1,0:T(8,128)(2,1)S(1)}, bf16[80,256]{1,0:T(8,128)(2,1)S(1)}, u32[]{:S(2)}, u32[]{:S(2)}) collective-permute-start(bf16[80,256]{1,0:T(8,128)(2,1)S(1)} %collective-permute-done.2.refs_4_), channel_id=1, source_target_pairs={{0,1},{1,0},{2,3},{3,2},{4,5},{5,4},{6,7},{7,6},{8,9},{9,8},{10,11... | collective-permute-start | bytes 122888 | tf_op jit(solution)/shard_map/ppermute | solution.py:272
  15.6 0.0 collective-permute-done.9.refs_2_
  15.6 0.0 collective-permute-start.10
  15.6 0.0 collective-permute-done.7.refs_0_
  15.6 0.5 %collective-permute-start.8 = (bf16[1,256,256]{2,1,0:T(8,128)(2,1)S(1)}, bf16[1,256,256]{2,1,0:T(8,128)(2,1)S(1)}, u32[]{:S(2)}, u32[]{:S(2)}) collective-permute-start(bf16[1,256,256]{2,1,0:T(8,128)(2,1)S(1)} %collective-permute-done.7.refs_0_), channel_id=1, source_target_pairs={{0,1},{1,0},{2,3},{3,2},{4,5},{5,4},{6,7},{7,6},{8,9},{9,8},{10,11... | collective-permute-start | bytes 393224 | tf_op jit(solution)/shard_map/ppermute | solution.py:269
  16.1 0.2 collective-permute-done.5.refs_3_
  16.3 0.2 collective-permute-done.6.refs_5_
  16.5 0.0 copy-start
  16.5 1.2 %stage.1.sum_ref = f32[64,32,256]{2,1,0:T(8,128)S(1)} custom-call(bf16[64,32,256]{2,1,0:T(8,128)(2,1)S(1)} %get-tuple-element.20.pumped_ref, f32[64,32,256]{2,1,0:T(8,128)S(1)} %get-tuple-element.25.sum_ref, bf16[1,256,256]{2,1,0:T(8,128)(2,1)S(1)} %collective-permute-done.refs_0_, ...), custom_call_target="tpu_custom_call", output_to_operand_aliasing={{}: (1, {})} | custom-call | flops 4000000000 | bytes 8388608 | tf_op jit(solution)/shard_map/stage/pallas_call | solution.py:283
  17.7 0.0 collective-permute-done.10.refs_3_
  17.7 0.0 collective-permute-done.8.refs_1_
  17.7 0.0 copy-done
  17.7 1.9 %last_stage.1 = f32[64,32,256]{2,1,0:T(8,128)} custom-call(bf16[64,32,256]{2,1,0:T(8,128)(2,1)S(1)} %get-tuple-element.20.pumped_ref, f32[64,32,256]{2,1,0:T(8,128)S(1)} %stage.1.sum_ref, bf16[256,256]{1,0:T(8,128)(2,1)S(1)} %copy-done, bf16[1,256,256]{2,1,0:T(8,128)(2,1)S(1)} %collective-permute-done.7.refs_0_, ...), custom_call_target="tpu_custom_call" | custom-call | tf_op jit(solution)/shard_map/last_stage/pallas_call | solution.py:300
Async XLA Ops:
  0.0 11.2 %collective-permute-start = (bf16[1,256,256]{2,1,0:T(8,128)(2,1)}, bf16[1,256,256]{2,1,0:T(8,128)(2,1)S(1)}, u32[]{:S(2)}, u32[]{:S(2)}) collective-permute-start(bf16[1,256,256]{2,1,0:T(8,128)(2,1)} %basis_ref.1), channel_id=1, source_target_pairs={{0,8},{1,5},{2,14},{3,7},{4,12},{5,1},{6,10},{7,3},{8,0},{9,13},{1... | collective-permute-start | bytes 393224 | tf_op jit(solution)/shard_map/ppermute | solution.py:219
  4.7 8.2 %copy-start.1 = (bf16[128,32,256]{2,1,0:T(8,128)(2,1)S(1)}, bf16[128,32,256]{2,1,0:T(8,128)(2,1)}, u32[]{:S(2)}) copy-start(bf16[128,32,256]{2,1,0:T(8,128)(2,1)} %mortar_ref.1) | copy-start | bytes 6291460
  4.7 8.2 %copy-start.2 = (bf16[1,256,256]{2,1,0:T(8,128)(2,1)S(1)}, bf16[1,256,256]{2,1,0:T(8,128)(2,1)}, u32[]{:S(2)}) copy-start(bf16[1,256,256]{2,1,0:T(8,128)(2,1)} %basis_ref.1) | copy-start | bytes 393220
  4.7 8.2 %copy-start.3 = (bf16[128,256]{1,0:T(8,128)(2,1)S(1)}, bf16[128,256]{1,0:T(8,128)(2,1)}, u32[]{:S(2)}) copy-start(bf16[128,256]{1,0:T(8,128)(2,1)} %scale_ref.3) | copy-start | bytes 196612
  4.7 8.2 %copy-start.4 = (f32[32]{0:T(128)S(1)}, f32[32]{0:T(128)}, u32[]{:S(2)}) copy-start(f32[32]{0:T(128)} %rate_ref.1) | copy-start | bytes 388
  4.7 8.2 %copy-start.5 = (s32[32]{0:T(128)S(1)}, s32[32]{0:T(128)}, u32[]{:S(2)}) copy-start(s32[32]{0:T(128)} %cell_ref.1) | copy-start | bytes 388
  4.7 8.2 %copy-start.6 = (s32[128,1]{0,1:T(1,128)S(1)}, s32[128,1]{0,1:T(1,128)}, u32[]{:S(2)}) copy-start(s32[128,1]{0,1:T(1,128)} %param.12) | copy-start | bytes 1540
  4.7 8.2 %copy-start.7 = (s32[128]{0:T(128)S(1)}, s32[128]{0:T(128)}, u32[]{:S(2)}) copy-start(s32[128]{0:T(128)} %param.13) | copy-start | bytes 1540
  6.8 4.4 %collective-permute-start.1 = (bf16[80,256]{1,0:T(8,128)(2,1)}, bf16[80,256]{1,0:T(8,128)(2,1)S(1)}, u32[]{:S(2)}, u32[]{:S(2)}) collective-permute-start(bf16[80,256]{1,0:T(8,128)(2,1)} %get-tuple-element.18), channel_id=1, source_target_pairs={{0,1},{1,0},{2,3},{3,2},{4,5},{5,4},{6,7},{7,6},{8,9},{9,8},{10,11... | collective-permute-start | bytes 122888 | tf_op jit(solution)/shard_map/ppermute | solution.py:242
  6.8 7.8 %collective-permute-start.2 = (bf16[80,256]{1,0:T(8,128)(2,1)}, bf16[80,256]{1,0:T(8,128)(2,1)S(1)}, u32[]{:S(2)}, u32[]{:S(2)}) collective-permute-start(bf16[80,256]{1,0:T(8,128)(2,1)} %get-tuple-element.21), channel_id=1, source_target_pairs={{0,4},{2,6},{4,0},{6,2},{8,12},{10,14},{12,8},{14,10},{1,5},{3,7},... | collective-permute-start | bytes 122888 | tf_op jit(solution)/shard_map/ppermute | solution.py:239
  8.3 6.8 %collective-permute-start.3 = (bf16[80,256]{1,0:T(8,128)(2,1)}, bf16[80,256]{1,0:T(8,128)(2,1)S(1)}, u32[]{:S(2)}, u32[]{:S(2)}) collective-permute-start(bf16[80,256]{1,0:T(8,128)(2,1)} %get-tuple-element.22), channel_id=1, source_target_pairs={{0,8},{2,14},{4,12},{6,10},{8,0},{10,6},{12,4},{14,2},{1,9},{3,15}... | collective-permute-start | bytes 122888 | tf_op jit(solution)/shard_map/ppermute | solution.py:239
  8.7 6.9 %collective-permute-start.9 = (bf16[80,256]{1,0:T(8,128)(2,1)}, bf16[80,256]{1,0:T(8,128)(2,1)S(1)}, u32[]{:S(2)}, u32[]{:S(2)}) collective-permute-start(bf16[80,256]{1,0:T(8,128)(2,1)} %get-tuple-element.30), channel_id=1, source_target_pairs={{0,12},{2,10},{4,8},{6,14},{8,4},{10,2},{12,0},{14,6},{1,13},{3,11... | collective-permute-start | bytes 122888 | tf_op jit(solution)/shard_map/ppermute | solution.py:239
  11.2 3.9 %collective-permute-start.4 = (bf16[1,256,256]{2,1,0:T(8,128)(2,1)S(1)}, bf16[1,256,256]{2,1,0:T(8,128)(2,1)S(1)}, u32[]{:S(2)}, u32[]{:S(2)}) collective-permute-start(bf16[1,256,256]{2,1,0:T(8,128)(2,1)S(1)} %collective-permute-done.refs_0_), channel_id=1, source_target_pairs={{0,1},{1,0},{2,3},{3,2},{4,5},{5,4},{6,7},{7,6},{8,9},{9,8},{10,11... | collective-permute-start | bytes 393224 | tf_op jit(solution)/shard_map/ppermute | solution.py:266
  11.2 4.5 %collective-permute-start.7 = (bf16[1,256,256]{2,1,0:T(8,128)(2,1)S(1)}, bf16[1,256,256]{2,1,0:T(8,128)(2,1)S(1)}, u32[]{:S(2)}, u32[]{:S(2)}) collective-permute-start(bf16[1,256,256]{2,1,0:T(8,128)(2,1)S(1)} %collective-permute-done.refs_0_), channel_id=1, source_target_pairs={{0,3},{1,0},{2,1},{3,2},{4,7},{5,4},{6,5},{7,6},{8,11},{9,8},{10,9... | collective-permute-start | bytes 393224 | tf_op jit(solution)/shard_map/ppermute | solution.py:268
  15.1 1.2 %collective-permute-start.5 = (bf16[80,256]{1,0:T(8,128)(2,1)S(1)}, bf16[80,256]{1,0:T(8,128)(2,1)S(1)}, u32[]{:S(2)}, u32[]{:S(2)}) collective-permute-start(bf16[80,256]{1,0:T(8,128)(2,1)S(1)} %collective-permute-done.3.refs_2_), channel_id=1, source_target_pairs={{0,1},{1,0},{2,3},{3,2},{4,5},{5,4},{6,7},{7,6},{8,9},{9,8},{10,11... | collective-permute-start | bytes 122888 | tf_op jit(solution)/shard_map/ppermute | solution.py:272
  15.1 1.4 %collective-permute-start.6 = (bf16[80,256]{1,0:T(8,128)(2,1)S(1)}, bf16[80,256]{1,0:T(8,128)(2,1)S(1)}, u32[]{:S(2)}, u32[]{:S(2)}) collective-permute-start(bf16[80,256]{1,0:T(8,128)(2,1)S(1)} %collective-permute-done.2.refs_4_), channel_id=1, source_target_pairs={{0,1},{1,0},{2,3},{3,2},{4,5},{5,4},{6,7},{7,6},{8,9},{9,8},{10,11... | collective-permute-start | bytes 122888 | tf_op jit(solution)/shard_map/ppermute | solution.py:272
  15.6 2.1 %collective-permute-start.10 = (bf16[80,256]{1,0:T(8,128)(2,1)S(1)}, bf16[80,256]{1,0:T(8,128)(2,1)S(1)}, u32[]{:S(2)}, u32[]{:S(2)}) collective-permute-start(bf16[80,256]{1,0:T(8,128)(2,1)S(1)} %collective-permute-done.9.refs_2_), channel_id=1, source_target_pairs={{0,1},{1,0},{2,3},{3,2},{4,5},{5,4},{6,7},{7,6},{8,9},{9,8},{10,11... | collective-permute-start | bytes 122888 | tf_op jit(solution)/shard_map/ppermute | solution.py:272
  15.6 2.1 %collective-permute-start.8 = (bf16[1,256,256]{2,1,0:T(8,128)(2,1)S(1)}, bf16[1,256,256]{2,1,0:T(8,128)(2,1)S(1)}, u32[]{:S(2)}, u32[]{:S(2)}) collective-permute-start(bf16[1,256,256]{2,1,0:T(8,128)(2,1)S(1)} %collective-permute-done.7.refs_0_), channel_id=1, source_target_pairs={{0,1},{1,0},{2,3},{3,2},{4,5},{5,4},{6,7},{7,6},{8,9},{9,8},{10,11... | collective-permute-start | bytes 393224 | tf_op jit(solution)/shard_map/ppermute | solution.py:269
  16.5 1.2 %copy-start = (bf16[256,256]{1,0:T(8,128)(2,1)S(1)}, bf16[256,256]{1,0:T(8,128)(2,1)}, u32[]{:S(2)}) copy-start(bf16[256,256]{1,0:T(8,128)(2,1)} %projection_ref.1) | copy-start | bytes 393220

commit v10 on v9

--- a/solution.py
+++ b/solution.py
@@ -8,6 +8,7 @@
 from jax.sharding import PartitionSpec as P
 
 ROW_TILE = 16
+SLOT_ROWS = 8
 VMEM = pl.BlockSpec(memory_space=pltpu.VMEM)
 HBM = pl.BlockSpec(memory_space=pltpu.HBM)
 SMEM = pl.BlockSpec(memory_space=pltpu.SMEM)
@@ -24,7 +25,7 @@
 
 def pack_kernel(partners, owner_ref, slot_ref, scale_ref, section_ref, *packs):
     rows, dof_count = packs[0].shape
-    rows -= ROW_TILE
+    rows -= SLOT_ROWS
     faces = owner_ref.shape[1]
     sign = (1 - 2 * section_ref[0]).astype(jnp.float32)
     here = lax.axis_index("sub")
@@ -52,7 +53,7 @@
         meta = jnp.concatenate(
             [listed[:, p * rows : (p + 1) * rows], jnp.zeros((1, dof_count - rows), jnp.float32)], axis=1
         )
-        pack_ref[rows:, :] = jnp.broadcast_to(meta, (ROW_TILE, dof_count)).astype(jnp.bfloat16)
+        pack_ref[rows:, :] = jnp.broadcast_to(meta, (SLOT_ROWS, dof_count)).astype(jnp.bfloat16)
 
 
 def block_weights(packs, rows, blocks_own):
@@ -60,7 +61,7 @@
     block_ids = first + lax.broadcasted_iota(jnp.int32, (blocks_own, rows), 0)
     total = None
     for pack in packs:
-        slots = pack[rows : rows + ROW_TILE, :].astype(jnp.int32)[:1, :rows]
+        slots = pack[rows : rows + SLOT_ROWS, :].astype(jnp.int32)[:1, :rows]
         hit = (slots == block_ids).astype(jnp.bfloat16)
         part = jnp.dot(hit, pack[:rows, :], preferred_element_type=jnp.float32)
         total = part if total is None else total + part
@@ -89,13 +90,14 @@
     block_ids = first_block + lax.broadcasted_iota(jnp.int32, (blocks_own, faces), 0)
     hit = (slot_ref[...] == block_ids) & (owner_ref[...] == here)
     weight = jnp.dot(hit.astype(jnp.bfloat16), scale_ref[...], preferred_element_type=jnp.float32) * sign
-    weight_ref[...] = weight + block_weights((swapped_ref,), swapped_ref.shape[0] - ROW_TILE, blocks_own)
+    weight_ref[...] = weight + block_weights((swapped_ref,), swapped_ref.shape[0] - SLOT_ROWS, blocks_own)
     pumped_ref[...] = mortar_ref[pl.ds(first_block, blocks_own)]
 
     base = here * mortar_ref.shape[0] + first_block
+    bits = dof_count.bit_length() - 1
     for column in range(columns):
-        block = lax.div(cell_ref[column], dof_count) - base
-        dof = lax.rem(cell_ref[column], dof_count)
+        block = (cell_ref[column] >> bits) - base
+        dof = cell_ref[column] & (dof_count - 1)
 
         @pl.when((block >= 0) & (block < blocks_own))
         def _():
@@ -124,7 +126,7 @@
     packs, (out_ref, weight_ref, basis_ref, scaled_ref) = refs[:-4], refs[-4:]
     blocks_own, columns, dof_count = pumped_ref.shape
     face_id = lax.axis_index("face")
-    rows = packs[0].shape[0] - ROW_TILE
+    rows = packs[0].shape[0] - SLOT_ROWS
     count = weight_ref.shape[0]
     for spot in range(count):
         weight_ref[spot] = block_weights(packs[2 * spot : 2 * spot + 2], rows, blocks_own)
@@ -159,7 +161,7 @@
     count = weight_ref.shape[0]
     for at in range(count):
         basis, basis_swapped, pack, pack_swapped = arrays[4 * at : 4 * at + 4]
-        weight_ref[at] = block_weights((pack, pack_swapped), pack.shape[0] - ROW_TILE, blocks_own)
+        weight_ref[at] = block_weights((pack, pack_swapped), pack.shape[0] - SLOT_ROWS, blocks_own)
         for core, array in ((1, basis), (0, basis_swapped)):
 
             @pl.when(lax.axis_index("face") == core)
@@ -198,7 +200,7 @@
     others = subdomains - 1
     blocks_own = blocks_dev // halves
     capacity = max(2, 2 * faces_dev // subdomains)
-    pack_rows = -(-capacity // ROW_TILE) * ROW_TILE + ROW_TILE
+    pack_rows = -(-capacity // ROW_TILE) * ROW_TILE + SLOT_ROWS
     block_shape = (blocks_own, cols_dev, dof_count)
     swap = [(i, i ^ 1) for i in range(halves)]
 
@@ -238,7 +240,8 @@
         ]
         return lax.ppermute(pack, ("sub", "rhs"), pairs)
 
-    arrived = [along_sub(way, pack) for way, pack in zip(ways[1:], packs[1:])]
+    soon = len(near) + len(far)
+    arrived = [along_sub(way, pack) for way, pack in zip(ways[1 : 1 + soon], packs[1:])]
     own_swapped = lax.ppermute(packs[0], "face", swap)
 
     firsts, own_swapped = lax.optimization_barrier((firsts, own_swapped))
@@ -267,8 +270,10 @@
         if has_far:
             second = lax.ppermute(first, ("rhs", "face"), pairs)
             late.append([second, lax.ppermute(second, "face", swap)])
-    soon = len(near) + len(far)
-    arrived[:soon], own_sum, early = lax.optimization_barrier((arrived[:soon], own_sum, early))
+    late_packs, own_sum = lax.optimization_barrier((packs[1 + soon :], own_sum))
+    late_arrived = [along_sub(way, pack) for way, pack in zip(ways[1 + soon :], late_packs)]
+    arrived, own_sum, early = lax.optimization_barrier((arrived, own_sum, early))
+    arrived += late_arrived
     swapped = [lax.ppermute(array, "face", swap) for array in arrived]
     places = dict(zip(ways[1:], zip(arrived, swapped)))
     weights = []

time: 19.7 us -> 22.1 us (1.12)
  waiting for transfers between devices: 0.94 us -> 2.45 us
  starting transfers between devices: 11.2 us -> 12.1 us
    ppermute x3, waiting for transfers between devices: 0.57 us -> 2.43 us  [along_sub(): return lax.ppermute(pack, ('sub', 'rhs'), pairs)]
    ppermute x1, starting transfers between devices: 1.71 us -> 2.28 us  [on_device(): second = lax.ppermute(first, ('rhs', 'face'), pairs)]
    ppermute x3, waiting for transfers between devices: 0.35 us -> 0.01 us  [on_device(): swapped = [lax.ppermute(array, 'face', swap) for array in arrived]]
    ppermute x3, starting transfers between devices: 4.39 us -> 4.72 us  [along_sub(): return lax.ppermute(pack, ('sub', 'rhs'), pairs)]
  transfers between devices with their start and end apart: 11 -> 11, of which waited for: 3 -> 1; matrix products, arithmetic and copies ran while one was open for 0% -> 0% of each run, Pallas kernels for 24% -> 21%
where the time goes in v10:
time: 22.1 us; the launch traced here: 22 us
  starting transfers between devices  12.1 us (55%)
  Pallas kernels  6.58 us (30%)
  waiting for transfers between devices  2.45 us (11%)
  between operations  0.81 us (4%)
    ppermute x3, starting transfers between devices, along_sub(): return lax.ppermute(pack, ('sub', 'rhs'), pairs)  4.72 us
    ppermute x1, starting transfers between devices, on_device(): firsts.append(lax.ppermute(basis, ('sub', 'rhs', 'face'), pairs))  4.04 us
    ppermute x3, waiting for transfers between devices, along_sub(): return lax.ppermute(pack, ('sub', 'rhs'), pairs)  2.43 us
    ppermute x1, starting transfers between devices, on_device(): second = lax.ppermute(first, ('rhs', 'face'), pairs)  2.28 us
    pallas_call x1, Pallas kernels, on_device(): pl.pallas_call(functools.partial(pack_kernel, ways), out_shape=[jax.Shape...  2 us
    pallas_call x1, Pallas kernels, on_device(): pl.pallas_call(last_kernel, out_shape=jax.ShapeDtypeStruct(block_shape, j...  1.88 us
    pallas_call x1, Pallas kernels, on_device(): pl.pallas_call(own_kernel, out_shape=[jax.ShapeDtypeStruct(block_shape, j...  1.52 us
    pallas_call x1, Pallas kernels, on_device(): pl.pallas_call(functools.partial(stage_kernel, kinds), out_shape=jax.Shap...  1.18 us
  transfers between devices with their start and end apart: 11, of which 1 were waited for; matrix products, arithmetic and copies ran while one was open for 0% of the time, Pallas kernels for 21%

profile of v10, /device:TPU:0, one launch (start us, length us, event | category | flops | bytes accessed | tf_op | source)
XLA Modules:
  0.0 22.0 jit_solution(10987707802197209622)
XLA Ops:
  0.0 4.0 %collective-permute-start = (bf16[1,256,256]{2,1,0:T(8,128)(2,1)}, bf16[1,256,256]{2,1,0:T(8,128)(2,1)S(1)}, u32[]{:S(2)}, u32[]{:S(2)}) collective-permute-start(bf16[1,256,256]{2,1,0:T(8,128)(2,1)} %basis_ref.1), channel_id=1, source_target_pairs={{0,8},{1,5},{2,14},{3,7},{4,12},{5,1},{6,10},{7,3},{8,0},{9,13},{1... | collective-permute-start | bytes 393224 | tf_op jit(solution)/shard_map/ppermute | solution.py:221
  4.7 0.0 copy-start.1
  4.7 0.0 copy-start.2
  4.7 0.0 copy-start.3
  4.7 0.0 copy-start.4
  4.7 0.0 copy-start.5
  4.7 0.0 copy-start.6
  4.7 0.0 copy-start.7
  4.8 2.0 %pack_weights.1 = (bf16[72,256]{1,0:T(8,128)(2,1)}, bf16[72,256]{1,0:T(8,128)(2,1)}, bf16[72,256]{1,0:T(8,128)(2,1)}, bf16[72,256]{1,0:T(8,128)(2,1)}) custom-call(s32[1,128]{1,0:T(1,128)} %bitcast.2, s32[1,128]{1,0:T(1,128)} %bitcast.4, bf16[128,256]{1,0:T(8,128)(2,1)} %scale_ref.3, s32[1]{0:T(128)S(6)} %copy.12.section_ref), custom_call_target="tpu_custom_call" | custom-call | flops 4000000000 | bytes 8388608 | tf_op jit(solution)/shard_map/pack_weights/pallas_call | solution.py:228
  6.8 0.0 collective-permute-start.1
  6.8 1.6 %collective-permute-start.2 = (bf16[72,256]{1,0:T(8,128)(2,1)}, bf16[72,256]{1,0:T(8,128)(2,1)S(1)}, u32[]{:S(2)}, u32[]{:S(2)}) collective-permute-start(bf16[72,256]{1,0:T(8,128)(2,1)} %get-tuple-element.23), channel_id=1, source_target_pairs={{0,4},{2,6},{4,0},{6,2},{8,12},{10,14},{12,8},{14,10},{1,5},{3,7},... | collective-permute-start | bytes 110600 | tf_op jit(solution)/shard_map/ppermute | solution.py:241
  8.3 0.0 copy-start.8
  8.3 0.3 %collective-permute-start.3 = (bf16[72,256]{1,0:T(8,128)(2,1)}, bf16[72,256]{1,0:T(8,128)(2,1)S(1)}, u32[]{:S(2)}, u32[]{:S(2)}) collective-permute-start(bf16[72,256]{1,0:T(8,128)(2,1)} %get-tuple-element.24), channel_id=1, source_target_pairs={{0,8},{2,14},{4,12},{6,10},{8,0},{10,6},{12,4},{14,2},{1,9},{3,15}... | collective-permute-start | bytes 110600 | tf_op jit(solution)/shard_map/ppermute | solution.py:241
  8.7 0.0 collective-permute-done.1.swapped_ref
  8.7 0.0 collective-permute-done.refs_0_
  8.7 0.0 collective-permute-start.4
  8.7 2.3 %collective-permute-start.7 = (bf16[1,256,256]{2,1,0:T(8,128)(2,1)S(1)}, bf16[1,256,256]{2,1,0:T(8,128)(2,1)S(1)}, u32[]{:S(2)}, u32[]{:S(2)}) collective-permute-start(bf16[1,256,256]{2,1,0:T(8,128)(2,1)S(1)} %collective-permute-done.refs_0_), channel_id=1, source_target_pairs={{0,3},{1,0},{2,1},{3,2},{4,7},{5,4},{6,5},{7,6},{8,11},{9,8},{10,9... | collective-permute-start | bytes 393224 | tf_op jit(solution)/shard_map/ppermute | solution.py:271
  11.0 0.0 copy-done.1
  11.0 0.0 copy-done.2
  11.0 0.0 copy-done.3
  11.0 0.0 copy-done.4
  11.0 0.0 copy-done.5
  11.0 0.0 copy-done.6
  11.0 0.0 copy-done.7
  11.0 1.5 %own_blocks.1 = (bf16[64,32,256]{2,1,0:T(8,128)(2,1)S(1)}, f32[64,32,256]{2,1,0:T(8,128)S(1)}) custom-call(bf16[128,32,256]{2,1,0:T(8,128)(2,1)S(1)} %copy-done.1, f32[32]{0:T(128)S(1)} %copy-done.4, s32[32]{0:T(128)S(1)} %copy-done.5, s32[1,128]{1,0:T(1,128)S(1)} %bitcast.3, s32[1,128]{1,0:T(1,128)S(1)} %bitcast.5, bf16[128,256]{1,0:T(8,128)(2,1)S(1)} %copy-done.3, ...), custom_call_target="tpu_custom_call" | custom-call | flops 4000000000 | bytes 8388608 | tf_op jit(solution)/shard_map/own_blocks/pallas_call | solution.py:248
  12.5 0.0 copy-done.8
  12.5 2.8 %collective-permute-start.9 = (bf16[72,256]{1,0:T(8,128)(2,1)S(1)}, bf16[72,256]{1,0:T(8,128)(2,1)S(1)}, u32[]{:S(2)}, u32[]{:S(2)}) collective-permute-start(bf16[72,256]{1,0:T(8,128)(2,1)S(1)} %copy-done.8), channel_id=1, source_target_pairs={{0,12},{2,10},{4,8},{6,14},{8,4},{10,2},{12,0},{14,6},{1,13},{3,11... | collective-permute-start | bytes 110600 | tf_op jit(solution)/shard_map/ppermute | solution.py:241
  15.4 0.0 collective-permute-done.2.refs_4_
  15.4 0.0 collective-permute-done.3.refs_2_
  15.4 0.0 collective-permute-done.4.refs_1_
  15.4 0.1 collective-permute-start.5
  15.4 0.5 %collective-permute-start.6 = (bf16[72,256]{1,0:T(8,128)(2,1)S(1)}, bf16[72,256]{1,0:T(8,128)(2,1)S(1)}, u32[]{:S(2)}, u32[]{:S(2)}) collective-permute-start(bf16[72,256]{1,0:T(8,128)(2,1)S(1)} %collective-permute-done.2.refs_4_), channel_id=1, source_target_pairs={{0,1},{1,0},{2,3},{3,2},{4,5},{5,4},{6,7},{7,6},{8,9},{9,8},{10,11... | collective-permute-start | bytes 110600 | tf_op jit(solution)/shard_map/ppermute | solution.py:277
  15.9 2.4 %collective-permute-done.9.refs_2_ = bf16[72,256]{1,0:T(8,128)(2,1)S(1)} collective-permute-done((bf16[72,256]{1,0:T(8,128)(2,1)S(1)}, bf16[72,256]{1,0:T(8,128)(2,1)S(1)}, u32[]{:S(2)}, u32[]{:S(2)}) %collective-permute-start.9) | collective-permute-done | bytes 36896 | tf_op jit(solution)/shard_map/ppermute | solution.py:241
  18.4 0.0 collective-permute-start.10
  18.4 0.0 collective-permute-done.7.refs_0_
  18.4 0.5 %collective-permute-start.8 = (bf16[1,256,256]{2,1,0:T(8,128)(2,1)S(1)}, bf16[1,256,256]{2,1,0:T(8,128)(2,1)S(1)}, u32[]{:S(2)}, u32[]{:S(2)}) collective-permute-start(bf16[1,256,256]{2,1,0:T(8,128)(2,1)S(1)} %collective-permute-done.7.refs_0_), channel_id=1, source_target_pairs={{0,1},{1,0},{2,3},{3,2},{4,5},{5,4},{6,7},{7,6},{8,9},{9,8},{10,11... | collective-permute-start | bytes 393224 | tf_op jit(solution)/shard_map/ppermute | solution.py:272
  18.9 0.0 collective-permute-done.5.refs_3_
  18.9 0.0 collective-permute-done.6.refs_5_
  18.9 0.0 copy-start
  18.9 1.2 %stage.1.sum_ref = f32[64,32,256]{2,1,0:T(8,128)S(1)} custom-call(bf16[64,32,256]{2,1,0:T(8,128)(2,1)S(1)} %get-tuple-element.22.pumped_ref, f32[64,32,256]{2,1,0:T(8,128)S(1)} %get-tuple-element.29.sum_ref, bf16[1,256,256]{2,1,0:T(8,128)(2,1)S(1)} %collective-permute-done.refs_0_, ...), custom_call_target="tpu_custom_call", output_to_operand_aliasing={{}: (1, {})} | custom-call | flops 4000000000 | bytes 8388608 | tf_op jit(solution)/shard_map/stage/pallas_call | solution.py:288
  20.1 0.0 collective-permute-done.10.refs_3_
  20.1 0.0 collective-permute-done.8.refs_1_
  20.1 0.0 copy-done
  20.1 1.9 %last_stage.1 = f32[64,32,256]{2,1,0:T(8,128)} custom-call(bf16[64,32,256]{2,1,0:T(8,128)(2,1)S(1)} %get-tuple-element.22.pumped_ref, f32[64,32,256]{2,1,0:T(8,128)S(1)} %stage.1.sum_ref, bf16[256,256]{1,0:T(8,128)(2,1)S(1)} %copy-done, bf16[1,256,256]{2,1,0:T(8,128)(2,1)S(1)} %collective-permute-done.7.refs_0_, ...), custom_call_target="tpu_custom_call" | custom-call | tf_op jit(solution)/shard_map/last_stage/pallas_call | solution.py:305
Async XLA Ops:
  0.0 8.7 %collective-permute-start = (bf16[1,256,256]{2,1,0:T(8,128)(2,1)}, bf16[1,256,256]{2,1,0:T(8,128)(2,1)S(1)}, u32[]{:S(2)}, u32[]{:S(2)}) collective-permute-start(bf16[1,256,256]{2,1,0:T(8,128)(2,1)} %basis_ref.1), channel_id=1, source_target_pairs={{0,8},{1,5},{2,14},{3,7},{4,12},{5,1},{6,10},{7,3},{8,0},{9,13},{1... | collective-permute-start | bytes 393224 | tf_op jit(solution)/shard_map/ppermute | solution.py:221
  4.7 6.3 %copy-start.1 = (bf16[128,32,256]{2,1,0:T(8,128)(2,1)S(1)}, bf16[128,32,256]{2,1,0:T(8,128)(2,1)}, u32[]{:S(2)}) copy-start(bf16[128,32,256]{2,1,0:T(8,128)(2,1)} %mortar_ref.1) | copy-start | bytes 6291460
  4.7 6.3 %copy-start.2 = (bf16[1,256,256]{2,1,0:T(8,128)(2,1)S(1)}, bf16[1,256,256]{2,1,0:T(8,128)(2,1)}, u32[]{:S(2)}) copy-start(bf16[1,256,256]{2,1,0:T(8,128)(2,1)} %basis_ref.1) | copy-start | bytes 393220
  4.7 6.3 %copy-start.3 = (bf16[128,256]{1,0:T(8,128)(2,1)S(1)}, bf16[128,256]{1,0:T(8,128)(2,1)}, u32[]{:S(2)}) copy-start(bf16[128,256]{1,0:T(8,128)(2,1)} %scale_ref.3) | copy-start | bytes 196612
  4.7 6.3 %copy-start.4 = (f32[32]{0:T(128)S(1)}, f32[32]{0:T(128)}, u32[]{:S(2)}) copy-start(f32[32]{0:T(128)} %rate_ref.1) | copy-start | bytes 388
  4.7 6.3 %copy-start.5 = (s32[32]{0:T(128)S(1)}, s32[32]{0:T(128)}, u32[]{:S(2)}) copy-start(s32[32]{0:T(128)} %cell_ref.1) | copy-start | bytes 388
  4.7 6.3 %copy-start.6 = (s32[128,1]{0,1:T(1,128)S(1)}, s32[128,1]{0,1:T(1,128)}, u32[]{:S(2)}) copy-start(s32[128,1]{0,1:T(1,128)} %param.12) | copy-start | bytes 1540
  4.7 6.3 %copy-start.7 = (s32[128]{0:T(128)S(1)}, s32[128]{0:T(128)}, u32[]{:S(2)}) copy-start(s32[128]{0:T(128)} %param.13) | copy-start | bytes 1540
  6.8 1.9 %collective-permute-start.1 = (bf16[72,256]{1,0:T(8,128)(2,1)}, bf16[72,256]{1,0:T(8,128)(2,1)S(1)}, u32[]{:S(2)}, u32[]{:S(2)}) collective-permute-start(bf16[72,256]{1,0:T(8,128)(2,1)} %get-tuple-element.20), channel_id=1, source_target_pairs={{0,1},{1,0},{2,3},{3,2},{4,5},{5,4},{6,7},{7,6},{8,9},{9,8},{10,11... | collective-permute-start | bytes 110600 | tf_op jit(solution)/shard_map/ppermute | solution.py:245
  6.8 8.6 %collective-permute-start.2 = (bf16[72,256]{1,0:T(8,128)(2,1)}, bf16[72,256]{1,0:T(8,128)(2,1)S(1)}, u32[]{:S(2)}, u32[]{:S(2)}) collective-permute-start(bf16[72,256]{1,0:T(8,128)(2,1)} %get-tuple-element.23), channel_id=1, source_target_pairs={{0,4},{2,6},{4,0},{6,2},{8,12},{10,14},{12,8},{14,10},{1,5},{3,7},... | collective-permute-start | bytes 110600 | tf_op jit(solution)/shard_map/ppermute | solution.py:241
  8.3 4.2 %copy-start.8 = (bf16[72,256]{1,0:T(8,128)(2,1)S(1)}, bf16[72,256]{1,0:T(8,128)(2,1)}, u32[]{:S(2)}) copy-start(bf16[72,256]{1,0:T(8,128)(2,1)} %get-tuple-element.34) | copy-start | bytes 110596
  8.3 7.0 %collective-permute-start.3 = (bf16[72,256]{1,0:T(8,128)(2,1)}, bf16[72,256]{1,0:T(8,128)(2,1)S(1)}, u32[]{:S(2)}, u32[]{:S(2)}) collective-permute-start(bf16[72,256]{1,0:T(8,128)(2,1)} %get-tuple-element.24), channel_id=1, source_target_pairs={{0,8},{2,14},{4,12},{6,10},{8,0},{10,6},{12,4},{14,2},{1,9},{3,15}... | collective-permute-start | bytes 110600 | tf_op jit(solution)/shard_map/ppermute | solution.py:241
  8.7 6.7 %collective-permute-start.4 = (bf16[1,256,256]{2,1,0:T(8,128)(2,1)S(1)}, bf16[1,256,256]{2,1,0:T(8,128)(2,1)S(1)}, u32[]{:S(2)}, u32[]{:S(2)}) collective-permute-start(bf16[1,256,256]{2,1,0:T(8,128)(2,1)S(1)} %collective-permute-done.refs_0_), channel_id=1, source_target_pairs={{0,1},{1,0},{2,3},{3,2},{4,5},{5,4},{6,7},{7,6},{8,9},{9,8},{10,11... | collective-permute-start | bytes 393224 | tf_op jit(solution)/shard_map/ppermute | solution.py:269
  8.7 9.7 %collective-permute-start.7 = (bf16[1,256,256]{2,1,0:T(8,128)(2,1)S(1)}, bf16[1,256,256]{2,1,0:T(8,128)(2,1)S(1)}, u32[]{:S(2)}, u32[]{:S(2)}) collective-permute-start(bf16[1,256,256]{2,1,0:T(8,128)(2,1)S(1)} %collective-permute-done.refs_0_), channel_id=1, source_target_pairs={{0,3},{1,0},{2,1},{3,2},{4,7},{5,4},{6,5},{7,6},{8,11},{9,8},{10,9... | collective-permute-start | bytes 393224 | tf_op jit(solution)/shard_map/ppermute | solution.py:271
  12.5 5.8 %collective-permute-start.9 = (bf16[72,256]{1,0:T(8,128)(2,1)S(1)}, bf16[72,256]{1,0:T(8,128)(2,1)S(1)}, u32[]{:S(2)}, u32[]{:S(2)}) collective-permute-start(bf16[72,256]{1,0:T(8,128)(2,1)S(1)} %copy-done.8), channel_id=1, source_target_pairs={{0,12},{2,10},{4,8},{6,14},{8,4},{10,2},{12,0},{14,6},{1,13},{3,11... | collective-permute-start | bytes 110600 | tf_op jit(solution)/shard_map/ppermute | solution.py:241
  15.4 3.5 %collective-permute-start.5 = (bf16[72,256]{1,0:T(8,128)(2,1)S(1)}, bf16[72,256]{1,0:T(8,128)(2,1)S(1)}, u32[]{:S(2)}, u32[]{:S(2)}) collective-permute-start(bf16[72,256]{1,0:T(8,128)(2,1)S(1)} %collective-permute-done.3.refs_2_), channel_id=1, source_target_pairs={{0,1},{1,0},{2,3},{3,2},{4,5},{5,4},{6,7},{7,6},{8,9},{9,8},{10,11... | collective-permute-start | bytes 110600 | tf_op jit(solution)/shard_map/ppermute | solution.py:277
  15.4 3.4 %collective-permute-start.6 = (bf16[72,256]{1,0:T(8,128)(2,1)S(1)}, bf16[72,256]{1,0:T(8,128)(2,1)S(1)}, u32[]{:S(2)}, u32[]{:S(2)}) collective-permute-start(bf16[72,256]{1,0:T(8,128)(2,1)S(1)} %collective-permute-done.2.refs_4_), channel_id=1, source_target_pairs={{0,1},{1,0},{2,3},{3,2},{4,5},{5,4},{6,7},{7,6},{8,9},{9,8},{10,11... | collective-permute-start | bytes 110600 | tf_op jit(solution)/shard_map/ppermute | solution.py:277
  18.4 1.7 %collective-permute-start.10 = (bf16[72,256]{1,0:T(8,128)(2,1)S(1)}, bf16[72,256]{1,0:T(8,128)(2,1)S(1)}, u32[]{:S(2)}, u32[]{:S(2)}) collective-permute-start(bf16[72,256]{1,0:T(8,128)(2,1)S(1)} %collective-permute-done.9.refs_2_), channel_id=1, source_target_pairs={{0,1},{1,0},{2,3},{3,2},{4,5},{5,4},{6,7},{7,6},{8,9},{9,8},{10,11... | collective-permute-start | bytes 110600 | tf_op jit(solution)/shard_map/ppermute | solution.py:277
  18.4 1.7 %collective-permute-start.8 = (bf16[1,256,256]{2,1,0:T(8,128)(2,1)S(1)}, bf16[1,256,256]{2,1,0:T(8,128)(2,1)S(1)}, u32[]{:S(2)}, u32[]{:S(2)}) collective-permute-start(bf16[1,256,256]{2,1,0:T(8,128)(2,1)S(1)} %collective-permute-done.7.refs_0_), channel_id=1, source_target_pairs={{0,1},{1,0},{2,3},{3,2},{4,5},{5,4},{6,7},{7,6},{8,9},{9,8},{10,11... | collective-permute-start | bytes 393224 | tf_op jit(solution)/shard_map/ppermute | solution.py:272
  18.9 1.2 %copy-start = (bf16[256,256]{1,0:T(8,128)(2,1)S(1)}, bf16[256,256]{1,0:T(8,128)(2,1)}, u32[]{:S(2)}) copy-start(bf16[256,256]{1,0:T(8,128)(2,1)} %projection_ref.1) | copy-start | bytes 393220

commit v11 on v10

--- a/solution.py
+++ b/solution.py
@@ -91,30 +91,24 @@
     hit = (slot_ref[...] == block_ids) & (owner_ref[...] == here)
     weight = jnp.dot(hit.astype(jnp.bfloat16), scale_ref[...], preferred_element_type=jnp.float32) * sign
     weight_ref[...] = weight + block_weights((swapped_ref,), swapped_ref.shape[0] - SLOT_ROWS, blocks_own)
-    pumped_ref[...] = mortar_ref[pl.ds(first_block, blocks_own)]
-
-    base = here * mortar_ref.shape[0] + first_block
-    bits = dof_count.bit_length() - 1
-    for column in range(columns):
-        block = (cell_ref[column] >> bits) - base
-        dof = cell_ref[column] & (dof_count - 1)
-
-        @pl.when((block >= 0) & (block < blocks_own))
-        def _():
-            slab = slice(column // ROW_TILE * ROW_TILE, (column // ROW_TILE + 1) * ROW_TILE)
-            shape = (ROW_TILE, dof_count)
-            at_well = (lax.broadcasted_iota(jnp.int32, shape, 0) == column % ROW_TILE) & (
-                lax.broadcasted_iota(jnp.int32, shape, 1) == dof
-            )
-            well = jnp.where(at_well, rate_ref[column], 0.0)
-            pumped_ref[block, slab, :] = (pumped_ref[block, slab, :].astype(jnp.float32) + well).astype(
-                jnp.bfloat16
-            )
-
+
+    square = (columns, columns)
+    diagonal = lax.broadcasted_iota(jnp.int32, square, 0) == lax.broadcasted_iota(jnp.int32, square, 1)
+    cells = jnp.sum(jnp.where(diagonal, cell_ref[...], 0), axis=1, keepdims=True)
+    rates = jnp.sum(jnp.where(diagonal, rate_ref[...], 0.0), axis=1, keepdims=True)
+    base = (here * mortar_ref.shape[0] + first_block) * dof_count
+    offsets = cells - base - lax.broadcasted_iota(jnp.int32, (columns, dof_count), 1)
+    rates = jnp.broadcast_to(rates, (columns, dof_count))
     tile_blocks = blocks_own // TILES
     for tile in range(TILES):
         at = slice(tile * tile_blocks, (tile + 1) * tile_blocks)
-        scaled = (pumped_ref[at].astype(jnp.float32) * weight_ref[at][:, None, :]).astype(jnp.bfloat16)
+        values = mortar_ref[pl.ds(first_block + tile * tile_blocks, tile_blocks)].astype(jnp.float32)
+        wells = jnp.stack(
+            [jnp.where(offsets == block * dof_count, rates, 0.0) for block in range(at.start, at.stop)], axis=0
+        )
+        pumped = (values + wells).astype(jnp.bfloat16)
+        pumped_ref[at] = pumped
+        scaled = (pumped.astype(jnp.float32) * weight_ref[at][:, None, :]).astype(jnp.bfloat16)
         flux = jnp.dot(
             scaled.reshape(tile_blocks * columns, dof_count), basis_ref[0], preferred_element_type=jnp.float32
         )
@@ -223,7 +217,7 @@
     kinds = [(a != b, c != a or a == b) for a, b, c in groups]
     near = [(c, c) for (_, _, c), (_, has) in zip(groups, kinds) if has]
     far = [(a, b) for (a, b, _), (has, _) in zip(groups, kinds) if has]
-    ways = [(0, 0), *near, *far, *[(b, a) for a, b in far]]
+    ways = [(0, 0), *far, *[(b, a) for a, b in far], *near]
     faces = [face_owner.reshape(1, faces_dev), face_slot.reshape(1, faces_dev), face_scale]
     packs = pl.pallas_call(
         functools.partial(pack_kernel, ways),
@@ -240,8 +234,7 @@
         ]
         return lax.ppermute(pack, ("sub", "rhs"), pairs)
 
-    soon = len(near) + len(far)
-    arrived = [along_sub(way, pack) for way, pack in zip(ways[1 : 1 + soon], packs[1:])]
+    arrived = [along_sub(way, pack) for way, pack in zip(ways[1:], packs[1:])]
     own_swapped = lax.ppermute(packs[0], "face", swap)
 
     firsts, own_swapped = lax.optimization_barrier((firsts, own_swapped))
@@ -251,13 +244,21 @@
             jax.ShapeDtypeStruct(block_shape, jnp.bfloat16),
             jax.ShapeDtypeStruct(block_shape, jnp.float32),
         ],
-        in_specs=[VMEM, SMEM, SMEM, VMEM, VMEM, VMEM, SMEM, VMEM, VMEM],
+        in_specs=[VMEM] * 6 + [SMEM, VMEM, VMEM],
         out_specs=[VMEM, VMEM],
         scratch_shapes=[pltpu.VMEM((blocks_own, dof_count), jnp.float32)],
         compiler_params=pltpu.CompilerParams(vmem_limit_bytes=32 * MIB),
         cost_estimate=WORK,
         name="own_blocks",
-    )(mortar_in, pump_rate, well_cell, *faces, section, basis, own_swapped)
+    )(
+        mortar_in,
+        pump_rate.reshape(1, cols_dev),
+        well_cell.reshape(1, cols_dev),
+        *faces,
+        section,
+        basis,
+        own_swapped,
+    )
 
     pairs = [
         (r * halves + face, r * halves if face else (r ^ 1) * halves + 1)
@@ -270,10 +271,9 @@
         if has_far:
             second = lax.ppermute(first, ("rhs", "face"), pairs)
             late.append([second, lax.ppermute(second, "face", swap)])
-    late_packs, own_sum = lax.optimization_barrier((packs[1 + soon :], own_sum))
-    late_arrived = [along_sub(way, pack) for way, pack in zip(ways[1 + soon :], late_packs)]
-    arrived, own_sum, early = lax.optimization_barrier((arrived, own_sum, early))
-    arrived += late_arrived
+    count = len(far)
+    soon, own_sum, early = lax.optimization_barrier((arrived[:count] + arrived[2 * count :], own_sum, early))
+    arrived = soon[:count] + arrived[count : 2 * count] + soon[count:]
     swapped = [lax.ppermute(array, "face", swap) for array in arrived]
     places = dict(zip(ways[1:], zip(arrived, swapped)))
     weights = []

time: 22.1 us -> 19.8 us (0.90)
  waiting for transfers between devices: 2.45 us -> 1.03 us
  Pallas kernels: 6.58 us -> 5.84 us
    ppermute x3, waiting for transfers between devices: 2.43 us -> 0.01 us  [along_sub(): return lax.ppermute(pack, ('sub', 'rhs'), pairs)]
    ppermute x1, waiting for transfers between devices: 0.01 us -> 1 us  [on_device(): second = lax.ppermute(first, ('rhs', 'face'), pairs)]
    pallas_call x1, Pallas kernels: 1.52 us -> 0.78 us  [on_device(): pl.pallas_call(own_kernel, out_shape=[jax.ShapeDtypeStruct(block_shape, j...]
    ppermute x3, starting transfers between devices: 4.72 us -> 4.39 us  [along_sub(): return lax.ppermute(pack, ('sub', 'rhs'), pairs)]
    ppermute x1, starting transfers between devices: 2.28 us -> 2.61 us  [on_device(): second = lax.ppermute(first, ('rhs', 'face'), pairs)]
    ppermute x1, starting transfers between devices: 0.51 us -> 0.19 us  [on_device(): late.append([second, lax.ppermute(second, 'face', swap)])]
  transfers between devices with their start and end apart: 11 -> 11, of which waited for: 1 -> 1; matrix products, arithmetic and copies ran while one was open for 0% -> 0% of each run, Pallas kernels for 21% -> 20%
where the time goes in v11:
time: 19.8 us; the launch traced here: 19.6 us
  starting transfers between devices  11.9 us (60%)
  Pallas kernels  5.84 us (29%)
  waiting for transfers between devices  1.03 us (5%)
  between operations  0.82 us (4%)
    ppermute x3, starting transfers between devices, along_sub(): return lax.ppermute(pack, ('sub', 'rhs'), pairs)  4.39 us
    ppermute x1, starting transfers between devices, on_device(): firsts.append(lax.ppermute(basis, ('sub', 'rhs', 'face'), pairs))  4.04 us
    ppermute x1, starting transfers between devices, on_device(): second = lax.ppermute(first, ('rhs', 'face'), pairs)  2.61 us
    pallas_call x1, Pallas kernels, on_device(): pl.pallas_call(functools.partial(pack_kernel, ways), out_shape=[jax.Shape...  2 us
    pallas_call x1, Pallas kernels, on_device(): pl.pallas_call(last_kernel, out_shape=jax.ShapeDtypeStruct(block_shape, j...  1.88 us
    pallas_call x1, Pallas kernels, on_device(): pl.pallas_call(functools.partial(stage_kernel, kinds), out_shape=jax.Shap...  1.18 us
    ppermute x1, waiting for transfers between devices, on_device(): second = lax.ppermute(first, ('rhs', 'face'), pairs)  1 us
    pallas_call x1, Pallas kernels, on_device(): pl.pallas_call(own_kernel, out_shape=[jax.ShapeDtypeStruct(block_shape, j...  0.78 us
  transfers between devices with their start and end apart: 11, of which 1 were waited for; matrix products, arithmetic and copies ran while one was open for 0% of the time, Pallas kernels for 20%

profile of v11, /device:TPU:0, one launch (start us, length us, event | category | flops | bytes accessed | tf_op | source)
XLA Modules:
  0.0 19.6 jit_solution(9609343574699312851)
XLA Ops:
  0.0 4.0 %collective-permute-start = (bf16[1,256,256]{2,1,0:T(8,128)(2,1)}, bf16[1,256,256]{2,1,0:T(8,128)(2,1)S(1)}, u32[]{:S(2)}, u32[]{:S(2)}) collective-permute-start(bf16[1,256,256]{2,1,0:T(8,128)(2,1)} %basis_ref.1), channel_id=1, source_target_pairs={{0,8},{1,5},{2,14},{3,7},{4,12},{5,1},{6,10},{7,3},{8,0},{9,13},{1... | collective-permute-start | bytes 393224 | tf_op jit(solution)/shard_map/ppermute | solution.py:215
  4.7 0.0 copy-start.1
  4.7 0.0 copy-start.2
  4.7 0.0 copy-start.3
  4.7 0.0 copy-start.4
  4.7 0.0 copy-start.5
  4.7 0.0 copy-start.6
  4.7 0.0 copy-start.7
  4.8 2.0 %pack_weights.1 = (bf16[72,256]{1,0:T(8,128)(2,1)}, bf16[72,256]{1,0:T(8,128)(2,1)}, bf16[72,256]{1,0:T(8,128)(2,1)}, bf16[72,256]{1,0:T(8,128)(2,1)}) custom-call(s32[1,128]{1,0:T(1,128)} %bitcast.6, s32[1,128]{1,0:T(1,128)} %bitcast.8, bf16[128,256]{1,0:T(8,128)(2,1)} %scale_ref.3, s32[1]{0:T(128)S(6)} %copy.12.section_ref), custom_call_target="tpu_custom_call" | custom-call | flops 4000000000 | bytes 8388608 | tf_op jit(solution)/shard_map/pack_weights/pallas_call | solution.py:222
  6.8 0.0 collective-permute-start.1
  6.8 1.1 %collective-permute-start.2 = (bf16[72,256]{1,0:T(8,128)(2,1)}, bf16[72,256]{1,0:T(8,128)(2,1)S(1)}, u32[]{:S(2)}, u32[]{:S(2)}) collective-permute-start(bf16[72,256]{1,0:T(8,128)(2,1)} %get-tuple-element.21), channel_id=1, source_target_pairs={{0,8},{2,14},{4,12},{6,10},{8,0},{10,6},{12,4},{14,2},{1,9},{3,15}... | collective-permute-start | bytes 110600 | tf_op jit(solution)/shard_map/ppermute | solution.py:235
  7.9 0.8 %collective-permute-start.3 = (bf16[72,256]{1,0:T(8,128)(2,1)}, bf16[72,256]{1,0:T(8,128)(2,1)S(1)}, u32[]{:S(2)}, u32[]{:S(2)}) collective-permute-start(bf16[72,256]{1,0:T(8,128)(2,1)} %get-tuple-element.22), channel_id=1, source_target_pairs={{0,4},{2,6},{4,0},{6,2},{8,12},{10,14},{12,8},{14,10},{1,5},{3,7},... | collective-permute-start | bytes 110600 | tf_op jit(solution)/shard_map/ppermute | solution.py:235
  8.7 2.5 %collective-permute-start.9 = (bf16[72,256]{1,0:T(8,128)(2,1)}, bf16[72,256]{1,0:T(8,128)(2,1)S(1)}, u32[]{:S(2)}, u32[]{:S(2)}) collective-permute-start(bf16[72,256]{1,0:T(8,128)(2,1)} %get-tuple-element.30), channel_id=1, source_target_pairs={{0,12},{2,10},{4,8},{6,14},{8,4},{10,2},{12,0},{14,6},{1,13},{3,11... | collective-permute-start | bytes 110600 | tf_op jit(solution)/shard_map/ppermute | solution.py:235
  11.2 0.0 collective-permute-done.1.swapped_ref
  11.2 0.0 collective-permute-done.refs_0_
  11.2 0.0 collective-permute-start.4
  11.2 2.6 %collective-permute-start.7 = (bf16[1,256,256]{2,1,0:T(8,128)(2,1)S(1)}, bf16[1,256,256]{2,1,0:T(8,128)(2,1)S(1)}, u32[]{:S(2)}, u32[]{:S(2)}) collective-permute-start(bf16[1,256,256]{2,1,0:T(8,128)(2,1)S(1)} %collective-permute-done.refs_0_), channel_id=1, source_target_pairs={{0,3},{1,0},{2,1},{3,2},{4,7},{5,4},{6,5},{7,6},{8,11},{9,8},{10,9... | collective-permute-start | bytes 393224 | tf_op jit(solution)/shard_map/ppermute | solution.py:272
  13.8 0.0 copy-done.1
  13.8 0.0 copy-done.2
  13.8 0.0 copy-done.3
  13.8 0.0 copy-done.4
  13.8 0.0 copy-done.5
  13.8 0.0 copy-done.6
  13.8 0.0 copy-done.7
  13.8 0.8 %own_blocks.1 = (bf16[64,32,256]{2,1,0:T(8,128)(2,1)S(1)}, f32[64,32,256]{2,1,0:T(8,128)S(1)}) custom-call(bf16[128,32,256]{2,1,0:T(8,128)(2,1)S(1)} %copy-done.1, f32[1,32]{1,0:T(1,128)S(1)} %bitcast.4, s32[1,32]{1,0:T(1,128)S(1)} %bitcast.5, s32[1,128]{1,0:T(1,128)S(1)} %bitcast.7, s32[1,128]{1,0:T(1,128)S(1)} %bitcast.9, bf16[128,256]{1,0:T(8,128)(2,1)S(1)} %copy-done.3, ...), custom_call_target="tpu_custom_call" | custom-call | flops 4000000000 | bytes 8388608 | tf_op jit(solution)/shard_map/own_blocks/pallas_call | solution.py:241
  14.6 0.0 collective-permute-done.2.refs_2_
  14.6 0.0 collective-permute-done.3.refs_4_
  14.6 0.0 collective-permute-done.4.refs_1_
  14.6 0.1 collective-permute-start.5
  14.7 0.5 %collective-permute-start.6 = (bf16[72,256]{1,0:T(8,128)(2,1)S(1)}, bf16[72,256]{1,0:T(8,128)(2,1)S(1)}, u32[]{:S(2)}, u32[]{:S(2)}) collective-permute-start(bf16[72,256]{1,0:T(8,128)(2,1)S(1)} %collective-permute-done.3.refs_4_), channel_id=1, source_target_pairs={{0,1},{1,0},{2,3},{3,2},{4,5},{5,4},{6,7},{7,6},{8,9},{9,8},{10,11... | collective-permute-start | bytes 110600 | tf_op jit(solution)/shard_map/ppermute | solution.py:277
  15.2 0.0 collective-permute-done.9.refs_2_
  15.2 0.1 collective-permute-start.10
  15.3 1.0 %collective-permute-done.7.refs_0_ = bf16[1,256,256]{2,1,0:T(8,128)(2,1)S(1)} collective-permute-done((bf16[1,256,256]{2,1,0:T(8,128)(2,1)S(1)}, bf16[1,256,256]{2,1,0:T(8,128)(2,1)S(1)}, u32[]{:S(2)}, u32[]{:S(2)}) %collective-permute-start.7) | collective-permute-done | bytes 131104 | tf_op jit(solution)/shard_map/ppermute | solution.py:272
  16.3 0.2 collective-permute-start.8
  16.5 0.0 collective-permute-done.5.refs_3_
  16.5 0.0 collective-permute-done.6.refs_5_
  16.5 0.0 copy-start
  16.5 1.2 %stage.1.sum_ref = f32[64,32,256]{2,1,0:T(8,128)S(1)} custom-call(bf16[64,32,256]{2,1,0:T(8,128)(2,1)S(1)} %get-tuple-element.20.pumped_ref, f32[64,32,256]{2,1,0:T(8,128)S(1)} %get-tuple-element.25.sum_ref, bf16[1,256,256]{2,1,0:T(8,128)(2,1)S(1)} %collective-permute-done.refs_0_, ...), custom_call_target="tpu_custom_call", output_to_operand_aliasing={{}: (1, {})} | custom-call | flops 4000000000 | bytes 8388608 | tf_op jit(solution)/shard_map/stage/pallas_call | solution.py:288
  17.7 0.0 collective-permute-done.10.refs_3_
  17.7 0.0 collective-permute-done.8.refs_1_
  17.7 0.0 copy-done
  17.7 1.9 %last_stage.1 = f32[64,32,256]{2,1,0:T(8,128)} custom-call(bf16[64,32,256]{2,1,0:T(8,128)(2,1)S(1)} %get-tuple-element.20.pumped_ref, f32[64,32,256]{2,1,0:T(8,128)S(1)} %stage.1.sum_ref, bf16[256,256]{1,0:T(8,128)(2,1)S(1)} %copy-done, bf16[1,256,256]{2,1,0:T(8,128)(2,1)S(1)} %collective-permute-done.7.refs_0_, ...), custom_call_target="tpu_custom_call" | custom-call | tf_op jit(solution)/shard_map/last_stage/pallas_call | solution.py:305
Async XLA Ops:
  0.0 11.2 %collective-permute-start = (bf16[1,256,256]{2,1,0:T(8,128)(2,1)}, bf16[1,256,256]{2,1,0:T(8,128)(2,1)S(1)}, u32[]{:S(2)}, u32[]{:S(2)}) collective-permute-start(bf16[1,256,256]{2,1,0:T(8,128)(2,1)} %basis_ref.1), channel_id=1, source_target_pairs={{0,8},{1,5},{2,14},{3,7},{4,12},{5,1},{6,10},{7,3},{8,0},{9,13},{1... | collective-permute-start | bytes 393224 | tf_op jit(solution)/shard_map/ppermute | solution.py:215
  4.7 9.1 %copy-start.1 = (bf16[128,32,256]{2,1,0:T(8,128)(2,1)S(1)}, bf16[128,32,256]{2,1,0:T(8,128)(2,1)}, u32[]{:S(2)}) copy-start(bf16[128,32,256]{2,1,0:T(8,128)(2,1)} %mortar_ref.1) | copy-start | bytes 6291460
  4.7 9.1 %copy-start.2 = (bf16[1,256,256]{2,1,0:T(8,128)(2,1)S(1)}, bf16[1,256,256]{2,1,0:T(8,128)(2,1)}, u32[]{:S(2)}) copy-start(bf16[1,256,256]{2,1,0:T(8,128)(2,1)} %basis_ref.1) | copy-start | bytes 393220
  4.7 9.1 %copy-start.3 = (bf16[128,256]{1,0:T(8,128)(2,1)S(1)}, bf16[128,256]{1,0:T(8,128)(2,1)}, u32[]{:S(2)}) copy-start(bf16[128,256]{1,0:T(8,128)(2,1)} %scale_ref.3) | copy-start | bytes 196612
  4.7 9.1 %copy-start.4 = (f32[32]{0:T(128)S(1)}, f32[32]{0:T(128)}, u32[]{:S(2)}) copy-start(f32[32]{0:T(128)} %param.10) | copy-start | bytes 388
  4.7 9.1 %copy-start.5 = (s32[32]{0:T(128)S(1)}, s32[32]{0:T(128)}, u32[]{:S(2)}) copy-start(s32[32]{0:T(128)} %param.11) | copy-start | bytes 388
  4.7 9.1 %copy-start.6 = (s32[128,1]{0,1:T(1,128)S(1)}, s32[128,1]{0,1:T(1,128)}, u32[]{:S(2)}) copy-start(s32[128,1]{0,1:T(1,128)} %param.12) | copy-start | bytes 1540
  4.7 9.1 %copy-start.7 = (s32[128]{0:T(128)S(1)}, s32[128]{0:T(128)}, u32[]{:S(2)}) copy-start(s32[128]{0:T(128)} %param.13) | copy-start | bytes 1540
  6.8 4.4 %collective-permute-start.1 = (bf16[72,256]{1,0:T(8,128)(2,1)}, bf16[72,256]{1,0:T(8,128)(2,1)S(1)}, u32[]{:S(2)}, u32[]{:S(2)}) collective-permute-start(bf16[72,256]{1,0:T(8,128)(2,1)} %get-tuple-element.18), channel_id=1, source_target_pairs={{0,1},{1,0},{2,3},{3,2},{4,5},{5,4},{6,7},{7,6},{8,9},{9,8},{10,11... | collective-permute-start | bytes 110600 | tf_op jit(solution)/shard_map/ppermute | solution.py:238
  6.8 7.8 %collective-permute-start.2 = (bf16[72,256]{1,0:T(8,128)(2,1)}, bf16[72,256]{1,0:T(8,128)(2,1)S(1)}, u32[]{:S(2)}, u32[]{:S(2)}) collective-permute-start(bf16[72,256]{1,0:T(8,128)(2,1)} %get-tuple-element.21), channel_id=1, source_target_pairs={{0,8},{2,14},{4,12},{6,10},{8,0},{10,6},{12,4},{14,2},{1,9},{3,15}... | collective-permute-start | bytes 110600 | tf_op jit(solution)/shard_map/ppermute | solution.py:235
  7.9 6.7 %collective-permute-start.3 = (bf16[72,256]{1,0:T(8,128)(2,1)}, bf16[72,256]{1,0:T(8,128)(2,1)S(1)}, u32[]{:S(2)}, u32[]{:S(2)}) collective-permute-start(bf16[72,256]{1,0:T(8,128)(2,1)} %get-tuple-element.22), channel_id=1, source_target_pairs={{0,4},{2,6},{4,0},{6,2},{8,12},{10,14},{12,8},{14,10},{1,5},{3,7},... | collective-permute-start | bytes 110600 | tf_op jit(solution)/shard_map/ppermute | solution.py:235
  8.7 6.5 %collective-permute-start.9 = (bf16[72,256]{1,0:T(8,128)(2,1)}, bf16[72,256]{1,0:T(8,128)(2,1)S(1)}, u32[]{:S(2)}, u32[]{:S(2)}) collective-permute-start(bf16[72,256]{1,0:T(8,128)(2,1)} %get-tuple-element.30), channel_id=1, source_target_pairs={{0,12},{2,10},{4,8},{6,14},{8,4},{10,2},{12,0},{14,6},{1,13},{3,11... | collective-permute-start | bytes 110600 | tf_op jit(solution)/shard_map/ppermute | solution.py:235
  11.2 3.5 %collective-permute-start.4 = (bf16[1,256,256]{2,1,0:T(8,128)(2,1)S(1)}, bf16[1,256,256]{2,1,0:T(8,128)(2,1)S(1)}, u32[]{:S(2)}, u32[]{:S(2)}) collective-permute-start(bf16[1,256,256]{2,1,0:T(8,128)(2,1)S(1)} %collective-permute-done.refs_0_), channel_id=1, source_target_pairs={{0,1},{1,0},{2,3},{3,2},{4,5},{5,4},{6,7},{7,6},{8,9},{9,8},{10,11... | collective-permute-start | bytes 393224 | tf_op jit(solution)/shard_map/ppermute | solution.py:270
  11.2 5.1 %collective-permute-start.7 = (bf16[1,256,256]{2,1,0:T(8,128)(2,1)S(1)}, bf16[1,256,256]{2,1,0:T(8,128)(2,1)S(1)}, u32[]{:S(2)}, u32[]{:S(2)}) collective-permute-start(bf16[1,256,256]{2,1,0:T(8,128)(2,1)S(1)} %collective-permute-done.refs_0_), channel_id=1, source_target_pairs={{0,3},{1,0},{2,1},{3,2},{4,7},{5,4},{6,5},{7,6},{8,11},{9,8},{10,9... | collective-permute-start | bytes 393224 | tf_op jit(solution)/shard_map/ppermute | solution.py:272
  14.6 1.9 %collective-permute-start.5 = (bf16[72,256]{1,0:T(8,128)(2,1)S(1)}, bf16[72,256]{1,0:T(8,128)(2,1)S(1)}, u32[]{:S(2)}, u32[]{:S(2)}) collective-permute-start(bf16[72,256]{1,0:T(8,128)(2,1)S(1)} %collective-permute-done.2.refs_2_), channel_id=1, source_target_pairs={{0,1},{1,0},{2,3},{3,2},{4,5},{5,4},{6,7},{7,6},{8,9},{9,8},{10,11... | collective-permute-start | bytes 110600 | tf_op jit(solution)/shard_map/ppermute | solution.py:277
  14.7 1.8 %collective-permute-start.6 = (bf16[72,256]{1,0:T(8,128)(2,1)S(1)}, bf16[72,256]{1,0:T(8,128)(2,1)S(1)}, u32[]{:S(2)}, u32[]{:S(2)}) collective-permute-start(bf16[72,256]{1,0:T(8,128)(2,1)S(1)} %collective-permute-done.3.refs_4_), channel_id=1, source_target_pairs={{0,1},{1,0},{2,3},{3,2},{4,5},{5,4},{6,7},{7,6},{8,9},{9,8},{10,11... | collective-permute-start | bytes 110600 | tf_op jit(solution)/shard_map/ppermute | solution.py:277
  15.2 2.5 %collective-permute-start.10 = (bf16[72,256]{1,0:T(8,128)(2,1)S(1)}, bf16[72,256]{1,0:T(8,128)(2,1)S(1)}, u32[]{:S(2)}, u32[]{:S(2)}) collective-permute-start(bf16[72,256]{1,0:T(8,128)(2,1)S(1)} %collective-permute-done.9.refs_2_), channel_id=1, source_target_pairs={{0,1},{1,0},{2,3},{3,2},{4,5},{5,4},{6,7},{7,6},{8,9},{9,8},{10,11... | collective-permute-start | bytes 110600 | tf_op jit(solution)/shard_map/ppermute | solution.py:277
  16.3 1.4 %collective-permute-start.8 = (bf16[1,256,256]{2,1,0:T(8,128)(2,1)S(1)}, bf16[1,256,256]{2,1,0:T(8,128)(2,1)S(1)}, u32[]{:S(2)}, u32[]{:S(2)}) collective-permute-start(bf16[1,256,256]{2,1,0:T(8,128)(2,1)S(1)} %collective-permute-done.7.refs_0_), channel_id=1, source_target_pairs={{0,1},{1,0},{2,3},{3,2},{4,5},{5,4},{6,7},{7,6},{8,9},{9,8},{10,11... | collective-permute-start | bytes 393224 | tf_op jit(solution)/shard_map/ppermute | solution.py:273
  16.5 1.2 %copy-start = (bf16[256,256]{1,0:T(8,128)(2,1)S(1)}, bf16[256,256]{1,0:T(8,128)(2,1)}, u32[]{:S(2)}) copy-start(bf16[256,256]{1,0:T(8,128)(2,1)} %projection_ref.1) | copy-start | bytes 393220

commit v12 on v11

v12 whole, which is shorter than its diff:
```python
import functools

import jax
import jax.numpy as jnp
from jax import lax
from jax.experimental import pallas as pl
from jax.experimental.pallas import tpu as pltpu
from jax.sharding import PartitionSpec as P

ROW_TILE = 16
SLOT_ROWS = 8
VMEM = pl.BlockSpec(memory_space=pltpu.VMEM)
HBM = pl.BlockSpec(memory_space=pltpu.HBM)
SMEM = pl.BlockSpec(memory_space=pltpu.SMEM)
MIB = 1024 * 1024
TILES = 4
LAST_TILES = 8
LIGHT = pl.CostEstimate(flops=1_000_000, bytes_accessed=1024, transcendentals=0)
WORK = pl.CostEstimate(flops=4_000_000_000, bytes_accessed=8 * MIB, transcendentals=0)


def pack_kernel(partners, owner_ref, slot_ref, scale_ref, section_ref, *packs):
    rows, dof_count = packs[0].shape
    rows -= SLOT_ROWS
    faces = owner_ref.shape[1]
    sign = (1 - 2 * section_ref[0]).astype(jnp.float32)
    here = lax.axis_index("sub")
    owners = jnp.concatenate(
        [jnp.full((1, faces), here ^ partner, jnp.int32) for partner in partners], axis=0
    )
    named = owners == owner_ref[...]
    earlier = lax.broadcasted_iota(jnp.int32, (faces, faces), 0) < lax.broadcasted_iota(
        jnp.int32, (faces, faces), 1
    )
    rank = jnp.dot(
        named.astype(jnp.bfloat16), earlier.astype(jnp.bfloat16), preferred_element_type=jnp.float32
    )
    place = jnp.where(named, rank, -1.0)
    at = lax.broadcasted_iota(jnp.int32, (rows, faces), 0).astype(jnp.float32)
    hit = jnp.concatenate([place[p : p + 1, :] == at for p in range(len(packs))], axis=0)
    hit = hit.astype(jnp.bfloat16)
    packed = jnp.dot(hit, scale_ref[...], preferred_element_type=jnp.float32) * sign
    listed = lax.dot_general(
        slot_ref[...].astype(jnp.bfloat16), hit, (((1,), (1,)), ((), ())), preferred_element_type=jnp.float32
    )
    packed = packed.astype(jnp.bfloat16)
    for p, pack_ref in enumerate(packs):
        pack_ref[:rows, :] = packed[p * rows : (p + 1) * rows, :]
        meta = jnp.concatenate(
            [listed[:, p * rows : (p + 1) * rows], jnp.zeros((1, dof_count - rows), jnp.float32)], axis=1
        )
        pack_ref[rows:, :] = jnp.broadcast_to(meta, (SLOT_ROWS, dof_count)).astype(jnp.bfloat16)


def block_weights(packs, rows, blocks_own):
    first = lax.axis_index("face") * blocks_own
    block_ids = first + lax.broadcasted_iota(jnp.int32, (blocks_own, rows), 0)
    total = None
    for pack in packs:
        slots = pack[rows : rows + SLOT_ROWS, :].astype(jnp.int32)[:1, :rows]
        hit = (slots == block_ids).astype(jnp.bfloat16)
        part = jnp.dot(hit, pack[:rows, :], preferred_element_type=jnp.float32)
        total = part if total is None else total + part
    return total


def own_kernel(
    mortar_ref,
    rate_ref,
    cell_ref,
    owner_ref,
    slot_ref,
    scale_ref,
    section_ref,
    basis_ref,
    swapped_ref,
    pumped_ref,
    sum_ref,
    weight_ref,
):
    blocks_own, columns, dof_count = pumped_ref.shape
    faces = owner_ref.shape[1]
    here = lax.axis_index("sub")
    first_block = lax.axis_index("face") * blocks_own
    sign = (1 - 2 * section_ref[0]).astype(jnp.float32)
    block_ids = first_block + lax.broadcasted_iota(jnp.int32, (blocks_own, faces), 0)
    hit = (slot_ref[...] == block_ids) & (owner_ref[...] == here)
    weight = jnp.dot(hit.astype(jnp.bfloat16), scale_ref[...], preferred_element_type=jnp.float32) * sign
    weight_ref[...] = weight + block_weights((swapped_ref,), swapped_ref.shape[0] - SLOT_ROWS, blocks_own)

    square = (columns, columns)
    diagonal = lax.broadcasted_iota(jnp.int32, square, 0) == lax.broadcasted_iota(jnp.int32, square, 1)
    cells = jnp.sum(jnp.where(diagonal, cell_ref[...], 0), axis=1, keepdims=True)
    rates = jnp.sum(jnp.where(diagonal, rate_ref[...], 0.0), axis=1, keepdims=True)
    base = (here * mortar_ref.shape[0] + first_block) * dof_count
    offsets = cells - base - lax.broadcasted_iota(jnp.int32, (columns, dof_count), 1)
    rates = jnp.broadcast_to(rates, (columns, dof_count))
    tile_blocks = blocks_own // TILES
    for tile in range(TILES):
        at = slice(tile * tile_blocks, (tile + 1) * tile_blocks)
        values = mortar_ref[pl.ds(first_block + tile * tile_blocks, tile_blocks)].astype(jnp.float32)
        wells = jnp.stack(
            [jnp.where(offsets == block * dof_count, rates, 0.0) for block in range(at.start, at.stop)], axis=0
        )
        pumped = (values + wells).astype(jnp.bfloat16)
        pumped_ref[at] = pumped
        scaled = (pumped.astype(jnp.float32) * weight_ref[at][:, None, :]).astype(jnp.bfloat16)
        flux = jnp.dot(
            scaled.reshape(tile_blocks * columns, dof_count), basis_ref[0], preferred_element_type=jnp.float32
        )
        sum_ref[at] = flux.reshape(tile_blocks, columns, dof_count)


def gather_partners(arrays, weight_ref, basis_ref):
    count, blocks_own, dof_count = weight_ref.shape
    for at in range(count):
        base_0, base_1, pack, pack_swapped = arrays[4 * at : 4 * at + 4]
        weight_ref[at] = block_weights((pack, pack_swapped), pack.shape[0] - SLOT_ROWS, blocks_own)
        for core, base in enumerate((base_0, base_1)):

            @pl.when(lax.axis_index("face") == core)
            def _():
                basis_ref[at * dof_count : (at + 1) * dof_count, :] = base[0]


def tile_flux(at, slot, pumped_ref, sum_ref, weight_ref, basis_ref, scaled_ref):
    count, _, dof_count = weight_ref.shape
    rows = scaled_ref.shape[1]
    values = pumped_ref[at].astype(jnp.float32)
    for spot in range(count):
        scaled = (values * weight_ref[spot, at][:, None, :]).astype(jnp.bfloat16)
        scaled_ref[slot, :, spot * dof_count : (spot + 1) * dof_count] = scaled.reshape(rows, dof_count)
    total = jnp.dot(scaled_ref[slot], basis_ref[...], preferred_element_type=jnp.float32)
    return total + sum_ref[at].reshape(rows, dof_count)


def stage_kernel(pumped_ref, sum_ref, *refs):
    arrays, (out_ref, weight_ref, basis_ref, scaled_ref) = refs[:-4], refs[-4:]
    gather_partners(arrays, weight_ref, basis_ref)
    tile_blocks = pumped_ref.shape[0] // TILES
    for tile in range(TILES):
        at = slice(tile * tile_blocks, (tile + 1) * tile_blocks)
        total = tile_flux(at, tile % 2, pumped_ref, sum_ref, weight_ref, basis_ref, scaled_ref)
        out_ref[at] = total.reshape(pumped_ref[at].shape)


def last_kernel(pumped_ref, sum_ref, projection_ref, *refs):
    arrays, (result_ref, weight_ref, basis_ref, scaled_ref, out_ref, sems) = refs[:-6], refs[-6:]
    gather_partners(arrays, weight_ref, basis_ref)
    tiles = sems.shape[0]
    tile_blocks = pumped_ref.shape[0] // tiles
    copies = []
    for tile in range(tiles):
        at = slice(tile * tile_blocks, (tile + 1) * tile_blocks)
        total = tile_flux(at, tile % 2, pumped_ref, sum_ref, weight_ref, basis_ref, scaled_ref)
        result = jnp.dot(
            total.astype(jnp.bfloat16), projection_ref[...], preferred_element_type=jnp.float32
        )
        out_ref[at] = result.reshape(pumped_ref[at].shape)
        copies.append(pltpu.make_async_copy(out_ref.at[at], result_ref.at[at], sems.at[tile]))
        copies[-1].start()
    for copy in copies:
        copy.wait()


def on_device(
    mortar_in, pump_rate, well_cell, face_owner, face_slot, face_scale, section, basis, projection
):
    blocks_dev, cols_dev, dof_count = mortar_in.shape
    faces_dev = face_slot.shape[0]
    subdomains, halves = lax.axis_size("sub"), lax.axis_size("face")
    blocks_own = blocks_dev // halves
    capacity = max(2, 2 * faces_dev // subdomains)
    pack_rows = -(-capacity // ROW_TILE) * ROW_TILE + SLOT_ROWS
    block_shape = (blocks_own, cols_dev, dof_count)
    swap = [(i, i ^ 1) for i in range(halves)]

    def flat(sub, face):
        return sub * halves + face

    evens = list(range(2, subdomains, 2))
    cells = [(s, face) for s in range(subdomains) for face in range(halves)]
    firsts = [
        lax.ppermute(
            basis, ("sub", "face"), [(flat(s, face), flat(s ^ (1 if face else p), face)) for s, face in cells]
        )
        for p in evens
    ]
    partners = [0, *evens, 1, *[p + 1 for p in evens]]
    early_count = 1 + len(evens) + 1
    faces = [face_owner.reshape(1, faces_dev), face_slot.reshape(1, faces_dev), face_scale]
    packs = pl.pallas_call(
        functools.partial(pack_kernel, partners),
        out_shape=[jax.ShapeDtypeStruct((pack_rows, dof_count), jnp.bfloat16)] * len(partners),
        in_specs=[VMEM, VMEM, VMEM, SMEM],
        out_specs=[VMEM] * len(partners),
        cost_estimate=WORK,
        name="pack_weights",
    )(*faces, section)

    arrived = [
        lax.ppermute(pack, "sub", [(i, i ^ p) for i in range(subdomains)]) for p, pack in zip(partners[1:], packs[1:])
    ]
    own_swapped = lax.ppermute(packs[0], "face", swap)

    firsts, own_swapped = lax.optimization_barrier((firsts, own_swapped))
    pumped, own_sum = pl.pallas_call(
        own_kernel,
        out_shape=[
            jax.ShapeDtypeStruct(block_shape, jnp.bfloat16),
            jax.ShapeDtypeStruct(block_shape, jnp.float32),
        ],
        in_specs=[VMEM] * 6 + [SMEM, VMEM, VMEM],
        out_specs=[VMEM, VMEM],
        scratch_shapes=[pltpu.VMEM((blocks_own, dof_count), jnp.float32)],
        compiler_params=pltpu.CompilerParams(vmem_limit_bytes=32 * MIB),
        cost_estimate=WORK,
        name="own_blocks",
    )(
        mortar_in,
        pump_rate.reshape(1, cols_dev),
        well_cell.reshape(1, cols_dev),
        *faces,
        section,
        basis,
        own_swapped,
    )

    pairs = [(flat(s, face), flat(s, 0) if face else flat(s ^ 1, 1)) for s, face in cells]
    seconds = [lax.ppermute(first, ("sub", "face"), pairs) for first in firsts]
    firsts_swapped = [lax.ppermute(first, "face", swap) for first in firsts]
    seconds_swapped = [lax.ppermute(second, "face", swap) for second in seconds]
    soon, own_sum, firsts_swapped = lax.optimization_barrier(
        (arrived[: early_count - 1], own_sum, firsts_swapped)
    )
    arrived = soon + arrived[early_count - 1 :]
    swapped = [lax.ppermute(array, "face", swap) for array in arrived]
    weights = dict(zip(partners[1:], zip(arrived, swapped)))
    early = [[first, other, *weights[p]] for p, first, other in zip(evens, firsts, firsts_swapped)]
    early.append([firsts_swapped[0], firsts[0], *weights[1]])
    late = [[other, second, *weights[p + 1]] for p, second, other in zip(evens, seconds, seconds_swapped)]

    def scratch(count, tiles):
        return [
            pltpu.VMEM((count, blocks_own, dof_count), jnp.float32),
            pltpu.VMEM((count * dof_count, dof_count), jnp.bfloat16),
            pltpu.VMEM((2, blocks_own // tiles * cols_dev, count * dof_count), jnp.bfloat16),
        ]

    operands = [pumped, own_sum, *sum(early, [])]
    total = pl.pallas_call(
        stage_kernel,
        out_shape=jax.ShapeDtypeStruct(block_shape, jnp.float32),
        in_specs=[VMEM] * len(operands),
        out_specs=VMEM,
        scratch_shapes=scratch(len(early), TILES),
        input_output_aliases={1: 0},
        compiler_params=pltpu.CompilerParams(vmem_limit_bytes=40 * MIB),
        cost_estimate=WORK,
        name="stage",
    )(*operands)

    operands = [pumped, total, projection, *sum(late, [])]
    return pl.pallas_call(
        last_kernel,
        out_shape=jax.ShapeDtypeStruct(block_shape, jnp.float32),
        in_specs=[VMEM] * len(operands),
        out_specs=HBM,
        scratch_shapes=[
            *scratch(len(late), LAST_TILES),
            pltpu.VMEM(block_shape, jnp.float32),
            pltpu.SemaphoreType.DMA((LAST_TILES,)),
        ],
        compiler_params=pltpu.CompilerParams(vmem_limit_bytes=40 * MIB),
        name="last_stage",
    )(*operands)


def solution(mesh):
    in_specs = (
        P(("groups", "sub"), "rhs", None),
        P(("groups", "rhs")),
        P(("groups", "rhs")),
        P(("groups", "sub", "face"), None),
        P(("groups", "sub", "face")),
        P(("groups", "sub", "face"), None),
        P(("groups", "sub")),
        P(("groups", "sub"), None, None),
        P(),
    )
    out_specs = P(("groups", "sub", "face"), "rhs", None)
    return jax.shard_map(
        on_device, mesh=mesh, in_specs=in_specs, out_specs=out_specs, check_vma=False
    )
```

time: 19.8 us -> 19.3 us (0.975)
  starting transfers between devices: 11.9 us -> 11.2 us
  waiting for transfers between devices: 1.03 us -> 1.28 us
    ppermute x7, starting transfers between devices: 11.2 us -> 10.6 us  [the longest x3 4.39 us: on_device(): lax.ppermute(pack, 'sub', [(i, i ^ p) for i in range(subdomains)])]
    ppermute x7, waiting for transfers between devices: 1.02 us -> 1.27 us  [the longest x3 1.26 us: on_device(): lax.ppermute(pack, 'sub', [(i, i ^ p) for i in range(subdomains)])]
  transfers between devices with their start and end apart: 11 -> 11, of which waited for: 1 -> 1; matrix products, arithmetic and copies ran while one was open for 0% -> 0% of each run, Pallas kernels for 20% -> 21%
where the time goes in v12:
time: 19.3 us; the launch traced here: 19.1 us
  starting transfers between devices  11.2 us (58%)
  Pallas kernels  5.81 us (30%)
  waiting for transfers between devices  1.28 us (7%)
  between operations  0.82 us (4%)
    ppermute x3, starting transfers between devices, on_device(): lax.ppermute(pack, 'sub', [(i, i ^ p) for i in range(subdomains)])  4.39 us
    ppermute x1, starting transfers between devices, on_device(): lax.ppermute(basis, ('sub', 'face'), [(flat(s, face), flat(s ^ (1 if face...  4.04 us
    pallas_call x1, Pallas kernels, on_device(): pl.pallas_call(functools.partial(pack_kernel, partners), out_shape=[jax.S...  2 us
    pallas_call x1, Pallas kernels, on_device(): pl.pallas_call(last_kernel, out_shape=jax.ShapeDtypeStruct(block_shape, j...  1.88 us
    ppermute x1, starting transfers between devices, on_device(): seconds_swapped = [lax.ppermute(second, 'face', swap) for second in seconds]  1.41 us
    ppermute x3, waiting for transfers between devices, on_device(): lax.ppermute(pack, 'sub', [(i, i ^ p) for i in range(subdomains)])  1.26 us
    pallas_call x1, Pallas kernels, on_device(): pl.pallas_call(stage_kernel, out_shape=jax.ShapeDtypeStruct(block_shape,...  1.14 us
    ppermute x1, starting transfers between devices, on_device(): seconds = [lax.ppermute(first, ('sub', 'face'), pairs) for first in firsts]  0.79 us
  transfers between devices with their start and end apart: 11, of which 1 were waited for; matrix products, arithmetic and copies ran while one was open for 0% of the time, Pallas kernels for 21%

profile of v12, /device:TPU:0, one launch (start us, length us, event | category | flops | bytes accessed | tf_op | source)
XLA Modules:
  0.0 19.1 jit_solution(12054951114822869755)
XLA Ops:
  0.0 4.0 %collective-permute-start = (bf16[1,256,256]{2,1,0:T(8,128)(2,1)}, bf16[1,256,256]{2,1,0:T(8,128)(2,1)S(1)}, u32[]{:S(2)}, u32[]{:S(2)}) collective-permute-start(bf16[1,256,256]{2,1,0:T(8,128)(2,1)} %basis_ref.1), channel_id=1, source_target_pairs={{0,8},{1,5},{4,12},{5,1},{8,0},{9,13},{12,4},{13,9},{2,10},{3,7},{... | collective-permute-start | bytes 393224 | tf_op jit(solution)/shard_map/ppermute | solution.py:184
  4.7 0.0 copy-start.1
  4.7 0.0 copy-start.2
  4.7 0.0 copy-start.3
  4.7 0.0 copy-start.4
  4.7 0.0 copy-start.5
  4.7 0.0 copy-start.6
  4.7 0.0 copy-start.7
  4.8 2.0 %pack_weights.1 = (bf16[72,256]{1,0:T(8,128)(2,1)}, bf16[72,256]{1,0:T(8,128)(2,1)}, bf16[72,256]{1,0:T(8,128)(2,1)}, bf16[72,256]{1,0:T(8,128)(2,1)}) custom-call(s32[1,128]{1,0:T(1,128)} %bitcast.6, s32[1,128]{1,0:T(1,128)} %bitcast.8, bf16[128,256]{1,0:T(8,128)(2,1)} %scale_ref.3, s32[1]{0:T(128)S(6)} %copy.12.section_ref), custom_call_target="tpu_custom_call" | custom-call | flops 4000000000 | bytes 8388608 | tf_op jit(solution)/shard_map/pack_weights/pallas_call | solution.py:192
  6.8 0.0 collective-permute-start.1
  6.8 1.1 %collective-permute-start.2 = (bf16[72,256]{1,0:T(8,128)(2,1)}, bf16[72,256]{1,0:T(8,128)(2,1)S(1)}, u32[]{:S(2)}, u32[]{:S(2)}) collective-permute-start(bf16[72,256]{1,0:T(8,128)(2,1)} %get-tuple-element.20), channel_id=1, source_target_pairs={{0,8},{4,12},{8,0},{12,4},{1,9},{5,13},{9,1},{13,5},{2,10},{6,14},... | collective-permute-start | bytes 110600 | tf_op jit(solution)/shard_map/ppermute | solution.py:202
  7.9 0.8 %collective-permute-start.3 = (bf16[72,256]{1,0:T(8,128)(2,1)}, bf16[72,256]{1,0:T(8,128)(2,1)S(1)}, u32[]{:S(2)}, u32[]{:S(2)}) collective-permute-start(bf16[72,256]{1,0:T(8,128)(2,1)} %get-tuple-element.21), channel_id=1, source_target_pairs={{0,4},{4,0},{8,12},{12,8},{1,5},{5,1},{9,13},{13,9},{2,6},{6,2},{1... | collective-permute-start | bytes 110600 | tf_op jit(solution)/shard_map/ppermute | solution.py:202
  8.7 2.5 %collective-permute-start.9 = (bf16[72,256]{1,0:T(8,128)(2,1)}, bf16[72,256]{1,0:T(8,128)(2,1)S(1)}, u32[]{:S(2)}, u32[]{:S(2)}) collective-permute-start(bf16[72,256]{1,0:T(8,128)(2,1)} %get-tuple-element.28), channel_id=1, source_target_pairs={{0,12},{4,8},{8,4},{12,0},{1,13},{5,9},{9,5},{13,1},{2,14},{6,10},... | collective-permute-start | bytes 110600 | tf_op jit(solution)/shard_map/ppermute | solution.py:202
  11.2 0.0 collective-permute-done.1.swapped_ref
  11.2 0.0 collective-permute-done.refs_0_.refs_5_
  11.2 0.0 collective-permute-start.4
  11.2 0.8 %collective-permute-start.7 = (bf16[1,256,256]{2,1,0:T(8,128)(2,1)S(1)}, bf16[1,256,256]{2,1,0:T(8,128)(2,1)S(1)}, u32[]{:S(2)}, u32[]{:S(2)}) collective-permute-start(bf16[1,256,256]{2,1,0:T(8,128)(2,1)S(1)} %collective-permute-done.refs_0_.refs_5_), channel_id=1, source_target_pairs={{0,5},{1,0},{4,1},{5,4},{8,13},{9,8},{12,9},{13,12},{2,7},{3,2},{6... | collective-permute-start | bytes 393224 | tf_op jit(solution)/shard_map/ppermute | solution.py:230
  12.0 0.0 copy-done.1
  12.0 0.0 copy-done.2
  12.0 0.0 copy-done.3
  12.0 0.0 copy-done.4
  12.0 0.0 copy-done.5
  12.0 0.0 copy-done.6
  12.0 0.0 copy-done.7
  12.0 0.8 %own_blocks.1 = (bf16[64,32,256]{2,1,0:T(8,128)(2,1)S(1)}, f32[64,32,256]{2,1,0:T(8,128)S(1)}) custom-call(bf16[128,32,256]{2,1,0:T(8,128)(2,1)S(1)} %copy-done.1, f32[1,32]{1,0:T(1,128)S(1)} %bitcast.4, s32[1,32]{1,0:T(1,128)S(1)} %bitcast.5, s32[1,128]{1,0:T(1,128)S(1)} %bitcast.7, s32[1,128]{1,0:T(1,128)S(1)} %bitcast.9, bf16[128,256]{1,0:T(8,128)(2,1)S(1)} %copy-done.3, ...), custom_call_target="tpu_custom_call" | custom-call | flops 4000000000 | bytes 8388608 | tf_op jit(solution)/shard_map/own_blocks/pallas_call | solution.py:207
  12.8 0.0 collective-permute-done.2.refs_2_
  12.8 0.0 collective-permute-done.3.refs_6_
  12.8 0.0 collective-permute-done.4.refs_1_.refs_4_
  12.8 0.1 collective-permute-start.5
  12.9 0.5 %collective-permute-start.6 = (bf16[72,256]{1,0:T(8,128)(2,1)S(1)}, bf16[72,256]{1,0:T(8,128)(2,1)S(1)}, u32[]{:S(2)}, u32[]{:S(2)}) collective-permute-start(bf16[72,256]{1,0:T(8,128)(2,1)S(1)} %collective-permute-done.3.refs_6_), channel_id=1, source_target_pairs={{0,1},{1,0},{2,3},{3,2},{4,5},{5,4},{6,7},{7,6},{8,9},{9,8},{10,11... | collective-permute-start | bytes 110600 | tf_op jit(solution)/shard_map/ppermute | solution.py:237
  13.4 1.3 %collective-permute-done.9.refs_2_ = bf16[72,256]{1,0:T(8,128)(2,1)S(1)} collective-permute-done((bf16[72,256]{1,0:T(8,128)(2,1)}, bf16[72,256]{1,0:T(8,128)(2,1)S(1)}, u32[]{:S(2)}, u32[]{:S(2)}) %collective-permute-start.9) | collective-permute-done | bytes 36896 | tf_op jit(solution)/shard_map/ppermute | solution.py:202
  14.6 0.0 collective-permute-start.10
  14.6 0.0 collective-permute-done.7.refs_1_
  14.7 1.4 %collective-permute-start.8 = (bf16[1,256,256]{2,1,0:T(8,128)(2,1)S(1)}, bf16[1,256,256]{2,1,0:T(8,128)(2,1)S(1)}, u32[]{:S(2)}, u32[]{:S(2)}) collective-permute-start(bf16[1,256,256]{2,1,0:T(8,128)(2,1)S(1)} %collective-permute-done.7.refs_1_), channel_id=1, source_target_pairs={{0,1},{1,0},{2,3},{3,2},{4,5},{5,4},{6,7},{7,6},{8,9},{9,8},{10,11... | collective-permute-start | bytes 393224 | tf_op jit(solution)/shard_map/ppermute | solution.py:232
  16.1 0.0 collective-permute-done.5.refs_3_
  16.1 0.0 collective-permute-done.6.refs_7_
  16.1 0.0 copy-start
  16.1 1.1 %stage.1.sum_ref = f32[64,32,256]{2,1,0:T(8,128)S(1)} custom-call(bf16[64,32,256]{2,1,0:T(8,128)(2,1)S(1)} %get-tuple-element.19.pumped_ref, f32[64,32,256]{2,1,0:T(8,128)S(1)} %get-tuple-element.24.sum_ref, bf16[1,256,256]{2,1,0:T(8,128)(2,1)S(1)} %collective-permute-done.refs_0_.refs_5_, ...), custom_call_target="tpu_custom_call", output_to_operand_aliasing={{}: (1, {})} | custom-call | flops 4000000000 | bytes 8388608 | tf_op jit(solution)/shard_map/stage/pallas_call | solution.py:251
  17.2 0.0 collective-permute-done.10.refs_3_
  17.2 0.0 collective-permute-done.8.refs_0_
  17.2 0.0 copy-done
  17.3 1.9 %last_stage.1 = f32[64,32,256]{2,1,0:T(8,128)} custom-call(bf16[64,32,256]{2,1,0:T(8,128)(2,1)S(1)} %get-tuple-element.19.pumped_ref, f32[64,32,256]{2,1,0:T(8,128)S(1)} %stage.1.sum_ref, bf16[256,256]{1,0:T(8,128)(2,1)S(1)} %copy-done, bf16[1,256,256]{2,1,0:T(8,128)(2,1)S(1)} %collective-permute-done.8.refs_0_, ...), custom_call_target="tpu_custom_call" | custom-call | tf_op jit(solution)/shard_map/last_stage/pallas_call | solution.py:264
Async XLA Ops:
  0.0 11.2 %collective-permute-start = (bf16[1,256,256]{2,1,0:T(8,128)(2,1)}, bf16[1,256,256]{2,1,0:T(8,128)(2,1)S(1)}, u32[]{:S(2)}, u32[]{:S(2)}) collective-permute-start(bf16[1,256,256]{2,1,0:T(8,128)(2,1)} %basis_ref.1), channel_id=1, source_target_pairs={{0,8},{1,5},{4,12},{5,1},{8,0},{9,13},{12,4},{13,9},{2,10},{3,7},{... | collective-permute-start | bytes 393224 | tf_op jit(solution)/shard_map/ppermute | solution.py:184
  4.7 7.3 %copy-start.1 = (bf16[128,32,256]{2,1,0:T(8,128)(2,1)S(1)}, bf16[128,32,256]{2,1,0:T(8,128)(2,1)}, u32[]{:S(2)}) copy-start(bf16[128,32,256]{2,1,0:T(8,128)(2,1)} %mortar_ref.1) | copy-start | bytes 6291460
  4.7 7.3 %copy-start.2 = (bf16[1,256,256]{2,1,0:T(8,128)(2,1)S(1)}, bf16[1,256,256]{2,1,0:T(8,128)(2,1)}, u32[]{:S(2)}) copy-start(bf16[1,256,256]{2,1,0:T(8,128)(2,1)} %basis_ref.1) | copy-start | bytes 393220
  4.7 7.3 %copy-start.3 = (bf16[128,256]{1,0:T(8,128)(2,1)S(1)}, bf16[128,256]{1,0:T(8,128)(2,1)}, u32[]{:S(2)}) copy-start(bf16[128,256]{1,0:T(8,128)(2,1)} %scale_ref.3) | copy-start | bytes 196612
  4.7 7.2 %copy-start.4 = (f32[32]{0:T(128)S(1)}, f32[32]{0:T(128)}, u32[]{:S(2)}) copy-start(f32[32]{0:T(128)} %param.10) | copy-start | bytes 388
  4.7 7.2 %copy-start.5 = (s32[32]{0:T(128)S(1)}, s32[32]{0:T(128)}, u32[]{:S(2)}) copy-start(s32[32]{0:T(128)} %param.11) | copy-start | bytes 388
  4.7 7.2 %copy-start.6 = (s32[128,1]{0,1:T(1,128)S(1)}, s32[128,1]{0,1:T(1,128)}, u32[]{:S(2)}) copy-start(s32[128,1]{0,1:T(1,128)} %param.12) | copy-start | bytes 1540
  4.7 7.2 %copy-start.7 = (s32[128]{0:T(128)S(1)}, s32[128]{0:T(128)}, u32[]{:S(2)}) copy-start(s32[128]{0:T(128)} %param.13) | copy-start | bytes 1540
  6.8 4.4 %collective-permute-start.1 = (bf16[72,256]{1,0:T(8,128)(2,1)}, bf16[72,256]{1,0:T(8,128)(2,1)S(1)}, u32[]{:S(2)}, u32[]{:S(2)}) collective-permute-start(bf16[72,256]{1,0:T(8,128)(2,1)} %get-tuple-element.17), channel_id=1, source_target_pairs={{0,1},{1,0},{2,3},{3,2},{4,5},{5,4},{6,7},{7,6},{8,9},{9,8},{10,11... | collective-permute-start | bytes 110600 | tf_op jit(solution)/shard_map/ppermute | solution.py:204
  6.8 6.0 %collective-permute-start.2 = (bf16[72,256]{1,0:T(8,128)(2,1)}, bf16[72,256]{1,0:T(8,128)(2,1)S(1)}, u32[]{:S(2)}, u32[]{:S(2)}) collective-permute-start(bf16[72,256]{1,0:T(8,128)(2,1)} %get-tuple-element.20), channel_id=1, source_target_pairs={{0,8},{4,12},{8,0},{12,4},{1,9},{5,13},{9,1},{13,5},{2,10},{6,14},... | collective-permute-start | bytes 110600 | tf_op jit(solution)/shard_map/ppermute | solution.py:202
  7.9 4.9 %collective-permute-start.3 = (bf16[72,256]{1,0:T(8,128)(2,1)}, bf16[72,256]{1,0:T(8,128)(2,1)S(1)}, u32[]{:S(2)}, u32[]{:S(2)}) collective-permute-start(bf16[72,256]{1,0:T(8,128)(2,1)} %get-tuple-element.21), channel_id=1, source_target_pairs={{0,4},{4,0},{8,12},{12,8},{1,5},{5,1},{9,13},{13,9},{2,6},{6,2},{1... | collective-permute-start | bytes 110600 | tf_op jit(solution)/shard_map/ppermute | solution.py:202
  8.7 6.0 %collective-permute-start.9 = (bf16[72,256]{1,0:T(8,128)(2,1)}, bf16[72,256]{1,0:T(8,128)(2,1)S(1)}, u32[]{:S(2)}, u32[]{:S(2)}) collective-permute-start(bf16[72,256]{1,0:T(8,128)(2,1)} %get-tuple-element.28), channel_id=1, source_target_pairs={{0,12},{4,8},{8,4},{12,0},{1,13},{5,9},{9,5},{13,1},{2,14},{6,10},... | collective-permute-start | bytes 110600 | tf_op jit(solution)/shard_map/ppermute | solution.py:202
  11.2 1.6 %collective-permute-start.4 = (bf16[1,256,256]{2,1,0:T(8,128)(2,1)S(1)}, bf16[1,256,256]{2,1,0:T(8,128)(2,1)S(1)}, u32[]{:S(2)}, u32[]{:S(2)}) collective-permute-start(bf16[1,256,256]{2,1,0:T(8,128)(2,1)S(1)} %collective-permute-done.refs_0_.refs_5_), channel_id=1, source_target_pairs={{0,1},{1,0},{2,3},{3,2},{4,5},{5,4},{6,7},{7,6},{8,9},{9,8},{10,11... | collective-permute-start | bytes 393224 | tf_op jit(solution)/shard_map/ppermute | solution.py:231
  11.2 3.5 %collective-permute-start.7 = (bf16[1,256,256]{2,1,0:T(8,128)(2,1)S(1)}, bf16[1,256,256]{2,1,0:T(8,128)(2,1)S(1)}, u32[]{:S(2)}, u32[]{:S(2)}) collective-permute-start(bf16[1,256,256]{2,1,0:T(8,128)(2,1)S(1)} %collective-permute-done.refs_0_.refs_5_), channel_id=1, source_target_pairs={{0,5},{1,0},{4,1},{5,4},{8,13},{9,8},{12,9},{13,12},{2,7},{3,2},{6... | collective-permute-start | bytes 393224 | tf_op jit(solution)/shard_map/ppermute | solution.py:230
  12.8 3.3 %collective-permute-start.5 = (bf16[72,256]{1,0:T(8,128)(2,1)S(1)}, bf16[72,256]{1,0:T(8,128)(2,1)S(1)}, u32[]{:S(2)}, u32[]{:S(2)}) collective-permute-start(bf16[72,256]{1,0:T(8,128)(2,1)S(1)} %collective-permute-done.2.refs_2_), channel_id=1, source_target_pairs={{0,1},{1,0},{2,3},{3,2},{4,5},{5,4},{6,7},{7,6},{8,9},{9,8},{10,11... | collective-permute-start | bytes 110600 | tf_op jit(solution)/shard_map/ppermute | solution.py:237
  12.9 3.2 %collective-permute-start.6 = (bf16[72,256]{1,0:T(8,128)(2,1)S(1)}, bf16[72,256]{1,0:T(8,128)(2,1)S(1)}, u32[]{:S(2)}, u32[]{:S(2)}) collective-permute-start(bf16[72,256]{1,0:T(8,128)(2,1)S(1)} %collective-permute-done.3.refs_6_), channel_id=1, source_target_pairs={{0,1},{1,0},{2,3},{3,2},{4,5},{5,4},{6,7},{7,6},{8,9},{9,8},{10,11... | collective-permute-start | bytes 110600 | tf_op jit(solution)/shard_map/ppermute | solution.py:237
  14.6 2.6 %collective-permute-start.10 = (bf16[72,256]{1,0:T(8,128)(2,1)S(1)}, bf16[72,256]{1,0:T(8,128)(2,1)S(1)}, u32[]{:S(2)}, u32[]{:S(2)}) collective-permute-start(bf16[72,256]{1,0:T(8,128)(2,1)S(1)} %collective-permute-done.9.refs_2_), channel_id=1, source_target_pairs={{0,1},{1,0},{2,3},{3,2},{4,5},{5,4},{6,7},{7,6},{8,9},{9,8},{10,11... | collective-permute-start | bytes 110600 | tf_op jit(solution)/shard_map/ppermute | solution.py:237
  14.7 2.6 %collective-permute-start.8 = (bf16[1,256,256]{2,1,0:T(8,128)(2,1)S(1)}, bf16[1,256,256]{2,1,0:T(8,128)(2,1)S(1)}, u32[]{:S(2)}, u32[]{:S(2)}) collective-permute-start(bf16[1,256,256]{2,1,0:T(8,128)(2,1)S(1)} %collective-permute-done.7.refs_1_), channel_id=1, source_target_pairs={{0,1},{1,0},{2,3},{3,2},{4,5},{5,4},{6,7},{7,6},{8,9},{9,8},{10,11... | collective-permute-start | bytes 393224 | tf_op jit(solution)/shard_map/ppermute | solution.py:232
  16.1 1.2 %copy-start = (bf16[256,256]{1,0:T(8,128)(2,1)S(1)}, bf16[256,256]{1,0:T(8,128)(2,1)}, u32[]{:S(2)}) copy-start(bf16[256,256]{1,0:T(8,128)(2,1)} %projection_ref.1) | copy-start | bytes 393220

commit v13 on v12

--- a/solution.py
+++ b/solution.py
@@ -229,16 +229,18 @@
     pairs = [(flat(s, face), flat(s, 0) if face else flat(s ^ 1, 1)) for s, face in cells]
     seconds = [lax.ppermute(first, ("sub", "face"), pairs) for first in firsts]
     firsts_swapped = [lax.ppermute(first, "face", swap) for first in firsts]
-    seconds_swapped = [lax.ppermute(second, "face", swap) for second in seconds]
     soon, own_sum, firsts_swapped = lax.optimization_barrier(
         (arrived[: early_count - 1], own_sum, firsts_swapped)
     )
-    arrived = soon + arrived[early_count - 1 :]
-    swapped = [lax.ppermute(array, "face", swap) for array in arrived]
-    weights = dict(zip(partners[1:], zip(arrived, swapped)))
-    early = [[first, other, *weights[p]] for p, first, other in zip(evens, firsts, firsts_swapped)]
-    early.append([firsts_swapped[0], firsts[0], *weights[1]])
-    late = [[other, second, *weights[p + 1]] for p, second, other in zip(evens, seconds, seconds_swapped)]
+
+    def with_swapped(arrays):
+        return [(array, lax.ppermute(array, "face", swap)) for array in arrays]
+
+    weights = with_swapped(soon)
+    own_sum, later = lax.optimization_barrier((own_sum, arrived[early_count - 1 :]))
+    later = with_swapped(later)
+    early = [[first, other, *pair] for first, other, pair in zip(firsts, firsts_swapped, weights)]
+    early.append([firsts_swapped[0], firsts[0], *weights[-1]])
 
     def scratch(count, tiles):
         return [
@@ -256,9 +258,12 @@
         scratch_shapes=scratch(len(early), TILES),
         input_output_aliases={1: 0},
         compiler_params=pltpu.CompilerParams(vmem_limit_bytes=40 * MIB),
-        cost_estimate=WORK,
+        cost_estimate=LIGHT,
         name="stage",
     )(*operands)
+
+    seconds, total = lax.optimization_barrier((seconds, total))
+    late = [[other, second, *pair] for (second, other), pair in zip(with_swapped(seconds), later)]
 
     operands = [pumped, total, projection, *sum(late, [])]
     return pl.pallas_call(

time: 19.3 us -> 19.3 us (level)
  waiting for transfers between devices: 1.28 us -> 2.17 us
  starting transfers between devices: 11.2 us -> 10.4 us
    ppermute x4, waiting for transfers between devices: 0.01 us -> 0.9 us  [with_swapped(): return [(array, lax.ppermute(array, 'face', swap)) for array in arrays]]
    ppermute x4, starting transfers between devices: 1.98 us -> 1.14 us  [with_swapped(): return [(array, lax.ppermute(array, 'face', swap)) for array in arrays]]
  transfers between devices with their start and end apart: 11 -> 11, of which waited for: 1 -> 2; matrix products, arithmetic and copies ran while one was open for 0% -> 0% of each run, Pallas kernels for 21% -> 20%
where the time goes in v13:
time: 19.3 us; the launch traced here: 19.2 us
  starting transfers between devices  10.4 us (54%)
  Pallas kernels  5.8 us (30%)
  waiting for transfers between devices  2.17 us (11%)
  between operations  0.8 us (4%)
    ppermute x3, starting transfers between devices, on_device(): lax.ppermute(pack, 'sub', [(i, i ^ p) for i in range(subdomains)])  4.39 us
    ppermute x1, starting transfers between devices, on_device(): lax.ppermute(basis, ('sub', 'face'), [(flat(s, face), flat(s ^ (1 if face...  4.04 us
    pallas_call x1, Pallas kernels, on_device(): pl.pallas_call(functools.partial(pack_kernel, partners), out_shape=[jax.S...  2 us
    pallas_call x1, Pallas kernels, on_device(): pl.pallas_call(last_kernel, out_shape=jax.ShapeDtypeStruct(block_shape, j...  1.88 us
    ppermute x3, waiting for transfers between devices, on_device(): lax.ppermute(pack, 'sub', [(i, i ^ p) for i in range(subdomains)])  1.26 us
    ppermute x4, starting transfers between devices, with_swapped(): return [(array, lax.ppermute(array, 'face', swap)) for array in arrays]  1.14 us
    pallas_call x1, Pallas kernels, on_device(): pl.pallas_call(stage_kernel, out_shape=jax.ShapeDtypeStruct(block_shape,...  1.14 us
    ppermute x4, waiting for transfers between devices, with_swapped(): return [(array, lax.ppermute(array, 'face', swap)) for array in arrays]  0.9 us
  transfers between devices with their start and end apart: 11, of which 2 were waited for; matrix products, arithmetic and copies ran while one was open for 0% of the time, Pallas kernels for 20%

profile of v13, /device:TPU:0, one launch (start us, length us, event | category | flops | bytes accessed | tf_op | source)
XLA Modules:
  0.0 19.2 jit_solution(11810549293975325661)
XLA Ops:
  0.0 4.0 %collective-permute-start = (bf16[1,256,256]{2,1,0:T(8,128)(2,1)}, bf16[1,256,256]{2,1,0:T(8,128)(2,1)S(1)}, u32[]{:S(2)}, u32[]{:S(2)}) collective-permute-start(bf16[1,256,256]{2,1,0:T(8,128)(2,1)} %basis_ref.1), channel_id=1, source_target_pairs={{0,8},{1,5},{4,12},{5,1},{8,0},{9,13},{12,4},{13,9},{2,10},{3,7},{... | collective-permute-start | bytes 393224 | tf_op jit(solution)/shard_map/ppermute | solution.py:184
  4.7 0.0 copy-start.1
  4.7 0.0 copy-start.2
  4.7 0.0 copy-start.3
  4.7 0.0 copy-start.4
  4.7 0.0 copy-start.5
  4.7 0.0 copy-start.6
  4.7 0.0 copy-start.7
  4.8 2.0 %pack_weights.1 = (bf16[72,256]{1,0:T(8,128)(2,1)}, bf16[72,256]{1,0:T(8,128)(2,1)}, bf16[72,256]{1,0:T(8,128)(2,1)}, bf16[72,256]{1,0:T(8,128)(2,1)}) custom-call(s32[1,128]{1,0:T(1,128)} %bitcast.6, s32[1,128]{1,0:T(1,128)} %bitcast.8, bf16[128,256]{1,0:T(8,128)(2,1)} %scale_ref.3, s32[1]{0:T(128)S(6)} %copy.12.section_ref), custom_call_target="tpu_custom_call" | custom-call | flops 4000000000 | bytes 8388608 | tf_op jit(solution)/shard_map/pack_weights/pallas_call | solution.py:192
  6.8 0.0 collective-permute-start.1
  6.8 1.1 %collective-permute-start.3 = (bf16[72,256]{1,0:T(8,128)(2,1)}, bf16[72,256]{1,0:T(8,128)(2,1)S(1)}, u32[]{:S(2)}, u32[]{:S(2)}) collective-permute-start(bf16[72,256]{1,0:T(8,128)(2,1)} %get-tuple-element.25), channel_id=1, source_target_pairs={{0,8},{4,12},{8,0},{12,4},{1,9},{5,13},{9,1},{13,5},{2,10},{6,14},... | collective-permute-start | bytes 110600 | tf_op jit(solution)/shard_map/ppermute | solution.py:202
  7.9 0.8 %collective-permute-start.4 = (bf16[72,256]{1,0:T(8,128)(2,1)}, bf16[72,256]{1,0:T(8,128)(2,1)S(1)}, u32[]{:S(2)}, u32[]{:S(2)}) collective-permute-start(bf16[72,256]{1,0:T(8,128)(2,1)} %get-tuple-element.26), channel_id=1, source_target_pairs={{0,4},{4,0},{8,12},{12,8},{1,5},{5,1},{9,13},{13,9},{2,6},{6,2},{1... | collective-permute-start | bytes 110600 | tf_op jit(solution)/shard_map/ppermute | solution.py:202
  8.7 2.5 %collective-permute-start.6 = (bf16[72,256]{1,0:T(8,128)(2,1)}, bf16[72,256]{1,0:T(8,128)(2,1)S(1)}, u32[]{:S(2)}, u32[]{:S(2)}) collective-permute-start(bf16[72,256]{1,0:T(8,128)(2,1)} %get-tuple-element.29), channel_id=1, source_target_pairs={{0,12},{4,8},{8,4},{12,0},{1,13},{5,9},{9,5},{13,1},{2,14},{6,10},... | collective-permute-start | bytes 110600 | tf_op jit(solution)/shard_map/ppermute | solution.py:202
  11.2 0.0 collective-permute-done.1.swapped_ref
  11.2 0.0 collective-permute-done.refs_0_.refs_5_
  11.2 0.0 collective-permute-start.5
  11.2 0.8 %collective-permute-start.2 = (bf16[1,256,256]{2,1,0:T(8,128)(2,1)S(1)}, bf16[1,256,256]{2,1,0:T(8,128)(2,1)S(1)}, u32[]{:S(2)}, u32[]{:S(2)}) collective-permute-start(bf16[1,256,256]{2,1,0:T(8,128)(2,1)S(1)} %collective-permute-done.refs_0_.refs_5_), channel_id=1, source_target_pairs={{0,5},{1,0},{4,1},{5,4},{8,13},{9,8},{12,9},{13,12},{2,7},{3,2},{6... | collective-permute-start | bytes 393224 | tf_op jit(solution)/shard_map/ppermute | solution.py:230
  12.0 0.0 copy-done.1
  12.0 0.0 copy-done.2
  12.0 0.0 copy-done.3
  12.0 0.0 copy-done.4
  12.0 0.0 copy-done.5
  12.0 0.0 copy-done.6
  12.0 0.0 copy-done.7
  12.0 0.8 %own_blocks.1 = (bf16[64,32,256]{2,1,0:T(8,128)(2,1)S(1)}, f32[64,32,256]{2,1,0:T(8,128)S(1)}) custom-call(bf16[128,32,256]{2,1,0:T(8,128)(2,1)S(1)} %copy-done.1, f32[1,32]{1,0:T(1,128)S(1)} %bitcast.4, s32[1,32]{1,0:T(1,128)S(1)} %bitcast.5, s32[1,128]{1,0:T(1,128)S(1)} %bitcast.7, s32[1,128]{1,0:T(1,128)S(1)} %bitcast.9, bf16[128,256]{1,0:T(8,128)(2,1)S(1)} %copy-done.3, ...), custom_call_target="tpu_custom_call" | custom-call | flops 4000000000 | bytes 8388608 | tf_op jit(solution)/shard_map/own_blocks/pallas_call | solution.py:207
  12.8 0.0 collective-permute-done.3.refs_2_
  12.8 0.0 collective-permute-done.4.refs_6_
  12.8 0.0 collective-permute-done.5.refs_1_.refs_4_
  12.8 0.1 collective-permute-start.7
  12.9 0.5 %collective-permute-start.8 = (bf16[72,256]{1,0:T(8,128)(2,1)S(1)}, bf16[72,256]{1,0:T(8,128)(2,1)S(1)}, u32[]{:S(2)}, u32[]{:S(2)}) collective-permute-start(bf16[72,256]{1,0:T(8,128)(2,1)S(1)} %collective-permute-done.4.refs_6_), channel_id=1, source_target_pairs={{0,1},{1,0},{2,3},{3,2},{4,5},{5,4},{6,7},{7,6},{8,9},{9,8},{10,11... | collective-permute-start | bytes 110600 | tf_op jit(solution)/shard_map/ppermute | solution.py:237
  13.4 1.3 %collective-permute-done.6.refs_2_ = bf16[72,256]{1,0:T(8,128)(2,1)S(1)} collective-permute-done((bf16[72,256]{1,0:T(8,128)(2,1)}, bf16[72,256]{1,0:T(8,128)(2,1)S(1)}, u32[]{:S(2)}, u32[]{:S(2)}) %collective-permute-start.6) | collective-permute-done | bytes 36896 | tf_op jit(solution)/shard_map/ppermute | solution.py:202
  14.6 0.0 collective-permute-done.7.refs_3_
  14.6 0.0 collective-permute-done.8.refs_7_
  14.7 0.0 copy-start
  14.7 1.1 %stage.1.sum_ref = f32[64,32,256]{2,1,0:T(8,128)S(1)} custom-call(bf16[64,32,256]{2,1,0:T(8,128)(2,1)S(1)} %get-tuple-element.23.pumped_ref, f32[64,32,256]{2,1,0:T(8,128)S(1)} %get-tuple-element.30.sum_ref, bf16[1,256,256]{2,1,0:T(8,128)(2,1)S(1)} %collective-permute-done.refs_0_.refs_5_, ...), custom_call_target="tpu_custom_call", output_to_operand_aliasing={{}: (1, {})} | custom-call | flops 1000000 | bytes 1024 | tf_op jit(solution)/shard_map/stage/pallas_call | solution.py:253
  15.8 0.0 collective-permute-done.2.refs_1_
  15.8 0.3 %collective-permute-start.9 = (bf16[1,256,256]{2,1,0:T(8,128)(2,1)S(1)}, bf16[1,256,256]{2,1,0:T(8,128)(2,1)S(1)}, u32[]{:S(2)}, u32[]{:S(2)}) collective-permute-start(bf16[1,256,256]{2,1,0:T(8,128)(2,1)S(1)} %collective-permute-done.2.refs_1_), channel_id=1, source_target_pairs={{0,1},{1,0},{2,3},{3,2},{4,5},{5,4},{6,7},{7,6},{8,9},{9,8},{10,11... | collective-permute-start | bytes 393224 | tf_op jit(solution)/shard_map/ppermute | solution.py:237
  16.1 0.3 %collective-permute-start.10 = (bf16[72,256]{1,0:T(8,128)(2,1)S(1)}, bf16[72,256]{1,0:T(8,128)(2,1)S(1)}, u32[]{:S(2)}, u32[]{:S(2)}) collective-permute-start(bf16[72,256]{1,0:T(8,128)(2,1)S(1)} %collective-permute-done.6.refs_2_), channel_id=1, source_target_pairs={{0,1},{1,0},{2,3},{3,2},{4,5},{5,4},{6,7},{7,6},{8,9},{9,8},{10,11... | collective-permute-start | bytes 110600 | tf_op jit(solution)/shard_map/ppermute | solution.py:237
  16.4 0.9 %collective-permute-done.10.refs_3_ = bf16[72,256]{1,0:T(8,128)(2,1)S(1)} collective-permute-done((bf16[72,256]{1,0:T(8,128)(2,1)S(1)}, bf16[72,256]{1,0:T(8,128)(2,1)S(1)}, u32[]{:S(2)}, u32[]{:S(2)}) %collective-permute-start.10) | collective-permute-done | bytes 36896 | tf_op jit(solution)/shard_map/ppermute | solution.py:237
  17.3 0.0 collective-permute-done.9.refs_0_
  17.3 0.0 copy-done
  17.3 1.9 %last_stage.1 = f32[64,32,256]{2,1,0:T(8,128)} custom-call(bf16[64,32,256]{2,1,0:T(8,128)(2,1)S(1)} %get-tuple-element.23.pumped_ref, f32[64,32,256]{2,1,0:T(8,128)S(1)} %stage.1.sum_ref, bf16[256,256]{1,0:T(8,128)(2,1)S(1)} %copy-done, bf16[1,256,256]{2,1,0:T(8,128)(2,1)S(1)} %collective-permute-done.9.refs_0_, ...), custom_call_target="tpu_custom_call" | custom-call | tf_op jit(solution)/shard_map/last_stage/pallas_call | solution.py:269
Async XLA Ops:
  0.0 11.2 %collective-permute-start = (bf16[1,256,256]{2,1,0:T(8,128)(2,1)}, bf16[1,256,256]{2,1,0:T(8,128)(2,1)S(1)}, u32[]{:S(2)}, u32[]{:S(2)}) collective-permute-start(bf16[1,256,256]{2,1,0:T(8,128)(2,1)} %basis_ref.1), channel_id=1, source_target_pairs={{0,8},{1,5},{4,12},{5,1},{8,0},{9,13},{12,4},{13,9},{2,10},{3,7},{... | collective-permute-start | bytes 393224 | tf_op jit(solution)/shard_map/ppermute | solution.py:184
  4.7 7.3 %copy-start.1 = (bf16[128,32,256]{2,1,0:T(8,128)(2,1)S(1)}, bf16[128,32,256]{2,1,0:T(8,128)(2,1)}, u32[]{:S(2)}) copy-start(bf16[128,32,256]{2,1,0:T(8,128)(2,1)} %mortar_ref.1) | copy-start | bytes 6291460
  4.7 7.3 %copy-start.2 = (bf16[1,256,256]{2,1,0:T(8,128)(2,1)S(1)}, bf16[1,256,256]{2,1,0:T(8,128)(2,1)}, u32[]{:S(2)}) copy-start(bf16[1,256,256]{2,1,0:T(8,128)(2,1)} %basis_ref.1) | copy-start | bytes 393220
  4.7 7.3 %copy-start.3 = (bf16[128,256]{1,0:T(8,128)(2,1)S(1)}, bf16[128,256]{1,0:T(8,128)(2,1)}, u32[]{:S(2)}) copy-start(bf16[128,256]{1,0:T(8,128)(2,1)} %scale_ref.3) | copy-start | bytes 196612
  4.7 7.2 %copy-start.4 = (f32[32]{0:T(128)S(1)}, f32[32]{0:T(128)}, u32[]{:S(2)}) copy-start(f32[32]{0:T(128)} %param.10) | copy-start | bytes 388
  4.7 7.2 %copy-start.5 = (s32[32]{0:T(128)S(1)}, s32[32]{0:T(128)}, u32[]{:S(2)}) copy-start(s32[32]{0:T(128)} %param.11) | copy-start | bytes 388
  4.7 7.2 %copy-start.6 = (s32[128,1]{0,1:T(1,128)S(1)}, s32[128,1]{0,1:T(1,128)}, u32[]{:S(2)}) copy-start(s32[128,1]{0,1:T(1,128)} %param.12) | copy-start | bytes 1540
  4.7 7.2 %copy-start.7 = (s32[128]{0:T(128)S(1)}, s32[128]{0:T(128)}, u32[]{:S(2)}) copy-start(s32[128]{0:T(128)} %param.13) | copy-start | bytes 1540
  6.8 4.4 %collective-permute-start.1 = (bf16[72,256]{1,0:T(8,128)(2,1)}, bf16[72,256]{1,0:T(8,128)(2,1)S(1)}, u32[]{:S(2)}, u32[]{:S(2)}) collective-permute-start(bf16[72,256]{1,0:T(8,128)(2,1)} %get-tuple-element.21), channel_id=1, source_target_pairs={{0,1},{1,0},{2,3},{3,2},{4,5},{5,4},{6,7},{7,6},{8,9},{9,8},{10,11... | collective-permute-start | bytes 110600 | tf_op jit(solution)/shard_map/ppermute | solution.py:204
  6.8 6.0 %collective-permute-start.3 = (bf16[72,256]{1,0:T(8,128)(2,1)}, bf16[72,256]{1,0:T(8,128)(2,1)S(1)}, u32[]{:S(2)}, u32[]{:S(2)}) collective-permute-start(bf16[72,256]{1,0:T(8,128)(2,1)} %get-tuple-element.25), channel_id=1, source_target_pairs={{0,8},{4,12},{8,0},{12,4},{1,9},{5,13},{9,1},{13,5},{2,10},{6,14},... | collective-permute-start | bytes 110600 | tf_op jit(solution)/shard_map/ppermute | solution.py:202
  7.9 4.9 %collective-permute-start.4 = (bf16[72,256]{1,0:T(8,128)(2,1)}, bf16[72,256]{1,0:T(8,128)(2,1)S(1)}, u32[]{:S(2)}, u32[]{:S(2)}) collective-permute-start(bf16[72,256]{1,0:T(8,128)(2,1)} %get-tuple-element.26), channel_id=1, source_target_pairs={{0,4},{4,0},{8,12},{12,8},{1,5},{5,1},{9,13},{13,9},{2,6},{6,2},{1... | collective-permute-start | bytes 110600 | tf_op jit(solution)/shard_map/ppermute | solution.py:202
  8.7 6.0 %collective-permute-start.6 = (bf16[72,256]{1,0:T(8,128)(2,1)}, bf16[72,256]{1,0:T(8,128)(2,1)S(1)}, u32[]{:S(2)}, u32[]{:S(2)}) collective-permute-start(bf16[72,256]{1,0:T(8,128)(2,1)} %get-tuple-element.29), channel_id=1, source_target_pairs={{0,12},{4,8},{8,4},{12,0},{1,13},{5,9},{9,5},{13,1},{2,14},{6,10},... | collective-permute-start | bytes 110600 | tf_op jit(solution)/shard_map/ppermute | solution.py:202
  11.2 1.6 %collective-permute-start.5 = (bf16[1,256,256]{2,1,0:T(8,128)(2,1)S(1)}, bf16[1,256,256]{2,1,0:T(8,128)(2,1)S(1)}, u32[]{:S(2)}, u32[]{:S(2)}) collective-permute-start(bf16[1,256,256]{2,1,0:T(8,128)(2,1)S(1)} %collective-permute-done.refs_0_.refs_5_), channel_id=1, source_target_pairs={{0,1},{1,0},{2,3},{3,2},{4,5},{5,4},{6,7},{7,6},{8,9},{9,8},{10,11... | collective-permute-start | bytes 393224 | tf_op jit(solution)/shard_map/ppermute | solution.py:231
  11.2 4.6 %collective-permute-start.2 = (bf16[1,256,256]{2,1,0:T(8,128)(2,1)S(1)}, bf16[1,256,256]{2,1,0:T(8,128)(2,1)S(1)}, u32[]{:S(2)}, u32[]{:S(2)}) collective-permute-start(bf16[1,256,256]{2,1,0:T(8,128)(2,1)S(1)} %collective-permute-done.refs_0_.refs_5_), channel_id=1, source_target_pairs={{0,5},{1,0},{4,1},{5,4},{8,13},{9,8},{12,9},{13,12},{2,7},{3,2},{6... | collective-permute-start | bytes 393224 | tf_op jit(solution)/shard_map/ppermute | solution.py:230
  12.8 1.8 %collective-permute-start.7 = (bf16[72,256]{1,0:T(8,128)(2,1)S(1)}, bf16[72,256]{1,0:T(8,128)(2,1)S(1)}, u32[]{:S(2)}, u32[]{:S(2)}) collective-permute-start(bf16[72,256]{1,0:T(8,128)(2,1)S(1)} %collective-permute-done.3.refs_2_), channel_id=1, source_target_pairs={{0,1},{1,0},{2,3},{3,2},{4,5},{5,4},{6,7},{7,6},{8,9},{9,8},{10,11... | collective-permute-start | bytes 110600 | tf_op jit(solution)/shard_map/ppermute | solution.py:237
  12.9 1.8 %collective-permute-start.8 = (bf16[72,256]{1,0:T(8,128)(2,1)S(1)}, bf16[72,256]{1,0:T(8,128)(2,1)S(1)}, u32[]{:S(2)}, u32[]{:S(2)}) collective-permute-start(bf16[72,256]{1,0:T(8,128)(2,1)S(1)} %collective-permute-done.4.refs_6_), channel_id=1, source_target_pairs={{0,1},{1,0},{2,3},{3,2},{4,5},{5,4},{6,7},{7,6},{8,9},{9,8},{10,11... | collective-permute-start | bytes 110600 | tf_op jit(solution)/shard_map/ppermute | solution.py:237
  14.7 2.6 %copy-start = (bf16[256,256]{1,0:T(8,128)(2,1)S(1)}, bf16[256,256]{1,0:T(8,128)(2,1)}, u32[]{:S(2)}) copy-start(bf16[256,256]{1,0:T(8,128)(2,1)} %projection_ref.1) | copy-start | bytes 393220
  15.8 1.5 %collective-permute-start.9 = (bf16[1,256,256]{2,1,0:T(8,128)(2,1)S(1)}, bf16[1,256,256]{2,1,0:T(8,128)(2,1)S(1)}, u32[]{:S(2)}, u32[]{:S(2)}) collective-permute-start(bf16[1,256,256]{2,1,0:T(8,128)(2,1)S(1)} %collective-permute-done.2.refs_1_), channel_id=1, source_target_pairs={{0,1},{1,0},{2,3},{3,2},{4,5},{5,4},{6,7},{7,6},{8,9},{9,8},{10,11... | collective-permute-start | bytes 393224 | tf_op jit(solution)/shard_map/ppermute | solution.py:237
  16.1 1.2 %collective-permute-start.10 = (bf16[72,256]{1,0:T(8,128)(2,1)S(1)}, bf16[72,256]{1,0:T(8,128)(2,1)S(1)}, u32[]{:S(2)}, u32[]{:S(2)}) collective-permute-start(bf16[72,256]{1,0:T(8,128)(2,1)S(1)} %collective-permute-done.6.refs_2_), channel_id=1, source_target_pairs={{0,1},{1,0},{2,3},{3,2},{4,5},{5,4},{6,7},{7,6},{8,9},{9,8},{10,11... | collective-permute-start | bytes 110600 | tf_op jit(solution)/shard_map/ppermute | solution.py:237

commit v14 on v13

--- a/solution.py
+++ b/solution.py
@@ -8,7 +8,7 @@
 from jax.sharding import PartitionSpec as P
 
 ROW_TILE = 16
-SLOT_ROWS = 8
+SLOT_ROWS = 16
 VMEM = pl.BlockSpec(memory_space=pltpu.VMEM)
 HBM = pl.BlockSpec(memory_space=pltpu.HBM)
 SMEM = pl.BlockSpec(memory_space=pltpu.SMEM)
@@ -19,8 +19,17 @@
 WORK = pl.CostEstimate(flops=4_000_000_000, bytes_accessed=8 * MIB, transcendentals=0)
 
 
-def pack_kernel(partners, owner_ref, slot_ref, scale_ref, section_ref, *packs):
-    rows, dof_count = packs[0].shape
+def pack_kernel(partners, owner_any, slot_any, scale_any, section_ref, *refs):
+    packs, (owner_ref, slot_ref, scale_ref, packed_ref, fetch_sems, sems) = refs[:-6], refs[-6:]
+    fetches = [
+        pltpu.make_async_copy(source, target, fetch_sems.at[i])
+        for i, (source, target) in enumerate(
+            [(owner_any, owner_ref), (slot_any, slot_ref), (scale_any, scale_ref)]
+        )
+    ]
+    for fetch in fetches:
+        fetch.start()
+    _, rows, dof_count = packed_ref.shape
     rows -= SLOT_ROWS
     faces = owner_ref.shape[1]
     sign = (1 - 2 * section_ref[0]).astype(jnp.float32)
@@ -28,28 +37,32 @@
     owners = jnp.concatenate(
         [jnp.full((1, faces), here ^ partner, jnp.int32) for partner in partners], axis=0
     )
-    named = owners == owner_ref[...]
     earlier = lax.broadcasted_iota(jnp.int32, (faces, faces), 0) < lax.broadcasted_iota(
         jnp.int32, (faces, faces), 1
     )
-    rank = jnp.dot(
-        named.astype(jnp.bfloat16), earlier.astype(jnp.bfloat16), preferred_element_type=jnp.float32
-    )
+    earlier = earlier.astype(jnp.bfloat16)
+    at = lax.broadcasted_iota(jnp.int32, (rows, faces), 0).astype(jnp.float32)
+    fetches[0].wait()
+    named = owners == owner_ref[...]
+    rank = jnp.dot(named.astype(jnp.bfloat16), earlier, preferred_element_type=jnp.float32)
     place = jnp.where(named, rank, -1.0)
-    at = lax.broadcasted_iota(jnp.int32, (rows, faces), 0).astype(jnp.float32)
-    hit = jnp.concatenate([place[p : p + 1, :] == at for p in range(len(packs))], axis=0)
-    hit = hit.astype(jnp.bfloat16)
-    packed = jnp.dot(hit, scale_ref[...], preferred_element_type=jnp.float32) * sign
-    listed = lax.dot_general(
-        slot_ref[...].astype(jnp.bfloat16), hit, (((1,), (1,)), ((), ())), preferred_element_type=jnp.float32
-    )
-    packed = packed.astype(jnp.bfloat16)
-    for p, pack_ref in enumerate(packs):
-        pack_ref[:rows, :] = packed[p * rows : (p + 1) * rows, :]
-        meta = jnp.concatenate(
-            [listed[:, p * rows : (p + 1) * rows], jnp.zeros((1, dof_count - rows), jnp.float32)], axis=1
-        )
-        pack_ref[rows:, :] = jnp.broadcast_to(meta, (SLOT_ROWS, dof_count)).astype(jnp.bfloat16)
+    fetches[1].wait()
+    slots = slot_ref[...].astype(jnp.bfloat16)
+    fetches[2].wait()
+    copies = []
+    for p in [*range(1, len(partners)), 0]:
+        hit = (place[p : p + 1, :] == at).astype(jnp.bfloat16)
+        packed = jnp.dot(hit, scale_ref[...], preferred_element_type=jnp.float32) * sign
+        listed = lax.dot_general(
+            slots, hit, (((1,), (1,)), ((), ())), preferred_element_type=jnp.float32
+        )
+        meta = jnp.concatenate([listed, jnp.zeros((1, dof_count - rows), jnp.float32)], axis=1)
+        packed_ref[p, :rows, :] = packed.astype(jnp.bfloat16)
+        packed_ref[p, rows:, :] = jnp.broadcast_to(meta, (SLOT_ROWS, dof_count)).astype(jnp.bfloat16)
+        copies.append(pltpu.make_async_copy(packed_ref.at[p], packs[p], sems.at[p]))
+        copies[-1].start()
+    for copy in copies:
+        copy.wait()
 
 
 def block_weights(packs, rows, blocks_own):
@@ -192,8 +205,16 @@
     packs = pl.pallas_call(
         functools.partial(pack_kernel, partners),
         out_shape=[jax.ShapeDtypeStruct((pack_rows, dof_count), jnp.bfloat16)] * len(partners),
-        in_specs=[VMEM, VMEM, VMEM, SMEM],
-        out_specs=[VMEM] * len(partners),
+        in_specs=[HBM, HBM, HBM, SMEM],
+        out_specs=[HBM] * len(partners),
+        scratch_shapes=[
+            pltpu.VMEM((1, faces_dev), jnp.int32),
+            pltpu.VMEM((1, faces_dev), jnp.int32),
+            pltpu.VMEM((faces_dev, dof_count), jnp.bfloat16),
+            pltpu.VMEM((len(partners), pack_rows, dof_count), jnp.bfloat16),
+            pltpu.SemaphoreType.DMA((3,)),
+            pltpu.SemaphoreType.DMA((len(partners),)),
+        ],
         cost_estimate=WORK,
         name="pack_weights",
     )(*faces, section)

time: 19.3 us -> 19.4 us (level)
  no operation moved by 1% of the time
where the time goes in v14:
time: 19.4 us; the launch traced here: 19.2 us
  starting transfers between devices  10.5 us (54%)
  Pallas kernels  5.67 us (29%)
  waiting for transfers between devices  2.22 us (11%)
  between operations  0.82 us (4%)
    ppermute x3, starting transfers between devices, on_device(): lax.ppermute(pack, 'sub', [(i, i ^ p) for i in range(subdomains)])  4.45 us
    ppermute x1, starting transfers between devices, on_device(): lax.ppermute(basis, ('sub', 'face'), [(flat(s, face), flat(s ^ (1 if face...  4.04 us
    pallas_call x1, Pallas kernels, on_device(): pl.pallas_call(functools.partial(pack_kernel, partners), out_shape=[jax.S...  1.89 us
    pallas_call x1, Pallas kernels, on_device(): pl.pallas_call(last_kernel, out_shape=jax.ShapeDtypeStruct(block_shape, j...  1.86 us
    ppermute x3, waiting for transfers between devices, on_device(): lax.ppermute(pack, 'sub', [(i, i ^ p) for i in range(subdomains)])  1.3 us
    ppermute x4, starting transfers between devices, with_swapped(): return [(array, lax.ppermute(array, 'face', swap)) for array in arrays]  1.14 us
    pallas_call x1, Pallas kernels, on_device(): pl.pallas_call(stage_kernel, out_shape=jax.ShapeDtypeStruct(block_shape,...  1.14 us
    ppermute x4, waiting for transfers between devices, with_swapped(): return [(array, lax.ppermute(array, 'face', swap)) for array in arrays]  0.9 us
  transfers between devices with their start and end apart: 11, of which 2 were waited for; matrix products, arithmetic and copies ran while one was open for 0% of the time, Pallas kernels for 20%

profile of v14, /device:TPU:0, one launch (start us, length us, event | category | flops | bytes accessed | tf_op | source)
XLA Modules:
  0.0 19.2 jit_solution(12686639170666492940)
XLA Ops:
  0.0 4.0 %collective-permute-start = (bf16[1,256,256]{2,1,0:T(8,128)(2,1)}, bf16[1,256,256]{2,1,0:T(8,128)(2,1)S(1)}, u32[]{:S(2)}, u32[]{:S(2)}) collective-permute-start(bf16[1,256,256]{2,1,0:T(8,128)(2,1)} %basis_ref.1), channel_id=1, source_target_pairs={{0,8},{1,5},{4,12},{5,1},{8,0},{9,13},{12,4},{13,9},{2,10},{3,7},{... | collective-permute-start | bytes 393224 | tf_op jit(solution)/shard_map/ppermute | solution.py:197
  4.7 0.0 copy-start.1
  4.7 0.0 copy-start.2
  4.7 0.0 copy-start.3
  4.7 0.0 copy-start.4
  4.7 0.0 copy-start.5
  4.7 0.0 copy-start.6
  4.7 0.0 copy-start.7
  4.8 1.9 %pack_weights.1 = (bf16[80,256]{1,0:T(8,128)(2,1)}, bf16[80,256]{1,0:T(8,128)(2,1)}, bf16[80,256]{1,0:T(8,128)(2,1)}, bf16[80,256]{1,0:T(8,128)(2,1)}) custom-call(s32[1,128]{1,0:T(1,128)} %bitcast.6, s32[1,128]{1,0:T(1,128)} %bitcast.8, bf16[128,256]{1,0:T(8,128)(2,1)} %scale_ref.1, s32[1]{0:T(128)S(6)} %copy.12.section_ref), custom_call_target="tpu_custom_call" | custom-call | flops 4000000000 | bytes 8388608 | tf_op jit(solution)/shard_map/pack_weights/pallas_call | solution.py:205
  6.7 0.1 collective-permute-start.1
  6.7 1.1 %collective-permute-start.3 = (bf16[80,256]{1,0:T(8,128)(2,1)}, bf16[80,256]{1,0:T(8,128)(2,1)S(1)}, u32[]{:S(2)}, u32[]{:S(2)}) collective-permute-start(bf16[80,256]{1,0:T(8,128)(2,1)} %get-tuple-element.25), channel_id=1, source_target_pairs={{0,8},{4,12},{8,0},{12,4},{1,9},{5,13},{9,1},{13,5},{2,10},{6,14},... | collective-permute-start | bytes 122888 | tf_op jit(solution)/shard_map/ppermute | solution.py:223
  7.9 0.9 %collective-permute-start.4 = (bf16[80,256]{1,0:T(8,128)(2,1)}, bf16[80,256]{1,0:T(8,128)(2,1)S(1)}, u32[]{:S(2)}, u32[]{:S(2)}) collective-permute-start(bf16[80,256]{1,0:T(8,128)(2,1)} %get-tuple-element.26), channel_id=1, source_target_pairs={{0,4},{4,0},{8,12},{12,8},{1,5},{5,1},{9,13},{13,9},{2,6},{6,2},{1... | collective-permute-start | bytes 122888 | tf_op jit(solution)/shard_map/ppermute | solution.py:223
  8.7 2.5 %collective-permute-start.6 = (bf16[80,256]{1,0:T(8,128)(2,1)}, bf16[80,256]{1,0:T(8,128)(2,1)S(1)}, u32[]{:S(2)}, u32[]{:S(2)}) collective-permute-start(bf16[80,256]{1,0:T(8,128)(2,1)} %get-tuple-element.29), channel_id=1, source_target_pairs={{0,12},{4,8},{8,4},{12,0},{1,13},{5,9},{9,5},{13,1},{2,14},{6,10},... | collective-permute-start | bytes 122888 | tf_op jit(solution)/shard_map/ppermute | solution.py:223
  11.2 0.0 collective-permute-done.1.swapped_ref
  11.2 0.0 collective-permute-done.refs_0_.refs_5_
  11.2 0.0 collective-permute-start.5
  11.2 0.8 %collective-permute-start.2 = (bf16[1,256,256]{2,1,0:T(8,128)(2,1)S(1)}, bf16[1,256,256]{2,1,0:T(8,128)(2,1)S(1)}, u32[]{:S(2)}, u32[]{:S(2)}) collective-permute-start(bf16[1,256,256]{2,1,0:T(8,128)(2,1)S(1)} %collective-permute-done.refs_0_.refs_5_), channel_id=1, source_target_pairs={{0,5},{1,0},{4,1},{5,4},{8,13},{9,8},{12,9},{13,12},{2,7},{3,2},{6... | collective-permute-start | bytes 393224 | tf_op jit(solution)/shard_map/ppermute | solution.py:251
  12.0 0.0 copy-done.1
  12.0 0.0 copy-done.2
  12.0 0.0 copy-done.3
  12.0 0.0 copy-done.4
  12.0 0.0 copy-done.5
  12.0 0.0 copy-done.6
  12.0 0.0 copy-done.7
  12.0 0.8 %own_blocks.1 = (bf16[64,32,256]{2,1,0:T(8,128)(2,1)S(1)}, f32[64,32,256]{2,1,0:T(8,128)S(1)}) custom-call(bf16[128,32,256]{2,1,0:T(8,128)(2,1)S(1)} %copy-done.1, f32[1,32]{1,0:T(1,128)S(1)} %bitcast.4, s32[1,32]{1,0:T(1,128)S(1)} %bitcast.5, s32[1,128]{1,0:T(1,128)S(1)} %bitcast.7, s32[1,128]{1,0:T(1,128)S(1)} %bitcast.9, bf16[128,256]{1,0:T(8,128)(2,1)S(1)} %copy-done.3, ...), custom_call_target="tpu_custom_call" | custom-call | flops 4000000000 | bytes 8388608 | tf_op jit(solution)/shard_map/own_blocks/pallas_call | solution.py:228
  12.8 0.0 collective-permute-done.3.refs_2_
  12.8 0.0 collective-permute-done.4.refs_6_
  12.8 0.0 collective-permute-done.5.refs_1_.refs_4_
  12.8 0.1 collective-permute-start.7
  12.9 0.5 %collective-permute-start.8 = (bf16[80,256]{1,0:T(8,128)(2,1)S(1)}, bf16[80,256]{1,0:T(8,128)(2,1)S(1)}, u32[]{:S(2)}, u32[]{:S(2)}) collective-permute-start(bf16[80,256]{1,0:T(8,128)(2,1)S(1)} %collective-permute-done.4.refs_6_), channel_id=1, source_target_pairs={{0,1},{1,0},{2,3},{3,2},{4,5},{5,4},{6,7},{7,6},{8,9},{9,8},{10,11... | collective-permute-start | bytes 122888 | tf_op jit(solution)/shard_map/ppermute | solution.py:258
  13.4 1.3 %collective-permute-done.6.refs_2_ = bf16[80,256]{1,0:T(8,128)(2,1)S(1)} collective-permute-done((bf16[80,256]{1,0:T(8,128)(2,1)}, bf16[80,256]{1,0:T(8,128)(2,1)S(1)}, u32[]{:S(2)}, u32[]{:S(2)}) %collective-permute-start.6) | collective-permute-done | bytes 40992 | tf_op jit(solution)/shard_map/ppermute | solution.py:223
  14.7 0.0 collective-permute-done.7.refs_3_
  14.7 0.0 collective-permute-done.8.refs_7_
  14.7 0.0 copy-start
  14.7 1.1 %stage.1.sum_ref = f32[64,32,256]{2,1,0:T(8,128)S(1)} custom-call(bf16[64,32,256]{2,1,0:T(8,128)(2,1)S(1)} %get-tuple-element.23.pumped_ref, f32[64,32,256]{2,1,0:T(8,128)S(1)} %get-tuple-element.30.sum_ref, bf16[1,256,256]{2,1,0:T(8,128)(2,1)S(1)} %collective-permute-done.refs_0_.refs_5_, ...), custom_call_target="tpu_custom_call", output_to_operand_aliasing={{}: (1, {})} | custom-call | flops 1000000 | bytes 1024 | tf_op jit(solution)/shard_map/stage/pallas_call | solution.py:274
  15.9 0.0 collective-permute-done.2.refs_1_
  15.9 0.2 %collective-permute-start.9 = (bf16[1,256,256]{2,1,0:T(8,128)(2,1)S(1)}, bf16[1,256,256]{2,1,0:T(8,128)(2,1)S(1)}, u32[]{:S(2)}, u32[]{:S(2)}) collective-permute-start(bf16[1,256,256]{2,1,0:T(8,128)(2,1)S(1)} %collective-permute-done.2.refs_1_), channel_id=1, source_target_pairs={{0,1},{1,0},{2,3},{3,2},{4,5},{5,4},{6,7},{7,6},{8,9},{9,8},{10,11... | collective-permute-start | bytes 393224 | tf_op jit(solution)/shard_map/ppermute | solution.py:258
  16.1 0.4 %collective-permute-start.10 = (bf16[80,256]{1,0:T(8,128)(2,1)S(1)}, bf16[80,256]{1,0:T(8,128)(2,1)S(1)}, u32[]{:S(2)}, u32[]{:S(2)}) collective-permute-start(bf16[80,256]{1,0:T(8,128)(2,1)S(1)} %collective-permute-done.6.refs_2_), channel_id=1, source_target_pairs={{0,1},{1,0},{2,3},{3,2},{4,5},{5,4},{6,7},{7,6},{8,9},{9,8},{10,11... | collective-permute-start | bytes 122888 | tf_op jit(solution)/shard_map/ppermute | solution.py:258
  16.5 0.9 %collective-permute-done.10.refs_3_ = bf16[80,256]{1,0:T(8,128)(2,1)S(1)} collective-permute-done((bf16[80,256]{1,0:T(8,128)(2,1)S(1)}, bf16[80,256]{1,0:T(8,128)(2,1)S(1)}, u32[]{:S(2)}, u32[]{:S(2)}) %collective-permute-start.10) | collective-permute-done | bytes 40992 | tf_op jit(solution)/shard_map/ppermute | solution.py:258
  17.4 0.0 collective-permute-done.9.refs_0_
  17.4 0.0 copy-done
  17.4 1.9 %last_stage.1 = f32[64,32,256]{2,1,0:T(8,128)} custom-call(bf16[64,32,256]{2,1,0:T(8,128)(2,1)S(1)} %get-tuple-element.23.pumped_ref, f32[64,32,256]{2,1,0:T(8,128)S(1)} %stage.1.sum_ref, bf16[256,256]{1,0:T(8,128)(2,1)S(1)} %copy-done, bf16[1,256,256]{2,1,0:T(8,128)(2,1)S(1)} %collective-permute-done.9.refs_0_, ...), custom_call_target="tpu_custom_call" | custom-call | tf_op jit(solution)/shard_map/last_stage/pallas_call | solution.py:290
Async XLA Ops:
  0.0 11.2 %collective-permute-start = (bf16[1,256,256]{2,1,0:T(8,128)(2,1)}, bf16[1,256,256]{2,1,0:T(8,128)(2,1)S(1)}, u32[]{:S(2)}, u32[]{:S(2)}) collective-permute-start(bf16[1,256,256]{2,1,0:T(8,128)(2,1)} %basis_ref.1), channel_id=1, source_target_pairs={{0,8},{1,5},{4,12},{5,1},{8,0},{9,13},{12,4},{13,9},{2,10},{3,7},{... | collective-permute-start | bytes 393224 | tf_op jit(solution)/shard_map/ppermute | solution.py:197
  4.7 7.3 %copy-start.1 = (bf16[128,32,256]{2,1,0:T(8,128)(2,1)S(1)}, bf16[128,32,256]{2,1,0:T(8,128)(2,1)}, u32[]{:S(2)}) copy-start(bf16[128,32,256]{2,1,0:T(8,128)(2,1)} %mortar_ref.1) | copy-start | bytes 6291460
  4.7 7.3 %copy-start.2 = (bf16[1,256,256]{2,1,0:T(8,128)(2,1)S(1)}, bf16[1,256,256]{2,1,0:T(8,128)(2,1)}, u32[]{:S(2)}) copy-start(bf16[1,256,256]{2,1,0:T(8,128)(2,1)} %basis_ref.1) | copy-start | bytes 393220
  4.7 7.3 %copy-start.3 = (bf16[128,256]{1,0:T(8,128)(2,1)S(1)}, bf16[128,256]{1,0:T(8,128)(2,1)}, u32[]{:S(2)}) copy-start(bf16[128,256]{1,0:T(8,128)(2,1)} %scale_ref.1) | copy-start | bytes 196612
  4.7 7.3 %copy-start.4 = (f32[32]{0:T(128)S(1)}, f32[32]{0:T(128)}, u32[]{:S(2)}) copy-start(f32[32]{0:T(128)} %param.10) | copy-start | bytes 388
  4.7 7.3 %copy-start.5 = (s32[32]{0:T(128)S(1)}, s32[32]{0:T(128)}, u32[]{:S(2)}) copy-start(s32[32]{0:T(128)} %param.11) | copy-start | bytes 388
  4.7 7.3 %copy-start.6 = (s32[128,1]{0,1:T(1,128)S(1)}, s32[128,1]{0,1:T(1,128)}, u32[]{:S(2)}) copy-start(s32[128,1]{0,1:T(1,128)} %param.12) | copy-start | bytes 1540
  4.7 7.3 %copy-start.7 = (s32[128]{0:T(128)S(1)}, s32[128]{0:T(128)}, u32[]{:S(2)}) copy-start(s32[128]{0:T(128)} %param.13) | copy-start | bytes 1540
  6.7 4.5 %collective-permute-start.1 = (bf16[80,256]{1,0:T(8,128)(2,1)}, bf16[80,256]{1,0:T(8,128)(2,1)S(1)}, u32[]{:S(2)}, u32[]{:S(2)}) collective-permute-start(bf16[80,256]{1,0:T(8,128)(2,1)} %get-tuple-element.21), channel_id=1, source_target_pairs={{0,1},{1,0},{2,3},{3,2},{4,5},{5,4},{6,7},{7,6},{8,9},{9,8},{10,11... | collective-permute-start | bytes 122888 | tf_op jit(solution)/shard_map/ppermute | solution.py:225
  6.7 6.1 %collective-permute-start.3 = (bf16[80,256]{1,0:T(8,128)(2,1)}, bf16[80,256]{1,0:T(8,128)(2,1)S(1)}, u32[]{:S(2)}, u32[]{:S(2)}) collective-permute-start(bf16[80,256]{1,0:T(8,128)(2,1)} %get-tuple-element.25), channel_id=1, source_target_pairs={{0,8},{4,12},{8,0},{12,4},{1,9},{5,13},{9,1},{13,5},{2,10},{6,14},... | collective-permute-start | bytes 122888 | tf_op jit(solution)/shard_map/ppermute | solution.py:223
  7.9 5.0 %collective-permute-start.4 = (bf16[80,256]{1,0:T(8,128)(2,1)}, bf16[80,256]{1,0:T(8,128)(2,1)S(1)}, u32[]{:S(2)}, u32[]{:S(2)}) collective-permute-start(bf16[80,256]{1,0:T(8,128)(2,1)} %get-tuple-element.26), channel_id=1, source_target_pairs={{0,4},{4,0},{8,12},{12,8},{1,5},{5,1},{9,13},{13,9},{2,6},{6,2},{1... | collective-permute-start | bytes 122888 | tf_op jit(solution)/shard_map/ppermute | solution.py:223
  8.7 6.0 %collective-permute-start.6 = (bf16[80,256]{1,0:T(8,128)(2,1)}, bf16[80,256]{1,0:T(8,128)(2,1)S(1)}, u32[]{:S(2)}, u32[]{:S(2)}) collective-permute-start(bf16[80,256]{1,0:T(8,128)(2,1)} %get-tuple-element.29), channel_id=1, source_target_pairs={{0,12},{4,8},{8,4},{12,0},{1,13},{5,9},{9,5},{13,1},{2,14},{6,10},... | collective-permute-start | bytes 122888 | tf_op jit(solution)/shard_map/ppermute | solution.py:223
  11.2 1.6 %collective-permute-start.5 = (bf16[1,256,256]{2,1,0:T(8,128)(2,1)S(1)}, bf16[1,256,256]{2,1,0:T(8,128)(2,1)S(1)}, u32[]{:S(2)}, u32[]{:S(2)}) collective-permute-start(bf16[1,256,256]{2,1,0:T(8,128)(2,1)S(1)} %collective-permute-done.refs_0_.refs_5_), channel_id=1, source_target_pairs={{0,1},{1,0},{2,3},{3,2},{4,5},{5,4},{6,7},{7,6},{8,9},{9,8},{10,11... | collective-permute-start | bytes 393224 | tf_op jit(solution)/shard_map/ppermute | solution.py:252
  11.2 4.7 %collective-permute-start.2 = (bf16[1,256,256]{2,1,0:T(8,128)(2,1)S(1)}, bf16[1,256,256]{2,1,0:T(8,128)(2,1)S(1)}, u32[]{:S(2)}, u32[]{:S(2)}) collective-permute-start(bf16[1,256,256]{2,1,0:T(8,128)(2,1)S(1)} %collective-permute-done.refs_0_.refs_5_), channel_id=1, source_target_pairs={{0,5},{1,0},{4,1},{5,4},{8,13},{9,8},{12,9},{13,12},{2,7},{3,2},{6... | collective-permute-start | bytes 393224 | tf_op jit(solution)/shard_map/ppermute | solution.py:251
  12.8 1.9 %collective-permute-start.7 = (bf16[80,256]{1,0:T(8,128)(2,1)S(1)}, bf16[80,256]{1,0:T(8,128)(2,1)S(1)}, u32[]{:S(2)}, u32[]{:S(2)}) collective-permute-start(bf16[80,256]{1,0:T(8,128)(2,1)S(1)} %collective-permute-done.3.refs_2_), channel_id=1, source_target_pairs={{0,1},{1,0},{2,3},{3,2},{4,5},{5,4},{6,7},{7,6},{8,9},{9,8},{10,11... | collective-permute-start | bytes 122888 | tf_op jit(solution)/shard_map/ppermute | solution.py:258
  12.9 1.8 %collective-permute-start.8 = (bf16[80,256]{1,0:T(8,128)(2,1)S(1)}, bf16[80,256]{1,0:T(8,128)(2,1)S(1)}, u32[]{:S(2)}, u32[]{:S(2)}) collective-permute-start(bf16[80,256]{1,0:T(8,128)(2,1)S(1)} %collective-permute-done.4.refs_6_), channel_id=1, source_target_pairs={{0,1},{1,0},{2,3},{3,2},{4,5},{5,4},{6,7},{7,6},{8,9},{9,8},{10,11... | collective-permute-start | bytes 122888 | tf_op jit(solution)/shard_map/ppermute | solution.py:258
  14.7 2.6 %copy-start = (bf16[256,256]{1,0:T(8,128)(2,1)S(1)}, bf16[256,256]{1,0:T(8,128)(2,1)}, u32[]{:S(2)}) copy-start(bf16[256,256]{1,0:T(8,128)(2,1)} %projection_ref.1) | copy-start | bytes 393220
  15.9 1.5 %collective-permute-start.9 = (bf16[1,256,256]{2,1,0:T(8,128)(2,1)S(1)}, bf16[1,256,256]{2,1,0:T(8,128)(2,1)S(1)}, u32[]{:S(2)}, u32[]{:S(2)}) collective-permute-start(bf16[1,256,256]{2,1,0:T(8,128)(2,1)S(1)} %collective-permute-done.2.refs_1_), channel_id=1, source_target_pairs={{0,1},{1,0},{2,3},{3,2},{4,5},{5,4},{6,7},{7,6},{8,9},{9,8},{10,11... | collective-permute-start | bytes 393224 | tf_op jit(solution)/shard_map/ppermute | solution.py:258
  16.1 1.3 %collective-permute-start.10 = (bf16[80,256]{1,0:T(8,128)(2,1)S(1)}, bf16[80,256]{1,0:T(8,128)(2,1)S(1)}, u32[]{:S(2)}, u32[]{:S(2)}) collective-permute-start(bf16[80,256]{1,0:T(8,128)(2,1)S(1)} %collective-permute-done.6.refs_2_), channel_id=1, source_target_pairs={{0,1},{1,0},{2,3},{3,2},{4,5},{5,4},{6,7},{7,6},{8,9},{9,8},{10,11... | collective-permute-start | bytes 122888 | tf_op jit(solution)/shard_map/ppermute | solution.py:258

commit v15 on v13

--- a/solution.py
+++ b/solution.py
@@ -8,7 +8,7 @@
 from jax.sharding import PartitionSpec as P
 
 ROW_TILE = 16
-SLOT_ROWS = 8
+SLOT_ROWS = 16
 VMEM = pl.BlockSpec(memory_space=pltpu.VMEM)
 HBM = pl.BlockSpec(memory_space=pltpu.HBM)
 SMEM = pl.BlockSpec(memory_space=pltpu.SMEM)
@@ -191,7 +191,7 @@
     faces = [face_owner.reshape(1, faces_dev), face_slot.reshape(1, faces_dev), face_scale]
     packs = pl.pallas_call(
         functools.partial(pack_kernel, partners),
-        out_shape=[jax.ShapeDtypeStruct((pack_rows, dof_count), jnp.bfloat16)] * len(partners),
+        out_shape=[pltpu.VMEM((pack_rows, dof_count), jnp.bfloat16)] * len(partners),
         in_specs=[VMEM, VMEM, VMEM, SMEM],
         out_specs=[VMEM] * len(partners),
         cost_estimate=WORK,

time: 19.3 us -> 18.8 us (0.974)
  Pallas kernels: 5.8 us -> 5.14 us
    pallas_call x1, Pallas kernels: 2 us -> 1.36 us  [on_device(): pl.pallas_call(functools.partial(pack_kernel, partners), out_shape=[pltpu...]
  transfers between devices with their start and end apart: 11 -> 11, of which waited for: 2 -> 2; matrix products, arithmetic and copies ran while one was open for 0% -> 0% of each run, Pallas kernels for 20% -> 18%
where the time goes in v15:
time: 18.8 us; the launch traced here: 18.6 us
  starting transfers between devices  10.5 us (56%)
  Pallas kernels  5.14 us (27%)
  waiting for transfers between devices  2.18 us (12%)
  between operations  0.81 us (4%)
    ppermute x3, starting transfers between devices, on_device(): lax.ppermute(pack, 'sub', [(i, i ^ p) for i in range(subdomains)])  4.45 us
    ppermute x1, starting transfers between devices, on_device(): lax.ppermute(basis, ('sub', 'face'), [(flat(s, face), flat(s ^ (1 if face...  4.04 us
    pallas_call x1, Pallas kernels, on_device(): pl.pallas_call(last_kernel, out_shape=jax.ShapeDtypeStruct(block_shape, j...  1.86 us
    pallas_call x1, Pallas kernels, on_device(): pl.pallas_call(functools.partial(pack_kernel, partners), out_shape=[pltpu...  1.36 us
    ppermute x4, starting transfers between devices, with_swapped(): return [(array, lax.ppermute(array, 'face', swap)) for array in arrays]  1.14 us
    pallas_call x1, Pallas kernels, on_device(): pl.pallas_call(stage_kernel, out_shape=jax.ShapeDtypeStruct(block_shape,...  1.14 us
    ppermute x3, waiting for transfers between devices, on_device(): lax.ppermute(pack, 'sub', [(i, i ^ p) for i in range(subdomains)])  1.09 us
    ppermute x4, waiting for transfers between devices, with_swapped(): return [(array, lax.ppermute(array, 'face', swap)) for array in arrays]  1.07 us
  transfers between devices with their start and end apart: 11, of which 2 were waited for; matrix products, arithmetic and copies ran while one was open for 0% of the time, Pallas kernels for 18%

profile of v15, /device:TPU:0, one launch (start us, length us, event | category | flops | bytes accessed | tf_op | source)
XLA Modules:
  0.0 18.6 jit_solution(1507869272181731364)
XLA Ops:
  0.0 4.0 %collective-permute-start = (bf16[1,256,256]{2,1,0:T(8,128)(2,1)}, bf16[1,256,256]{2,1,0:T(8,128)(2,1)S(1)}, u32[]{:S(2)}, u32[]{:S(2)}) collective-permute-start(bf16[1,256,256]{2,1,0:T(8,128)(2,1)} %basis_ref.1), channel_id=1, source_target_pairs={{0,8},{1,5},{4,12},{5,1},{8,0},{9,13},{12,4},{13,9},{2,10},{3,7},{... | collective-permute-start | bytes 393224 | tf_op jit(solution)/shard_map/ppermute | solution.py:184
  4.7 0.0 copy-start.1
  4.7 0.0 copy-start.2
  4.7 0.0 copy-start.3
  4.7 0.0 copy-start.4
  4.7 0.0 copy-start.5
  4.7 0.0 copy-start.6
  4.7 0.0 copy-start.7
  4.8 1.4 %pack_weights.1 = (bf16[80,256]{1,0:T(8,128)(2,1)S(1)}, bf16[80,256]{1,0:T(8,128)(2,1)S(1)}, bf16[80,256]{1,0:T(8,128)(2,1)S(1)}, bf16[80,256]{1,0:T(8,128)(2,1)S(1)}) custom-call(s32[1,128]{1,0:T(1,128)} %bitcast.6, s32[1,128]{1,0:T(1,128)} %bitcast.8, bf16[128,256]{1,0:T(8,128)(2,1)} %scale_ref.3, s32[1]{0:T(128)S(6)} %copy.12.section_ref), custom_call_target="tpu_custom_call" | custom-call | flops 4000000000 | bytes 8388608 | tf_op jit(solution)/shard_map/pack_weights/pallas_call | solution.py:192
  6.1 0.0 collective-permute-start.1
  6.2 1.1 %collective-permute-start.3 = (bf16[80,256]{1,0:T(8,128)(2,1)S(1)}, bf16[80,256]{1,0:T(8,128)(2,1)S(1)}, u32[]{:S(2)}, u32[]{:S(2)}) collective-permute-start(bf16[80,256]{1,0:T(8,128)(2,1)S(1)} %get-tuple-element.25), channel_id=1, source_target_pairs={{0,8},{4,12},{8,0},{12,4},{1,9},{5,13},{9,1},{13,5},{2,10},{6,14},... | collective-permute-start | bytes 122888 | tf_op jit(solution)/shard_map/ppermute | solution.py:202
  7.3 0.9 %collective-permute-start.4 = (bf16[80,256]{1,0:T(8,128)(2,1)S(1)}, bf16[80,256]{1,0:T(8,128)(2,1)S(1)}, u32[]{:S(2)}, u32[]{:S(2)}) collective-permute-start(bf16[80,256]{1,0:T(8,128)(2,1)S(1)} %get-tuple-element.26), channel_id=1, source_target_pairs={{0,4},{4,0},{8,12},{12,8},{1,5},{5,1},{9,13},{13,9},{2,6},{6,2},{1... | collective-permute-start | bytes 122888 | tf_op jit(solution)/shard_map/ppermute | solution.py:202
  8.1 2.5 %collective-permute-start.6 = (bf16[80,256]{1,0:T(8,128)(2,1)S(1)}, bf16[80,256]{1,0:T(8,128)(2,1)S(1)}, u32[]{:S(2)}, u32[]{:S(2)}) collective-permute-start(bf16[80,256]{1,0:T(8,128)(2,1)S(1)} %get-tuple-element.29), channel_id=1, source_target_pairs={{0,12},{4,8},{8,4},{12,0},{1,13},{5,9},{9,5},{13,1},{2,14},{6,10},... | collective-permute-start | bytes 122888 | tf_op jit(solution)/shard_map/ppermute | solution.py:202
  10.6 0.0 collective-permute-done.1.swapped_ref
  10.6 0.0 collective-permute-done.refs_0_.refs_5_
  10.6 0.0 collective-permute-start.5
  10.6 0.8 %collective-permute-start.2 = (bf16[1,256,256]{2,1,0:T(8,128)(2,1)S(1)}, bf16[1,256,256]{2,1,0:T(8,128)(2,1)S(1)}, u32[]{:S(2)}, u32[]{:S(2)}) collective-permute-start(bf16[1,256,256]{2,1,0:T(8,128)(2,1)S(1)} %collective-permute-done.refs_0_.refs_5_), channel_id=1, source_target_pairs={{0,5},{1,0},{4,1},{5,4},{8,13},{9,8},{12,9},{13,12},{2,7},{3,2},{6... | collective-permute-start | bytes 393224 | tf_op jit(solution)/shard_map/ppermute | solution.py:230
  11.4 0.0 copy-done.1
  11.4 0.0 copy-done.2
  11.4 0.0 copy-done.3
  11.4 0.0 copy-done.4
  11.4 0.0 copy-done.5
  11.4 0.0 copy-done.6
  11.5 0.0 copy-done.7
  11.5 0.8 %own_blocks.1 = (bf16[64,32,256]{2,1,0:T(8,128)(2,1)S(1)}, f32[64,32,256]{2,1,0:T(8,128)S(1)}) custom-call(bf16[128,32,256]{2,1,0:T(8,128)(2,1)S(1)} %copy-done.1, f32[1,32]{1,0:T(1,128)S(1)} %bitcast.4, s32[1,32]{1,0:T(1,128)S(1)} %bitcast.5, s32[1,128]{1,0:T(1,128)S(1)} %bitcast.7, s32[1,128]{1,0:T(1,128)S(1)} %bitcast.9, bf16[128,256]{1,0:T(8,128)(2,1)S(1)} %copy-done.3, ...), custom_call_target="tpu_custom_call" | custom-call | flops 4000000000 | bytes 8388608 | tf_op jit(solution)/shard_map/own_blocks/pallas_call | solution.py:207
  12.2 0.0 collective-permute-done.3.refs_2_
  12.3 0.0 collective-permute-done.4.refs_6_
  12.3 0.0 collective-permute-done.5.refs_1_.refs_4_
  12.3 0.1 collective-permute-start.7
  12.4 0.5 %collective-permute-start.8 = (bf16[80,256]{1,0:T(8,128)(2,1)S(1)}, bf16[80,256]{1,0:T(8,128)(2,1)S(1)}, u32[]{:S(2)}, u32[]{:S(2)}) collective-permute-start(bf16[80,256]{1,0:T(8,128)(2,1)S(1)} %collective-permute-done.4.refs_6_), channel_id=1, source_target_pairs={{0,1},{1,0},{2,3},{3,2},{4,5},{5,4},{6,7},{7,6},{8,9},{9,8},{10,11... | collective-permute-start | bytes 122888 | tf_op jit(solution)/shard_map/ppermute | solution.py:237
  12.9 1.1 %collective-permute-done.6.refs_2_ = bf16[80,256]{1,0:T(8,128)(2,1)S(1)} collective-permute-done((bf16[80,256]{1,0:T(8,128)(2,1)S(1)}, bf16[80,256]{1,0:T(8,128)(2,1)S(1)}, u32[]{:S(2)}, u32[]{:S(2)}) %collective-permute-start.6) | collective-permute-done | bytes 40992 | tf_op jit(solution)/shard_map/ppermute | solution.py:202
  13.9 0.0 collective-permute-done.7.refs_3_
  14.0 0.0 collective-permute-done.8.refs_7_
  14.0 0.0 copy-start
  14.0 1.1 %stage.1.sum_ref = f32[64,32,256]{2,1,0:T(8,128)S(1)} custom-call(bf16[64,32,256]{2,1,0:T(8,128)(2,1)S(1)} %get-tuple-element.23.pumped_ref, f32[64,32,256]{2,1,0:T(8,128)S(1)} %get-tuple-element.30.sum_ref, bf16[1,256,256]{2,1,0:T(8,128)(2,1)S(1)} %collective-permute-done.refs_0_.refs_5_, ...), custom_call_target="tpu_custom_call", output_to_operand_aliasing={{}: (1, {})} | custom-call | flops 1000000 | bytes 1024 | tf_op jit(solution)/shard_map/stage/pallas_call | solution.py:253
  15.1 0.0 collective-permute-done.2.refs_1_
  15.1 0.4 %collective-permute-start.9 = (bf16[1,256,256]{2,1,0:T(8,128)(2,1)S(1)}, bf16[1,256,256]{2,1,0:T(8,128)(2,1)S(1)}, u32[]{:S(2)}, u32[]{:S(2)}) collective-permute-start(bf16[1,256,256]{2,1,0:T(8,128)(2,1)S(1)} %collective-permute-done.2.refs_1_), channel_id=1, source_target_pairs={{0,1},{1,0},{2,3},{3,2},{4,5},{5,4},{6,7},{7,6},{8,9},{9,8},{10,11... | collective-permute-start | bytes 393224 | tf_op jit(solution)/shard_map/ppermute | solution.py:237
  15.5 0.2 collective-permute-start.10
  15.7 1.1 %collective-permute-done.10.refs_3_ = bf16[80,256]{1,0:T(8,128)(2,1)S(1)} collective-permute-done((bf16[80,256]{1,0:T(8,128)(2,1)S(1)}, bf16[80,256]{1,0:T(8,128)(2,1)S(1)}, u32[]{:S(2)}, u32[]{:S(2)}) %collective-permute-start.10) | collective-permute-done | bytes 40992 | tf_op jit(solution)/shard_map/ppermute | solution.py:237
  16.8 0.0 collective-permute-done.9.refs_0_
  16.8 0.0 copy-done
  16.8 1.9 %last_stage.1 = f32[64,32,256]{2,1,0:T(8,128)} custom-call(bf16[64,32,256]{2,1,0:T(8,128)(2,1)S(1)} %get-tuple-element.23.pumped_ref, f32[64,32,256]{2,1,0:T(8,128)S(1)} %stage.1.sum_ref, bf16[256,256]{1,0:T(8,128)(2,1)S(1)} %copy-done, bf16[1,256,256]{2,1,0:T(8,128)(2,1)S(1)} %collective-permute-done.9.refs_0_, ...), custom_call_target="tpu_custom_call" | custom-call | tf_op jit(solution)/shard_map/last_stage/pallas_call | solution.py:269
Async XLA Ops:
  0.0 10.6 %collective-permute-start = (bf16[1,256,256]{2,1,0:T(8,128)(2,1)}, bf16[1,256,256]{2,1,0:T(8,128)(2,1)S(1)}, u32[]{:S(2)}, u32[]{:S(2)}) collective-permute-start(bf16[1,256,256]{2,1,0:T(8,128)(2,1)} %basis_ref.1), channel_id=1, source_target_pairs={{0,8},{1,5},{4,12},{5,1},{8,0},{9,13},{12,4},{13,9},{2,10},{3,7},{... | collective-permute-start | bytes 393224 | tf_op jit(solution)/shard_map/ppermute | solution.py:184
  4.7 6.7 %copy-start.1 = (bf16[128,32,256]{2,1,0:T(8,128)(2,1)S(1)}, bf16[128,32,256]{2,1,0:T(8,128)(2,1)}, u32[]{:S(2)}) copy-start(bf16[128,32,256]{2,1,0:T(8,128)(2,1)} %mortar_ref.1) | copy-start | bytes 6291460
  4.7 6.7 %copy-start.2 = (bf16[1,256,256]{2,1,0:T(8,128)(2,1)S(1)}, bf16[1,256,256]{2,1,0:T(8,128)(2,1)}, u32[]{:S(2)}) copy-start(bf16[1,256,256]{2,1,0:T(8,128)(2,1)} %basis_ref.1) | copy-start | bytes 393220
  4.7 6.7 %copy-start.3 = (bf16[128,256]{1,0:T(8,128)(2,1)S(1)}, bf16[128,256]{1,0:T(8,128)(2,1)}, u32[]{:S(2)}) copy-start(bf16[128,256]{1,0:T(8,128)(2,1)} %scale_ref.3) | copy-start | bytes 196612
  4.7 6.7 %copy-start.4 = (f32[32]{0:T(128)S(1)}, f32[32]{0:T(128)}, u32[]{:S(2)}) copy-start(f32[32]{0:T(128)} %param.10) | copy-start | bytes 388
  4.7 6.7 %copy-start.5 = (s32[32]{0:T(128)S(1)}, s32[32]{0:T(128)}, u32[]{:S(2)}) copy-start(s32[32]{0:T(128)} %param.11) | copy-start | bytes 388
  4.7 6.7 %copy-start.6 = (s32[128,1]{0,1:T(1,128)S(1)}, s32[128,1]{0,1:T(1,128)}, u32[]{:S(2)}) copy-start(s32[128,1]{0,1:T(1,128)} %param.12) | copy-start | bytes 1540
  4.7 6.7 %copy-start.7 = (s32[128]{0:T(128)S(1)}, s32[128]{0:T(128)}, u32[]{:S(2)}) copy-start(s32[128]{0:T(128)} %param.13) | copy-start | bytes 1540
  6.1 4.5 %collective-permute-start.1 = (bf16[80,256]{1,0:T(8,128)(2,1)S(1)}, bf16[80,256]{1,0:T(8,128)(2,1)S(1)}, u32[]{:S(2)}, u32[]{:S(2)}) collective-permute-start(bf16[80,256]{1,0:T(8,128)(2,1)S(1)} %get-tuple-element.21), channel_id=1, source_target_pairs={{0,1},{1,0},{2,3},{3,2},{4,5},{5,4},{6,7},{7,6},{8,9},{9,8},{10,11... | collective-permute-start | bytes 122888 | tf_op jit(solution)/shard_map/ppermute | solution.py:204
  6.2 6.1 %collective-permute-start.3 = (bf16[80,256]{1,0:T(8,128)(2,1)S(1)}, bf16[80,256]{1,0:T(8,128)(2,1)S(1)}, u32[]{:S(2)}, u32[]{:S(2)}) collective-permute-start(bf16[80,256]{1,0:T(8,128)(2,1)S(1)} %get-tuple-element.25), channel_id=1, source_target_pairs={{0,8},{4,12},{8,0},{12,4},{1,9},{5,13},{9,1},{13,5},{2,10},{6,14},... | collective-permute-start | bytes 122888 | tf_op jit(solution)/shard_map/ppermute | solution.py:202
  7.3 5.0 %collective-permute-start.4 = (bf16[80,256]{1,0:T(8,128)(2,1)S(1)}, bf16[80,256]{1,0:T(8,128)(2,1)S(1)}, u32[]{:S(2)}, u32[]{:S(2)}) collective-permute-start(bf16[80,256]{1,0:T(8,128)(2,1)S(1)} %get-tuple-element.26), channel_id=1, source_target_pairs={{0,4},{4,0},{8,12},{12,8},{1,5},{5,1},{9,13},{13,9},{2,6},{6,2},{1... | collective-permute-start | bytes 122888 | tf_op jit(solution)/shard_map/ppermute | solution.py:202
  8.1 5.8 %collective-permute-start.6 = (bf16[80,256]{1,0:T(8,128)(2,1)S(1)}, bf16[80,256]{1,0:T(8,128)(2,1)S(1)}, u32[]{:S(2)}, u32[]{:S(2)}) collective-permute-start(bf16[80,256]{1,0:T(8,128)(2,1)S(1)} %get-tuple-element.29), channel_id=1, source_target_pairs={{0,12},{4,8},{8,4},{12,0},{1,13},{5,9},{9,5},{13,1},{2,14},{6,10},... | collective-permute-start | bytes 122888 | tf_op jit(solution)/shard_map/ppermute | solution.py:202
  10.6 1.6 %collective-permute-start.5 = (bf16[1,256,256]{2,1,0:T(8,128)(2,1)S(1)}, bf16[1,256,256]{2,1,0:T(8,128)(2,1)S(1)}, u32[]{:S(2)}, u32[]{:S(2)}) collective-permute-start(bf16[1,256,256]{2,1,0:T(8,128)(2,1)S(1)} %collective-permute-done.refs_0_.refs_5_), channel_id=1, source_target_pairs={{0,1},{1,0},{2,3},{3,2},{4,5},{5,4},{6,7},{7,6},{8,9},{9,8},{10,11... | collective-permute-start | bytes 393224 | tf_op jit(solution)/shard_map/ppermute | solution.py:231
  10.6 4.5 %collective-permute-start.2 = (bf16[1,256,256]{2,1,0:T(8,128)(2,1)S(1)}, bf16[1,256,256]{2,1,0:T(8,128)(2,1)S(1)}, u32[]{:S(2)}, u32[]{:S(2)}) collective-permute-start(bf16[1,256,256]{2,1,0:T(8,128)(2,1)S(1)} %collective-permute-done.refs_0_.refs_5_), channel_id=1, source_target_pairs={{0,5},{1,0},{4,1},{5,4},{8,13},{9,8},{12,9},{13,12},{2,7},{3,2},{6... | collective-permute-start | bytes 393224 | tf_op jit(solution)/shard_map/ppermute | solution.py:230
  12.3 1.7 %collective-permute-start.7 = (bf16[80,256]{1,0:T(8,128)(2,1)S(1)}, bf16[80,256]{1,0:T(8,128)(2,1)S(1)}, u32[]{:S(2)}, u32[]{:S(2)}) collective-permute-start(bf16[80,256]{1,0:T(8,128)(2,1)S(1)} %collective-permute-done.3.refs_2_), channel_id=1, source_target_pairs={{0,1},{1,0},{2,3},{3,2},{4,5},{5,4},{6,7},{7,6},{8,9},{9,8},{10,11... | collective-permute-start | bytes 122888 | tf_op jit(solution)/shard_map/ppermute | solution.py:237
  12.4 1.6 %collective-permute-start.8 = (bf16[80,256]{1,0:T(8,128)(2,1)S(1)}, bf16[80,256]{1,0:T(8,128)(2,1)S(1)}, u32[]{:S(2)}, u32[]{:S(2)}) collective-permute-start(bf16[80,256]{1,0:T(8,128)(2,1)S(1)} %collective-permute-done.4.refs_6_), channel_id=1, source_target_pairs={{0,1},{1,0},{2,3},{3,2},{4,5},{5,4},{6,7},{7,6},{8,9},{9,8},{10,11... | collective-permute-start | bytes 122888 | tf_op jit(solution)/shard_map/ppermute | solution.py:237
  14.0 2.8 %copy-start = (bf16[256,256]{1,0:T(8,128)(2,1)S(1)}, bf16[256,256]{1,0:T(8,128)(2,1)}, u32[]{:S(2)}) copy-start(bf16[256,256]{1,0:T(8,128)(2,1)} %projection_ref.1) | copy-start | bytes 393220
  15.1 1.6 %collective-permute-start.9 = (bf16[1,256,256]{2,1,0:T(8,128)(2,1)S(1)}, bf16[1,256,256]{2,1,0:T(8,128)(2,1)S(1)}, u32[]{:S(2)}, u32[]{:S(2)}) collective-permute-start(bf16[1,256,256]{2,1,0:T(8,128)(2,1)S(1)} %collective-permute-done.2.refs_1_), channel_id=1, source_target_pairs={{0,1},{1,0},{2,3},{3,2},{4,5},{5,4},{6,7},{7,6},{8,9},{9,8},{10,11... | collective-permute-start | bytes 393224 | tf_op jit(solution)/shard_map/ppermute | solution.py:237
  15.5 1.2 %collective-permute-start.10 = (bf16[80,256]{1,0:T(8,128)(2,1)S(1)}, bf16[80,256]{1,0:T(8,128)(2,1)S(1)}, u32[]{:S(2)}, u32[]{:S(2)}) collective-permute-start(bf16[80,256]{1,0:T(8,128)(2,1)S(1)} %collective-permute-done.6.refs_2_), channel_id=1, source_target_pairs={{0,1},{1,0},{2,3},{3,2},{4,5},{5,4},{6,7},{7,6},{8,9},{9,8},{10,11... | collective-permute-start | bytes 122888 | tf_op jit(solution)/shard_map/ppermute | solution.py:237

commit v16 on v15

--- a/solution.py
+++ b/solution.py
@@ -228,6 +228,7 @@
 
     pairs = [(flat(s, face), flat(s, 0) if face else flat(s ^ 1, 1)) for s, face in cells]
     seconds = [lax.ppermute(first, ("sub", "face"), pairs) for first in firsts]
+    firsts, arrived[len(evens)] = lax.optimization_barrier((firsts, arrived[len(evens)]))
     firsts_swapped = [lax.ppermute(first, "face", swap) for first in firsts]
     soon, own_sum, firsts_swapped = lax.optimization_barrier(
         (arrived[: early_count - 1], own_sum, firsts_swapped)

time: 18.8 us -> 20.5 us (1.090)
  waiting for transfers between devices: 2.18 us -> 4.31 us
  starting transfers between devices: 10.5 us -> 10.1 us
    ppermute x3, waiting for transfers between devices: 1.09 us -> 2.36 us  [on_device(): lax.ppermute(pack, 'sub', [(i, i ^ p) for i in range(subdomains)])]
    ppermute x4, waiting for transfers between devices: 1.07 us -> 1.94 us  [with_swapped(): return [(array, lax.ppermute(array, 'face', swap)) for array in arrays]]
    ppermute x1, starting transfers between devices: 0.79 us -> 0.01 us  [on_device(): seconds = [lax.ppermute(first, ('sub', 'face'), pairs) for first in firsts]]
    ppermute x1, starting transfers between devices: 0.01 us -> 0.5 us  [on_device(): firsts_swapped = [lax.ppermute(first, 'face', swap) for first in firsts]]
  transfers between devices with their start and end apart: 11 -> 11, of which waited for: 2 -> 4; matrix products, arithmetic and copies ran while one was open for 0% -> 0% of each run, Pallas kernels for 18% -> 16%
where the time goes in v16:
time: 20.5 us; the launch traced here: 20.4 us
  starting transfers between devices  10.1 us (49%)
  Pallas kernels  5.13 us (25%)
  waiting for transfers between devices  4.31 us (21%)
  between operations  0.79 us (4%)
    ppermute x3, starting transfers between devices, on_device(): lax.ppermute(pack, 'sub', [(i, i ^ p) for i in range(subdomains)])  4.45 us
    ppermute x1, starting transfers between devices, on_device(): lax.ppermute(basis, ('sub', 'face'), [(flat(s, face), flat(s ^ (1 if face...  4.04 us
    ppermute x3, waiting for transfers between devices, on_device(): lax.ppermute(pack, 'sub', [(i, i ^ p) for i in range(subdomains)])  2.36 us
    ppermute x4, waiting for transfers between devices, with_swapped(): return [(array, lax.ppermute(array, 'face', swap)) for array in arrays]  1.94 us
    pallas_call x1, Pallas kernels, on_device(): pl.pallas_call(last_kernel, out_shape=jax.ShapeDtypeStruct(block_shape, j...  1.86 us
    pallas_call x1, Pallas kernels, on_device(): pl.pallas_call(functools.partial(pack_kernel, partners), out_shape=[pltpu...  1.36 us
    pallas_call x1, Pallas kernels, on_device(): pl.pallas_call(stage_kernel, out_shape=jax.ShapeDtypeStruct(block_shape,...  1.13 us
    ppermute x4, starting transfers between devices, with_swapped(): return [(array, lax.ppermute(array, 'face', swap)) for array in arrays]  1.09 us
  transfers between devices with their start and end apart: 11, of which 4 were waited for; matrix products, arithmetic and copies ran while one was open for 0% of the time, Pallas kernels for 16%

profile of v16, /device:TPU:0, one launch (start us, length us, event | category | flops | bytes accessed | tf_op | source)
XLA Modules:
  0.0 20.4 jit_solution(8982234892549447199)
XLA Ops:
  0.0 4.0 %collective-permute-start = (bf16[1,256,256]{2,1,0:T(8,128)(2,1)}, bf16[1,256,256]{2,1,0:T(8,128)(2,1)S(1)}, u32[]{:S(2)}, u32[]{:S(2)}) collective-permute-start(bf16[1,256,256]{2,1,0:T(8,128)(2,1)} %basis_ref.1), channel_id=1, source_target_pairs={{0,8},{1,5},{4,12},{5,1},{8,0},{9,13},{12,4},{13,9},{2,10},{3,7},{... | collective-permute-start | bytes 393224 | tf_op jit(solution)/shard_map/ppermute | solution.py:184
  4.7 0.0 copy-start.1
  4.7 0.0 copy-start.2
  4.7 0.0 copy-start.3
  4.7 0.0 copy-start.4
  4.7 0.0 copy-start.5
  4.7 0.0 copy-start.6
  4.7 0.0 copy-start.7
  4.8 1.4 %pack_weights.1 = (bf16[80,256]{1,0:T(8,128)(2,1)S(1)}, bf16[80,256]{1,0:T(8,128)(2,1)S(1)}, bf16[80,256]{1,0:T(8,128)(2,1)S(1)}, bf16[80,256]{1,0:T(8,128)(2,1)S(1)}) custom-call(s32[1,128]{1,0:T(1,128)} %bitcast.6, s32[1,128]{1,0:T(1,128)} %bitcast.8, bf16[128,256]{1,0:T(8,128)(2,1)} %scale_ref.3, s32[1]{0:T(128)S(6)} %copy.12.section_ref), custom_call_target="tpu_custom_call" | custom-call | flops 4000000000 | bytes 8388608 | tf_op jit(solution)/shard_map/pack_weights/pallas_call | solution.py:192
  6.1 0.0 collective-permute-start.1
  6.2 1.6 %collective-permute-start.4 = (bf16[80,256]{1,0:T(8,128)(2,1)S(1)}, bf16[80,256]{1,0:T(8,128)(2,1)S(1)}, u32[]{:S(2)}, u32[]{:S(2)}) collective-permute-start(bf16[80,256]{1,0:T(8,128)(2,1)S(1)} %get-tuple-element.28), channel_id=1, source_target_pairs={{0,4},{4,0},{8,12},{12,8},{1,5},{5,1},{9,13},{13,9},{2,6},{6,2},{1... | collective-permute-start | bytes 122888 | tf_op jit(solution)/shard_map/ppermute | solution.py:202
  7.8 0.3 %collective-permute-start.3 = (bf16[80,256]{1,0:T(8,128)(2,1)S(1)}, bf16[80,256]{1,0:T(8,128)(2,1)S(1)}, u32[]{:S(2)}, u32[]{:S(2)}) collective-permute-start(bf16[80,256]{1,0:T(8,128)(2,1)S(1)} %get-tuple-element.27), channel_id=1, source_target_pairs={{0,8},{4,12},{8,0},{12,4},{1,9},{5,13},{9,1},{13,5},{2,10},{6,14},... | collective-permute-start | bytes 122888 | tf_op jit(solution)/shard_map/ppermute | solution.py:202
  8.1 2.5 %collective-permute-start.6 = (bf16[80,256]{1,0:T(8,128)(2,1)S(1)}, bf16[80,256]{1,0:T(8,128)(2,1)S(1)}, u32[]{:S(2)}, u32[]{:S(2)}) collective-permute-start(bf16[80,256]{1,0:T(8,128)(2,1)S(1)} %get-tuple-element.33), channel_id=1, source_target_pairs={{0,12},{4,8},{8,4},{12,0},{1,13},{5,9},{9,5},{13,1},{2,14},{6,10},... | collective-permute-start | bytes 122888 | tf_op jit(solution)/shard_map/ppermute | solution.py:202
  10.6 0.0 collective-permute-done.1.swapped_ref
  10.6 0.0 collective-permute-done.refs_0_.refs_5_
  10.6 0.0 collective-permute-start.2
  10.6 0.0 collective-permute-done.4.refs_6_
  10.6 0.5 %collective-permute-start.5 = (bf16[1,256,256]{2,1,0:T(8,128)(2,1)S(1)}, bf16[1,256,256]{2,1,0:T(8,128)(2,1)S(1)}, u32[]{:S(2)}, u32[]{:S(2)}) collective-permute-start(bf16[1,256,256]{2,1,0:T(8,128)(2,1)S(1)} %collective-permute-done.refs_0_.refs_5_), channel_id=1, source_target_pairs={{0,1},{1,0},{2,3},{3,2},{4,5},{5,4},{6,7},{7,6},{8,9},{9,8},{10,11... | collective-permute-start | bytes 393224 | tf_op jit(solution)/shard_map/ppermute | solution.py:232
  11.1 0.0 copy-done.1
  11.1 0.0 copy-done.2
  11.2 0.0 copy-done.3
  11.2 0.0 copy-done.4
  11.2 0.0 copy-done.5
  11.2 0.0 copy-done.6
  11.2 0.0 copy-done.7
  11.2 0.8 %own_blocks.1 = (bf16[64,32,256]{2,1,0:T(8,128)(2,1)S(1)}, f32[64,32,256]{2,1,0:T(8,128)S(1)}) custom-call(bf16[128,32,256]{2,1,0:T(8,128)(2,1)S(1)} %copy-done.1, f32[1,32]{1,0:T(1,128)S(1)} %bitcast.4, s32[1,32]{1,0:T(1,128)S(1)} %bitcast.5, s32[1,128]{1,0:T(1,128)S(1)} %bitcast.7, s32[1,128]{1,0:T(1,128)S(1)} %bitcast.9, bf16[128,256]{1,0:T(8,128)(2,1)S(1)} %copy-done.3, ...), custom_call_target="tpu_custom_call" | custom-call | flops 4000000000 | bytes 8388608 | tf_op jit(solution)/shard_map/own_blocks/pallas_call | solution.py:207
  12.0 2.4 %collective-permute-done.3.refs_2_ = bf16[80,256]{1,0:T(8,128)(2,1)S(1)} collective-permute-done((bf16[80,256]{1,0:T(8,128)(2,1)S(1)}, bf16[80,256]{1,0:T(8,128)(2,1)S(1)}, u32[]{:S(2)}, u32[]{:S(2)}) %collective-permute-start.3) | collective-permute-done | bytes 40992 | tf_op jit(solution)/shard_map/ppermute | solution.py:202
  14.3 0.0 collective-permute-done.5.refs_1_.refs_4_
  14.3 0.0 collective-permute-start.7
  14.3 0.5 %collective-permute-start.8 = (bf16[80,256]{1,0:T(8,128)(2,1)S(1)}, bf16[80,256]{1,0:T(8,128)(2,1)S(1)}, u32[]{:S(2)}, u32[]{:S(2)}) collective-permute-start(bf16[80,256]{1,0:T(8,128)(2,1)S(1)} %collective-permute-done.4.refs_6_), channel_id=1, source_target_pairs={{0,1},{1,0},{2,3},{3,2},{4,5},{5,4},{6,7},{7,6},{8,9},{9,8},{10,11... | collective-permute-start | bytes 122888 | tf_op jit(solution)/shard_map/ppermute | solution.py:238
  14.8 0.0 collective-permute-done.6.refs_2_
  14.8 0.7 %collective-permute-done.7.refs_3_ = bf16[80,256]{1,0:T(8,128)(2,1)S(1)} collective-permute-done((bf16[80,256]{1,0:T(8,128)(2,1)S(1)}, bf16[80,256]{1,0:T(8,128)(2,1)S(1)}, u32[]{:S(2)}, u32[]{:S(2)}) %collective-permute-start.7) | collective-permute-done | bytes 40992 | tf_op jit(solution)/shard_map/ppermute | solution.py:238
  15.6 0.2 collective-permute-done.8.refs_7_
  15.7 0.0 copy-start
  15.7 1.1 %stage.1.sum_ref = f32[64,32,256]{2,1,0:T(8,128)S(1)} custom-call(bf16[64,32,256]{2,1,0:T(8,128)(2,1)S(1)} %get-tuple-element.25.pumped_ref, f32[64,32,256]{2,1,0:T(8,128)S(1)} %get-tuple-element.34.sum_ref, bf16[1,256,256]{2,1,0:T(8,128)(2,1)S(1)} %collective-permute-done.refs_0_.refs_5_, ...), custom_call_target="tpu_custom_call", output_to_operand_aliasing={{}: (1, {})} | custom-call | flops 1000000 | bytes 1024 | tf_op jit(solution)/shard_map/stage/pallas_call | solution.py:254
  16.9 0.0 collective-permute-done.2.refs_1_
  16.9 0.4 %collective-permute-start.9 = (bf16[1,256,256]{2,1,0:T(8,128)(2,1)S(1)}, bf16[1,256,256]{2,1,0:T(8,128)(2,1)S(1)}, u32[]{:S(2)}, u32[]{:S(2)}) collective-permute-start(bf16[1,256,256]{2,1,0:T(8,128)(2,1)S(1)} %collective-permute-done.2.refs_1_), channel_id=1, source_target_pairs={{0,1},{1,0},{2,3},{3,2},{4,5},{5,4},{6,7},{7,6},{8,9},{9,8},{10,11... | collective-permute-start | bytes 393224 | tf_op jit(solution)/shard_map/ppermute | solution.py:238
  17.3 0.1 collective-permute-start.10
  17.4 1.1 %collective-permute-done.10.refs_3_ = bf16[80,256]{1,0:T(8,128)(2,1)S(1)} collective-permute-done((bf16[80,256]{1,0:T(8,128)(2,1)S(1)}, bf16[80,256]{1,0:T(8,128)(2,1)S(1)}, u32[]{:S(2)}, u32[]{:S(2)}) %collective-permute-start.10) | collective-permute-done | bytes 40992 | tf_op jit(solution)/shard_map/ppermute | solution.py:238
  18.5 0.0 collective-permute-done.9.refs_0_
  18.5 0.0 copy-done
  18.5 1.9 %last_stage.1 = f32[64,32,256]{2,1,0:T(8,128)} custom-call(bf16[64,32,256]{2,1,0:T(8,128)(2,1)S(1)} %get-tuple-element.25.pumped_ref, f32[64,32,256]{2,1,0:T(8,128)S(1)} %stage.1.sum_ref, bf16[256,256]{1,0:T(8,128)(2,1)S(1)} %copy-done, bf16[1,256,256]{2,1,0:T(8,128)(2,1)S(1)} %collective-permute-done.9.refs_0_, ...), custom_call_target="tpu_custom_call" | custom-call | tf_op jit(solution)/shard_map/last_stage/pallas_call | solution.py:270
Async XLA Ops:
  0.0 10.6 %collective-permute-start = (bf16[1,256,256]{2,1,0:T(8,128)(2,1)}, bf16[1,256,256]{2,1,0:T(8,128)(2,1)S(1)}, u32[]{:S(2)}, u32[]{:S(2)}) collective-permute-start(bf16[1,256,256]{2,1,0:T(8,128)(2,1)} %basis_ref.1), channel_id=1, source_target_pairs={{0,8},{1,5},{4,12},{5,1},{8,0},{9,13},{12,4},{13,9},{2,10},{3,7},{... | collective-permute-start | bytes 393224 | tf_op jit(solution)/shard_map/ppermute | solution.py:184
  4.7 6.5 %copy-start.1 = (bf16[128,32,256]{2,1,0:T(8,128)(2,1)S(1)}, bf16[128,32,256]{2,1,0:T(8,128)(2,1)}, u32[]{:S(2)}) copy-start(bf16[128,32,256]{2,1,0:T(8,128)(2,1)} %mortar_ref.1) | copy-start | bytes 6291460
  4.7 6.5 %copy-start.2 = (bf16[1,256,256]{2,1,0:T(8,128)(2,1)S(1)}, bf16[1,256,256]{2,1,0:T(8,128)(2,1)}, u32[]{:S(2)}) copy-start(bf16[1,256,256]{2,1,0:T(8,128)(2,1)} %basis_ref.1) | copy-start | bytes 393220
  4.7 6.4 %copy-start.3 = (bf16[128,256]{1,0:T(8,128)(2,1)S(1)}, bf16[128,256]{1,0:T(8,128)(2,1)}, u32[]{:S(2)}) copy-start(bf16[128,256]{1,0:T(8,128)(2,1)} %scale_ref.3) | copy-start | bytes 196612
  4.7 6.4 %copy-start.4 = (f32[32]{0:T(128)S(1)}, f32[32]{0:T(128)}, u32[]{:S(2)}) copy-start(f32[32]{0:T(128)} %param.10) | copy-start | bytes 388
  4.7 6.4 %copy-start.5 = (s32[32]{0:T(128)S(1)}, s32[32]{0:T(128)}, u32[]{:S(2)}) copy-start(s32[32]{0:T(128)} %param.11) | copy-start | bytes 388
  4.7 6.4 %copy-start.6 = (s32[128,1]{0,1:T(1,128)S(1)}, s32[128,1]{0,1:T(1,128)}, u32[]{:S(2)}) copy-start(s32[128,1]{0,1:T(1,128)} %param.12) | copy-start | bytes 1540
  4.7 6.4 %copy-start.7 = (s32[128]{0:T(128)S(1)}, s32[128]{0:T(128)}, u32[]{:S(2)}) copy-start(s32[128]{0:T(128)} %param.13) | copy-start | bytes 1540
  6.1 4.5 %collective-permute-start.1 = (bf16[80,256]{1,0:T(8,128)(2,1)S(1)}, bf16[80,256]{1,0:T(8,128)(2,1)S(1)}, u32[]{:S(2)}, u32[]{:S(2)}) collective-permute-start(bf16[80,256]{1,0:T(8,128)(2,1)S(1)} %get-tuple-element.23), channel_id=1, source_target_pairs={{0,1},{1,0},{2,3},{3,2},{4,5},{5,4},{6,7},{7,6},{8,9},{9,8},{10,11... | collective-permute-start | bytes 122888 | tf_op jit(solution)/shard_map/ppermute | solution.py:204
  6.2 4.5 %collective-permute-start.4 = (bf16[80,256]{1,0:T(8,128)(2,1)S(1)}, bf16[80,256]{1,0:T(8,128)(2,1)S(1)}, u32[]{:S(2)}, u32[]{:S(2)}) collective-permute-start(bf16[80,256]{1,0:T(8,128)(2,1)S(1)} %get-tuple-element.28), channel_id=1, source_target_pairs={{0,4},{4,0},{8,12},{12,8},{1,5},{5,1},{9,13},{13,9},{2,6},{6,2},{1... | collective-permute-start | bytes 122888 | tf_op jit(solution)/shard_map/ppermute | solution.py:202
  7.8 6.5 %collective-permute-start.3 = (bf16[80,256]{1,0:T(8,128)(2,1)S(1)}, bf16[80,256]{1,0:T(8,128)(2,1)S(1)}, u32[]{:S(2)}, u32[]{:S(2)}) collective-permute-start(bf16[80,256]{1,0:T(8,128)(2,1)S(1)} %get-tuple-element.27), channel_id=1, source_target_pairs={{0,8},{4,12},{8,0},{12,4},{1,9},{5,13},{9,1},{13,5},{2,10},{6,14},... | collective-permute-start | bytes 122888 | tf_op jit(solution)/shard_map/ppermute | solution.py:202
  8.1 6.7 %collective-permute-start.6 = (bf16[80,256]{1,0:T(8,128)(2,1)S(1)}, bf16[80,256]{1,0:T(8,128)(2,1)S(1)}, u32[]{:S(2)}, u32[]{:S(2)}) collective-permute-start(bf16[80,256]{1,0:T(8,128)(2,1)S(1)} %get-tuple-element.33), channel_id=1, source_target_pairs={{0,12},{4,8},{8,4},{12,0},{1,13},{5,9},{9,5},{13,1},{2,14},{6,10},... | collective-permute-start | bytes 122888 | tf_op jit(solution)/shard_map/ppermute | solution.py:202
  10.6 6.2 %collective-permute-start.2 = (bf16[1,256,256]{2,1,0:T(8,128)(2,1)S(1)}, bf16[1,256,256]{2,1,0:T(8,128)(2,1)S(1)}, u32[]{:S(2)}, u32[]{:S(2)}) collective-permute-start(bf16[1,256,256]{2,1,0:T(8,128)(2,1)S(1)} %collective-permute-done.refs_0_.refs_5_), channel_id=1, source_target_pairs={{0,5},{1,0},{4,1},{5,4},{8,13},{9,8},{12,9},{13,12},{2,7},{3,2},{6... | collective-permute-start | bytes 393224 | tf_op jit(solution)/shard_map/ppermute | solution.py:230
  10.6 3.7 %collective-permute-start.5 = (bf16[1,256,256]{2,1,0:T(8,128)(2,1)S(1)}, bf16[1,256,256]{2,1,0:T(8,128)(2,1)S(1)}, u32[]{:S(2)}, u32[]{:S(2)}) collective-permute-start(bf16[1,256,256]{2,1,0:T(8,128)(2,1)S(1)} %collective-permute-done.refs_0_.refs_5_), channel_id=1, source_target_pairs={{0,1},{1,0},{2,3},{3,2},{4,5},{5,4},{6,7},{7,6},{8,9},{9,8},{10,11... | collective-permute-start | bytes 393224 | tf_op jit(solution)/shard_map/ppermute | solution.py:232
  14.3 1.2 %collective-permute-start.7 = (bf16[80,256]{1,0:T(8,128)(2,1)S(1)}, bf16[80,256]{1,0:T(8,128)(2,1)S(1)}, u32[]{:S(2)}, u32[]{:S(2)}) collective-permute-start(bf16[80,256]{1,0:T(8,128)(2,1)S(1)} %collective-permute-done.3.refs_2_), channel_id=1, source_target_pairs={{0,1},{1,0},{2,3},{3,2},{4,5},{5,4},{6,7},{7,6},{8,9},{9,8},{10,11... | collective-permute-start | bytes 122888 | tf_op jit(solution)/shard_map/ppermute | solution.py:238
  14.3 1.4 %collective-permute-start.8 = (bf16[80,256]{1,0:T(8,128)(2,1)S(1)}, bf16[80,256]{1,0:T(8,128)(2,1)S(1)}, u32[]{:S(2)}, u32[]{:S(2)}) collective-permute-start(bf16[80,256]{1,0:T(8,128)(2,1)S(1)} %collective-permute-done.4.refs_6_), channel_id=1, source_target_pairs={{0,1},{1,0},{2,3},{3,2},{4,5},{5,4},{6,7},{7,6},{8,9},{9,8},{10,11... | collective-permute-start | bytes 122888 | tf_op jit(solution)/shard_map/ppermute | solution.py:238
  15.7 2.8 %copy-start = (bf16[256,256]{1,0:T(8,128)(2,1)S(1)}, bf16[256,256]{1,0:T(8,128)(2,1)}, u32[]{:S(2)}) copy-start(bf16[256,256]{1,0:T(8,128)(2,1)} %projection_ref.1) | copy-start | bytes 393220
  16.9 1.7 %collective-permute-start.9 = (bf16[1,256,256]{2,1,0:T(8,128)(2,1)S(1)}, bf16[1,256,256]{2,1,0:T(8,128)(2,1)S(1)}, u32[]{:S(2)}, u32[]{:S(2)}) collective-permute-start(bf16[1,256,256]{2,1,0:T(8,128)(2,1)S(1)} %collective-permute-done.2.refs_1_), channel_id=1, source_target_pairs={{0,1},{1,0},{2,3},{3,2},{4,5},{5,4},{6,7},{7,6},{8,9},{9,8},{10,11... | collective-permute-start | bytes 393224 | tf_op jit(solution)/shard_map/ppermute | solution.py:238
  17.3 1.2 %collective-permute-start.10 = (bf16[80,256]{1,0:T(8,128)(2,1)S(1)}, bf16[80,256]{1,0:T(8,128)(2,1)S(1)}, u32[]{:S(2)}, u32[]{:S(2)}) collective-permute-start(bf16[80,256]{1,0:T(8,128)(2,1)S(1)} %collective-permute-done.6.refs_2_), channel_id=1, source_target_pairs={{0,1},{1,0},{2,3},{3,2},{4,5},{5,4},{6,7},{7,6},{8,9},{9,8},{10,11... | collective-permute-start | bytes 122888 | tf_op jit(solution)/shard_map/ppermute | solution.py:238

commit v17 on v15

--- a/solution.py
+++ b/solution.py
@@ -228,6 +228,7 @@
 
     pairs = [(flat(s, face), flat(s, 0) if face else flat(s ^ 1, 1)) for s, face in cells]
     seconds = [lax.ppermute(first, ("sub", "face"), pairs) for first in firsts]
+    firsts, arrived[:len(evens)] = lax.optimization_barrier((firsts, arrived[:len(evens)]))
     firsts_swapped = [lax.ppermute(first, "face", swap) for first in firsts]
     soon, own_sum, firsts_swapped = lax.optimization_barrier(
         (arrived[: early_count - 1], own_sum, firsts_swapped)

time: 18.8 us -> 18.7 us (level)
  starting transfers between devices: 10.5 us -> 9.62 us
  waiting for transfers between devices: 2.18 us -> 2.97 us
    ppermute x1, starting transfers between devices: 0.79 us -> 0.01 us  [on_device(): seconds = [lax.ppermute(first, ('sub', 'face'), pairs) for first in firsts]]
    ppermute x1, waiting for transfers between devices: 0.01 us -> 0.49 us  [on_device(): firsts_swapped = [lax.ppermute(first, 'face', swap) for first in firsts]]
    ppermute x3, waiting for transfers between devices: 1.09 us -> 1.56 us  [on_device(): lax.ppermute(pack, 'sub', [(i, i ^ p) for i in range(subdomains)])]
  transfers between devices with their start and end apart: 11 -> 11, of which waited for: 2 -> 4; matrix products, arithmetic and copies ran while one was open for 0% -> 0% of each run, Pallas kernels for 18% -> 18%
where the time goes in v17:
time: 18.7 us; the launch traced here: 18.6 us
  starting transfers between devices  9.62 us (51%)
  Pallas kernels  5.13 us (27%)
  waiting for transfers between devices  2.97 us (16%)
  between operations  0.8 us (4%)
    ppermute x3, starting transfers between devices, on_device(): lax.ppermute(pack, 'sub', [(i, i ^ p) for i in range(subdomains)])  4.45 us
    ppermute x1, starting transfers between devices, on_device(): lax.ppermute(basis, ('sub', 'face'), [(flat(s, face), flat(s ^ (1 if face...  4.04 us
    pallas_call x1, Pallas kernels, on_device(): pl.pallas_call(last_kernel, out_shape=jax.ShapeDtypeStruct(block_shape, j...  1.86 us
    ppermute x3, waiting for transfers between devices, on_device(): lax.ppermute(pack, 'sub', [(i, i ^ p) for i in range(subdomains)])  1.56 us
    pallas_call x1, Pallas kernels, on_device(): pl.pallas_call(functools.partial(pack_kernel, partners), out_shape=[pltpu...  1.36 us
    pallas_call x1, Pallas kernels, on_device(): pl.pallas_call(stage_kernel, out_shape=jax.ShapeDtypeStruct(block_shape,...  1.13 us
    ppermute x4, starting transfers between devices, with_swapped(): return [(array, lax.ppermute(array, 'face', swap)) for array in arrays]  1.09 us
    ppermute x4, waiting for transfers between devices, with_swapped(): return [(array, lax.ppermute(array, 'face', swap)) for array in arrays]  0.92 us
  transfers between devices with their start and end apart: 11, of which 4 were waited for; matrix products, arithmetic and copies ran while one was open for 0% of the time, Pallas kernels for 18%

profile of v17, /device:TPU:0, one launch (start us, length us, event | category | flops | bytes accessed | tf_op | source)
XLA Modules:
  0.0 18.6 jit_solution(2720019138343992586)
XLA Ops:
  0.0 4.0 %collective-permute-start = (bf16[1,256,256]{2,1,0:T(8,128)(2,1)}, bf16[1,256,256]{2,1,0:T(8,128)(2,1)S(1)}, u32[]{:S(2)}, u32[]{:S(2)}) collective-permute-start(bf16[1,256,256]{2,1,0:T(8,128)(2,1)} %basis_ref.1), channel_id=1, source_target_pairs={{0,8},{1,5},{4,12},{5,1},{8,0},{9,13},{12,4},{13,9},{2,10},{3,7},{... | collective-permute-start | bytes 393224 | tf_op jit(solution)/shard_map/ppermute | solution.py:184
  4.7 0.0 copy-start.1
  4.7 0.0 copy-start.2
  4.7 0.0 copy-start.3
  4.7 0.0 copy-start.4
  4.7 0.0 copy-start.5
  4.7 0.0 copy-start.6
  4.7 0.0 copy-start.7
  4.8 1.4 %pack_weights.1 = (bf16[80,256]{1,0:T(8,128)(2,1)S(1)}, bf16[80,256]{1,0:T(8,128)(2,1)S(1)}, bf16[80,256]{1,0:T(8,128)(2,1)S(1)}, bf16[80,256]{1,0:T(8,128)(2,1)S(1)}) custom-call(s32[1,128]{1,0:T(1,128)} %bitcast.6, s32[1,128]{1,0:T(1,128)} %bitcast.8, bf16[128,256]{1,0:T(8,128)(2,1)} %scale_ref.3, s32[1]{0:T(128)S(6)} %copy.12.section_ref), custom_call_target="tpu_custom_call" | custom-call | flops 4000000000 | bytes 8388608 | tf_op jit(solution)/shard_map/pack_weights/pallas_call | solution.py:192
  6.1 0.0 collective-permute-start.1
  6.2 1.1 %collective-permute-start.3 = (bf16[80,256]{1,0:T(8,128)(2,1)S(1)}, bf16[80,256]{1,0:T(8,128)(2,1)S(1)}, u32[]{:S(2)}, u32[]{:S(2)}) collective-permute-start(bf16[80,256]{1,0:T(8,128)(2,1)S(1)} %get-tuple-element.27), channel_id=1, source_target_pairs={{0,8},{4,12},{8,0},{12,4},{1,9},{5,13},{9,1},{13,5},{2,10},{6,14},... | collective-permute-start | bytes 122888 | tf_op jit(solution)/shard_map/ppermute | solution.py:202
  7.3 0.9 %collective-permute-start.4 = (bf16[80,256]{1,0:T(8,128)(2,1)S(1)}, bf16[80,256]{1,0:T(8,128)(2,1)S(1)}, u32[]{:S(2)}, u32[]{:S(2)}) collective-permute-start(bf16[80,256]{1,0:T(8,128)(2,1)S(1)} %get-tuple-element.29), channel_id=1, source_target_pairs={{0,4},{4,0},{8,12},{12,8},{1,5},{5,1},{9,13},{13,9},{2,6},{6,2},{1... | collective-permute-start | bytes 122888 | tf_op jit(solution)/shard_map/ppermute | solution.py:202
  8.1 2.5 %collective-permute-start.6 = (bf16[80,256]{1,0:T(8,128)(2,1)S(1)}, bf16[80,256]{1,0:T(8,128)(2,1)S(1)}, u32[]{:S(2)}, u32[]{:S(2)}) collective-permute-start(bf16[80,256]{1,0:T(8,128)(2,1)S(1)} %get-tuple-element.33), channel_id=1, source_target_pairs={{0,12},{4,8},{8,4},{12,0},{1,13},{5,9},{9,5},{13,1},{2,14},{6,10},... | collective-permute-start | bytes 122888 | tf_op jit(solution)/shard_map/ppermute | solution.py:202
  10.6 0.0 collective-permute-done.1.swapped_ref
  10.6 0.0 collective-permute-done.refs_0_.refs_5_
  10.6 0.0 collective-permute-start.2
  10.6 0.5 %collective-permute-done.3.refs_2_ = bf16[80,256]{1,0:T(8,128)(2,1)S(1)} collective-permute-done((bf16[80,256]{1,0:T(8,128)(2,1)S(1)}, bf16[80,256]{1,0:T(8,128)(2,1)S(1)}, u32[]{:S(2)}, u32[]{:S(2)}) %collective-permute-start.3) | collective-permute-done | bytes 40992 | tf_op jit(solution)/shard_map/ppermute | solution.py:202
  11.2 0.0 collective-permute-start.5
  11.2 0.0 copy-done.1
  11.2 0.0 copy-done.2
  11.2 0.0 copy-done.3
  11.2 0.0 copy-done.4
  11.2 0.0 copy-done.5
  11.2 0.0 copy-done.6
  11.2 0.0 copy-done.7
  11.2 0.8 %own_blocks.1 = (bf16[64,32,256]{2,1,0:T(8,128)(2,1)S(1)}, f32[64,32,256]{2,1,0:T(8,128)S(1)}) custom-call(bf16[128,32,256]{2,1,0:T(8,128)(2,1)S(1)} %copy-done.1, f32[1,32]{1,0:T(1,128)S(1)} %bitcast.4, s32[1,32]{1,0:T(1,128)S(1)} %bitcast.5, s32[1,128]{1,0:T(1,128)S(1)} %bitcast.7, s32[1,128]{1,0:T(1,128)S(1)} %bitcast.9, bf16[128,256]{1,0:T(8,128)(2,1)S(1)} %copy-done.3, ...), custom_call_target="tpu_custom_call" | custom-call | flops 4000000000 | bytes 8388608 | tf_op jit(solution)/shard_map/own_blocks/pallas_call | solution.py:207
  12.0 0.0 collective-permute-done.4.refs_6_
  12.0 0.5 %collective-permute-done.5.refs_1_.refs_4_ = bf16[1,256,256]{2,1,0:T(8,128)(2,1)S(1)} collective-permute-done((bf16[1,256,256]{2,1,0:T(8,128)(2,1)S(1)}, bf16[1,256,256]{2,1,0:T(8,128)(2,1)S(1)}, u32[]{:S(2)}, u32[]{:S(2)}) %collective-permute-start.5) | collective-permute-done | bytes 131104 | tf_op jit(solution)/shard_map/ppermute | solution.py:232
  12.5 0.1 collective-permute-start.7
  12.7 0.4 %collective-permute-start.8 = (bf16[80,256]{1,0:T(8,128)(2,1)S(1)}, bf16[80,256]{1,0:T(8,128)(2,1)S(1)}, u32[]{:S(2)}, u32[]{:S(2)}) collective-permute-start(bf16[80,256]{1,0:T(8,128)(2,1)S(1)} %collective-permute-done.4.refs_6_), channel_id=1, source_target_pairs={{0,1},{1,0},{2,3},{3,2},{4,5},{5,4},{6,7},{7,6},{8,9},{9,8},{10,11... | collective-permute-start | bytes 122888 | tf_op jit(solution)/shard_map/ppermute | solution.py:238
  13.0 1.0 %collective-permute-done.6.refs_2_ = bf16[80,256]{1,0:T(8,128)(2,1)S(1)} collective-permute-done((bf16[80,256]{1,0:T(8,128)(2,1)S(1)}, bf16[80,256]{1,0:T(8,128)(2,1)S(1)}, u32[]{:S(2)}, u32[]{:S(2)}) %collective-permute-start.6) | collective-permute-done | bytes 40992 | tf_op jit(solution)/shard_map/ppermute | solution.py:202
  14.1 0.0 collective-permute-done.7.refs_3_
  14.1 0.0 collective-permute-done.8.refs_7_
  14.1 0.0 copy-start
  14.1 1.1 %stage.1.sum_ref = f32[64,32,256]{2,1,0:T(8,128)S(1)} custom-call(bf16[64,32,256]{2,1,0:T(8,128)(2,1)S(1)} %get-tuple-element.25.pumped_ref, f32[64,32,256]{2,1,0:T(8,128)S(1)} %get-tuple-element.34.sum_ref, bf16[1,256,256]{2,1,0:T(8,128)(2,1)S(1)} %collective-permute-done.refs_0_.refs_5_, ...), custom_call_target="tpu_custom_call", output_to_operand_aliasing={{}: (1, {})} | custom-call | flops 1000000 | bytes 1024 | tf_op jit(solution)/shard_map/stage/pallas_call | solution.py:254
  15.2 0.0 collective-permute-done.2.refs_1_
  15.2 0.3 %collective-permute-start.9 = (bf16[1,256,256]{2,1,0:T(8,128)(2,1)S(1)}, bf16[1,256,256]{2,1,0:T(8,128)(2,1)S(1)}, u32[]{:S(2)}, u32[]{:S(2)}) collective-permute-start(bf16[1,256,256]{2,1,0:T(8,128)(2,1)S(1)} %collective-permute-done.2.refs_1_), channel_id=1, source_target_pairs={{0,1},{1,0},{2,3},{3,2},{4,5},{5,4},{6,7},{7,6},{8,9},{9,8},{10,11... | collective-permute-start | bytes 393224 | tf_op jit(solution)/shard_map/ppermute | solution.py:238
  15.5 0.3 %collective-permute-start.10 = (bf16[80,256]{1,0:T(8,128)(2,1)S(1)}, bf16[80,256]{1,0:T(8,128)(2,1)S(1)}, u32[]{:S(2)}, u32[]{:S(2)}) collective-permute-start(bf16[80,256]{1,0:T(8,128)(2,1)S(1)} %collective-permute-done.6.refs_2_), channel_id=1, source_target_pairs={{0,1},{1,0},{2,3},{3,2},{4,5},{5,4},{6,7},{7,6},{8,9},{9,8},{10,11... | collective-permute-start | bytes 122888 | tf_op jit(solution)/shard_map/ppermute | solution.py:238
  15.8 0.9 %collective-permute-done.10.refs_3_ = bf16[80,256]{1,0:T(8,128)(2,1)S(1)} collective-permute-done((bf16[80,256]{1,0:T(8,128)(2,1)S(1)}, bf16[80,256]{1,0:T(8,128)(2,1)S(1)}, u32[]{:S(2)}, u32[]{:S(2)}) %collective-permute-start.10) | collective-permute-done | bytes 40992 | tf_op jit(solution)/shard_map/ppermute | solution.py:238
  16.7 0.0 collective-permute-done.9.refs_0_
  16.7 0.0 copy-done
  16.7 1.9 %last_stage.1 = f32[64,32,256]{2,1,0:T(8,128)} custom-call(bf16[64,32,256]{2,1,0:T(8,128)(2,1)S(1)} %get-tuple-element.25.pumped_ref, f32[64,32,256]{2,1,0:T(8,128)S(1)} %stage.1.sum_ref, bf16[256,256]{1,0:T(8,128)(2,1)S(1)} %copy-done, bf16[1,256,256]{2,1,0:T(8,128)(2,1)S(1)} %collective-permute-done.9.refs_0_, ...), custom_call_target="tpu_custom_call" | custom-call | tf_op jit(solution)/shard_map/last_stage/pallas_call | solution.py:270
Async XLA Ops:
  0.0 10.6 %collective-permute-start = (bf16[1,256,256]{2,1,0:T(8,128)(2,1)}, bf16[1,256,256]{2,1,0:T(8,128)(2,1)S(1)}, u32[]{:S(2)}, u32[]{:S(2)}) collective-permute-start(bf16[1,256,256]{2,1,0:T(8,128)(2,1)} %basis_ref.1), channel_id=1, source_target_pairs={{0,8},{1,5},{4,12},{5,1},{8,0},{9,13},{12,4},{13,9},{2,10},{3,7},{... | collective-permute-start | bytes 393224 | tf_op jit(solution)/shard_map/ppermute | solution.py:184
  4.7 6.5 %copy-start.1 = (bf16[128,32,256]{2,1,0:T(8,128)(2,1)S(1)}, bf16[128,32,256]{2,1,0:T(8,128)(2,1)}, u32[]{:S(2)}) copy-start(bf16[128,32,256]{2,1,0:T(8,128)(2,1)} %mortar_ref.1) | copy-start | bytes 6291460
  4.7 6.5 %copy-start.2 = (bf16[1,256,256]{2,1,0:T(8,128)(2,1)S(1)}, bf16[1,256,256]{2,1,0:T(8,128)(2,1)}, u32[]{:S(2)}) copy-start(bf16[1,256,256]{2,1,0:T(8,128)(2,1)} %basis_ref.1) | copy-start | bytes 393220
  4.7 6.5 %copy-start.3 = (bf16[128,256]{1,0:T(8,128)(2,1)S(1)}, bf16[128,256]{1,0:T(8,128)(2,1)}, u32[]{:S(2)}) copy-start(bf16[128,256]{1,0:T(8,128)(2,1)} %scale_ref.3) | copy-start | bytes 196612
  4.7 6.5 %copy-start.4 = (f32[32]{0:T(128)S(1)}, f32[32]{0:T(128)}, u32[]{:S(2)}) copy-start(f32[32]{0:T(128)} %param.10) | copy-start | bytes 388
  4.7 6.5 %copy-start.5 = (s32[32]{0:T(128)S(1)}, s32[32]{0:T(128)}, u32[]{:S(2)}) copy-start(s32[32]{0:T(128)} %param.11) | copy-start | bytes 388
  4.7 6.5 %copy-start.6 = (s32[128,1]{0,1:T(1,128)S(1)}, s32[128,1]{0,1:T(1,128)}, u32[]{:S(2)}) copy-start(s32[128,1]{0,1:T(1,128)} %param.12) | copy-start | bytes 1540
  4.7 6.5 %copy-start.7 = (s32[128]{0:T(128)S(1)}, s32[128]{0:T(128)}, u32[]{:S(2)}) copy-start(s32[128]{0:T(128)} %param.13) | copy-start | bytes 1540
  6.1 4.5 %collective-permute-start.1 = (bf16[80,256]{1,0:T(8,128)(2,1)S(1)}, bf16[80,256]{1,0:T(8,128)(2,1)S(1)}, u32[]{:S(2)}, u32[]{:S(2)}) collective-permute-start(bf16[80,256]{1,0:T(8,128)(2,1)S(1)} %get-tuple-element.23), channel_id=1, source_target_pairs={{0,1},{1,0},{2,3},{3,2},{4,5},{5,4},{6,7},{7,6},{8,9},{9,8},{10,11... | collective-permute-start | bytes 122888 | tf_op jit(solution)/shard_map/ppermute | solution.py:204
  6.2 5.0 %collective-permute-start.3 = (bf16[80,256]{1,0:T(8,128)(2,1)S(1)}, bf16[80,256]{1,0:T(8,128)(2,1)S(1)}, u32[]{:S(2)}, u32[]{:S(2)}) collective-permute-start(bf16[80,256]{1,0:T(8,128)(2,1)S(1)} %get-tuple-element.27), channel_id=1, source_target_pairs={{0,8},{4,12},{8,0},{12,4},{1,9},{5,13},{9,1},{13,5},{2,10},{6,14},... | collective-permute-start | bytes 122888 | tf_op jit(solution)/shard_map/ppermute | solution.py:202
  7.3 4.7 %collective-permute-start.4 = (bf16[80,256]{1,0:T(8,128)(2,1)S(1)}, bf16[80,256]{1,0:T(8,128)(2,1)S(1)}, u32[]{:S(2)}, u32[]{:S(2)}) collective-permute-start(bf16[80,256]{1,0:T(8,128)(2,1)S(1)} %get-tuple-element.29), channel_id=1, source_target_pairs={{0,4},{4,0},{8,12},{12,8},{1,5},{5,1},{9,13},{13,9},{2,6},{6,2},{1... | collective-permute-start | bytes 122888 | tf_op jit(solution)/shard_map/ppermute | solution.py:202
  8.1 5.9 %collective-permute-start.6 = (bf16[80,256]{1,0:T(8,128)(2,1)S(1)}, bf16[80,256]{1,0:T(8,128)(2,1)S(1)}, u32[]{:S(2)}, u32[]{:S(2)}) collective-permute-start(bf16[80,256]{1,0:T(8,128)(2,1)S(1)} %get-tuple-element.33), channel_id=1, source_target_pairs={{0,12},{4,8},{8,4},{12,0},{1,13},{5,9},{9,5},{13,1},{2,14},{6,10},... | collective-permute-start | bytes 122888 | tf_op jit(solution)/shard_map/ppermute | solution.py:202
  10.6 4.6 %collective-permute-start.2 = (bf16[1,256,256]{2,1,0:T(8,128)(2,1)S(1)}, bf16[1,256,256]{2,1,0:T(8,128)(2,1)S(1)}, u32[]{:S(2)}, u32[]{:S(2)}) collective-permute-start(bf16[1,256,256]{2,1,0:T(8,128)(2,1)S(1)} %collective-permute-done.refs_0_.refs_5_), channel_id=1, source_target_pairs={{0,5},{1,0},{4,1},{5,4},{8,13},{9,8},{12,9},{13,12},{2,7},{3,2},{6... | collective-permute-start | bytes 393224 | tf_op jit(solution)/shard_map/ppermute | solution.py:230
  11.2 1.3 %collective-permute-start.5 = (bf16[1,256,256]{2,1,0:T(8,128)(2,1)S(1)}, bf16[1,256,256]{2,1,0:T(8,128)(2,1)S(1)}, u32[]{:S(2)}, u32[]{:S(2)}) collective-permute-start(bf16[1,256,256]{2,1,0:T(8,128)(2,1)S(1)} %collective-permute-done.refs_0_.refs_5_), channel_id=1, source_target_pairs={{0,1},{1,0},{2,3},{3,2},{4,5},{5,4},{6,7},{7,6},{8,9},{9,8},{10,11... | collective-permute-start | bytes 393224 | tf_op jit(solution)/shard_map/ppermute | solution.py:232
  12.5 1.5 %collective-permute-start.7 = (bf16[80,256]{1,0:T(8,128)(2,1)S(1)}, bf16[80,256]{1,0:T(8,128)(2,1)S(1)}, u32[]{:S(2)}, u32[]{:S(2)}) collective-permute-start(bf16[80,256]{1,0:T(8,128)(2,1)S(1)} %collective-permute-done.3.refs_2_), channel_id=1, source_target_pairs={{0,1},{1,0},{2,3},{3,2},{4,5},{5,4},{6,7},{7,6},{8,9},{9,8},{10,11... | collective-permute-start | bytes 122888 | tf_op jit(solution)/shard_map/ppermute | solution.py:238
  12.7 1.4 %collective-permute-start.8 = (bf16[80,256]{1,0:T(8,128)(2,1)S(1)}, bf16[80,256]{1,0:T(8,128)(2,1)S(1)}, u32[]{:S(2)}, u32[]{:S(2)}) collective-permute-start(bf16[80,256]{1,0:T(8,128)(2,1)S(1)} %collective-permute-done.4.refs_6_), channel_id=1, source_target_pairs={{0,1},{1,0},{2,3},{3,2},{4,5},{5,4},{6,7},{7,6},{8,9},{9,8},{10,11... | collective-permute-start | bytes 122888 | tf_op jit(solution)/shard_map/ppermute | solution.py:238
  14.1 2.6 %copy-start = (bf16[256,256]{1,0:T(8,128)(2,1)S(1)}, bf16[256,256]{1,0:T(8,128)(2,1)}, u32[]{:S(2)}) copy-start(bf16[256,256]{1,0:T(8,128)(2,1)} %projection_ref.1) | copy-start | bytes 393220
  15.2 1.5 %collective-permute-start.9 = (bf16[1,256,256]{2,1,0:T(8,128)(2,1)S(1)}, bf16[1,256,256]{2,1,0:T(8,128)(2,1)S(1)}, u32[]{:S(2)}, u32[]{:S(2)}) collective-permute-start(bf16[1,256,256]{2,1,0:T(8,128)(2,1)S(1)} %collective-permute-done.2.refs_1_), channel_id=1, source_target_pairs={{0,1},{1,0},{2,3},{3,2},{4,5},{5,4},{6,7},{7,6},{8,9},{9,8},{10,11... | collective-permute-start | bytes 393224 | tf_op jit(solution)/shard_map/ppermute | solution.py:238
  15.5 1.2 %collective-permute-start.10 = (bf16[80,256]{1,0:T(8,128)(2,1)S(1)}, bf16[80,256]{1,0:T(8,128)(2,1)S(1)}, u32[]{:S(2)}, u32[]{:S(2)}) collective-permute-start(bf16[80,256]{1,0:T(8,128)(2,1)S(1)} %collective-permute-done.6.refs_2_), channel_id=1, source_target_pairs={{0,1},{1,0},{2,3},{3,2},{4,5},{5,4},{6,7},{7,6},{8,9},{9,8},{10,11... | collective-permute-start | bytes 122888 | tf_op jit(solution)/shard_map/ppermute | solution.py:238

commit v18 on v17

--- a/solution.py
+++ b/solution.py
@@ -259,11 +259,10 @@
         scratch_shapes=scratch(len(early), TILES),
         input_output_aliases={1: 0},
         compiler_params=pltpu.CompilerParams(vmem_limit_bytes=40 * MIB),
-        cost_estimate=LIGHT,
+        cost_estimate=WORK,
         name="stage",
     )(*operands)
 
-    seconds, total = lax.optimization_barrier((seconds, total))
     late = [[other, second, *pair] for (second, other), pair in zip(with_swapped(seconds), later)]
 
     operands = [pumped, total, projection, *sum(late, [])]

time: 18.7 us -> 18.3 us (0.979)
  waiting for transfers between devices: 2.97 us -> 2.07 us
  starting transfers between devices: 9.62 us -> 10.1 us
    ppermute x4, waiting for transfers between devices: 0.92 us -> 0.01 us  [with_swapped(): return [(array, lax.ppermute(array, 'face', swap)) for array in arrays]]
    ppermute x4, starting transfers between devices: 1.09 us -> 1.52 us  [with_swapped(): return [(array, lax.ppermute(array, 'face', swap)) for array in arrays]]
  transfers between devices with their start and end apart: 11 -> 11, of which waited for: 4 -> 3; matrix products, arithmetic and copies ran while one was open for 0% -> 0% of each run, Pallas kernels for 18% -> 18%
where the time goes in v18:
time: 18.3 us; the launch traced here: 18.1 us
  starting transfers between devices  10.1 us (55%)
  Pallas kernels  5.14 us (28%)
  waiting for transfers between devices  2.07 us (11%)
  between operations  0.82 us (4%)
    ppermute x3, starting transfers between devices, on_device(): lax.ppermute(pack, 'sub', [(i, i ^ p) for i in range(subdomains)])  4.45 us
    ppermute x1, starting transfers between devices, on_device(): lax.ppermute(basis, ('sub', 'face'), [(flat(s, face), flat(s ^ (1 if face...  4.04 us
    pallas_call x1, Pallas kernels, on_device(): pl.pallas_call(last_kernel, out_shape=jax.ShapeDtypeStruct(block_shape, j...  1.86 us
    ppermute x3, waiting for transfers between devices, on_device(): lax.ppermute(pack, 'sub', [(i, i ^ p) for i in range(subdomains)])  1.56 us
    ppermute x4, starting transfers between devices, with_swapped(): return [(array, lax.ppermute(array, 'face', swap)) for array in arrays]  1.52 us
    pallas_call x1, Pallas kernels, on_device(): pl.pallas_call(functools.partial(pack_kernel, partners), out_shape=[pltpu...  1.36 us
    pallas_call x1, Pallas kernels, on_device(): pl.pallas_call(stage_kernel, out_shape=jax.ShapeDtypeStruct(block_shape,...  1.14 us
    pallas_call x1, Pallas kernels, on_device(): pl.pallas_call(own_kernel, out_shape=[jax.ShapeDtypeStruct(block_shape, j...  0.78 us
  transfers between devices with their start and end apart: 11, of which 3 were waited for; matrix products, arithmetic and copies ran while one was open for 0% of the time, Pallas kernels for 18%

profile of v18, /device:TPU:0, one launch (start us, length us, event | category | flops | bytes accessed | tf_op | source)
XLA Modules:
  0.0 18.1 jit_solution(1240954599503368416)
XLA Ops:
  0.0 4.0 %collective-permute-start = (bf16[1,256,256]{2,1,0:T(8,128)(2,1)}, bf16[1,256,256]{2,1,0:T(8,128)(2,1)S(1)}, u32[]{:S(2)}, u32[]{:S(2)}) collective-permute-start(bf16[1,256,256]{2,1,0:T(8,128)(2,1)} %basis_ref.1), channel_id=1, source_target_pairs={{0,8},{1,5},{4,12},{5,1},{8,0},{9,13},{12,4},{13,9},{2,10},{3,7},{... | collective-permute-start | bytes 393224 | tf_op jit(solution)/shard_map/ppermute | solution.py:184
  4.7 0.0 copy-start.1
  4.7 0.0 copy-start.2
  4.7 0.0 copy-start.3
  4.7 0.0 copy-start.4
  4.7 0.0 copy-start.5
  4.7 0.0 copy-start.6
  4.7 0.0 copy-start.7
  4.8 1.4 %pack_weights.1 = (bf16[80,256]{1,0:T(8,128)(2,1)S(1)}, bf16[80,256]{1,0:T(8,128)(2,1)S(1)}, bf16[80,256]{1,0:T(8,128)(2,1)S(1)}, bf16[80,256]{1,0:T(8,128)(2,1)S(1)}) custom-call(s32[1,128]{1,0:T(1,128)} %bitcast.6, s32[1,128]{1,0:T(1,128)} %bitcast.8, bf16[128,256]{1,0:T(8,128)(2,1)} %scale_ref.3, s32[1]{0:T(128)S(6)} %copy.12.section_ref), custom_call_target="tpu_custom_call" | custom-call | flops 4000000000 | bytes 8388608 | tf_op jit(solution)/shard_map/pack_weights/pallas_call | solution.py:192
  6.1 0.0 collective-permute-start.1
  6.2 1.1 %collective-permute-start.2 = (bf16[80,256]{1,0:T(8,128)(2,1)S(1)}, bf16[80,256]{1,0:T(8,128)(2,1)S(1)}, u32[]{:S(2)}, u32[]{:S(2)}) collective-permute-start(bf16[80,256]{1,0:T(8,128)(2,1)S(1)} %get-tuple-element.25), channel_id=1, source_target_pairs={{0,8},{4,12},{8,0},{12,4},{1,9},{5,13},{9,1},{13,5},{2,10},{6,14},... | collective-permute-start | bytes 122888 | tf_op jit(solution)/shard_map/ppermute | solution.py:202
  7.3 0.9 %collective-permute-start.3 = (bf16[80,256]{1,0:T(8,128)(2,1)S(1)}, bf16[80,256]{1,0:T(8,128)(2,1)S(1)}, u32[]{:S(2)}, u32[]{:S(2)}) collective-permute-start(bf16[80,256]{1,0:T(8,128)(2,1)S(1)} %get-tuple-element.27), channel_id=1, source_target_pairs={{0,4},{4,0},{8,12},{12,8},{1,5},{5,1},{9,13},{13,9},{2,6},{6,2},{1... | collective-permute-start | bytes 122888 | tf_op jit(solution)/shard_map/ppermute | solution.py:202
  8.1 2.5 %collective-permute-start.5 = (bf16[80,256]{1,0:T(8,128)(2,1)S(1)}, bf16[80,256]{1,0:T(8,128)(2,1)S(1)}, u32[]{:S(2)}, u32[]{:S(2)}) collective-permute-start(bf16[80,256]{1,0:T(8,128)(2,1)S(1)} %get-tuple-element.31), channel_id=1, source_target_pairs={{0,12},{4,8},{8,4},{12,0},{1,13},{5,9},{9,5},{13,1},{2,14},{6,10},... | collective-permute-start | bytes 122888 | tf_op jit(solution)/shard_map/ppermute | solution.py:202
  10.6 0.0 collective-permute-done.1.swapped_ref
  10.6 0.0 collective-permute-done.refs_0_.refs_5_
  10.6 0.0 collective-permute-start.8
  10.6 0.5 %collective-permute-done.2.refs_2_ = bf16[80,256]{1,0:T(8,128)(2,1)S(1)} collective-permute-done((bf16[80,256]{1,0:T(8,128)(2,1)S(1)}, bf16[80,256]{1,0:T(8,128)(2,1)S(1)}, u32[]{:S(2)}, u32[]{:S(2)}) %collective-permute-start.2) | collective-permute-done | bytes 40992 | tf_op jit(solution)/shard_map/ppermute | solution.py:202
  11.2 0.0 collective-permute-start.4
  11.2 0.0 copy-done.1
  11.2 0.0 copy-done.2
  11.2 0.0 copy-done.3
  11.2 0.0 copy-done.4
  11.2 0.0 copy-done.5
  11.2 0.0 copy-done.6
  11.2 0.0 copy-done.7
  11.2 0.8 %own_blocks.1 = (bf16[64,32,256]{2,1,0:T(8,128)(2,1)S(1)}, f32[64,32,256]{2,1,0:T(8,128)S(1)}) custom-call(bf16[128,32,256]{2,1,0:T(8,128)(2,1)S(1)} %copy-done.1, f32[1,32]{1,0:T(1,128)S(1)} %bitcast.4, s32[1,32]{1,0:T(1,128)S(1)} %bitcast.5, s32[1,128]{1,0:T(1,128)S(1)} %bitcast.7, s32[1,128]{1,0:T(1,128)S(1)} %bitcast.9, bf16[128,256]{1,0:T(8,128)(2,1)S(1)} %copy-done.3, ...), custom_call_target="tpu_custom_call" | custom-call | flops 4000000000 | bytes 8388608 | tf_op jit(solution)/shard_map/own_blocks/pallas_call | solution.py:207
  12.0 0.0 collective-permute-done.3.refs_6_
  12.0 0.5 %collective-permute-done.4.refs_1_.refs_4_ = bf16[1,256,256]{2,1,0:T(8,128)(2,1)S(1)} collective-permute-done((bf16[1,256,256]{2,1,0:T(8,128)(2,1)S(1)}, bf16[1,256,256]{2,1,0:T(8,128)(2,1)S(1)}, u32[]{:S(2)}, u32[]{:S(2)}) %collective-permute-start.4) | collective-permute-done | bytes 131104 | tf_op jit(solution)/shard_map/ppermute | solution.py:232
  12.5 0.1 collective-permute-start.6
  12.7 0.4 %collective-permute-start.7 = (bf16[80,256]{1,0:T(8,128)(2,1)S(1)}, bf16[80,256]{1,0:T(8,128)(2,1)S(1)}, u32[]{:S(2)}, u32[]{:S(2)}) collective-permute-start(bf16[80,256]{1,0:T(8,128)(2,1)S(1)} %collective-permute-done.3.refs_6_), channel_id=1, source_target_pairs={{0,1},{1,0},{2,3},{3,2},{4,5},{5,4},{6,7},{7,6},{8,9},{9,8},{10,11... | collective-permute-start | bytes 122888 | tf_op jit(solution)/shard_map/ppermute | solution.py:238
  13.0 1.0 %collective-permute-done.5.refs_2_ = bf16[80,256]{1,0:T(8,128)(2,1)S(1)} collective-permute-done((bf16[80,256]{1,0:T(8,128)(2,1)S(1)}, bf16[80,256]{1,0:T(8,128)(2,1)S(1)}, u32[]{:S(2)}, u32[]{:S(2)}) %collective-permute-start.5) | collective-permute-done | bytes 40992 | tf_op jit(solution)/shard_map/ppermute | solution.py:202
  14.1 0.0 collective-permute-start.10
  14.1 0.0 collective-permute-done.8.refs_1_
  14.1 1.0 %collective-permute-start.9 = (bf16[1,256,256]{2,1,0:T(8,128)(2,1)S(1)}, bf16[1,256,256]{2,1,0:T(8,128)(2,1)S(1)}, u32[]{:S(2)}, u32[]{:S(2)}) collective-permute-start(bf16[1,256,256]{2,1,0:T(8,128)(2,1)S(1)} %collective-permute-done.8.refs_1_), channel_id=1, source_target_pairs={{0,1},{1,0},{2,3},{3,2},{4,5},{5,4},{6,7},{7,6},{8,9},{9,8},{10,11... | collective-permute-start | bytes 393224 | tf_op jit(solution)/shard_map/ppermute | solution.py:238
  15.1 0.0 collective-permute-done.6.refs_3_
  15.1 0.0 collective-permute-done.7.refs_7_
  15.1 0.0 copy-start
  15.1 1.1 %stage.1.sum_ref = f32[64,32,256]{2,1,0:T(8,128)S(1)} custom-call(bf16[64,32,256]{2,1,0:T(8,128)(2,1)S(1)} %get-tuple-element.23.pumped_ref, f32[64,32,256]{2,1,0:T(8,128)S(1)} %get-tuple-element.32.sum_ref, bf16[1,256,256]{2,1,0:T(8,128)(2,1)S(1)} %collective-permute-done.refs_0_.refs_5_, ...), custom_call_target="tpu_custom_call", output_to_operand_aliasing={{}: (1, {})} | custom-call | flops 4000000000 | bytes 8388608 | tf_op jit(solution)/shard_map/stage/pallas_call | solution.py:254
  16.2 0.0 collective-permute-done.10.refs_3_
  16.2 0.0 collective-permute-done.9.refs_0_
  16.2 0.0 copy-done
  16.3 1.9 %last_stage.1 = f32[64,32,256]{2,1,0:T(8,128)} custom-call(bf16[64,32,256]{2,1,0:T(8,128)(2,1)S(1)} %get-tuple-element.23.pumped_ref, f32[64,32,256]{2,1,0:T(8,128)S(1)} %stage.1.sum_ref, bf16[256,256]{1,0:T(8,128)(2,1)S(1)} %copy-done, bf16[1,256,256]{2,1,0:T(8,128)(2,1)S(1)} %collective-permute-done.9.refs_0_, ...), custom_call_target="tpu_custom_call" | custom-call | tf_op jit(solution)/shard_map/last_stage/pallas_call | solution.py:269
Async XLA Ops:
  0.0 10.6 %collective-permute-start = (bf16[1,256,256]{2,1,0:T(8,128)(2,1)}, bf16[1,256,256]{2,1,0:T(8,128)(2,1)S(1)}, u32[]{:S(2)}, u32[]{:S(2)}) collective-permute-start(bf16[1,256,256]{2,1,0:T(8,128)(2,1)} %basis_ref.1), channel_id=1, source_target_pairs={{0,8},{1,5},{4,12},{5,1},{8,0},{9,13},{12,4},{13,9},{2,10},{3,7},{... | collective-permute-start | bytes 393224 | tf_op jit(solution)/shard_map/ppermute | solution.py:184
  4.7 6.5 %copy-start.1 = (bf16[128,32,256]{2,1,0:T(8,128)(2,1)S(1)}, bf16[128,32,256]{2,1,0:T(8,128)(2,1)}, u32[]{:S(2)}) copy-start(bf16[128,32,256]{2,1,0:T(8,128)(2,1)} %mortar_ref.1) | copy-start | bytes 6291460
  4.7 6.5 %copy-start.2 = (bf16[1,256,256]{2,1,0:T(8,128)(2,1)S(1)}, bf16[1,256,256]{2,1,0:T(8,128)(2,1)}, u32[]{:S(2)}) copy-start(bf16[1,256,256]{2,1,0:T(8,128)(2,1)} %basis_ref.1) | copy-start | bytes 393220
  4.7 6.5 %copy-start.3 = (bf16[128,256]{1,0:T(8,128)(2,1)S(1)}, bf16[128,256]{1,0:T(8,128)(2,1)}, u32[]{:S(2)}) copy-start(bf16[128,256]{1,0:T(8,128)(2,1)} %scale_ref.3) | copy-start | bytes 196612
  4.7 6.5 %copy-start.4 = (f32[32]{0:T(128)S(1)}, f32[32]{0:T(128)}, u32[]{:S(2)}) copy-start(f32[32]{0:T(128)} %param.10) | copy-start | bytes 388
  4.7 6.5 %copy-start.5 = (s32[32]{0:T(128)S(1)}, s32[32]{0:T(128)}, u32[]{:S(2)}) copy-start(s32[32]{0:T(128)} %param.11) | copy-start | bytes 388
  4.7 6.5 %copy-start.6 = (s32[128,1]{0,1:T(1,128)S(1)}, s32[128,1]{0,1:T(1,128)}, u32[]{:S(2)}) copy-start(s32[128,1]{0,1:T(1,128)} %param.12) | copy-start | bytes 1540
  4.7 6.5 %copy-start.7 = (s32[128]{0:T(128)S(1)}, s32[128]{0:T(128)}, u32[]{:S(2)}) copy-start(s32[128]{0:T(128)} %param.13) | copy-start | bytes 1540
  6.1 4.5 %collective-permute-start.1 = (bf16[80,256]{1,0:T(8,128)(2,1)S(1)}, bf16[80,256]{1,0:T(8,128)(2,1)S(1)}, u32[]{:S(2)}, u32[]{:S(2)}) collective-permute-start(bf16[80,256]{1,0:T(8,128)(2,1)S(1)} %get-tuple-element.21), channel_id=1, source_target_pairs={{0,1},{1,0},{2,3},{3,2},{4,5},{5,4},{6,7},{7,6},{8,9},{9,8},{10,11... | collective-permute-start | bytes 122888 | tf_op jit(solution)/shard_map/ppermute | solution.py:204
  6.2 5.0 %collective-permute-start.2 = (bf16[80,256]{1,0:T(8,128)(2,1)S(1)}, bf16[80,256]{1,0:T(8,128)(2,1)S(1)}, u32[]{:S(2)}, u32[]{:S(2)}) collective-permute-start(bf16[80,256]{1,0:T(8,128)(2,1)S(1)} %get-tuple-element.25), channel_id=1, source_target_pairs={{0,8},{4,12},{8,0},{12,4},{1,9},{5,13},{9,1},{13,5},{2,10},{6,14},... | collective-permute-start | bytes 122888 | tf_op jit(solution)/shard_map/ppermute | solution.py:202
  7.3 4.7 %collective-permute-start.3 = (bf16[80,256]{1,0:T(8,128)(2,1)S(1)}, bf16[80,256]{1,0:T(8,128)(2,1)S(1)}, u32[]{:S(2)}, u32[]{:S(2)}) collective-permute-start(bf16[80,256]{1,0:T(8,128)(2,1)S(1)} %get-tuple-element.27), channel_id=1, source_target_pairs={{0,4},{4,0},{8,12},{12,8},{1,5},{5,1},{9,13},{13,9},{2,6},{6,2},{1... | collective-permute-start | bytes 122888 | tf_op jit(solution)/shard_map/ppermute | solution.py:202
  8.1 5.9 %collective-permute-start.5 = (bf16[80,256]{1,0:T(8,128)(2,1)S(1)}, bf16[80,256]{1,0:T(8,128)(2,1)S(1)}, u32[]{:S(2)}, u32[]{:S(2)}) collective-permute-start(bf16[80,256]{1,0:T(8,128)(2,1)S(1)} %get-tuple-element.31), channel_id=1, source_target_pairs={{0,12},{4,8},{8,4},{12,0},{1,13},{5,9},{9,5},{13,1},{2,14},{6,10},... | collective-permute-start | bytes 122888 | tf_op jit(solution)/shard_map/ppermute | solution.py:202
  10.6 3.4 %collective-permute-start.8 = (bf16[1,256,256]{2,1,0:T(8,128)(2,1)S(1)}, bf16[1,256,256]{2,1,0:T(8,128)(2,1)S(1)}, u32[]{:S(2)}, u32[]{:S(2)}) collective-permute-start(bf16[1,256,256]{2,1,0:T(8,128)(2,1)S(1)} %collective-permute-done.refs_0_.refs_5_), channel_id=1, source_target_pairs={{0,5},{1,0},{4,1},{5,4},{8,13},{9,8},{12,9},{13,12},{2,7},{3,2},{6... | collective-permute-start | bytes 393224 | tf_op jit(solution)/shard_map/ppermute | solution.py:230
  11.2 1.3 %collective-permute-start.4 = (bf16[1,256,256]{2,1,0:T(8,128)(2,1)S(1)}, bf16[1,256,256]{2,1,0:T(8,128)(2,1)S(1)}, u32[]{:S(2)}, u32[]{:S(2)}) collective-permute-start(bf16[1,256,256]{2,1,0:T(8,128)(2,1)S(1)} %collective-permute-done.refs_0_.refs_5_), channel_id=1, source_target_pairs={{0,1},{1,0},{2,3},{3,2},{4,5},{5,4},{6,7},{7,6},{8,9},{9,8},{10,11... | collective-permute-start | bytes 393224 | tf_op jit(solution)/shard_map/ppermute | solution.py:232
  12.5 2.6 %collective-permute-start.6 = (bf16[80,256]{1,0:T(8,128)(2,1)S(1)}, bf16[80,256]{1,0:T(8,128)(2,1)S(1)}, u32[]{:S(2)}, u32[]{:S(2)}) collective-permute-start(bf16[80,256]{1,0:T(8,128)(2,1)S(1)} %collective-permute-done.2.refs_2_), channel_id=1, source_target_pairs={{0,1},{1,0},{2,3},{3,2},{4,5},{5,4},{6,7},{7,6},{8,9},{9,8},{10,11... | collective-permute-start | bytes 122888 | tf_op jit(solution)/shard_map/ppermute | solution.py:238
  12.7 2.4 %collective-permute-start.7 = (bf16[80,256]{1,0:T(8,128)(2,1)S(1)}, bf16[80,256]{1,0:T(8,128)(2,1)S(1)}, u32[]{:S(2)}, u32[]{:S(2)}) collective-permute-start(bf16[80,256]{1,0:T(8,128)(2,1)S(1)} %collective-permute-done.3.refs_6_), channel_id=1, source_target_pairs={{0,1},{1,0},{2,3},{3,2},{4,5},{5,4},{6,7},{7,6},{8,9},{9,8},{10,11... | collective-permute-start | bytes 122888 | tf_op jit(solution)/shard_map/ppermute | solution.py:238
  14.1 2.2 %collective-permute-start.10 = (bf16[80,256]{1,0:T(8,128)(2,1)S(1)}, bf16[80,256]{1,0:T(8,128)(2,1)S(1)}, u32[]{:S(2)}, u32[]{:S(2)}) collective-permute-start(bf16[80,256]{1,0:T(8,128)(2,1)S(1)} %collective-permute-done.5.refs_2_), channel_id=1, source_target_pairs={{0,1},{1,0},{2,3},{3,2},{4,5},{5,4},{6,7},{7,6},{8,9},{9,8},{10,11... | collective-permute-start | bytes 122888 | tf_op jit(solution)/shard_map/ppermute | solution.py:238
  14.1 2.2 %collective-permute-start.9 = (bf16[1,256,256]{2,1,0:T(8,128)(2,1)S(1)}, bf16[1,256,256]{2,1,0:T(8,128)(2,1)S(1)}, u32[]{:S(2)}, u32[]{:S(2)}) collective-permute-start(bf16[1,256,256]{2,1,0:T(8,128)(2,1)S(1)} %collective-permute-done.8.refs_1_), channel_id=1, source_target_pairs={{0,1},{1,0},{2,3},{3,2},{4,5},{5,4},{6,7},{7,6},{8,9},{9,8},{10,11... | collective-permute-start | bytes 393224 | tf_op jit(solution)/shard_map/ppermute | solution.py:238
  15.1 1.2 %copy-start = (bf16[256,256]{1,0:T(8,128)(2,1)S(1)}, bf16[256,256]{1,0:T(8,128)(2,1)}, u32[]{:S(2)}) copy-start(bf16[256,256]{1,0:T(8,128)(2,1)} %projection_ref.1) | copy-start | bytes 393220

commit v19 on v18

--- a/solution.py
+++ b/solution.py
@@ -15,6 +15,7 @@
 MIB = 1024 * 1024
 TILES = 4
 LAST_TILES = 8
+HANDED_PARTS = 2
 LIGHT = pl.CostEstimate(flops=1_000_000, bytes_accessed=1024, transcendentals=0)
 WORK = pl.CostEstimate(flops=4_000_000_000, bytes_accessed=8 * MIB, transcendentals=0)
 
@@ -111,16 +112,19 @@
         sum_ref[at] = flux.reshape(tile_blocks, columns, dof_count)
 
 
-def gather_partners(arrays, weight_ref, basis_ref):
+def gather_partners(parts, arrays, weight_ref, basis_ref):
     count, blocks_own, dof_count = weight_ref.shape
+    each, rows = 2 * parts + 2, dof_count // parts
     for at in range(count):
-        base_0, base_1, pack, pack_swapped = arrays[4 * at : 4 * at + 4]
+        *bases, pack, pack_swapped = arrays[each * at : each * (at + 1)]
         weight_ref[at] = block_weights((pack, pack_swapped), pack.shape[0] - SLOT_ROWS, blocks_own)
-        for core, base in enumerate((base_0, base_1)):
+        for core in range(2):
 
             @pl.when(lax.axis_index("face") == core)
             def _():
-                basis_ref[at * dof_count : (at + 1) * dof_count, :] = base[0]
+                for part, base in enumerate(bases[core * parts : (core + 1) * parts]):
+                    start = at * dof_count + part * rows
+                    basis_ref[start : start + rows, :] = base[0]
 
 
 def tile_flux(at, slot, pumped_ref, sum_ref, weight_ref, basis_ref, scaled_ref):
@@ -136,7 +140,7 @@
 
 def stage_kernel(pumped_ref, sum_ref, *refs):
     arrays, (out_ref, weight_ref, basis_ref, scaled_ref) = refs[:-4], refs[-4:]
-    gather_partners(arrays, weight_ref, basis_ref)
+    gather_partners(1, arrays, weight_ref, basis_ref)
     tile_blocks = pumped_ref.shape[0] // TILES
     for tile in range(TILES):
         at = slice(tile * tile_blocks, (tile + 1) * tile_blocks)
@@ -146,7 +150,7 @@
 
 def last_kernel(pumped_ref, sum_ref, projection_ref, *refs):
     arrays, (result_ref, weight_ref, basis_ref, scaled_ref, out_ref, sems) = refs[:-6], refs[-6:]
-    gather_partners(arrays, weight_ref, basis_ref)
+    gather_partners(HANDED_PARTS, arrays, weight_ref, basis_ref)
     tiles = sems.shape[0]
     tile_blocks = pumped_ref.shape[0] // tiles
     copies = []
@@ -227,7 +231,12 @@
     )
 
     pairs = [(flat(s, face), flat(s, 0) if face else flat(s ^ 1, 1)) for s, face in cells]
-    seconds = [lax.ppermute(first, ("sub", "face"), pairs) for first in firsts]
+    part_rows = dof_count // HANDED_PARTS
+    seconds = [
+        lax.ppermute(first[:, i * part_rows : (i + 1) * part_rows], ("sub", "face"), pairs)
+        for first in firsts
+        for i in range(HANDED_PARTS)
+    ]
     firsts, arrived[:len(evens)] = lax.optimization_barrier((firsts, arrived[:len(evens)]))
     firsts_swapped = [lax.ppermute(first, "face", swap) for first in firsts]
     soon, own_sum, firsts_swapped = lax.optimization_barrier(
@@ -263,7 +272,11 @@
         name="stage",
     )(*operands)
 
-    late = [[other, second, *pair] for (second, other), pair in zip(with_swapped(seconds), later)]
+    seconds = with_swapped(seconds)
+    late = []
+    for at, pair in enumerate(later):
+        handed = seconds[at * HANDED_PARTS : (at + 1) * HANDED_PARTS]
+        late.append([*[other for _, other in handed], *[second for second, _ in handed], *pair])
 
     operands = [pumped, total, projection, *sum(late, [])]
     return pl.pallas_call(

time: 18.3 us -> 19.4 us (1.060)
  starting transfers between devices: 10.1 us -> 12 us
  waiting for transfers between devices: 2.07 us -> 1.3 us
    ppermute x1 -> x2, starting transfers between devices: 0.01 us -> 2.06 us  [on_device(): lax.ppermute(first[:, i * part_rows:(i + 1) * part_rows], ('sub', 'face')...]
    ppermute x3, waiting for transfers between devices: 1.56 us -> 0.52 us  [on_device(): lax.ppermute(pack, 'sub', [(i, i ^ p) for i in range(subdomains)])]
    ppermute x1 -> x2, waiting for transfers between devices: 0.01 us -> 0.75 us  [on_device(): lax.ppermute(first[:, i * part_rows:(i + 1) * part_rows], ('sub', 'face')...]
    ppermute x1, waiting for transfers between devices: 0.49 us -> 0.01 us  [on_device(): firsts_swapped = [lax.ppermute(first, 'face', swap) for first in firsts]]
    ppermute x4 -> x5, starting transfers between devices: 1.52 us -> 1.4 us  [with_swapped(): return [(array, lax.ppermute(array, 'face', swap)) for array in arrays]]
  transfers between devices with their start and end apart: 11 -> 13, of which waited for: 3 -> 3; matrix products, arithmetic and copies ran while one was open for 0% -> 0% of each run, Pallas kernels for 18% -> 17%
where the time goes in v19:
time: 19.4 us; the launch traced here: 19.3 us
  starting transfers between devices  12 us (62%)
  Pallas kernels  5.14 us (26%)
  waiting for transfers between devices  1.3 us (7%)
  between operations  0.82 us (4%)
    ppermute x3, starting transfers between devices, on_device(): lax.ppermute(pack, 'sub', [(i, i ^ p) for i in range(subdomains)])  4.45 us
    ppermute x1, starting transfers between devices, on_device(): lax.ppermute(basis, ('sub', 'face'), [(flat(s, face), flat(s ^ (1 if face...  4.04 us
    ppermute x2, starting transfers between devices, on_device(): lax.ppermute(first[:, i * part_rows:(i + 1) * part_rows], ('sub', 'face')...  2.06 us
    pallas_call x1, Pallas kernels, on_device(): pl.pallas_call(last_kernel, out_shape=jax.ShapeDtypeStruct(block_shape, j...  1.86 us
    ppermute x5, starting transfers between devices, with_swapped(): return [(array, lax.ppermute(array, 'face', swap)) for array in arrays]  1.4 us
    pallas_call x1, Pallas kernels, on_device(): pl.pallas_call(functools.partial(pack_kernel, partners), out_shape=[pltpu...  1.36 us
    pallas_call x1, Pallas kernels, on_device(): pl.pallas_call(stage_kernel, out_shape=jax.ShapeDtypeStruct(block_shape,...  1.14 us
    pallas_call x1, Pallas kernels, on_device(): pl.pallas_call(own_kernel, out_shape=[jax.ShapeDtypeStruct(block_shape, j...  0.78 us
  transfers between devices with their start and end apart: 13, of which 3 were waited for; matrix products, arithmetic and copies ran while one was open for 0% of the time, Pallas kernels for 17%

profile of v19, /device:TPU:0, one launch (start us, length us, event | category | flops | bytes accessed | tf_op | source)
XLA Modules:
  0.0 19.3 jit_solution(17449018978693794974)
XLA Ops:
  0.0 4.0 %collective-permute-start = (bf16[1,256,256]{2,1,0:T(8,128)(2,1)}, bf16[1,256,256]{2,1,0:T(8,128)(2,1)S(1)}, u32[]{:S(2)}, u32[]{:S(2)}) collective-permute-start(bf16[1,256,256]{2,1,0:T(8,128)(2,1)} %basis_ref.1), channel_id=1, source_target_pairs={{0,8},{1,5},{4,12},{5,1},{8,0},{9,13},{12,4},{13,9},{2,10},{3,7},{... | collective-permute-start | bytes 393224 | tf_op jit(solution)/shard_map/ppermute | solution.py:188
  4.7 0.0 copy-start.1
  4.7 0.0 copy-start.2
  4.7 0.0 copy-start.3
  4.7 0.0 copy-start.4
  4.7 0.0 copy-start.5
  4.7 0.0 copy-start.6
  4.7 0.0 copy-start.7
  4.8 1.4 %pack_weights.1 = (bf16[80,256]{1,0:T(8,128)(2,1)S(1)}, bf16[80,256]{1,0:T(8,128)(2,1)S(1)}, bf16[80,256]{1,0:T(8,128)(2,1)S(1)}, bf16[80,256]{1,0:T(8,128)(2,1)S(1)}) custom-call(s32[1,128]{1,0:T(1,128)} %bitcast.6, s32[1,128]{1,0:T(1,128)} %bitcast.8, bf16[128,256]{1,0:T(8,128)(2,1)} %scale_ref.3, s32[1]{0:T(128)S(6)} %copy.12.section_ref), custom_call_target="tpu_custom_call" | custom-call | flops 4000000000 | bytes 8388608 | tf_op jit(solution)/shard_map/pack_weights/pallas_call | solution.py:196
  6.1 0.0 collective-permute-start.1
  6.2 1.1 %collective-permute-start.2 = (bf16[80,256]{1,0:T(8,128)(2,1)S(1)}, bf16[80,256]{1,0:T(8,128)(2,1)S(1)}, u32[]{:S(2)}, u32[]{:S(2)}) collective-permute-start(bf16[80,256]{1,0:T(8,128)(2,1)S(1)} %get-tuple-element.25), channel_id=1, source_target_pairs={{0,8},{4,12},{8,0},{12,4},{1,9},{5,13},{9,1},{13,5},{2,10},{6,14},... | collective-permute-start | bytes 122888 | tf_op jit(solution)/shard_map/ppermute | solution.py:206
  7.3 0.9 %collective-permute-start.3 = (bf16[80,256]{1,0:T(8,128)(2,1)S(1)}, bf16[80,256]{1,0:T(8,128)(2,1)S(1)}, u32[]{:S(2)}, u32[]{:S(2)}) collective-permute-start(bf16[80,256]{1,0:T(8,128)(2,1)S(1)} %get-tuple-element.27), channel_id=1, source_target_pairs={{0,4},{4,0},{8,12},{12,8},{1,5},{5,1},{9,13},{13,9},{2,6},{6,2},{1... | collective-permute-start | bytes 122888 | tf_op jit(solution)/shard_map/ppermute | solution.py:206
  8.1 2.5 %collective-permute-start.5 = (bf16[80,256]{1,0:T(8,128)(2,1)S(1)}, bf16[80,256]{1,0:T(8,128)(2,1)S(1)}, u32[]{:S(2)}, u32[]{:S(2)}) collective-permute-start(bf16[80,256]{1,0:T(8,128)(2,1)S(1)} %get-tuple-element.31), channel_id=1, source_target_pairs={{0,12},{4,8},{8,4},{12,0},{1,13},{5,9},{9,5},{13,1},{2,14},{6,10},... | collective-permute-start | bytes 122888 | tf_op jit(solution)/shard_map/ppermute | solution.py:206
  10.6 0.0 collective-permute-done.1.swapped_ref
  10.6 0.0 collective-permute-done.refs_0_.refs_5_
  10.6 0.5 %collective-permute-done.2.refs_2_ = bf16[80,256]{1,0:T(8,128)(2,1)S(1)} collective-permute-done((bf16[80,256]{1,0:T(8,128)(2,1)S(1)}, bf16[80,256]{1,0:T(8,128)(2,1)S(1)}, u32[]{:S(2)}, u32[]{:S(2)}) %collective-permute-start.2) | collective-permute-done | bytes 40992 | tf_op jit(solution)/shard_map/ppermute | solution.py:206
  11.2 0.0 collective-permute-start.4
  11.2 2.0 %collective-permute-start.10 = (bf16[1,128,256]{2,1,0:T(8,128)(2,1)S(1)}, bf16[1,128,256]{2,1,0:T(8,128)(2,1)S(1)}, u32[]{:S(2)}, u32[]{:S(2)}) collective-permute-start(bf16[1,128,256]{2,1,0:T(8,128)(2,1)S(1)} %get-tuple-element.37), channel_id=1, source_target_pairs={{0,5},{1,0},{4,1},{5,4},{8,13},{9,8},{12,9},{13,12},{2,7},{3,2},{6... | collective-permute-start | bytes 196616 | tf_op jit(solution)/shard_map/ppermute | solution.py:236
  13.2 0.0 collective-permute-start.8
  13.2 0.0 copy-done.1
  13.2 0.0 copy-done.2
  13.2 0.0 copy-done.3
  13.2 0.0 copy-done.4
  13.2 0.0 copy-done.5
  13.2 0.0 copy-done.6
  13.3 0.0 copy-done.7
  13.3 0.8 %own_blocks.1 = (bf16[64,32,256]{2,1,0:T(8,128)(2,1)S(1)}, f32[64,32,256]{2,1,0:T(8,128)S(1)}) custom-call(bf16[128,32,256]{2,1,0:T(8,128)(2,1)S(1)} %copy-done.1, f32[1,32]{1,0:T(1,128)S(1)} %bitcast.4, s32[1,32]{1,0:T(1,128)S(1)} %bitcast.5, s32[1,128]{1,0:T(1,128)S(1)} %bitcast.7, s32[1,128]{1,0:T(1,128)S(1)} %bitcast.9, bf16[128,256]{1,0:T(8,128)(2,1)S(1)} %copy-done.3, ...), custom_call_target="tpu_custom_call" | custom-call | flops 4000000000 | bytes 8388608 | tf_op jit(solution)/shard_map/own_blocks/pallas_call | solution.py:211
  14.1 0.0 collective-permute-done.3.refs_6_
  14.1 0.0 collective-permute-done.4.refs_1_.refs_4_
  14.1 0.5 %collective-permute-start.6 = (bf16[80,256]{1,0:T(8,128)(2,1)S(1)}, bf16[80,256]{1,0:T(8,128)(2,1)S(1)}, u32[]{:S(2)}, u32[]{:S(2)}) collective-permute-start(bf16[80,256]{1,0:T(8,128)(2,1)S(1)} %collective-permute-done.2.refs_2_), channel_id=1, source_target_pairs={{0,1},{1,0},{2,3},{3,2},{4,5},{5,4},{6,7},{7,6},{8,9},{9,8},{10,11... | collective-permute-start | bytes 122888 | tf_op jit(solution)/shard_map/ppermute | solution.py:247
  14.6 0.1 collective-permute-start.7
  14.7 0.4 %collective-permute-done.10.refs_3_ = bf16[1,128,256]{2,1,0:T(8,128)(2,1)S(1)} collective-permute-done((bf16[1,128,256]{2,1,0:T(8,128)(2,1)S(1)}, bf16[1,128,256]{2,1,0:T(8,128)(2,1)S(1)}, u32[]{:S(2)}, u32[]{:S(2)}) %collective-permute-start.10) | collective-permute-done | bytes 65568 | tf_op jit(solution)/shard_map/ppermute | solution.py:236
  15.1 0.3 %collective-permute-start.11 = (bf16[1,128,256]{2,1,0:T(8,128)(2,1)S(1)}, bf16[1,128,256]{2,1,0:T(8,128)(2,1)S(1)}, u32[]{:S(2)}, u32[]{:S(2)}) collective-permute-start(bf16[1,128,256]{2,1,0:T(8,128)(2,1)S(1)} %collective-permute-done.10.refs_3_), channel_id=1, source_target_pairs={{0,1},{1,0},{2,3},{3,2},{4,5},{5,4},{6,7},{7,6},{8,9},{9,8},{10,11... | collective-permute-start | bytes 196616 | tf_op jit(solution)/shard_map/ppermute | solution.py:247
  15.4 0.3 %collective-permute-done.8.refs_2_ = bf16[1,128,256]{2,1,0:T(8,128)(2,1)S(1)} collective-permute-done((bf16[1,128,256]{2,1,0:T(8,128)(2,1)S(1)}, bf16[1,128,256]{2,1,0:T(8,128)(2,1)S(1)}, u32[]{:S(2)}, u32[]{:S(2)}) %collective-permute-start.8) | collective-permute-done | bytes 65568 | tf_op jit(solution)/shard_map/ppermute | solution.py:236
  15.7 0.4 %collective-permute-start.9 = (bf16[1,128,256]{2,1,0:T(8,128)(2,1)S(1)}, bf16[1,128,256]{2,1,0:T(8,128)(2,1)S(1)}, u32[]{:S(2)}, u32[]{:S(2)}) collective-permute-start(bf16[1,128,256]{2,1,0:T(8,128)(2,1)S(1)} %collective-permute-done.8.refs_2_), channel_id=1, source_target_pairs={{0,1},{1,0},{2,3},{3,2},{4,5},{5,4},{6,7},{7,6},{8,9},{9,8},{10,11... | collective-permute-start | bytes 196616 | tf_op jit(solution)/shard_map/ppermute | solution.py:247
  16.1 0.0 collective-permute-done.5.refs_4_
  16.1 0.2 collective-permute-start.12
  16.2 0.0 collective-permute-done.6.refs_3_
  16.2 0.0 collective-permute-done.7.refs_7_
  16.2 0.0 copy-start
  16.2 1.1 %stage.1.sum_ref = f32[64,32,256]{2,1,0:T(8,128)S(1)} custom-call(bf16[64,32,256]{2,1,0:T(8,128)(2,1)S(1)} %get-tuple-element.23.pumped_ref, f32[64,32,256]{2,1,0:T(8,128)S(1)} %get-tuple-element.32.sum_ref, bf16[1,256,256]{2,1,0:T(8,128)(2,1)S(1)} %collective-permute-done.refs_0_.refs_5_, ...), custom_call_target="tpu_custom_call", output_to_operand_aliasing={{}: (1, {})} | custom-call | flops 4000000000 | bytes 8388608 | tf_op jit(solution)/shard_map/stage/pallas_call | solution.py:263
  17.4 0.0 collective-permute-done.11.refs_1_
  17.4 0.0 collective-permute-done.9.refs_0_
  17.4 0.0 collective-permute-done.12.refs_5_
  17.4 0.0 copy-done
  17.4 1.9 %last_stage.1 = f32[64,32,256]{2,1,0:T(8,128)} custom-call(bf16[64,32,256]{2,1,0:T(8,128)(2,1)S(1)} %get-tuple-element.23.pumped_ref, f32[64,32,256]{2,1,0:T(8,128)S(1)} %stage.1.sum_ref, bf16[256,256]{1,0:T(8,128)(2,1)S(1)} %copy-done, bf16[1,128,256]{2,1,0:T(8,128)(2,1)S(1)} %collective-permute-done.9.refs_0_, ...), custom_call_target="tpu_custom_call" | custom-call | tf_op jit(solution)/shard_map/last_stage/pallas_call | solution.py:282
  (1 shorter events, 0.0 us)
Async XLA Ops:
  0.0 10.6 %collective-permute-start = (bf16[1,256,256]{2,1,0:T(8,128)(2,1)}, bf16[1,256,256]{2,1,0:T(8,128)(2,1)S(1)}, u32[]{:S(2)}, u32[]{:S(2)}) collective-permute-start(bf16[1,256,256]{2,1,0:T(8,128)(2,1)} %basis_ref.1), channel_id=1, source_target_pairs={{0,8},{1,5},{4,12},{5,1},{8,0},{9,13},{12,4},{13,9},{2,10},{3,7},{... | collective-permute-start | bytes 393224 | tf_op jit(solution)/shard_map/ppermute | solution.py:188
  4.7 8.5 %copy-start.1 = (bf16[128,32,256]{2,1,0:T(8,128)(2,1)S(1)}, bf16[128,32,256]{2,1,0:T(8,128)(2,1)}, u32[]{:S(2)}) copy-start(bf16[128,32,256]{2,1,0:T(8,128)(2,1)} %mortar_ref.1) | copy-start | bytes 6291460
  4.7 8.5 %copy-start.2 = (bf16[1,256,256]{2,1,0:T(8,128)(2,1)S(1)}, bf16[1,256,256]{2,1,0:T(8,128)(2,1)}, u32[]{:S(2)}) copy-start(bf16[1,256,256]{2,1,0:T(8,128)(2,1)} %basis_ref.1) | copy-start | bytes 393220
  4.7 8.5 %copy-start.3 = (bf16[128,256]{1,0:T(8,128)(2,1)S(1)}, bf16[128,256]{1,0:T(8,128)(2,1)}, u32[]{:S(2)}) copy-start(bf16[128,256]{1,0:T(8,128)(2,1)} %scale_ref.3) | copy-start | bytes 196612
  4.7 8.5 %copy-start.4 = (f32[32]{0:T(128)S(1)}, f32[32]{0:T(128)}, u32[]{:S(2)}) copy-start(f32[32]{0:T(128)} %param.10) | copy-start | bytes 388
  4.7 8.5 %copy-start.5 = (s32[32]{0:T(128)S(1)}, s32[32]{0:T(128)}, u32[]{:S(2)}) copy-start(s32[32]{0:T(128)} %param.11) | copy-start | bytes 388
  4.7 8.5 %copy-start.6 = (s32[128,1]{0,1:T(1,128)S(1)}, s32[128,1]{0,1:T(1,128)}, u32[]{:S(2)}) copy-start(s32[128,1]{0,1:T(1,128)} %param.12) | copy-start | bytes 1540
  4.7 8.5 %copy-start.7 = (s32[128]{0:T(128)S(1)}, s32[128]{0:T(128)}, u32[]{:S(2)}) copy-start(s32[128]{0:T(128)} %param.13) | copy-start | bytes 1540
  6.1 4.5 %collective-permute-start.1 = (bf16[80,256]{1,0:T(8,128)(2,1)S(1)}, bf16[80,256]{1,0:T(8,128)(2,1)S(1)}, u32[]{:S(2)}, u32[]{:S(2)}) collective-permute-start(bf16[80,256]{1,0:T(8,128)(2,1)S(1)} %get-tuple-element.21), channel_id=1, source_target_pairs={{0,1},{1,0},{2,3},{3,2},{4,5},{5,4},{6,7},{7,6},{8,9},{9,8},{10,11... | collective-permute-start | bytes 122888 | tf_op jit(solution)/shard_map/ppermute | solution.py:208
  6.2 5.0 %collective-permute-start.2 = (bf16[80,256]{1,0:T(8,128)(2,1)S(1)}, bf16[80,256]{1,0:T(8,128)(2,1)S(1)}, u32[]{:S(2)}, u32[]{:S(2)}) collective-permute-start(bf16[80,256]{1,0:T(8,128)(2,1)S(1)} %get-tuple-element.25), channel_id=1, source_target_pairs={{0,8},{4,12},{8,0},{12,4},{1,9},{5,13},{9,1},{13,5},{2,10},{6,14},... | collective-permute-start | bytes 122888 | tf_op jit(solution)/shard_map/ppermute | solution.py:206
  7.3 6.8 %collective-permute-start.3 = (bf16[80,256]{1,0:T(8,128)(2,1)S(1)}, bf16[80,256]{1,0:T(8,128)(2,1)S(1)}, u32[]{:S(2)}, u32[]{:S(2)}) collective-permute-start(bf16[80,256]{1,0:T(8,128)(2,1)S(1)} %get-tuple-element.27), channel_id=1, source_target_pairs={{0,4},{4,0},{8,12},{12,8},{1,5},{5,1},{9,13},{13,9},{2,6},{6,2},{1... | collective-permute-start | bytes 122888 | tf_op jit(solution)/shard_map/ppermute | solution.py:206
  8.1 7.9 %collective-permute-start.5 = (bf16[80,256]{1,0:T(8,128)(2,1)S(1)}, bf16[80,256]{1,0:T(8,128)(2,1)S(1)}, u32[]{:S(2)}, u32[]{:S(2)}) collective-permute-start(bf16[80,256]{1,0:T(8,128)(2,1)S(1)} %get-tuple-element.31), channel_id=1, source_target_pairs={{0,12},{4,8},{8,4},{12,0},{1,13},{5,9},{9,5},{13,1},{2,14},{6,10},... | collective-permute-start | bytes 122888 | tf_op jit(solution)/shard_map/ppermute | solution.py:206
  11.2 2.9 %collective-permute-start.4 = (bf16[1,256,256]{2,1,0:T(8,128)(2,1)S(1)}, bf16[1,256,256]{2,1,0:T(8,128)(2,1)S(1)}, u32[]{:S(2)}, u32[]{:S(2)}) collective-permute-start(bf16[1,256,256]{2,1,0:T(8,128)(2,1)S(1)} %collective-permute-done.refs_0_.refs_5_), channel_id=1, source_target_pairs={{0,1},{1,0},{2,3},{3,2},{4,5},{5,4},{6,7},{7,6},{8,9},{9,8},{10,11... | collective-permute-start | bytes 393224 | tf_op jit(solution)/shard_map/ppermute | solution.py:241
  11.2 3.9 %collective-permute-start.10 = (bf16[1,128,256]{2,1,0:T(8,128)(2,1)S(1)}, bf16[1,128,256]{2,1,0:T(8,128)(2,1)S(1)}, u32[]{:S(2)}, u32[]{:S(2)}) collective-permute-start(bf16[1,128,256]{2,1,0:T(8,128)(2,1)S(1)} %get-tuple-element.37), channel_id=1, source_target_pairs={{0,5},{1,0},{4,1},{5,4},{8,13},{9,8},{12,9},{13,12},{2,7},{3,2},{6... | collective-permute-start | bytes 196616 | tf_op jit(solution)/shard_map/ppermute | solution.py:236
  13.2 2.5 %collective-permute-start.8 = (bf16[1,128,256]{2,1,0:T(8,128)(2,1)S(1)}, bf16[1,128,256]{2,1,0:T(8,128)(2,1)S(1)}, u32[]{:S(2)}, u32[]{:S(2)}) collective-permute-start(bf16[1,128,256]{2,1,0:T(8,128)(2,1)S(1)} %get-tuple-element.38), channel_id=1, source_target_pairs={{0,5},{1,0},{4,1},{5,4},{8,13},{9,8},{12,9},{13,12},{2,7},{3,2},{6... | collective-permute-start | bytes 196616 | tf_op jit(solution)/shard_map/ppermute | solution.py:236
  14.1 2.2 %collective-permute-start.6 = (bf16[80,256]{1,0:T(8,128)(2,1)S(1)}, bf16[80,256]{1,0:T(8,128)(2,1)S(1)}, u32[]{:S(2)}, u32[]{:S(2)}) collective-permute-start(bf16[80,256]{1,0:T(8,128)(2,1)S(1)} %collective-permute-done.2.refs_2_), channel_id=1, source_target_pairs={{0,1},{1,0},{2,3},{3,2},{4,5},{5,4},{6,7},{7,6},{8,9},{9,8},{10,11... | collective-permute-start | bytes 122888 | tf_op jit(solution)/shard_map/ppermute | solution.py:247
  14.6 1.6 %collective-permute-start.7 = (bf16[80,256]{1,0:T(8,128)(2,1)S(1)}, bf16[80,256]{1,0:T(8,128)(2,1)S(1)}, u32[]{:S(2)}, u32[]{:S(2)}) collective-permute-start(bf16[80,256]{1,0:T(8,128)(2,1)S(1)} %collective-permute-done.3.refs_6_), channel_id=1, source_target_pairs={{0,1},{1,0},{2,3},{3,2},{4,5},{5,4},{6,7},{7,6},{8,9},{9,8},{10,11... | collective-permute-start | bytes 122888 | tf_op jit(solution)/shard_map/ppermute | solution.py:247
  15.1 2.3 %collective-permute-start.11 = (bf16[1,128,256]{2,1,0:T(8,128)(2,1)S(1)}, bf16[1,128,256]{2,1,0:T(8,128)(2,1)S(1)}, u32[]{:S(2)}, u32[]{:S(2)}) collective-permute-start(bf16[1,128,256]{2,1,0:T(8,128)(2,1)S(1)} %collective-permute-done.10.refs_3_), channel_id=1, source_target_pairs={{0,1},{1,0},{2,3},{3,2},{4,5},{5,4},{6,7},{7,6},{8,9},{9,8},{10,11... | collective-permute-start | bytes 196616 | tf_op jit(solution)/shard_map/ppermute | solution.py:247
  15.7 1.7 %collective-permute-start.9 = (bf16[1,128,256]{2,1,0:T(8,128)(2,1)S(1)}, bf16[1,128,256]{2,1,0:T(8,128)(2,1)S(1)}, u32[]{:S(2)}, u32[]{:S(2)}) collective-permute-start(bf16[1,128,256]{2,1,0:T(8,128)(2,1)S(1)} %collective-permute-done.8.refs_2_), channel_id=1, source_target_pairs={{0,1},{1,0},{2,3},{3,2},{4,5},{5,4},{6,7},{7,6},{8,9},{9,8},{10,11... | collective-permute-start | bytes 196616 | tf_op jit(solution)/shard_map/ppermute | solution.py:247
  16.1 1.3 %collective-permute-start.12 = (bf16[80,256]{1,0:T(8,128)(2,1)S(1)}, bf16[80,256]{1,0:T(8,128)(2,1)S(1)}, u32[]{:S(2)}, u32[]{:S(2)}) collective-permute-start(bf16[80,256]{1,0:T(8,128)(2,1)S(1)} %collective-permute-done.5.refs_4_), channel_id=1, source_target_pairs={{0,1},{1,0},{2,3},{3,2},{4,5},{5,4},{6,7},{7,6},{8,9},{9,8},{10,11... | collective-permute-start | bytes 122888 | tf_op jit(solution)/shard_map/ppermute | solution.py:247
  16.2 1.2 %copy-start = (bf16[256,256]{1,0:T(8,128)(2,1)S(1)}, bf16[256,256]{1,0:T(8,128)(2,1)}, u32[]{:S(2)}) copy-start(bf16[256,256]{1,0:T(8,128)(2,1)} %projection_ref.1) | copy-start | bytes 393220

commit v20 on v18

--- a/solution.py
+++ b/solution.py
@@ -14,7 +14,7 @@
 SMEM = pl.BlockSpec(memory_space=pltpu.SMEM)
 MIB = 1024 * 1024
 TILES = 4
-LAST_TILES = 8
+LAST_TILES = 4
 LIGHT = pl.CostEstimate(flops=1_000_000, bytes_accessed=1024, transcendentals=0)
 WORK = pl.CostEstimate(flops=4_000_000_000, bytes_accessed=8 * MIB, transcendentals=0)
 

time: 18.3 us -> 18.3 us (level)
  no operation moved by 1% of the time
where the time goes in v20:
time: 18.3 us; the launch traced here: 18.2 us
  starting transfers between devices  10.1 us (55%)
  Pallas kernels  5.18 us (28%)
  waiting for transfers between devices  2.07 us (11%)
  between operations  0.82 us (4%)
    ppermute x3, starting transfers between devices, on_device(): lax.ppermute(pack, 'sub', [(i, i ^ p) for i in range(subdomains)])  4.45 us
    ppermute x1, starting transfers between devices, on_device(): lax.ppermute(basis, ('sub', 'face'), [(flat(s, face), flat(s ^ (1 if face...  4.04 us
    pallas_call x1, Pallas kernels, on_device(): pl.pallas_call(last_kernel, out_shape=jax.ShapeDtypeStruct(block_shape, j...  1.9 us
    ppermute x3, waiting for transfers between devices, on_device(): lax.ppermute(pack, 'sub', [(i, i ^ p) for i in range(subdomains)])  1.56 us
    ppermute x4, starting transfers between devices, with_swapped(): return [(array, lax.ppermute(array, 'face', swap)) for array in arrays]  1.52 us
    pallas_call x1, Pallas kernels, on_device(): pl.pallas_call(functools.partial(pack_kernel, partners), out_shape=[pltpu...  1.36 us
    pallas_call x1, Pallas kernels, on_device(): pl.pallas_call(stage_kernel, out_shape=jax.ShapeDtypeStruct(block_shape,...  1.14 us
    pallas_call x1, Pallas kernels, on_device(): pl.pallas_call(own_kernel, out_shape=[jax.ShapeDtypeStruct(block_shape, j...  0.78 us
  transfers between devices with their start and end apart: 11, of which 3 were waited for; matrix products, arithmetic and copies ran while one was open for 0% of the time, Pallas kernels for 18%

profile of v20, /device:TPU:0, one launch (start us, length us, event | category | flops | bytes accessed | tf_op | source)
XLA Modules:
  0.0 18.2 jit_solution(3151385891503992123)
XLA Ops:
  0.0 4.0 %collective-permute-start = (bf16[1,256,256]{2,1,0:T(8,128)(2,1)}, bf16[1,256,256]{2,1,0:T(8,128)(2,1)S(1)}, u32[]{:S(2)}, u32[]{:S(2)}) collective-permute-start(bf16[1,256,256]{2,1,0:T(8,128)(2,1)} %basis_ref.1), channel_id=1, source_target_pairs={{0,8},{1,5},{4,12},{5,1},{8,0},{9,13},{12,4},{13,9},{2,10},{3,7},{... | collective-permute-start | bytes 393224 | tf_op jit(solution)/shard_map/ppermute | solution.py:184
  4.7 0.0 copy-start.1
  4.7 0.0 copy-start.2
  4.7 0.0 copy-start.3
  4.7 0.0 copy-start.4
  4.7 0.0 copy-start.5
  4.7 0.0 copy-start.6
  4.7 0.0 copy-start.7
  4.8 1.4 %pack_weights.1 = (bf16[80,256]{1,0:T(8,128)(2,1)S(1)}, bf16[80,256]{1,0:T(8,128)(2,1)S(1)}, bf16[80,256]{1,0:T(8,128)(2,1)S(1)}, bf16[80,256]{1,0:T(8,128)(2,1)S(1)}) custom-call(s32[1,128]{1,0:T(1,128)} %bitcast.6, s32[1,128]{1,0:T(1,128)} %bitcast.8, bf16[128,256]{1,0:T(8,128)(2,1)} %scale_ref.3, s32[1]{0:T(128)S(6)} %copy.12.section_ref), custom_call_target="tpu_custom_call" | custom-call | flops 4000000000 | bytes 8388608 | tf_op jit(solution)/shard_map/pack_weights/pallas_call | solution.py:192
  6.1 0.0 collective-permute-start.1
  6.2 1.1 %collective-permute-start.2 = (bf16[80,256]{1,0:T(8,128)(2,1)S(1)}, bf16[80,256]{1,0:T(8,128)(2,1)S(1)}, u32[]{:S(2)}, u32[]{:S(2)}) collective-permute-start(bf16[80,256]{1,0:T(8,128)(2,1)S(1)} %get-tuple-element.25), channel_id=1, source_target_pairs={{0,8},{4,12},{8,0},{12,4},{1,9},{5,13},{9,1},{13,5},{2,10},{6,14},... | collective-permute-start | bytes 122888 | tf_op jit(solution)/shard_map/ppermute | solution.py:202
  7.3 0.9 %collective-permute-start.3 = (bf16[80,256]{1,0:T(8,128)(2,1)S(1)}, bf16[80,256]{1,0:T(8,128)(2,1)S(1)}, u32[]{:S(2)}, u32[]{:S(2)}) collective-permute-start(bf16[80,256]{1,0:T(8,128)(2,1)S(1)} %get-tuple-element.27), channel_id=1, source_target_pairs={{0,4},{4,0},{8,12},{12,8},{1,5},{5,1},{9,13},{13,9},{2,6},{6,2},{1... | collective-permute-start | bytes 122888 | tf_op jit(solution)/shard_map/ppermute | solution.py:202
  8.1 2.5 %collective-permute-start.5 = (bf16[80,256]{1,0:T(8,128)(2,1)S(1)}, bf16[80,256]{1,0:T(8,128)(2,1)S(1)}, u32[]{:S(2)}, u32[]{:S(2)}) collective-permute-start(bf16[80,256]{1,0:T(8,128)(2,1)S(1)} %get-tuple-element.31), channel_id=1, source_target_pairs={{0,12},{4,8},{8,4},{12,0},{1,13},{5,9},{9,5},{13,1},{2,14},{6,10},... | collective-permute-start | bytes 122888 | tf_op jit(solution)/shard_map/ppermute | solution.py:202
  10.6 0.0 collective-permute-done.1.swapped_ref
  10.6 0.0 collective-permute-done.refs_0_.refs_5_
  10.6 0.0 collective-permute-start.8
  10.6 0.5 %collective-permute-done.2.refs_2_ = bf16[80,256]{1,0:T(8,128)(2,1)S(1)} collective-permute-done((bf16[80,256]{1,0:T(8,128)(2,1)S(1)}, bf16[80,256]{1,0:T(8,128)(2,1)S(1)}, u32[]{:S(2)}, u32[]{:S(2)}) %collective-permute-start.2) | collective-permute-done | bytes 40992 | tf_op jit(solution)/shard_map/ppermute | solution.py:202
  11.2 0.0 collective-permute-start.4
  11.2 0.0 copy-done.1
  11.2 0.0 copy-done.2
  11.2 0.0 copy-done.3
  11.2 0.0 copy-done.4
  11.2 0.0 copy-done.5
  11.2 0.0 copy-done.6
  11.2 0.0 copy-done.7
  11.2 0.8 %own_blocks.1 = (bf16[64,32,256]{2,1,0:T(8,128)(2,1)S(1)}, f32[64,32,256]{2,1,0:T(8,128)S(1)}) custom-call(bf16[128,32,256]{2,1,0:T(8,128)(2,1)S(1)} %copy-done.1, f32[1,32]{1,0:T(1,128)S(1)} %bitcast.4, s32[1,32]{1,0:T(1,128)S(1)} %bitcast.5, s32[1,128]{1,0:T(1,128)S(1)} %bitcast.7, s32[1,128]{1,0:T(1,128)S(1)} %bitcast.9, bf16[128,256]{1,0:T(8,128)(2,1)S(1)} %copy-done.3, ...), custom_call_target="tpu_custom_call" | custom-call | flops 4000000000 | bytes 8388608 | tf_op jit(solution)/shard_map/own_blocks/pallas_call | solution.py:207
  12.0 0.0 collective-permute-done.3.refs_6_
  12.0 0.5 %collective-permute-done.4.refs_1_.refs_4_ = bf16[1,256,256]{2,1,0:T(8,128)(2,1)S(1)} collective-permute-done((bf16[1,256,256]{2,1,0:T(8,128)(2,1)S(1)}, bf16[1,256,256]{2,1,0:T(8,128)(2,1)S(1)}, u32[]{:S(2)}, u32[]{:S(2)}) %collective-permute-start.4) | collective-permute-done | bytes 131104 | tf_op jit(solution)/shard_map/ppermute | solution.py:232
  12.5 0.1 collective-permute-start.6
  12.7 0.4 %collective-permute-start.7 = (bf16[80,256]{1,0:T(8,128)(2,1)S(1)}, bf16[80,256]{1,0:T(8,128)(2,1)S(1)}, u32[]{:S(2)}, u32[]{:S(2)}) collective-permute-start(bf16[80,256]{1,0:T(8,128)(2,1)S(1)} %collective-permute-done.3.refs_6_), channel_id=1, source_target_pairs={{0,1},{1,0},{2,3},{3,2},{4,5},{5,4},{6,7},{7,6},{8,9},{9,8},{10,11... | collective-permute-start | bytes 122888 | tf_op jit(solution)/shard_map/ppermute | solution.py:238
  13.0 1.0 %collective-permute-done.5.refs_2_ = bf16[80,256]{1,0:T(8,128)(2,1)S(1)} collective-permute-done((bf16[80,256]{1,0:T(8,128)(2,1)S(1)}, bf16[80,256]{1,0:T(8,128)(2,1)S(1)}, u32[]{:S(2)}, u32[]{:S(2)}) %collective-permute-start.5) | collective-permute-done | bytes 40992 | tf_op jit(solution)/shard_map/ppermute | solution.py:202
  14.1 0.0 collective-permute-start.10
  14.1 0.0 collective-permute-done.8.refs_1_
  14.1 1.0 %collective-permute-start.9 = (bf16[1,256,256]{2,1,0:T(8,128)(2,1)S(1)}, bf16[1,256,256]{2,1,0:T(8,128)(2,1)S(1)}, u32[]{:S(2)}, u32[]{:S(2)}) collective-permute-start(bf16[1,256,256]{2,1,0:T(8,128)(2,1)S(1)} %collective-permute-done.8.refs_1_), channel_id=1, source_target_pairs={{0,1},{1,0},{2,3},{3,2},{4,5},{5,4},{6,7},{7,6},{8,9},{9,8},{10,11... | collective-permute-start | bytes 393224 | tf_op jit(solution)/shard_map/ppermute | solution.py:238
  15.1 0.0 collective-permute-done.6.refs_3_
  15.1 0.0 collective-permute-done.7.refs_7_
  15.1 0.0 copy-start
  15.1 1.1 %stage.1.sum_ref = f32[64,32,256]{2,1,0:T(8,128)S(1)} custom-call(bf16[64,32,256]{2,1,0:T(8,128)(2,1)S(1)} %get-tuple-element.23.pumped_ref, f32[64,32,256]{2,1,0:T(8,128)S(1)} %get-tuple-element.32.sum_ref, bf16[1,256,256]{2,1,0:T(8,128)(2,1)S(1)} %collective-permute-done.refs_0_.refs_5_, ...), custom_call_target="tpu_custom_call", output_to_operand_aliasing={{}: (1, {})} | custom-call | flops 4000000000 | bytes 8388608 | tf_op jit(solution)/shard_map/stage/pallas_call | solution.py:254
  16.2 0.0 collective-permute-done.10.refs_3_
  16.2 0.0 collective-permute-done.9.refs_0_
  16.2 0.0 copy-done
  16.3 1.9 %last_stage.1 = f32[64,32,256]{2,1,0:T(8,128)} custom-call(bf16[64,32,256]{2,1,0:T(8,128)(2,1)S(1)} %get-tuple-element.23.pumped_ref, f32[64,32,256]{2,1,0:T(8,128)S(1)} %stage.1.sum_ref, bf16[256,256]{1,0:T(8,128)(2,1)S(1)} %copy-done, bf16[1,256,256]{2,1,0:T(8,128)(2,1)S(1)} %collective-permute-done.9.refs_0_, ...), custom_call_target="tpu_custom_call" | custom-call | tf_op jit(solution)/shard_map/last_stage/pallas_call | solution.py:269
Async XLA Ops:
  0.0 10.6 %collective-permute-start = (bf16[1,256,256]{2,1,0:T(8,128)(2,1)}, bf16[1,256,256]{2,1,0:T(8,128)(2,1)S(1)}, u32[]{:S(2)}, u32[]{:S(2)}) collective-permute-start(bf16[1,256,256]{2,1,0:T(8,128)(2,1)} %basis_ref.1), channel_id=1, source_target_pairs={{0,8},{1,5},{4,12},{5,1},{8,0},{9,13},{12,4},{13,9},{2,10},{3,7},{... | collective-permute-start | bytes 393224 | tf_op jit(solution)/shard_map/ppermute | solution.py:184
  4.7 6.5 %copy-start.1 = (bf16[128,32,256]{2,1,0:T(8,128)(2,1)S(1)}, bf16[128,32,256]{2,1,0:T(8,128)(2,1)}, u32[]{:S(2)}) copy-start(bf16[128,32,256]{2,1,0:T(8,128)(2,1)} %mortar_ref.1) | copy-start | bytes 6291460
  4.7 6.5 %copy-start.2 = (bf16[1,256,256]{2,1,0:T(8,128)(2,1)S(1)}, bf16[1,256,256]{2,1,0:T(8,128)(2,1)}, u32[]{:S(2)}) copy-start(bf16[1,256,256]{2,1,0:T(8,128)(2,1)} %basis_ref.1) | copy-start | bytes 393220
  4.7 6.5 %copy-start.3 = (bf16[128,256]{1,0:T(8,128)(2,1)S(1)}, bf16[128,256]{1,0:T(8,128)(2,1)}, u32[]{:S(2)}) copy-start(bf16[128,256]{1,0:T(8,128)(2,1)} %scale_ref.3) | copy-start | bytes 196612
  4.7 6.5 %copy-start.4 = (f32[32]{0:T(128)S(1)}, f32[32]{0:T(128)}, u32[]{:S(2)}) copy-start(f32[32]{0:T(128)} %param.10) | copy-start | bytes 388
  4.7 6.5 %copy-start.5 = (s32[32]{0:T(128)S(1)}, s32[32]{0:T(128)}, u32[]{:S(2)}) copy-start(s32[32]{0:T(128)} %param.11) | copy-start | bytes 388
  4.7 6.5 %copy-start.6 = (s32[128,1]{0,1:T(1,128)S(1)}, s32[128,1]{0,1:T(1,128)}, u32[]{:S(2)}) copy-start(s32[128,1]{0,1:T(1,128)} %param.12) | copy-start | bytes 1540
  4.7 6.5 %copy-start.7 = (s32[128]{0:T(128)S(1)}, s32[128]{0:T(128)}, u32[]{:S(2)}) copy-start(s32[128]{0:T(128)} %param.13) | copy-start | bytes 1540
  6.1 4.5 %collective-permute-start.1 = (bf16[80,256]{1,0:T(8,128)(2,1)S(1)}, bf16[80,256]{1,0:T(8,128)(2,1)S(1)}, u32[]{:S(2)}, u32[]{:S(2)}) collective-permute-start(bf16[80,256]{1,0:T(8,128)(2,1)S(1)} %get-tuple-element.21), channel_id=1, source_target_pairs={{0,1},{1,0},{2,3},{3,2},{4,5},{5,4},{6,7},{7,6},{8,9},{9,8},{10,11... | collective-permute-start | bytes 122888 | tf_op jit(solution)/shard_map/ppermute | solution.py:204
  6.2 5.0 %collective-permute-start.2 = (bf16[80,256]{1,0:T(8,128)(2,1)S(1)}, bf16[80,256]{1,0:T(8,128)(2,1)S(1)}, u32[]{:S(2)}, u32[]{:S(2)}) collective-permute-start(bf16[80,256]{1,0:T(8,128)(2,1)S(1)} %get-tuple-element.25), channel_id=1, source_target_pairs={{0,8},{4,12},{8,0},{12,4},{1,9},{5,13},{9,1},{13,5},{2,10},{6,14},... | collective-permute-start | bytes 122888 | tf_op jit(solution)/shard_map/ppermute | solution.py:202
  7.3 4.7 %collective-permute-start.3 = (bf16[80,256]{1,0:T(8,128)(2,1)S(1)}, bf16[80,256]{1,0:T(8,128)(2,1)S(1)}, u32[]{:S(2)}, u32[]{:S(2)}) collective-permute-start(bf16[80,256]{1,0:T(8,128)(2,1)S(1)} %get-tuple-element.27), channel_id=1, source_target_pairs={{0,4},{4,0},{8,12},{12,8},{1,5},{5,1},{9,13},{13,9},{2,6},{6,2},{1... | collective-permute-start | bytes 122888 | tf_op jit(solution)/shard_map/ppermute | solution.py:202
  8.1 5.9 %collective-permute-start.5 = (bf16[80,256]{1,0:T(8,128)(2,1)S(1)}, bf16[80,256]{1,0:T(8,128)(2,1)S(1)}, u32[]{:S(2)}, u32[]{:S(2)}) collective-permute-start(bf16[80,256]{1,0:T(8,128)(2,1)S(1)} %get-tuple-element.31), channel_id=1, source_target_pairs={{0,12},{4,8},{8,4},{12,0},{1,13},{5,9},{9,5},{13,1},{2,14},{6,10},... | collective-permute-start | bytes 122888 | tf_op jit(solution)/shard_map/ppermute | solution.py:202
  10.6 3.4 %collective-permute-start.8 = (bf16[1,256,256]{2,1,0:T(8,128)(2,1)S(1)}, bf16[1,256,256]{2,1,0:T(8,128)(2,1)S(1)}, u32[]{:S(2)}, u32[]{:S(2)}) collective-permute-start(bf16[1,256,256]{2,1,0:T(8,128)(2,1)S(1)} %collective-permute-done.refs_0_.refs_5_), channel_id=1, source_target_pairs={{0,5},{1,0},{4,1},{5,4},{8,13},{9,8},{12,9},{13,12},{2,7},{3,2},{6... | collective-permute-start | bytes 393224 | tf_op jit(solution)/shard_map/ppermute | solution.py:230
  11.2 1.3 %collective-permute-start.4 = (bf16[1,256,256]{2,1,0:T(8,128)(2,1)S(1)}, bf16[1,256,256]{2,1,0:T(8,128)(2,1)S(1)}, u32[]{:S(2)}, u32[]{:S(2)}) collective-permute-start(bf16[1,256,256]{2,1,0:T(8,128)(2,1)S(1)} %collective-permute-done.refs_0_.refs_5_), channel_id=1, source_target_pairs={{0,1},{1,0},{2,3},{3,2},{4,5},{5,4},{6,7},{7,6},{8,9},{9,8},{10,11... | collective-permute-start | bytes 393224 | tf_op jit(solution)/shard_map/ppermute | solution.py:232
  12.5 2.6 %collective-permute-start.6 = (bf16[80,256]{1,0:T(8,128)(2,1)S(1)}, bf16[80,256]{1,0:T(8,128)(2,1)S(1)}, u32[]{:S(2)}, u32[]{:S(2)}) collective-permute-start(bf16[80,256]{1,0:T(8,128)(2,1)S(1)} %collective-permute-done.2.refs_2_), channel_id=1, source_target_pairs={{0,1},{1,0},{2,3},{3,2},{4,5},{5,4},{6,7},{7,6},{8,9},{9,8},{10,11... | collective-permute-start | bytes 122888 | tf_op jit(solution)/shard_map/ppermute | solution.py:238
  12.7 2.4 %collective-permute-start.7 = (bf16[80,256]{1,0:T(8,128)(2,1)S(1)}, bf16[80,256]{1,0:T(8,128)(2,1)S(1)}, u32[]{:S(2)}, u32[]{:S(2)}) collective-permute-start(bf16[80,256]{1,0:T(8,128)(2,1)S(1)} %collective-permute-done.3.refs_6_), channel_id=1, source_target_pairs={{0,1},{1,0},{2,3},{3,2},{4,5},{5,4},{6,7},{7,6},{8,9},{9,8},{10,11... | collective-permute-start | bytes 122888 | tf_op jit(solution)/shard_map/ppermute | solution.py:238
  14.1 2.2 %collective-permute-start.10 = (bf16[80,256]{1,0:T(8,128)(2,1)S(1)}, bf16[80,256]{1,0:T(8,128)(2,1)S(1)}, u32[]{:S(2)}, u32[]{:S(2)}) collective-permute-start(bf16[80,256]{1,0:T(8,128)(2,1)S(1)} %collective-permute-done.5.refs_2_), channel_id=1, source_target_pairs={{0,1},{1,0},{2,3},{3,2},{4,5},{5,4},{6,7},{7,6},{8,9},{9,8},{10,11... | collective-permute-start | bytes 122888 | tf_op jit(solution)/shard_map/ppermute | solution.py:238
  14.1 2.2 %collective-permute-start.9 = (bf16[1,256,256]{2,1,0:T(8,128)(2,1)S(1)}, bf16[1,256,256]{2,1,0:T(8,128)(2,1)S(1)}, u32[]{:S(2)}, u32[]{:S(2)}) collective-permute-start(bf16[1,256,256]{2,1,0:T(8,128)(2,1)S(1)} %collective-permute-done.8.refs_1_), channel_id=1, source_target_pairs={{0,1},{1,0},{2,3},{3,2},{4,5},{5,4},{6,7},{7,6},{8,9},{9,8},{10,11... | collective-permute-start | bytes 393224 | tf_op jit(solution)/shard_map/ppermute | solution.py:238
  15.1 1.2 %copy-start = (bf16[256,256]{1,0:T(8,128)(2,1)S(1)}, bf16[256,256]{1,0:T(8,128)(2,1)}, u32[]{:S(2)}) copy-start(bf16[256,256]{1,0:T(8,128)(2,1)} %projection_ref.1) | copy-start | bytes 393220

commit v21 on v20

--- a/solution.py
+++ b/solution.py
@@ -13,8 +13,8 @@
 HBM = pl.BlockSpec(memory_space=pltpu.HBM)
 SMEM = pl.BlockSpec(memory_space=pltpu.SMEM)
 MIB = 1024 * 1024
-TILES = 4
-LAST_TILES = 4
+TILES = 8
+LAST_TILES = 16
 LIGHT = pl.CostEstimate(flops=1_000_000, bytes_accessed=1024, transcendentals=0)
 WORK = pl.CostEstimate(flops=4_000_000_000, bytes_accessed=8 * MIB, transcendentals=0)
 

time: 18.3 us -> 18.3 us (level)
  no operation moved by 1% of the time
where the time goes in v21:
time: 18.3 us; the launch traced here: 18.1 us
  starting transfers between devices  10.1 us (55%)
  Pallas kernels  5.17 us (28%)
  waiting for transfers between devices  2.07 us (11%)
  between operations  0.82 us (4%)
    ppermute x3, starting transfers between devices, on_device(): lax.ppermute(pack, 'sub', [(i, i ^ p) for i in range(subdomains)])  4.45 us
    ppermute x1, starting transfers between devices, on_device(): lax.ppermute(basis, ('sub', 'face'), [(flat(s, face), flat(s ^ (1 if face...  4.04 us
    pallas_call x1, Pallas kernels, on_device(): pl.pallas_call(last_kernel, out_shape=jax.ShapeDtypeStruct(block_shape, j...  1.89 us
    ppermute x3, waiting for transfers between devices, on_device(): lax.ppermute(pack, 'sub', [(i, i ^ p) for i in range(subdomains)])  1.56 us
    ppermute x4, starting transfers between devices, with_swapped(): return [(array, lax.ppermute(array, 'face', swap)) for array in arrays]  1.52 us
    pallas_call x1, Pallas kernels, on_device(): pl.pallas_call(functools.partial(pack_kernel, partners), out_shape=[pltpu...  1.36 us
    pallas_call x1, Pallas kernels, on_device(): pl.pallas_call(stage_kernel, out_shape=jax.ShapeDtypeStruct(block_shape,...  1.14 us
    pallas_call x1, Pallas kernels, on_device(): pl.pallas_call(own_kernel, out_shape=[jax.ShapeDtypeStruct(block_shape, j...  0.78 us
  transfers between devices with their start and end apart: 11, of which 3 were waited for; matrix products, arithmetic and copies ran while one was open for 0% of the time, Pallas kernels for 18%

profile of v21, /device:TPU:0, one launch (start us, length us, event | category | flops | bytes accessed | tf_op | source)
XLA Modules:
  0.0 18.1 jit_solution(7812360638571169398)
XLA Ops:
  0.0 4.0 %collective-permute-start = (bf16[1,256,256]{2,1,0:T(8,128)(2,1)}, bf16[1,256,256]{2,1,0:T(8,128)(2,1)S(1)}, u32[]{:S(2)}, u32[]{:S(2)}) collective-permute-start(bf16[1,256,256]{2,1,0:T(8,128)(2,1)} %basis_ref.1), channel_id=1, source_target_pairs={{0,8},{1,5},{4,12},{5,1},{8,0},{9,13},{12,4},{13,9},{2,10},{3,7},{... | collective-permute-start | bytes 393224 | tf_op jit(solution)/shard_map/ppermute | solution.py:184
  4.7 0.0 copy-start.1
  4.7 0.0 copy-start.2
  4.7 0.0 copy-start.3
  4.7 0.0 copy-start.4
  4.7 0.0 copy-start.5
  4.7 0.0 copy-start.6
  4.7 0.0 copy-start.7
  4.8 1.4 %pack_weights.1 = (bf16[80,256]{1,0:T(8,128)(2,1)S(1)}, bf16[80,256]{1,0:T(8,128)(2,1)S(1)}, bf16[80,256]{1,0:T(8,128)(2,1)S(1)}, bf16[80,256]{1,0:T(8,128)(2,1)S(1)}) custom-call(s32[1,128]{1,0:T(1,128)} %bitcast.6, s32[1,128]{1,0:T(1,128)} %bitcast.8, bf16[128,256]{1,0:T(8,128)(2,1)} %scale_ref.3, s32[1]{0:T(128)S(6)} %copy.12.section_ref), custom_call_target="tpu_custom_call" | custom-call | flops 4000000000 | bytes 8388608 | tf_op jit(solution)/shard_map/pack_weights/pallas_call | solution.py:192
  6.1 0.0 collective-permute-start.1
  6.2 1.1 %collective-permute-start.2 = (bf16[80,256]{1,0:T(8,128)(2,1)S(1)}, bf16[80,256]{1,0:T(8,128)(2,1)S(1)}, u32[]{:S(2)}, u32[]{:S(2)}) collective-permute-start(bf16[80,256]{1,0:T(8,128)(2,1)S(1)} %get-tuple-element.25), channel_id=1, source_target_pairs={{0,8},{4,12},{8,0},{12,4},{1,9},{5,13},{9,1},{13,5},{2,10},{6,14},... | collective-permute-start | bytes 122888 | tf_op jit(solution)/shard_map/ppermute | solution.py:202
  7.3 0.9 %collective-permute-start.3 = (bf16[80,256]{1,0:T(8,128)(2,1)S(1)}, bf16[80,256]{1,0:T(8,128)(2,1)S(1)}, u32[]{:S(2)}, u32[]{:S(2)}) collective-permute-start(bf16[80,256]{1,0:T(8,128)(2,1)S(1)} %get-tuple-element.27), channel_id=1, source_target_pairs={{0,4},{4,0},{8,12},{12,8},{1,5},{5,1},{9,13},{13,9},{2,6},{6,2},{1... | collective-permute-start | bytes 122888 | tf_op jit(solution)/shard_map/ppermute | solution.py:202
  8.1 2.5 %collective-permute-start.5 = (bf16[80,256]{1,0:T(8,128)(2,1)S(1)}, bf16[80,256]{1,0:T(8,128)(2,1)S(1)}, u32[]{:S(2)}, u32[]{:S(2)}) collective-permute-start(bf16[80,256]{1,0:T(8,128)(2,1)S(1)} %get-tuple-element.31), channel_id=1, source_target_pairs={{0,12},{4,8},{8,4},{12,0},{1,13},{5,9},{9,5},{13,1},{2,14},{6,10},... | collective-permute-start | bytes 122888 | tf_op jit(solution)/shard_map/ppermute | solution.py:202
  10.6 0.0 collective-permute-done.1.swapped_ref
  10.6 0.0 collective-permute-done.refs_0_.refs_5_
  10.6 0.0 collective-permute-start.8
  10.6 0.5 %collective-permute-done.2.refs_2_ = bf16[80,256]{1,0:T(8,128)(2,1)S(1)} collective-permute-done((bf16[80,256]{1,0:T(8,128)(2,1)S(1)}, bf16[80,256]{1,0:T(8,128)(2,1)S(1)}, u32[]{:S(2)}, u32[]{:S(2)}) %collective-permute-start.2) | collective-permute-done | bytes 40992 | tf_op jit(solution)/shard_map/ppermute | solution.py:202
  11.2 0.0 collective-permute-start.4
  11.2 0.0 copy-done.1
  11.2 0.0 copy-done.2
  11.2 0.0 copy-done.3
  11.2 0.0 copy-done.4
  11.2 0.0 copy-done.5
  11.2 0.0 copy-done.6
  11.2 0.0 copy-done.7
  11.2 0.8 %own_blocks.1 = (bf16[64,32,256]{2,1,0:T(8,128)(2,1)S(1)}, f32[64,32,256]{2,1,0:T(8,128)S(1)}) custom-call(bf16[128,32,256]{2,1,0:T(8,128)(2,1)S(1)} %copy-done.1, f32[1,32]{1,0:T(1,128)S(1)} %bitcast.4, s32[1,32]{1,0:T(1,128)S(1)} %bitcast.5, s32[1,128]{1,0:T(1,128)S(1)} %bitcast.7, s32[1,128]{1,0:T(1,128)S(1)} %bitcast.9, bf16[128,256]{1,0:T(8,128)(2,1)S(1)} %copy-done.3, ...), custom_call_target="tpu_custom_call" | custom-call | flops 4000000000 | bytes 8388608 | tf_op jit(solution)/shard_map/own_blocks/pallas_call | solution.py:207
  12.0 0.0 collective-permute-done.3.refs_6_
  12.0 0.5 %collective-permute-done.4.refs_1_.refs_4_ = bf16[1,256,256]{2,1,0:T(8,128)(2,1)S(1)} collective-permute-done((bf16[1,256,256]{2,1,0:T(8,128)(2,1)S(1)}, bf16[1,256,256]{2,1,0:T(8,128)(2,1)S(1)}, u32[]{:S(2)}, u32[]{:S(2)}) %collective-permute-start.4) | collective-permute-done | bytes 131104 | tf_op jit(solution)/shard_map/ppermute | solution.py:232
  12.5 0.1 collective-permute-start.6
  12.7 0.4 %collective-permute-start.7 = (bf16[80,256]{1,0:T(8,128)(2,1)S(1)}, bf16[80,256]{1,0:T(8,128)(2,1)S(1)}, u32[]{:S(2)}, u32[]{:S(2)}) collective-permute-start(bf16[80,256]{1,0:T(8,128)(2,1)S(1)} %collective-permute-done.3.refs_6_), channel_id=1, source_target_pairs={{0,1},{1,0},{2,3},{3,2},{4,5},{5,4},{6,7},{7,6},{8,9},{9,8},{10,11... | collective-permute-start | bytes 122888 | tf_op jit(solution)/shard_map/ppermute | solution.py:238
  13.0 1.0 %collective-permute-done.5.refs_2_ = bf16[80,256]{1,0:T(8,128)(2,1)S(1)} collective-permute-done((bf16[80,256]{1,0:T(8,128)(2,1)S(1)}, bf16[80,256]{1,0:T(8,128)(2,1)S(1)}, u32[]{:S(2)}, u32[]{:S(2)}) %collective-permute-start.5) | collective-permute-done | bytes 40992 | tf_op jit(solution)/shard_map/ppermute | solution.py:202
  14.1 0.0 collective-permute-start.10
  14.1 0.0 collective-permute-done.8.refs_1_
  14.1 1.0 %collective-permute-start.9 = (bf16[1,256,256]{2,1,0:T(8,128)(2,1)S(1)}, bf16[1,256,256]{2,1,0:T(8,128)(2,1)S(1)}, u32[]{:S(2)}, u32[]{:S(2)}) collective-permute-start(bf16[1,256,256]{2,1,0:T(8,128)(2,1)S(1)} %collective-permute-done.8.refs_1_), channel_id=1, source_target_pairs={{0,1},{1,0},{2,3},{3,2},{4,5},{5,4},{6,7},{7,6},{8,9},{9,8},{10,11... | collective-permute-start | bytes 393224 | tf_op jit(solution)/shard_map/ppermute | solution.py:238
  15.1 0.0 collective-permute-done.6.refs_3_
  15.1 0.0 collective-permute-done.7.refs_7_
  15.1 0.0 copy-start
  15.1 1.1 %stage.1.sum_ref = f32[64,32,256]{2,1,0:T(8,128)S(1)} custom-call(bf16[64,32,256]{2,1,0:T(8,128)(2,1)S(1)} %get-tuple-element.23.pumped_ref, f32[64,32,256]{2,1,0:T(8,128)S(1)} %get-tuple-element.32.sum_ref, bf16[1,256,256]{2,1,0:T(8,128)(2,1)S(1)} %collective-permute-done.refs_0_.refs_5_, ...), custom_call_target="tpu_custom_call", output_to_operand_aliasing={{}: (1, {})} | custom-call | flops 4000000000 | bytes 8388608 | tf_op jit(solution)/shard_map/stage/pallas_call | solution.py:254
  16.2 0.0 collective-permute-done.10.refs_3_
  16.2 0.0 collective-permute-done.9.refs_0_
  16.2 0.0 copy-done
  16.3 1.9 %last_stage.1 = f32[64,32,256]{2,1,0:T(8,128)} custom-call(bf16[64,32,256]{2,1,0:T(8,128)(2,1)S(1)} %get-tuple-element.23.pumped_ref, f32[64,32,256]{2,1,0:T(8,128)S(1)} %stage.1.sum_ref, bf16[256,256]{1,0:T(8,128)(2,1)S(1)} %copy-done, bf16[1,256,256]{2,1,0:T(8,128)(2,1)S(1)} %collective-permute-done.9.refs_0_, ...), custom_call_target="tpu_custom_call" | custom-call | tf_op jit(solution)/shard_map/last_stage/pallas_call | solution.py:269
Async XLA Ops:
  0.0 10.6 %collective-permute-start = (bf16[1,256,256]{2,1,0:T(8,128)(2,1)}, bf16[1,256,256]{2,1,0:T(8,128)(2,1)S(1)}, u32[]{:S(2)}, u32[]{:S(2)}) collective-permute-start(bf16[1,256,256]{2,1,0:T(8,128)(2,1)} %basis_ref.1), channel_id=1, source_target_pairs={{0,8},{1,5},{4,12},{5,1},{8,0},{9,13},{12,4},{13,9},{2,10},{3,7},{... | collective-permute-start | bytes 393224 | tf_op jit(solution)/shard_map/ppermute | solution.py:184
  4.7 6.5 %copy-start.1 = (bf16[128,32,256]{2,1,0:T(8,128)(2,1)S(1)}, bf16[128,32,256]{2,1,0:T(8,128)(2,1)}, u32[]{:S(2)}) copy-start(bf16[128,32,256]{2,1,0:T(8,128)(2,1)} %mortar_ref.1) | copy-start | bytes 6291460
  4.7 6.5 %copy-start.2 = (bf16[1,256,256]{2,1,0:T(8,128)(2,1)S(1)}, bf16[1,256,256]{2,1,0:T(8,128)(2,1)}, u32[]{:S(2)}) copy-start(bf16[1,256,256]{2,1,0:T(8,128)(2,1)} %basis_ref.1) | copy-start | bytes 393220
  4.7 6.5 %copy-start.3 = (bf16[128,256]{1,0:T(8,128)(2,1)S(1)}, bf16[128,256]{1,0:T(8,128)(2,1)}, u32[]{:S(2)}) copy-start(bf16[128,256]{1,0:T(8,128)(2,1)} %scale_ref.3) | copy-start | bytes 196612
  4.7 6.5 %copy-start.4 = (f32[32]{0:T(128)S(1)}, f32[32]{0:T(128)}, u32[]{:S(2)}) copy-start(f32[32]{0:T(128)} %param.10) | copy-start | bytes 388
  4.7 6.5 %copy-start.5 = (s32[32]{0:T(128)S(1)}, s32[32]{0:T(128)}, u32[]{:S(2)}) copy-start(s32[32]{0:T(128)} %param.11) | copy-start | bytes 388
  4.7 6.5 %copy-start.6 = (s32[128,1]{0,1:T(1,128)S(1)}, s32[128,1]{0,1:T(1,128)}, u32[]{:S(2)}) copy-start(s32[128,1]{0,1:T(1,128)} %param.12) | copy-start | bytes 1540
  4.7 6.5 %copy-start.7 = (s32[128]{0:T(128)S(1)}, s32[128]{0:T(128)}, u32[]{:S(2)}) copy-start(s32[128]{0:T(128)} %param.13) | copy-start | bytes 1540
  6.1 4.5 %collective-permute-start.1 = (bf16[80,256]{1,0:T(8,128)(2,1)S(1)}, bf16[80,256]{1,0:T(8,128)(2,1)S(1)}, u32[]{:S(2)}, u32[]{:S(2)}) collective-permute-start(bf16[80,256]{1,0:T(8,128)(2,1)S(1)} %get-tuple-element.21), channel_id=1, source_target_pairs={{0,1},{1,0},{2,3},{3,2},{4,5},{5,4},{6,7},{7,6},{8,9},{9,8},{10,11... | collective-permute-start | bytes 122888 | tf_op jit(solution)/shard_map/ppermute | solution.py:204
  6.2 5.0 %collective-permute-start.2 = (bf16[80,256]{1,0:T(8,128)(2,1)S(1)}, bf16[80,256]{1,0:T(8,128)(2,1)S(1)}, u32[]{:S(2)}, u32[]{:S(2)}) collective-permute-start(bf16[80,256]{1,0:T(8,128)(2,1)S(1)} %get-tuple-element.25), channel_id=1, source_target_pairs={{0,8},{4,12},{8,0},{12,4},{1,9},{5,13},{9,1},{13,5},{2,10},{6,14},... | collective-permute-start | bytes 122888 | tf_op jit(solution)/shard_map/ppermute | solution.py:202
  7.3 4.7 %collective-permute-start.3 = (bf16[80,256]{1,0:T(8,128)(2,1)S(1)}, bf16[80,256]{1,0:T(8,128)(2,1)S(1)}, u32[]{:S(2)}, u32[]{:S(2)}) collective-permute-start(bf16[80,256]{1,0:T(8,128)(2,1)S(1)} %get-tuple-element.27), channel_id=1, source_target_pairs={{0,4},{4,0},{8,12},{12,8},{1,5},{5,1},{9,13},{13,9},{2,6},{6,2},{1... | collective-permute-start | bytes 122888 | tf_op jit(solution)/shard_map/ppermute | solution.py:202
  8.1 5.9 %collective-permute-start.5 = (bf16[80,256]{1,0:T(8,128)(2,1)S(1)}, bf16[80,256]{1,0:T(8,128)(2,1)S(1)}, u32[]{:S(2)}, u32[]{:S(2)}) collective-permute-start(bf16[80,256]{1,0:T(8,128)(2,1)S(1)} %get-tuple-element.31), channel_id=1, source_target_pairs={{0,12},{4,8},{8,4},{12,0},{1,13},{5,9},{9,5},{13,1},{2,14},{6,10},... | collective-permute-start | bytes 122888 | tf_op jit(solution)/shard_map/ppermute | solution.py:202
  10.6 3.4 %collective-permute-start.8 = (bf16[1,256,256]{2,1,0:T(8,128)(2,1)S(1)}, bf16[1,256,256]{2,1,0:T(8,128)(2,1)S(1)}, u32[]{:S(2)}, u32[]{:S(2)}) collective-permute-start(bf16[1,256,256]{2,1,0:T(8,128)(2,1)S(1)} %collective-permute-done.refs_0_.refs_5_), channel_id=1, source_target_pairs={{0,5},{1,0},{4,1},{5,4},{8,13},{9,8},{12,9},{13,12},{2,7},{3,2},{6... | collective-permute-start | bytes 393224 | tf_op jit(solution)/shard_map/ppermute | solution.py:230
  11.2 1.3 %collective-permute-start.4 = (bf16[1,256,256]{2,1,0:T(8,128)(2,1)S(1)}, bf16[1,256,256]{2,1,0:T(8,128)(2,1)S(1)}, u32[]{:S(2)}, u32[]{:S(2)}) collective-permute-start(bf16[1,256,256]{2,1,0:T(8,128)(2,1)S(1)} %collective-permute-done.refs_0_.refs_5_), channel_id=1, source_target_pairs={{0,1},{1,0},{2,3},{3,2},{4,5},{5,4},{6,7},{7,6},{8,9},{9,8},{10,11... | collective-permute-start | bytes 393224 | tf_op jit(solution)/shard_map/ppermute | solution.py:232
  12.5 2.6 %collective-permute-start.6 = (bf16[80,256]{1,0:T(8,128)(2,1)S(1)}, bf16[80,256]{1,0:T(8,128)(2,1)S(1)}, u32[]{:S(2)}, u32[]{:S(2)}) collective-permute-start(bf16[80,256]{1,0:T(8,128)(2,1)S(1)} %collective-permute-done.2.refs_2_), channel_id=1, source_target_pairs={{0,1},{1,0},{2,3},{3,2},{4,5},{5,4},{6,7},{7,6},{8,9},{9,8},{10,11... | collective-permute-start | bytes 122888 | tf_op jit(solution)/shard_map/ppermute | solution.py:238
  12.7 2.4 %collective-permute-start.7 = (bf16[80,256]{1,0:T(8,128)(2,1)S(1)}, bf16[80,256]{1,0:T(8,128)(2,1)S(1)}, u32[]{:S(2)}, u32[]{:S(2)}) collective-permute-start(bf16[80,256]{1,0:T(8,128)(2,1)S(1)} %collective-permute-done.3.refs_6_), channel_id=1, source_target_pairs={{0,1},{1,0},{2,3},{3,2},{4,5},{5,4},{6,7},{7,6},{8,9},{9,8},{10,11... | collective-permute-start | bytes 122888 | tf_op jit(solution)/shard_map/ppermute | solution.py:238
  14.1 2.2 %collective-permute-start.10 = (bf16[80,256]{1,0:T(8,128)(2,1)S(1)}, bf16[80,256]{1,0:T(8,128)(2,1)S(1)}, u32[]{:S(2)}, u32[]{:S(2)}) collective-permute-start(bf16[80,256]{1,0:T(8,128)(2,1)S(1)} %collective-permute-done.5.refs_2_), channel_id=1, source_target_pairs={{0,1},{1,0},{2,3},{3,2},{4,5},{5,4},{6,7},{7,6},{8,9},{9,8},{10,11... | collective-permute-start | bytes 122888 | tf_op jit(solution)/shard_map/ppermute | solution.py:238
  14.1 2.2 %collective-permute-start.9 = (bf16[1,256,256]{2,1,0:T(8,128)(2,1)S(1)}, bf16[1,256,256]{2,1,0:T(8,128)(2,1)S(1)}, u32[]{:S(2)}, u32[]{:S(2)}) collective-permute-start(bf16[1,256,256]{2,1,0:T(8,128)(2,1)S(1)} %collective-permute-done.8.refs_1_), channel_id=1, source_target_pairs={{0,1},{1,0},{2,3},{3,2},{4,5},{5,4},{6,7},{7,6},{8,9},{9,8},{10,11... | collective-permute-start | bytes 393224 | tf_op jit(solution)/shard_map/ppermute | solution.py:238
  15.1 1.2 %copy-start = (bf16[256,256]{1,0:T(8,128)(2,1)S(1)}, bf16[256,256]{1,0:T(8,128)(2,1)}, u32[]{:S(2)}) copy-start(bf16[256,256]{1,0:T(8,128)(2,1)} %projection_ref.1) | copy-start | bytes 393220

commit v22 on v17

--- a/solution.py
+++ b/solution.py
@@ -250,21 +250,24 @@
             pltpu.VMEM((2, blocks_own // tiles * cols_dev, count * dof_count), jnp.bfloat16),
         ]
 
-    operands = [pumped, own_sum, *sum(early, [])]
-    total = pl.pallas_call(
-        stage_kernel,
-        out_shape=jax.ShapeDtypeStruct(block_shape, jnp.float32),
-        in_specs=[VMEM] * len(operands),
-        out_specs=VMEM,
-        scratch_shapes=scratch(len(early), TILES),
-        input_output_aliases={1: 0},
-        compiler_params=pltpu.CompilerParams(vmem_limit_bytes=40 * MIB),
-        cost_estimate=LIGHT,
-        name="stage",
-    )(*operands)
-
+    def stage(total, arrays, cost):
+        operands = [pumped, total, *arrays]
+        return pl.pallas_call(
+            stage_kernel,
+            out_shape=jax.ShapeDtypeStruct(block_shape, jnp.float32),
+            in_specs=[VMEM] * len(operands),
+            out_specs=VMEM,
+            scratch_shapes=scratch(len(arrays) // 4, TILES),
+            input_output_aliases={1: 0},
+            compiler_params=pltpu.CompilerParams(vmem_limit_bytes=40 * MIB),
+            cost_estimate=cost,
+            name="stage",
+        )(*operands)
+
+    total = stage(own_sum, early[-1], LIGHT)
     seconds, total = lax.optimization_barrier((seconds, total))
     late = [[other, second, *pair] for (second, other), pair in zip(with_swapped(seconds), later)]
+    total = stage(total, sum(early[:-1], []), WORK)
 
     operands = [pumped, total, projection, *sum(late, [])]
     return pl.pallas_call(

time: 18.7 us -> 18.3 us (0.979)
  waiting for transfers between devices: 2.97 us -> 2.36 us
  Pallas kernels: 5.13 us -> 5.34 us
    ppermute x4, waiting for transfers between devices: 0.92 us -> 0.3 us  [with_swapped(): return [(array, lax.ppermute(array, 'face', swap)) for array in arrays]]
    pallas_call x1 -> x2, Pallas kernels: 1.13 us -> 1.34 us  [stage(): pl.pallas_call(stage_kernel, out_shape=jax.ShapeDtypeStruct(block_shape,...]
  transfers between devices with their start and end apart: 11 -> 11, of which waited for: 4 -> 4; matrix products, arithmetic and copies ran while one was open for 0% -> 0% of each run, Pallas kernels for 18% -> 19%
where the time goes in v22:
time: 18.3 us; the launch traced here: 18.2 us
  starting transfers between devices  9.63 us (53%)
  Pallas kernels  5.34 us (29%)
  waiting for transfers between devices  2.36 us (13%)
  between operations  0.82 us (4%)
    ppermute x3, starting transfers between devices, on_device(): lax.ppermute(pack, 'sub', [(i, i ^ p) for i in range(subdomains)])  4.45 us
    ppermute x1, starting transfers between devices, on_device(): lax.ppermute(basis, ('sub', 'face'), [(flat(s, face), flat(s ^ (1 if face...  4.04 us
    pallas_call x1, Pallas kernels, on_device(): pl.pallas_call(last_kernel, out_shape=jax.ShapeDtypeStruct(block_shape, j...  1.86 us
    ppermute x3, waiting for transfers between devices, on_device(): lax.ppermute(pack, 'sub', [(i, i ^ p) for i in range(subdomains)])  1.56 us
    pallas_call x1, Pallas kernels, on_device(): pl.pallas_call(functools.partial(pack_kernel, partners), out_shape=[pltpu...  1.36 us
    pallas_call x2, Pallas kernels, stage(): pl.pallas_call(stage_kernel, out_shape=jax.ShapeDtypeStruct(block_shape,...  1.34 us
    ppermute x4, starting transfers between devices, with_swapped(): return [(array, lax.ppermute(array, 'face', swap)) for array in arrays]  1.09 us
    pallas_call x1, Pallas kernels, on_device(): pl.pallas_call(own_kernel, out_shape=[jax.ShapeDtypeStruct(block_shape, j...  0.78 us
  transfers between devices with their start and end apart: 11, of which 4 were waited for; matrix products, arithmetic and copies ran while one was open for 0% of the time, Pallas kernels for 19%

profile of v22, /device:TPU:0, one launch (start us, length us, event | category | flops | bytes accessed | tf_op | source)
XLA Modules:
  0.0 18.2 jit_solution(4898291121022954969)
XLA Ops:
  0.0 4.0 %collective-permute-start = (bf16[1,256,256]{2,1,0:T(8,128)(2,1)}, bf16[1,256,256]{2,1,0:T(8,128)(2,1)S(1)}, u32[]{:S(2)}, u32[]{:S(2)}) collective-permute-start(bf16[1,256,256]{2,1,0:T(8,128)(2,1)} %basis_ref.1), channel_id=1, source_target_pairs={{0,8},{1,5},{4,12},{5,1},{8,0},{9,13},{12,4},{13,9},{2,10},{3,7},{... | collective-permute-start | bytes 393224 | tf_op jit(solution)/shard_map/ppermute | solution.py:184
  4.7 0.0 copy-start.1
  4.7 0.0 copy-start.2
  4.7 0.0 copy-start.3
  4.7 0.0 copy-start.4
  4.7 0.0 copy-start.5
  4.7 0.0 copy-start.6
  4.7 0.0 copy-start.7
  4.8 1.4 %pack_weights.1 = (bf16[80,256]{1,0:T(8,128)(2,1)S(1)}, bf16[80,256]{1,0:T(8,128)(2,1)S(1)}, bf16[80,256]{1,0:T(8,128)(2,1)S(1)}, bf16[80,256]{1,0:T(8,128)(2,1)S(1)}) custom-call(s32[1,128]{1,0:T(1,128)} %bitcast.6, s32[1,128]{1,0:T(1,128)} %bitcast.8, bf16[128,256]{1,0:T(8,128)(2,1)} %scale_ref.3, s32[1]{0:T(128)S(6)} %copy.14.section_ref), custom_call_target="tpu_custom_call" | custom-call | flops 4000000000 | bytes 8388608 | tf_op jit(solution)/shard_map/pack_weights/pallas_call | solution.py:192
  6.1 0.0 collective-permute-start.1
  6.2 1.1 %collective-permute-start.3 = (bf16[80,256]{1,0:T(8,128)(2,1)S(1)}, bf16[80,256]{1,0:T(8,128)(2,1)S(1)}, u32[]{:S(2)}, u32[]{:S(2)}) collective-permute-start(bf16[80,256]{1,0:T(8,128)(2,1)S(1)} %get-tuple-element.27), channel_id=1, source_target_pairs={{0,8},{4,12},{8,0},{12,4},{1,9},{5,13},{9,1},{13,5},{2,10},{6,14},... | collective-permute-start | bytes 122888 | tf_op jit(solution)/shard_map/ppermute | solution.py:202
  7.3 0.9 %collective-permute-start.4 = (bf16[80,256]{1,0:T(8,128)(2,1)S(1)}, bf16[80,256]{1,0:T(8,128)(2,1)S(1)}, u32[]{:S(2)}, u32[]{:S(2)}) collective-permute-start(bf16[80,256]{1,0:T(8,128)(2,1)S(1)} %get-tuple-element.29), channel_id=1, source_target_pairs={{0,4},{4,0},{8,12},{12,8},{1,5},{5,1},{9,13},{13,9},{2,6},{6,2},{1... | collective-permute-start | bytes 122888 | tf_op jit(solution)/shard_map/ppermute | solution.py:202
  8.1 2.5 %collective-permute-start.6 = (bf16[80,256]{1,0:T(8,128)(2,1)S(1)}, bf16[80,256]{1,0:T(8,128)(2,1)S(1)}, u32[]{:S(2)}, u32[]{:S(2)}) collective-permute-start(bf16[80,256]{1,0:T(8,128)(2,1)S(1)} %get-tuple-element.33), channel_id=1, source_target_pairs={{0,12},{4,8},{8,4},{12,0},{1,13},{5,9},{9,5},{13,1},{2,14},{6,10},... | collective-permute-start | bytes 122888 | tf_op jit(solution)/shard_map/ppermute | solution.py:202
  10.6 0.0 collective-permute-done.1.swapped_ref
  10.6 0.0 collective-permute-done.refs_1_.refs_0_
  10.6 0.0 collective-permute-start.2
  10.6 0.5 %collective-permute-done.3.refs_2_ = bf16[80,256]{1,0:T(8,128)(2,1)S(1)} collective-permute-done((bf16[80,256]{1,0:T(8,128)(2,1)S(1)}, bf16[80,256]{1,0:T(8,128)(2,1)S(1)}, u32[]{:S(2)}, u32[]{:S(2)}) %collective-permute-start.3) | collective-permute-done | bytes 40992 | tf_op jit(solution)/shard_map/ppermute | solution.py:202
  11.2 0.0 collective-permute-start.5
  11.2 0.0 copy-done.1
  11.2 0.0 copy-done.2
  11.2 0.0 copy-done.3
  11.2 0.0 copy-done.4
  11.2 0.0 copy-done.5
  11.2 0.0 copy-done.6
  11.2 0.0 copy-done.7
  11.2 0.8 %own_blocks.1 = (bf16[64,32,256]{2,1,0:T(8,128)(2,1)S(1)}, f32[64,32,256]{2,1,0:T(8,128)S(1)}) custom-call(bf16[128,32,256]{2,1,0:T(8,128)(2,1)S(1)} %copy-done.1, f32[1,32]{1,0:T(1,128)S(1)} %bitcast.4, s32[1,32]{1,0:T(1,128)S(1)} %bitcast.5, s32[1,128]{1,0:T(1,128)S(1)} %bitcast.7, s32[1,128]{1,0:T(1,128)S(1)} %bitcast.9, bf16[128,256]{1,0:T(8,128)(2,1)S(1)} %copy-done.3, ...), custom_call_target="tpu_custom_call" | custom-call | flops 4000000000 | bytes 8388608 | tf_op jit(solution)/shard_map/own_blocks/pallas_call | solution.py:207
  12.0 0.0 collective-permute-done.4.refs_2_
  12.0 0.5 %collective-permute-done.5.refs_0_.refs_1_ = bf16[1,256,256]{2,1,0:T(8,128)(2,1)S(1)} collective-permute-done((bf16[1,256,256]{2,1,0:T(8,128)(2,1)S(1)}, bf16[1,256,256]{2,1,0:T(8,128)(2,1)S(1)}, u32[]{:S(2)}, u32[]{:S(2)}) %collective-permute-start.5) | collective-permute-done | bytes 131104 | tf_op jit(solution)/shard_map/ppermute | solution.py:232
  12.5 0.1 collective-permute-start.7
  12.7 0.4 %collective-permute-start.8 = (bf16[80,256]{1,0:T(8,128)(2,1)S(1)}, bf16[80,256]{1,0:T(8,128)(2,1)S(1)}, u32[]{:S(2)}, u32[]{:S(2)}) collective-permute-start(bf16[80,256]{1,0:T(8,128)(2,1)S(1)} %collective-permute-done.3.refs_2_), channel_id=1, source_target_pairs={{0,1},{1,0},{2,3},{3,2},{4,5},{5,4},{6,7},{7,6},{8,9},{9,8},{10,11... | collective-permute-start | bytes 122888 | tf_op jit(solution)/shard_map/ppermute | solution.py:238
  13.0 1.0 %collective-permute-done.6.refs_2_ = bf16[80,256]{1,0:T(8,128)(2,1)S(1)} collective-permute-done((bf16[80,256]{1,0:T(8,128)(2,1)S(1)}, bf16[80,256]{1,0:T(8,128)(2,1)S(1)}, u32[]{:S(2)}, u32[]{:S(2)}) %collective-permute-start.6) | collective-permute-done | bytes 40992 | tf_op jit(solution)/shard_map/ppermute | solution.py:202
  14.1 0.0 collective-permute-start.10
  14.1 0.0 collective-permute-done.7.refs_3_
  14.1 0.7 %stage.2.sum_ref = f32[64,32,256]{2,1,0:T(8,128)S(1)} custom-call(bf16[64,32,256]{2,1,0:T(8,128)(2,1)S(1)} %get-tuple-element.25.pumped_ref, f32[64,32,256]{2,1,0:T(8,128)S(1)} %get-tuple-element.34.sum_ref, bf16[1,256,256]{2,1,0:T(8,128)(2,1)S(1)} %collective-permute-done.5.refs_0_.refs_1_, ...), custom_call_target="tpu_custom_call", output_to_operand_aliasing={{}: (1, {})} | custom-call | flops 1000000 | bytes 1024 | tf_op jit(solution)/shard_map/stage/pallas_call | solution.py:255
  14.7 0.0 copy-start
  14.8 0.0 collective-permute-done.2.refs_1_
  14.8 0.6 %collective-permute-start.9 = (bf16[1,256,256]{2,1,0:T(8,128)(2,1)S(1)}, bf16[1,256,256]{2,1,0:T(8,128)(2,1)S(1)}, u32[]{:S(2)}, u32[]{:S(2)}) collective-permute-start(bf16[1,256,256]{2,1,0:T(8,128)(2,1)S(1)} %collective-permute-done.2.refs_1_), channel_id=1, source_target_pairs={{0,1},{1,0},{2,3},{3,2},{4,5},{5,4},{6,7},{7,6},{8,9},{9,8},{10,11... | collective-permute-start | bytes 393224 | tf_op jit(solution)/shard_map/ppermute | solution.py:238
  15.3 0.0 collective-permute-done.8.refs_3_
  15.3 0.7 %stage.3.sum_ref = f32[64,32,256]{2,1,0:T(8,128)S(1)} custom-call(bf16[64,32,256]{2,1,0:T(8,128)(2,1)S(1)} %get-tuple-element.25.pumped_ref, f32[64,32,256]{2,1,0:T(8,128)S(1)} %stage.2.sum_ref, bf16[1,256,256]{2,1,0:T(8,128)(2,1)S(1)} %collective-permute-done.refs_1_.refs_0_, ...), custom_call_target="tpu_custom_call", output_to_operand_aliasing={{}: (1, {})} | custom-call | flops 4000000000 | bytes 8388608 | tf_op jit(solution)/shard_map/stage/pallas_call | solution.py:255
  16.0 0.0 collective-permute-done.10.refs_3_
  16.0 0.3 %collective-permute-done.9.refs_0_ = bf16[1,256,256]{2,1,0:T(8,128)(2,1)S(1)} collective-permute-done((bf16[1,256,256]{2,1,0:T(8,128)(2,1)S(1)}, bf16[1,256,256]{2,1,0:T(8,128)(2,1)S(1)}, u32[]{:S(2)}, u32[]{:S(2)}) %collective-permute-start.9) | collective-permute-done | bytes 131104 | tf_op jit(solution)/shard_map/ppermute | solution.py:238
  16.3 0.0 copy-done
  16.3 1.9 %last_stage.1 = f32[64,32,256]{2,1,0:T(8,128)} custom-call(bf16[64,32,256]{2,1,0:T(8,128)(2,1)S(1)} %get-tuple-element.25.pumped_ref, f32[64,32,256]{2,1,0:T(8,128)S(1)} %stage.3.sum_ref, bf16[256,256]{1,0:T(8,128)(2,1)S(1)} %copy-done, bf16[1,256,256]{2,1,0:T(8,128)(2,1)S(1)} %collective-permute-done.9.refs_0_, ...), custom_call_target="tpu_custom_call" | custom-call | tf_op jit(solution)/shard_map/last_stage/pallas_call | solution.py:273
Async XLA Ops:
  0.0 10.6 %collective-permute-start = (bf16[1,256,256]{2,1,0:T(8,128)(2,1)}, bf16[1,256,256]{2,1,0:T(8,128)(2,1)S(1)}, u32[]{:S(2)}, u32[]{:S(2)}) collective-permute-start(bf16[1,256,256]{2,1,0:T(8,128)(2,1)} %basis_ref.1), channel_id=1, source_target_pairs={{0,8},{1,5},{4,12},{5,1},{8,0},{9,13},{12,4},{13,9},{2,10},{3,7},{... | collective-permute-start | bytes 393224 | tf_op jit(solution)/shard_map/ppermute | solution.py:184
  4.7 6.5 %copy-start.1 = (bf16[128,32,256]{2,1,0:T(8,128)(2,1)S(1)}, bf16[128,32,256]{2,1,0:T(8,128)(2,1)}, u32[]{:S(2)}) copy-start(bf16[128,32,256]{2,1,0:T(8,128)(2,1)} %mortar_ref.1) | copy-start | bytes 6291460
  4.7 6.5 %copy-start.2 = (bf16[1,256,256]{2,1,0:T(8,128)(2,1)S(1)}, bf16[1,256,256]{2,1,0:T(8,128)(2,1)}, u32[]{:S(2)}) copy-start(bf16[1,256,256]{2,1,0:T(8,128)(2,1)} %basis_ref.1) | copy-start | bytes 393220
  4.7 6.5 %copy-start.3 = (bf16[128,256]{1,0:T(8,128)(2,1)S(1)}, bf16[128,256]{1,0:T(8,128)(2,1)}, u32[]{:S(2)}) copy-start(bf16[128,256]{1,0:T(8,128)(2,1)} %scale_ref.3) | copy-start | bytes 196612
  4.7 6.5 %copy-start.4 = (f32[32]{0:T(128)S(1)}, f32[32]{0:T(128)}, u32[]{:S(2)}) copy-start(f32[32]{0:T(128)} %param.10) | copy-start | bytes 388
  4.7 6.5 %copy-start.5 = (s32[32]{0:T(128)S(1)}, s32[32]{0:T(128)}, u32[]{:S(2)}) copy-start(s32[32]{0:T(128)} %param.11) | copy-start | bytes 388
  4.7 6.5 %copy-start.6 = (s32[128,1]{0,1:T(1,128)S(1)}, s32[128,1]{0,1:T(1,128)}, u32[]{:S(2)}) copy-start(s32[128,1]{0,1:T(1,128)} %param.12) | copy-start | bytes 1540
  4.7 6.5 %copy-start.7 = (s32[128]{0:T(128)S(1)}, s32[128]{0:T(128)}, u32[]{:S(2)}) copy-start(s32[128]{0:T(128)} %param.13) | copy-start | bytes 1540
  6.1 4.5 %collective-permute-start.1 = (bf16[80,256]{1,0:T(8,128)(2,1)S(1)}, bf16[80,256]{1,0:T(8,128)(2,1)S(1)}, u32[]{:S(2)}, u32[]{:S(2)}) collective-permute-start(bf16[80,256]{1,0:T(8,128)(2,1)S(1)} %get-tuple-element.23), channel_id=1, source_target_pairs={{0,1},{1,0},{2,3},{3,2},{4,5},{5,4},{6,7},{7,6},{8,9},{9,8},{10,11... | collective-permute-start | bytes 122888 | tf_op jit(solution)/shard_map/ppermute | solution.py:204
  6.2 5.0 %collective-permute-start.3 = (bf16[80,256]{1,0:T(8,128)(2,1)S(1)}, bf16[80,256]{1,0:T(8,128)(2,1)S(1)}, u32[]{:S(2)}, u32[]{:S(2)}) collective-permute-start(bf16[80,256]{1,0:T(8,128)(2,1)S(1)} %get-tuple-element.27), channel_id=1, source_target_pairs={{0,8},{4,12},{8,0},{12,4},{1,9},{5,13},{9,1},{13,5},{2,10},{6,14},... | collective-permute-start | bytes 122888 | tf_op jit(solution)/shard_map/ppermute | solution.py:202
  7.3 4.7 %collective-permute-start.4 = (bf16[80,256]{1,0:T(8,128)(2,1)S(1)}, bf16[80,256]{1,0:T(8,128)(2,1)S(1)}, u32[]{:S(2)}, u32[]{:S(2)}) collective-permute-start(bf16[80,256]{1,0:T(8,128)(2,1)S(1)} %get-tuple-element.29), channel_id=1, source_target_pairs={{0,4},{4,0},{8,12},{12,8},{1,5},{5,1},{9,13},{13,9},{2,6},{6,2},{1... | collective-permute-start | bytes 122888 | tf_op jit(solution)/shard_map/ppermute | solution.py:202
  8.1 5.9 %collective-permute-start.6 = (bf16[80,256]{1,0:T(8,128)(2,1)S(1)}, bf16[80,256]{1,0:T(8,128)(2,1)S(1)}, u32[]{:S(2)}, u32[]{:S(2)}) collective-permute-start(bf16[80,256]{1,0:T(8,128)(2,1)S(1)} %get-tuple-element.33), channel_id=1, source_target_pairs={{0,12},{4,8},{8,4},{12,0},{1,13},{5,9},{9,5},{13,1},{2,14},{6,10},... | collective-permute-start | bytes 122888 | tf_op jit(solution)/shard_map/ppermute | solution.py:202
  10.6 4.1 %collective-permute-start.2 = (bf16[1,256,256]{2,1,0:T(8,128)(2,1)S(1)}, bf16[1,256,256]{2,1,0:T(8,128)(2,1)S(1)}, u32[]{:S(2)}, u32[]{:S(2)}) collective-permute-start(bf16[1,256,256]{2,1,0:T(8,128)(2,1)S(1)} %collective-permute-done.refs_1_.refs_0_), channel_id=1, source_target_pairs={{0,5},{1,0},{4,1},{5,4},{8,13},{9,8},{12,9},{13,12},{2,7},{3,2},{6... | collective-permute-start | bytes 393224 | tf_op jit(solution)/shard_map/ppermute | solution.py:230
  11.2 1.3 %collective-permute-start.5 = (bf16[1,256,256]{2,1,0:T(8,128)(2,1)S(1)}, bf16[1,256,256]{2,1,0:T(8,128)(2,1)S(1)}, u32[]{:S(2)}, u32[]{:S(2)}) collective-permute-start(bf16[1,256,256]{2,1,0:T(8,128)(2,1)S(1)} %collective-permute-done.refs_1_.refs_0_), channel_id=1, source_target_pairs={{0,1},{1,0},{2,3},{3,2},{4,5},{5,4},{6,7},{7,6},{8,9},{9,8},{10,11... | collective-permute-start | bytes 393224 | tf_op jit(solution)/shard_map/ppermute | solution.py:232
  12.5 1.5 %collective-permute-start.7 = (bf16[80,256]{1,0:T(8,128)(2,1)S(1)}, bf16[80,256]{1,0:T(8,128)(2,1)S(1)}, u32[]{:S(2)}, u32[]{:S(2)}) collective-permute-start(bf16[80,256]{1,0:T(8,128)(2,1)S(1)} %collective-permute-done.4.refs_2_), channel_id=1, source_target_pairs={{0,1},{1,0},{2,3},{3,2},{4,5},{5,4},{6,7},{7,6},{8,9},{9,8},{10,11... | collective-permute-start | bytes 122888 | tf_op jit(solution)/shard_map/ppermute | solution.py:238
  12.7 2.7 %collective-permute-start.8 = (bf16[80,256]{1,0:T(8,128)(2,1)S(1)}, bf16[80,256]{1,0:T(8,128)(2,1)S(1)}, u32[]{:S(2)}, u32[]{:S(2)}) collective-permute-start(bf16[80,256]{1,0:T(8,128)(2,1)S(1)} %collective-permute-done.3.refs_2_), channel_id=1, source_target_pairs={{0,1},{1,0},{2,3},{3,2},{4,5},{5,4},{6,7},{7,6},{8,9},{9,8},{10,11... | collective-permute-start | bytes 122888 | tf_op jit(solution)/shard_map/ppermute | solution.py:238
  14.1 2.0 %collective-permute-start.10 = (bf16[80,256]{1,0:T(8,128)(2,1)S(1)}, bf16[80,256]{1,0:T(8,128)(2,1)S(1)}, u32[]{:S(2)}, u32[]{:S(2)}) collective-permute-start(bf16[80,256]{1,0:T(8,128)(2,1)S(1)} %collective-permute-done.6.refs_2_), channel_id=1, source_target_pairs={{0,1},{1,0},{2,3},{3,2},{4,5},{5,4},{6,7},{7,6},{8,9},{9,8},{10,11... | collective-permute-start | bytes 122888 | tf_op jit(solution)/shard_map/ppermute | solution.py:238
  14.7 1.6 %copy-start = (bf16[256,256]{1,0:T(8,128)(2,1)S(1)}, bf16[256,256]{1,0:T(8,128)(2,1)}, u32[]{:S(2)}) copy-start(bf16[256,256]{1,0:T(8,128)(2,1)} %projection_ref.1) | copy-start | bytes 393220
  14.8 1.6 %collective-permute-start.9 = (bf16[1,256,256]{2,1,0:T(8,128)(2,1)S(1)}, bf16[1,256,256]{2,1,0:T(8,128)(2,1)S(1)}, u32[]{:S(2)}, u32[]{:S(2)}) collective-permute-start(bf16[1,256,256]{2,1,0:T(8,128)(2,1)S(1)} %collective-permute-done.2.refs_1_), channel_id=1, source_target_pairs={{0,1},{1,0},{2,3},{3,2},{4,5},{5,4},{6,7},{7,6},{8,9},{9,8},{10,11... | collective-permute-start | bytes 393224 | tf_op jit(solution)/shard_map/ppermute | solution.py:238

commit v23 on v18

--- a/solution.py
+++ b/solution.py
@@ -230,9 +230,7 @@
     seconds = [lax.ppermute(first, ("sub", "face"), pairs) for first in firsts]
     firsts, arrived[:len(evens)] = lax.optimization_barrier((firsts, arrived[:len(evens)]))
     firsts_swapped = [lax.ppermute(first, "face", swap) for first in firsts]
-    soon, own_sum, firsts_swapped = lax.optimization_barrier(
-        (arrived[: early_count - 1], own_sum, firsts_swapped)
-    )
+    soon, own_sum = lax.optimization_barrier((arrived[: early_count - 1], own_sum))
 
     def with_swapped(arrays):
         return [(array, lax.ppermute(array, "face", swap)) for array in arrays]

time: 18.3 us -> 18.3 us (level)
    ppermute x1, waiting for transfers between devices: 0.49 us -> 0.01 us  [on_device(): firsts_swapped = [lax.ppermute(first, 'face', swap) for first in firsts]]
    ppermute x3, waiting for transfers between devices: 1.56 us -> 1.92 us  [on_device(): lax.ppermute(pack, 'sub', [(i, i ^ p) for i in range(subdomains)])]
  transfers between devices with their start and end apart: 11 -> 11, of which waited for: 3 -> 2; matrix products, arithmetic and copies ran while one was open for 0% -> 0% of each run, Pallas kernels for 18% -> 18%
where the time goes in v23:
time: 18.3 us; the launch traced here: 18.1 us
  starting transfers between devices  10.2 us (56%)
  Pallas kernels  5.12 us (28%)
  waiting for transfers between devices  1.94 us (11%)
  between operations  0.83 us (5%)
    ppermute x3, starting transfers between devices, on_device(): lax.ppermute(pack, 'sub', [(i, i ^ p) for i in range(subdomains)])  4.45 us
    ppermute x1, starting transfers between devices, on_device(): lax.ppermute(basis, ('sub', 'face'), [(flat(s, face), flat(s ^ (1 if face...  4.04 us
    ppermute x3, waiting for transfers between devices, on_device(): lax.ppermute(pack, 'sub', [(i, i ^ p) for i in range(subdomains)])  1.92 us
    pallas_call x1, Pallas kernels, on_device(): pl.pallas_call(last_kernel, out_shape=jax.ShapeDtypeStruct(block_shape, j...  1.86 us
    ppermute x4, starting transfers between devices, with_swapped(): return [(array, lax.ppermute(array, 'face', swap)) for array in arrays]  1.65 us
    pallas_call x1, Pallas kernels, on_device(): pl.pallas_call(functools.partial(pack_kernel, partners), out_shape=[pltpu...  1.36 us
    pallas_call x1, Pallas kernels, on_device(): pl.pallas_call(stage_kernel, out_shape=jax.ShapeDtypeStruct(block_shape,...  1.13 us
    pallas_call x1, Pallas kernels, on_device(): pl.pallas_call(own_kernel, out_shape=[jax.ShapeDtypeStruct(block_shape, j...  0.78 us
  transfers between devices with their start and end apart: 11, of which 2 were waited for; matrix products, arithmetic and copies ran while one was open for 0% of the time, Pallas kernels for 18%

profile of v23, /device:TPU:0, one launch (start us, length us, event | category | flops | bytes accessed | tf_op | source)
XLA Modules:
  0.0 18.1 jit_solution(2972946175606887385)
XLA Ops:
  0.0 4.0 %collective-permute-start = (bf16[1,256,256]{2,1,0:T(8,128)(2,1)}, bf16[1,256,256]{2,1,0:T(8,128)(2,1)S(1)}, u32[]{:S(2)}, u32[]{:S(2)}) collective-permute-start(bf16[1,256,256]{2,1,0:T(8,128)(2,1)} %basis_ref.1), channel_id=1, source_target_pairs={{0,8},{1,5},{4,12},{5,1},{8,0},{9,13},{12,4},{13,9},{2,10},{3,7},{... | collective-permute-start | bytes 393224 | tf_op jit(solution)/shard_map/ppermute | solution.py:184
  4.7 0.0 copy-start.1
  4.7 0.0 copy-start.2
  4.7 0.0 copy-start.3
  4.7 0.0 copy-start.4
  4.7 0.0 copy-start.5
  4.7 0.0 copy-start.6
  4.7 0.0 copy-start.7
  4.8 1.4 %pack_weights.1 = (bf16[80,256]{1,0:T(8,128)(2,1)S(1)}, bf16[80,256]{1,0:T(8,128)(2,1)S(1)}, bf16[80,256]{1,0:T(8,128)(2,1)S(1)}, bf16[80,256]{1,0:T(8,128)(2,1)S(1)}) custom-call(s32[1,128]{1,0:T(1,128)} %bitcast.6, s32[1,128]{1,0:T(1,128)} %bitcast.8, bf16[128,256]{1,0:T(8,128)(2,1)} %scale_ref.3, s32[1]{0:T(128)S(6)} %copy.12.section_ref), custom_call_target="tpu_custom_call" | custom-call | flops 4000000000 | bytes 8388608 | tf_op jit(solution)/shard_map/pack_weights/pallas_call | solution.py:192
  6.1 0.0 collective-permute-start.1
  6.2 1.1 %collective-permute-start.2 = (bf16[80,256]{1,0:T(8,128)(2,1)S(1)}, bf16[80,256]{1,0:T(8,128)(2,1)S(1)}, u32[]{:S(2)}, u32[]{:S(2)}) collective-permute-start(bf16[80,256]{1,0:T(8,128)(2,1)S(1)} %get-tuple-element.24), channel_id=1, source_target_pairs={{0,8},{4,12},{8,0},{12,4},{1,9},{5,13},{9,1},{13,5},{2,10},{6,14},... | collective-permute-start | bytes 122888 | tf_op jit(solution)/shard_map/ppermute | solution.py:202
  7.3 0.9 %collective-permute-start.3 = (bf16[80,256]{1,0:T(8,128)(2,1)S(1)}, bf16[80,256]{1,0:T(8,128)(2,1)S(1)}, u32[]{:S(2)}, u32[]{:S(2)}) collective-permute-start(bf16[80,256]{1,0:T(8,128)(2,1)S(1)} %get-tuple-element.26), channel_id=1, source_target_pairs={{0,4},{4,0},{8,12},{12,8},{1,5},{5,1},{9,13},{13,9},{2,6},{6,2},{1... | collective-permute-start | bytes 122888 | tf_op jit(solution)/shard_map/ppermute | solution.py:202
  8.1 2.5 %collective-permute-start.4 = (bf16[80,256]{1,0:T(8,128)(2,1)S(1)}, bf16[80,256]{1,0:T(8,128)(2,1)S(1)}, u32[]{:S(2)}, u32[]{:S(2)}) collective-permute-start(bf16[80,256]{1,0:T(8,128)(2,1)S(1)} %get-tuple-element.29), channel_id=1, source_target_pairs={{0,12},{4,8},{8,4},{12,0},{1,13},{5,9},{9,5},{13,1},{2,14},{6,10},... | collective-permute-start | bytes 122888 | tf_op jit(solution)/shard_map/ppermute | solution.py:202
  10.6 0.0 collective-permute-done.1.swapped_ref
  10.6 0.0 collective-permute-done.refs_0_.refs_5_
  10.6 0.0 collective-permute-start.8
  10.6 0.5 %collective-permute-done.2.refs_2_ = bf16[80,256]{1,0:T(8,128)(2,1)S(1)} collective-permute-done((bf16[80,256]{1,0:T(8,128)(2,1)S(1)}, bf16[80,256]{1,0:T(8,128)(2,1)S(1)}, u32[]{:S(2)}, u32[]{:S(2)}) %collective-permute-start.2) | collective-permute-done | bytes 40992 | tf_op jit(solution)/shard_map/ppermute | solution.py:202
  11.2 0.0 collective-permute-start.5
  11.2 0.0 copy-done.1
  11.2 0.0 copy-done.2
  11.2 0.0 copy-done.3
  11.2 0.0 copy-done.4
  11.2 0.0 copy-done.5
  11.2 0.0 copy-done.6
  11.2 0.0 copy-done.7
  11.2 0.8 %own_blocks.1 = (bf16[64,32,256]{2,1,0:T(8,128)(2,1)S(1)}, f32[64,32,256]{2,1,0:T(8,128)S(1)}) custom-call(bf16[128,32,256]{2,1,0:T(8,128)(2,1)S(1)} %copy-done.1, f32[1,32]{1,0:T(1,128)S(1)} %bitcast.4, s32[1,32]{1,0:T(1,128)S(1)} %bitcast.5, s32[1,128]{1,0:T(1,128)S(1)} %bitcast.7, s32[1,128]{1,0:T(1,128)S(1)} %bitcast.9, bf16[128,256]{1,0:T(8,128)(2,1)S(1)} %copy-done.3, ...), custom_call_target="tpu_custom_call" | custom-call | flops 4000000000 | bytes 8388608 | tf_op jit(solution)/shard_map/own_blocks/pallas_call | solution.py:207
  12.0 0.0 collective-permute-done.3.refs_6_
  12.0 0.6 %collective-permute-start.6 = (bf16[80,256]{1,0:T(8,128)(2,1)S(1)}, bf16[80,256]{1,0:T(8,128)(2,1)S(1)}, u32[]{:S(2)}, u32[]{:S(2)}) collective-permute-start(bf16[80,256]{1,0:T(8,128)(2,1)S(1)} %collective-permute-done.2.refs_2_), channel_id=1, source_target_pairs={{0,1},{1,0},{2,3},{3,2},{4,5},{5,4},{6,7},{7,6},{8,9},{9,8},{10,11... | collective-permute-start | bytes 122888 | tf_op jit(solution)/shard_map/ppermute | solution.py:236
  12.6 0.1 collective-permute-start.7
  12.7 1.4 %collective-permute-done.4.refs_2_ = bf16[80,256]{1,0:T(8,128)(2,1)S(1)} collective-permute-done((bf16[80,256]{1,0:T(8,128)(2,1)S(1)}, bf16[80,256]{1,0:T(8,128)(2,1)S(1)}, u32[]{:S(2)}, u32[]{:S(2)}) %collective-permute-start.4) | collective-permute-done | bytes 40992 | tf_op jit(solution)/shard_map/ppermute | solution.py:202
  14.1 0.0 collective-permute-start.10
  14.1 0.0 collective-permute-done.8.refs_1_
  14.1 1.0 %collective-permute-start.9 = (bf16[1,256,256]{2,1,0:T(8,128)(2,1)S(1)}, bf16[1,256,256]{2,1,0:T(8,128)(2,1)S(1)}, u32[]{:S(2)}, u32[]{:S(2)}) collective-permute-start(bf16[1,256,256]{2,1,0:T(8,128)(2,1)S(1)} %collective-permute-done.8.refs_1_), channel_id=1, source_target_pairs={{0,1},{1,0},{2,3},{3,2},{4,5},{5,4},{6,7},{7,6},{8,9},{9,8},{10,11... | collective-permute-start | bytes 393224 | tf_op jit(solution)/shard_map/ppermute | solution.py:236
  15.1 0.0 collective-permute-done.6.refs_3_
  15.1 0.0 collective-permute-done.7.refs_7_
  15.1 0.0 collective-permute-done.5.refs_1_.refs_4_
  15.1 0.0 copy-start
  15.1 1.1 %stage.1.sum_ref = f32[64,32,256]{2,1,0:T(8,128)S(1)} custom-call(bf16[64,32,256]{2,1,0:T(8,128)(2,1)S(1)} %get-tuple-element.22.pumped_ref, f32[64,32,256]{2,1,0:T(8,128)S(1)} %get-tuple-element.30.sum_ref, bf16[1,256,256]{2,1,0:T(8,128)(2,1)S(1)} %collective-permute-done.refs_0_.refs_5_, ...), custom_call_target="tpu_custom_call", output_to_operand_aliasing={{}: (1, {})} | custom-call | flops 4000000000 | bytes 8388608 | tf_op jit(solution)/shard_map/stage/pallas_call | solution.py:252
  16.2 0.0 collective-permute-done.10.refs_3_
  16.2 0.0 collective-permute-done.9.refs_0_
  16.3 0.0 copy-done
  16.3 1.9 %last_stage.1 = f32[64,32,256]{2,1,0:T(8,128)} custom-call(bf16[64,32,256]{2,1,0:T(8,128)(2,1)S(1)} %get-tuple-element.22.pumped_ref, f32[64,32,256]{2,1,0:T(8,128)S(1)} %stage.1.sum_ref, bf16[256,256]{1,0:T(8,128)(2,1)S(1)} %copy-done, bf16[1,256,256]{2,1,0:T(8,128)(2,1)S(1)} %collective-permute-done.9.refs_0_, ...), custom_call_target="tpu_custom_call" | custom-call | tf_op jit(solution)/shard_map/last_stage/pallas_call | solution.py:267
Async XLA Ops:
  0.0 10.6 %collective-permute-start = (bf16[1,256,256]{2,1,0:T(8,128)(2,1)}, bf16[1,256,256]{2,1,0:T(8,128)(2,1)S(1)}, u32[]{:S(2)}, u32[]{:S(2)}) collective-permute-start(bf16[1,256,256]{2,1,0:T(8,128)(2,1)} %basis_ref.1), channel_id=1, source_target_pairs={{0,8},{1,5},{4,12},{5,1},{8,0},{9,13},{12,4},{13,9},{2,10},{3,7},{... | collective-permute-start | bytes 393224 | tf_op jit(solution)/shard_map/ppermute | solution.py:184
  4.7 6.5 %copy-start.1 = (bf16[128,32,256]{2,1,0:T(8,128)(2,1)S(1)}, bf16[128,32,256]{2,1,0:T(8,128)(2,1)}, u32[]{:S(2)}) copy-start(bf16[128,32,256]{2,1,0:T(8,128)(2,1)} %mortar_ref.1) | copy-start | bytes 6291460
  4.7 6.5 %copy-start.2 = (bf16[1,256,256]{2,1,0:T(8,128)(2,1)S(1)}, bf16[1,256,256]{2,1,0:T(8,128)(2,1)}, u32[]{:S(2)}) copy-start(bf16[1,256,256]{2,1,0:T(8,128)(2,1)} %basis_ref.1) | copy-start | bytes 393220
  4.7 6.5 %copy-start.3 = (bf16[128,256]{1,0:T(8,128)(2,1)S(1)}, bf16[128,256]{1,0:T(8,128)(2,1)}, u32[]{:S(2)}) copy-start(bf16[128,256]{1,0:T(8,128)(2,1)} %scale_ref.3) | copy-start | bytes 196612
  4.7 6.5 %copy-start.4 = (f32[32]{0:T(128)S(1)}, f32[32]{0:T(128)}, u32[]{:S(2)}) copy-start(f32[32]{0:T(128)} %param.10) | copy-start | bytes 388
  4.7 6.5 %copy-start.5 = (s32[32]{0:T(128)S(1)}, s32[32]{0:T(128)}, u32[]{:S(2)}) copy-start(s32[32]{0:T(128)} %param.11) | copy-start | bytes 388
  4.7 6.5 %copy-start.6 = (s32[128,1]{0,1:T(1,128)S(1)}, s32[128,1]{0,1:T(1,128)}, u32[]{:S(2)}) copy-start(s32[128,1]{0,1:T(1,128)} %param.12) | copy-start | bytes 1540
  4.7 6.5 %copy-start.7 = (s32[128]{0:T(128)S(1)}, s32[128]{0:T(128)}, u32[]{:S(2)}) copy-start(s32[128]{0:T(128)} %param.13) | copy-start | bytes 1540
  6.1 4.5 %collective-permute-start.1 = (bf16[80,256]{1,0:T(8,128)(2,1)S(1)}, bf16[80,256]{1,0:T(8,128)(2,1)S(1)}, u32[]{:S(2)}, u32[]{:S(2)}) collective-permute-start(bf16[80,256]{1,0:T(8,128)(2,1)S(1)} %get-tuple-element.20), channel_id=1, source_target_pairs={{0,1},{1,0},{2,3},{3,2},{4,5},{5,4},{6,7},{7,6},{8,9},{9,8},{10,11... | collective-permute-start | bytes 122888 | tf_op jit(solution)/shard_map/ppermute | solution.py:204
  6.2 5.0 %collective-permute-start.2 = (bf16[80,256]{1,0:T(8,128)(2,1)S(1)}, bf16[80,256]{1,0:T(8,128)(2,1)S(1)}, u32[]{:S(2)}, u32[]{:S(2)}) collective-permute-start(bf16[80,256]{1,0:T(8,128)(2,1)S(1)} %get-tuple-element.24), channel_id=1, source_target_pairs={{0,8},{4,12},{8,0},{12,4},{1,9},{5,13},{9,1},{13,5},{2,10},{6,14},... | collective-permute-start | bytes 122888 | tf_op jit(solution)/shard_map/ppermute | solution.py:202
  7.3 4.7 %collective-permute-start.3 = (bf16[80,256]{1,0:T(8,128)(2,1)S(1)}, bf16[80,256]{1,0:T(8,128)(2,1)S(1)}, u32[]{:S(2)}, u32[]{:S(2)}) collective-permute-start(bf16[80,256]{1,0:T(8,128)(2,1)S(1)} %get-tuple-element.26), channel_id=1, source_target_pairs={{0,4},{4,0},{8,12},{12,8},{1,5},{5,1},{9,13},{13,9},{2,6},{6,2},{1... | collective-permute-start | bytes 122888 | tf_op jit(solution)/shard_map/ppermute | solution.py:202
  8.1 5.9 %collective-permute-start.4 = (bf16[80,256]{1,0:T(8,128)(2,1)S(1)}, bf16[80,256]{1,0:T(8,128)(2,1)S(1)}, u32[]{:S(2)}, u32[]{:S(2)}) collective-permute-start(bf16[80,256]{1,0:T(8,128)(2,1)S(1)} %get-tuple-element.29), channel_id=1, source_target_pairs={{0,12},{4,8},{8,4},{12,0},{1,13},{5,9},{9,5},{13,1},{2,14},{6,10},... | collective-permute-start | bytes 122888 | tf_op jit(solution)/shard_map/ppermute | solution.py:202
  10.6 3.4 %collective-permute-start.8 = (bf16[1,256,256]{2,1,0:T(8,128)(2,1)S(1)}, bf16[1,256,256]{2,1,0:T(8,128)(2,1)S(1)}, u32[]{:S(2)}, u32[]{:S(2)}) collective-permute-start(bf16[1,256,256]{2,1,0:T(8,128)(2,1)S(1)} %collective-permute-done.refs_0_.refs_5_), channel_id=1, source_target_pairs={{0,5},{1,0},{4,1},{5,4},{8,13},{9,8},{12,9},{13,12},{2,7},{3,2},{6... | collective-permute-start | bytes 393224 | tf_op jit(solution)/shard_map/ppermute | solution.py:230
  11.2 3.9 %collective-permute-start.5 = (bf16[1,256,256]{2,1,0:T(8,128)(2,1)S(1)}, bf16[1,256,256]{2,1,0:T(8,128)(2,1)S(1)}, u32[]{:S(2)}, u32[]{:S(2)}) collective-permute-start(bf16[1,256,256]{2,1,0:T(8,128)(2,1)S(1)} %collective-permute-done.refs_0_.refs_5_), channel_id=1, source_target_pairs={{0,1},{1,0},{2,3},{3,2},{4,5},{5,4},{6,7},{7,6},{8,9},{9,8},{10,11... | collective-permute-start | bytes 393224 | tf_op jit(solution)/shard_map/ppermute | solution.py:232
  12.0 3.1 %collective-permute-start.6 = (bf16[80,256]{1,0:T(8,128)(2,1)S(1)}, bf16[80,256]{1,0:T(8,128)(2,1)S(1)}, u32[]{:S(2)}, u32[]{:S(2)}) collective-permute-start(bf16[80,256]{1,0:T(8,128)(2,1)S(1)} %collective-permute-done.2.refs_2_), channel_id=1, source_target_pairs={{0,1},{1,0},{2,3},{3,2},{4,5},{5,4},{6,7},{7,6},{8,9},{9,8},{10,11... | collective-permute-start | bytes 122888 | tf_op jit(solution)/shard_map/ppermute | solution.py:236
  12.6 2.5 %collective-permute-start.7 = (bf16[80,256]{1,0:T(8,128)(2,1)S(1)}, bf16[80,256]{1,0:T(8,128)(2,1)S(1)}, u32[]{:S(2)}, u32[]{:S(2)}) collective-permute-start(bf16[80,256]{1,0:T(8,128)(2,1)S(1)} %collective-permute-done.3.refs_6_), channel_id=1, source_target_pairs={{0,1},{1,0},{2,3},{3,2},{4,5},{5,4},{6,7},{7,6},{8,9},{9,8},{10,11... | collective-permute-start | bytes 122888 | tf_op jit(solution)/shard_map/ppermute | solution.py:236
  14.1 2.2 %collective-permute-start.10 = (bf16[80,256]{1,0:T(8,128)(2,1)S(1)}, bf16[80,256]{1,0:T(8,128)(2,1)S(1)}, u32[]{:S(2)}, u32[]{:S(2)}) collective-permute-start(bf16[80,256]{1,0:T(8,128)(2,1)S(1)} %collective-permute-done.4.refs_2_), channel_id=1, source_target_pairs={{0,1},{1,0},{2,3},{3,2},{4,5},{5,4},{6,7},{7,6},{8,9},{9,8},{10,11... | collective-permute-start | bytes 122888 | tf_op jit(solution)/shard_map/ppermute | solution.py:236
  14.1 2.2 %collective-permute-start.9 = (bf16[1,256,256]{2,1,0:T(8,128)(2,1)S(1)}, bf16[1,256,256]{2,1,0:T(8,128)(2,1)S(1)}, u32[]{:S(2)}, u32[]{:S(2)}) collective-permute-start(bf16[1,256,256]{2,1,0:T(8,128)(2,1)S(1)} %collective-permute-done.8.refs_1_), channel_id=1, source_target_pairs={{0,1},{1,0},{2,3},{3,2},{4,5},{5,4},{6,7},{7,6},{8,9},{9,8},{10,11... | collective-permute-start | bytes 393224 | tf_op jit(solution)/shard_map/ppermute | solution.py:236
  15.1 1.2 %copy-start = (bf16[256,256]{1,0:T(8,128)(2,1)S(1)}, bf16[256,256]{1,0:T(8,128)(2,1)}, u32[]{:S(2)}) copy-start(bf16[256,256]{1,0:T(8,128)(2,1)} %projection_ref.1) | copy-start | bytes 393220
